TPU v7x, 512 devices: a whole 4x4x16 slice. The times are simulated.
512 devices in a mesh: tm: 16 (over z_lo, x), space: 32 (over z_hi, y, core).
Axes of the slice: x: 4, y: 4, z: 16 (z_hi: 4, z_lo: 4; z = z_hi * 4 + z_lo), core: 2. Of those that a mesh axis runs over, the one named last changes fastest.
Arguments:
- end_state: float32 [16, 64, 512, 128], P('tm', 'space'), may hold values from -8 to 8, as said below
- cond: float32 [64, 512, 128], P('space'), may hold values from 0.2 to 2
- receivers: int32 [16, 256], P('tm'), may hold values from 0 to 4194303
- residuals: float32 [16, 256], P('tm'), may hold values from -6 to 6
Outputs:
- corrected: float32 [16, 64, 512, 128], P('tm', 'space')
Inputs may be any that keep to these rules, and one draw needn't show every extreme that they name: `end_state`: each slice's field is a rough part plus a part that varies slowly over the grid.
All inputs are finite; a program needn't handle non-finite values.
Results may differ from a plain program's by a relative error of at most 0.00002.
Values sent between devices are 32-bit elements; how exact they have to be, the bound alone decides.
No kernel may reach another device: no remote copies, remote signals or barrier semaphores. Data moves between devices by JAX's collectives and lax.ppermute only.
A program may use at most 64 MiB of HBM per device.

v0:
```python
import jax
import jax.numpy as jnp
from jax import lax
from jax.sharding import PartitionSpec as P

FINE_STEPS = 2
SWEEPS = 2


def with_halo(value, sides, width):
    for axis, dim in sides:
        size, length = (lax.axis_size(axis), value.shape[dim])
        up = [(i, (i + 1) % size) for i in range(size - 1)]
        down = [(j, i) for i, j in up]
        last = lax.slice_in_dim(value, length - width, length, axis=dim)
        initial = lax.slice_in_dim(value, 0, width, axis=dim)
        before = lax.ppermute(last, axis, up)
        after = lax.ppermute(initial, axis, down)
        value = jnp.concatenate([before, value, after], axis=dim)
    return value


def shifted(value, axis, by):
    size = lax.axis_size(axis)
    pairs = [(i, i + by) for i in range(size) if 0 <= i + by < size]
    return lax.ppermute(value, axis, pairs)


def neighbors(padded):
    center = padded[1:-1]
    beside_all = padded[2:] + padded[:-2]
    planes = jnp.pad(center, ((0, 0), (1, 1), (1, 1)))
    beside_all = beside_all + planes[:, 2:, 1:-1] + planes[:, :-2, 1:-1]
    beside_all = beside_all + planes[:, 1:-1, 2:] + planes[:, 1:-1, :-2]
    return beside_all


def restrict(field):
    blocks = field.reshape(field.shape[0] // 2, 2, field.shape[1] // 2, 2, field.shape[2] // 2, 2)
    return blocks.mean(axis=(1, 3, 5))


def prolong(coarse):
    return jnp.repeat(jnp.repeat(jnp.repeat(coarse, 2, axis=0), 2, axis=1), 2, axis=2)


def per_device(end_state, cond, receivers, residuals):
    start_field = end_state[0]
    row_count = start_field.shape[0]
    width_y = start_field.shape[1]
    width_z = start_field.shape[2]
    plane_size = width_y * width_z
    slab_index = lax.axis_index("space")
    slice_index = lax.axis_index("tm")
    slice_total = lax.axis_size("tm")
    first_row = slab_index * row_count
    cell_ids = receivers[0]
    values = residuals[0]
    local_row = cell_ids // plane_size - first_row
    inside = (local_row >= 0) & (local_row < row_count)
    target = jnp.where(
        inside, local_row * plane_size + cell_ids % plane_size, row_count * plane_size
    )
    flat_source = (
        jnp.zeros((row_count * plane_size,), jnp.float32).at[target].add(values, mode="drop")
    )
    source = flat_source.reshape(row_count, width_y, width_z)
    diagonal = cond + 6.0
    field_now = start_field
    for step_index in range(FINE_STEPS):
        rhs_term = cond * field_now + source
        for sweep_index in range(SWEEPS):
            padded = with_halo(field_now, (("space", 0),), 1)
            field_now = (rhs_term + neighbors(padded)) / diagonal
    coarse_cond = restrict(cond) / FINE_STEPS

    def coarse_propagate(coarse_state):
        diagonal = coarse_cond + 1.5
        rhs_term = coarse_cond * coarse_state
        for sweep_index in range(SWEEPS):
            padded = with_halo(coarse_state, (("space", 0),), 1)
            coarse_state = (rhs_term + 0.25 * neighbors(padded)) / diagonal
        return coarse_state

    start_coarse = restrict(start_field)
    correction = field_now - prolong(coarse_propagate(start_coarse))
    coarse_term = restrict(correction)
    is_final = slice_index == slice_total - 1
    zero_field = jnp.zeros_like(coarse_term)

    def chain_link(turn_index, carried):
        outgoing = carried[0]
        arriving = shifted(outgoing, "tm", -1)
        incoming = jnp.where(is_final, start_coarse, arriving)
        propagated = coarse_propagate(incoming)
        return (coarse_term + propagated, propagated)

    final_carry, propagated = lax.fori_loop(0, slice_total, chain_link, (zero_field, zero_field))
    corrected = prolong(propagated) + correction
    return corrected[None]


def solution(mesh):
    in_specs = (P("tm", "space", None, None), P("space", None, None), P("tm", None), P("tm", None))
    out_specs = P("tm", "space", None, None)
    return jax.shard_map(
        per_device, mesh=mesh, in_specs=in_specs, out_specs=out_specs, check_vma=False
    )
```

profile of v0, /device:TPU:390, one launch (start us, length us, event | category | flops | bytes accessed | tf_op | source)
XLA Modules:
  0.0 817.7 jit_solution(4284221717342796443)
XLA Ops:
  1.2 7.3 collective-permute-start.5
  13.4 7.4 collective-permute-done.5
  20.8 9.4 %collective-permute-done.6 = f32[1,512,128]{2,1,0:T(8,128)S(1)} collective-permute-done((f32[1,512,128]{2,1,0:T(8,128)S(1)}, f32[1,512,128]{2,1,0:T(8,128)S(1)}, u32[]{:S(2)}, u32[]{:S(2)}) %collective-permute-start.6) | collective-permute-done | bytes 262176 | tf_op jit(solution)/shard_map/ppermute | solution.py:17
  35.0 5.9 collective-permute-done.7
  40.9 7.3 collective-permute-done.8
  50.6 9.7 %collective-permute-start.9 = (f32[1,512,128]{2,1,0:T(8,128)S(1)}, f32[1,512,128]{2,1,0:T(8,128)S(1)}, u32[]{:S(2)}, u32[]{:S(2)}) collective-permute-start(f32[1,512,128]{2,1,0:T(8,128)S(1)} %get-tuple-element.138), channel_id=1, source_target_pairs={{1,0},{2,1},{3,2},{4,3},{5,4},{6,5},{7,6},{8,7},{9,8},{10,9},{11,1... | collective-permute-start | bytes 786440 | tf_op jit(solution)/shard_map/ppermute | solution.py:18
  60.3 18.1 %reduce_sum.37 = f32[256,2,64,2]{3,2,1,0:T(8,128)} reshape(f32[512,128]{1,0:T(8,128)S(1)} %reduce_sum.36) | data formatting | bytes 524288 | tf_op jit(solution)/shard_map/reduce_sum | solution.py:40
  78.4 8.0 reduce_sum.38
  91.2 18.1 %reduce_sum.40 = f32[256,2,64,2]{3,2,1,0:T(8,128)} reshape(f32[512,128]{1,0:T(8,128)S(1)} %get-tuple-element.137) | data formatting | bytes 524288 | tf_op jit(solution)/shard_map/reduce_sum | solution.py:40
  109.3 8.0 reduce_sum.44
  117.5 9.2 %collective-permute-start.15 = (f32[1,256,64]{2,1,0:T(8,128)S(1)}, f32[1,256,64]{2,1,0:T(8,128)S(1)}, u32[]{:S(2)}, u32[]{:S(2)}) collective-permute-start(f32[1,256,64]{2,1,0:T(8,128)S(1)} %add_divide_fusion.2), channel_id=1, source_target_pairs={{1,0},{2,1},{3,2},{4,3},{5,4},{6,5},{7,6},{8,7},{9,8},{10,9},{11,1... | collective-permute-start | bytes 196616 | tf_op jit(solution)/shard_map/ppermute | solution.py:18
  129.4 9.6 %collective-permute-start.11 = (f32[1,512,128]{2,1,0:T(8,128)}, f32[1,512,128]{2,1,0:T(8,128)S(1)}, u32[]{:S(2)}, u32[]{:S(2)}) collective-permute-start(f32[1,512,128]{2,1,0:T(8,128)} %get-tuple-element.134), channel_id=1, source_target_pairs={{1,0},{2,1},{3,2},{4,3},{5,4},{6,5},{7,6},{8,7},{9,8},{10,9},{11,1... | collective-permute-start | bytes 786440 | tf_op jit(solution)/shard_map/ppermute | solution.py:18
  142.0 7.6 collective-permute-done.11
  154.8 18.1 %reduce_sum.55 = f32[256,2,64,2]{3,2,1,0:T(8,128)} reshape(f32[512,128]{1,0:T(8,128)S(1)} %get-tuple-element.132) | data formatting | bytes 524288 | tf_op jit(solution)/shard_map/reduce_sum | solution.py:40
  172.9 8.0 reduce_sum.56
  180.9 634.4 %while.18 = (s32[]{:T(128)}, f32[1,256,64]{2,1,0:T(8,128)S(1)}, f32[1,256,64]{2,1,0:T(8,128)}, pred[]{:T(512)}, f32[1,256,64]{2,1,0:T(8,128)S(1)}, /*index=5*/f3...) while((s32[]{:T(128)}, f32[1,256,64]{2,1,0:T(8,128)S(1)}, ...), condition=%wide.region_8.9_spmd.clone, body=%wide.region_7.8_spmd.clone.sunk | while | flops 360451 | bytes 2556208 | solution.py:98
  183.7 6.2 collective-permute-done
  200.8 7.3 collective-permute-done.2
  214.8 9.9 %collective-permute-done.4 = f32[1,256,64]{2,1,0:T(8,128)S(1)} collective-permute-done((f32[1,256,64]{2,1,0:T(8,128)S(1)}, f32[1,256,64]{2,1,0:T(8,128)S(1)}, u32[]{:S(2)}, u32[]{:S(2)}) %collective-permute-start.4) | collective-permute-done | bytes 65568 | tf_op jit(solution)/shard_map/while/body/eval_jaxpr/ppermute | solution.py:17
  227.4 7.0 collective-permute-done
  243.1 8.2 %collective-permute-done.2 = f32[1,256,64]{2,1,0:T(8,128)S(1)} collective-permute-done((f32[1,256,64]{2,1,0:T(8,128)S(1)}, f32[1,256,64]{2,1,0:T(8,128)S(1)}, u32[]{:S(2)}, u32[]{:S(2)}) %collective-permute-start.2) | collective-permute-done | bytes 65568 | tf_op jit(solution)/shard_map/while/body/eval_jaxpr/ppermute | solution.py:17
  255.9 9.8 %collective-permute-done.4 = f32[1,256,64]{2,1,0:T(8,128)S(1)} collective-permute-done((f32[1,256,64]{2,1,0:T(8,128)S(1)}, f32[1,256,64]{2,1,0:T(8,128)S(1)}, u32[]{:S(2)}, u32[]{:S(2)}) %collective-permute-start.4) | collective-permute-done | bytes 65568 | tf_op jit(solution)/shard_map/while/body/eval_jaxpr/ppermute | solution.py:17
  268.4 7.0 collective-permute-done
  280.2 9.5 %collective-permute-done.2 = f32[1,256,64]{2,1,0:T(8,128)S(1)} collective-permute-done((f32[1,256,64]{2,1,0:T(8,128)S(1)}, f32[1,256,64]{2,1,0:T(8,128)S(1)}, u32[]{:S(2)}, u32[]{:S(2)}) %collective-permute-start.2) | collective-permute-done | bytes 65568 | tf_op jit(solution)/shard_map/while/body/eval_jaxpr/ppermute | solution.py:17
  294.3 9.8 %collective-permute-done.4 = f32[1,256,64]{2,1,0:T(8,128)S(1)} collective-permute-done((f32[1,256,64]{2,1,0:T(8,128)S(1)}, f32[1,256,64]{2,1,0:T(8,128)S(1)}, u32[]{:S(2)}, u32[]{:S(2)}) %collective-permute-start.4) | collective-permute-done | bytes 65568 | tf_op jit(solution)/shard_map/while/body/eval_jaxpr/ppermute | solution.py:17
  306.8 7.0 collective-permute-done
  318.3 9.8 %collective-permute-done.2 = f32[1,256,64]{2,1,0:T(8,128)S(1)} collective-permute-done((f32[1,256,64]{2,1,0:T(8,128)S(1)}, f32[1,256,64]{2,1,0:T(8,128)S(1)}, u32[]{:S(2)}, u32[]{:S(2)}) %collective-permute-start.2) | collective-permute-done | bytes 65568 | tf_op jit(solution)/shard_map/while/body/eval_jaxpr/ppermute | solution.py:17
  332.8 9.8 %collective-permute-done.4 = f32[1,256,64]{2,1,0:T(8,128)S(1)} collective-permute-done((f32[1,256,64]{2,1,0:T(8,128)S(1)}, f32[1,256,64]{2,1,0:T(8,128)S(1)}, u32[]{:S(2)}, u32[]{:S(2)}) %collective-permute-start.4) | collective-permute-done | bytes 65568 | tf_op jit(solution)/shard_map/while/body/eval_jaxpr/ppermute | solution.py:17
  345.3 7.0 collective-permute-done
  356.8 9.8 %collective-permute-done.2 = f32[1,256,64]{2,1,0:T(8,128)S(1)} collective-permute-done((f32[1,256,64]{2,1,0:T(8,128)S(1)}, f32[1,256,64]{2,1,0:T(8,128)S(1)}, u32[]{:S(2)}, u32[]{:S(2)}) %collective-permute-start.2) | collective-permute-done | bytes 65568 | tf_op jit(solution)/shard_map/while/body/eval_jaxpr/ppermute | solution.py:17
  371.2 9.8 %collective-permute-done.4 = f32[1,256,64]{2,1,0:T(8,128)S(1)} collective-permute-done((f32[1,256,64]{2,1,0:T(8,128)S(1)}, f32[1,256,64]{2,1,0:T(8,128)S(1)}, u32[]{:S(2)}, u32[]{:S(2)}) %collective-permute-start.4) | collective-permute-done | bytes 65568 | tf_op jit(solution)/shard_map/while/body/eval_jaxpr/ppermute | solution.py:17
  383.7 7.0 collective-permute-done
  395.2 9.8 %collective-permute-done.2 = f32[1,256,64]{2,1,0:T(8,128)S(1)} collective-permute-done((f32[1,256,64]{2,1,0:T(8,128)S(1)}, f32[1,256,64]{2,1,0:T(8,128)S(1)}, u32[]{:S(2)}, u32[]{:S(2)}) %collective-permute-start.2) | collective-permute-done | bytes 65568 | tf_op jit(solution)/shard_map/while/body/eval_jaxpr/ppermute | solution.py:17
  409.6 9.8 %collective-permute-done.4 = f32[1,256,64]{2,1,0:T(8,128)S(1)} collective-permute-done((f32[1,256,64]{2,1,0:T(8,128)S(1)}, f32[1,256,64]{2,1,0:T(8,128)S(1)}, u32[]{:S(2)}, u32[]{:S(2)}) %collective-permute-start.4) | collective-permute-done | bytes 65568 | tf_op jit(solution)/shard_map/while/body/eval_jaxpr/ppermute | solution.py:17
  422.7 8.0 collective-permute-done
  435.1 11.3 %collective-permute-done.2 = f32[1,256,64]{2,1,0:T(8,128)S(1)} collective-permute-done((f32[1,256,64]{2,1,0:T(8,128)S(1)}, f32[1,256,64]{2,1,0:T(8,128)S(1)}, u32[]{:S(2)}, u32[]{:S(2)}) %collective-permute-start.2) | collective-permute-done | bytes 65568 | tf_op jit(solution)/shard_map/while/body/eval_jaxpr/ppermute | solution.py:17
  451.0 11.2 %collective-permute-done.4 = f32[1,256,64]{2,1,0:T(8,128)S(1)} collective-permute-done((f32[1,256,64]{2,1,0:T(8,128)S(1)}, f32[1,256,64]{2,1,0:T(8,128)S(1)}, u32[]{:S(2)}, u32[]{:S(2)}) %collective-permute-start.4) | collective-permute-done | bytes 65568 | tf_op jit(solution)/shard_map/while/body/eval_jaxpr/ppermute | solution.py:17
  464.9 8.3 %collective-permute-done = f32[1,256,64]{2,1,0:T(8,128)S(1)} collective-permute-done((f32[1,256,64]{2,1,0:T(8,128)S(1)}, f32[1,256,64]{2,1,0:T(8,128)S(1)}, u32[]{:S(2)}, u32[]{:S(2)}) %collective-permute-start) | collective-permute-done | bytes 65568 | tf_op jit(solution)/shard_map/while/body/eval_jaxpr/ppermute | solution.py:26
  478.5 9.0 %collective-permute-done.2 = f32[1,256,64]{2,1,0:T(8,128)S(1)} collective-permute-done((f32[1,256,64]{2,1,0:T(8,128)S(1)}, f32[1,256,64]{2,1,0:T(8,128)S(1)}, u32[]{:S(2)}, u32[]{:S(2)}) %collective-permute-start.2) | collective-permute-done | bytes 65568 | tf_op jit(solution)/shard_map/while/body/eval_jaxpr/ppermute | solution.py:17
  492.9 9.0 %collective-permute-done.4 = f32[1,256,64]{2,1,0:T(8,128)S(1)} collective-permute-done((f32[1,256,64]{2,1,0:T(8,128)S(1)}, f32[1,256,64]{2,1,0:T(8,128)S(1)}, u32[]{:S(2)}, u32[]{:S(2)}) %collective-permute-start.4) | collective-permute-done | bytes 65568 | tf_op jit(solution)/shard_map/while/body/eval_jaxpr/ppermute | solution.py:17
  504.6 8.3 %collective-permute-done = f32[1,256,64]{2,1,0:T(8,128)S(1)} collective-permute-done((f32[1,256,64]{2,1,0:T(8,128)S(1)}, f32[1,256,64]{2,1,0:T(8,128)S(1)}, u32[]{:S(2)}, u32[]{:S(2)}) %collective-permute-start) | collective-permute-done | bytes 65568 | tf_op jit(solution)/shard_map/while/body/eval_jaxpr/ppermute | solution.py:26
  517.3 11.2 %collective-permute-done.2 = f32[1,256,64]{2,1,0:T(8,128)S(1)} collective-permute-done((f32[1,256,64]{2,1,0:T(8,128)S(1)}, f32[1,256,64]{2,1,0:T(8,128)S(1)}, u32[]{:S(2)}, u32[]{:S(2)}) %collective-permute-start.2) | collective-permute-done | bytes 65568 | tf_op jit(solution)/shard_map/while/body/eval_jaxpr/ppermute | solution.py:17
  533.1 9.8 %collective-permute-done.4 = f32[1,256,64]{2,1,0:T(8,128)S(1)} collective-permute-done((f32[1,256,64]{2,1,0:T(8,128)S(1)}, f32[1,256,64]{2,1,0:T(8,128)S(1)}, u32[]{:S(2)}, u32[]{:S(2)}) %collective-permute-start.4) | collective-permute-done | bytes 65568 | tf_op jit(solution)/shard_map/while/body/eval_jaxpr/ppermute | solution.py:17
  545.7 8.4 %collective-permute-done = f32[1,256,64]{2,1,0:T(8,128)S(1)} collective-permute-done((f32[1,256,64]{2,1,0:T(8,128)S(1)}, f32[1,256,64]{2,1,0:T(8,128)S(1)}, u32[]{:S(2)}, u32[]{:S(2)}) %collective-permute-start) | collective-permute-done | bytes 65568 | tf_op jit(solution)/shard_map/while/body/eval_jaxpr/ppermute | solution.py:26
  560.0 8.4 %collective-permute-done.2 = f32[1,256,64]{2,1,0:T(8,128)S(1)} collective-permute-done((f32[1,256,64]{2,1,0:T(8,128)S(1)}, f32[1,256,64]{2,1,0:T(8,128)S(1)}, u32[]{:S(2)}, u32[]{:S(2)}) %collective-permute-start.2) | collective-permute-done | bytes 65568 | tf_op jit(solution)/shard_map/while/body/eval_jaxpr/ppermute | solution.py:17
  573.0 9.8 %collective-permute-done.4 = f32[1,256,64]{2,1,0:T(8,128)S(1)} collective-permute-done((f32[1,256,64]{2,1,0:T(8,128)S(1)}, f32[1,256,64]{2,1,0:T(8,128)S(1)}, u32[]{:S(2)}, u32[]{:S(2)}) %collective-permute-start.4) | collective-permute-done | bytes 65568 | tf_op jit(solution)/shard_map/while/body/eval_jaxpr/ppermute | solution.py:17
  585.5 8.3 %collective-permute-done = f32[1,256,64]{2,1,0:T(8,128)S(1)} collective-permute-done((f32[1,256,64]{2,1,0:T(8,128)S(1)}, f32[1,256,64]{2,1,0:T(8,128)S(1)}, u32[]{:S(2)}, u32[]{:S(2)}) %collective-permute-start) | collective-permute-done | bytes 65568 | tf_op jit(solution)/shard_map/while/body/eval_jaxpr/ppermute | solution.py:26
  598.3 9.8 %collective-permute-done.2 = f32[1,256,64]{2,1,0:T(8,128)S(1)} collective-permute-done((f32[1,256,64]{2,1,0:T(8,128)S(1)}, f32[1,256,64]{2,1,0:T(8,128)S(1)}, u32[]{:S(2)}, u32[]{:S(2)}) %collective-permute-start.2) | collective-permute-done | bytes 65568 | tf_op jit(solution)/shard_map/while/body/eval_jaxpr/ppermute | solution.py:17
  612.6 9.8 %collective-permute-done.4 = f32[1,256,64]{2,1,0:T(8,128)S(1)} collective-permute-done((f32[1,256,64]{2,1,0:T(8,128)S(1)}, f32[1,256,64]{2,1,0:T(8,128)S(1)}, u32[]{:S(2)}, u32[]{:S(2)}) %collective-permute-start.4) | collective-permute-done | bytes 65568 | tf_op jit(solution)/shard_map/while/body/eval_jaxpr/ppermute | solution.py:17
  625.2 7.0 collective-permute-done
  636.7 9.8 %collective-permute-done.2 = f32[1,256,64]{2,1,0:T(8,128)S(1)} collective-permute-done((f32[1,256,64]{2,1,0:T(8,128)S(1)}, f32[1,256,64]{2,1,0:T(8,128)S(1)}, u32[]{:S(2)}, u32[]{:S(2)}) %collective-permute-start.2) | collective-permute-done | bytes 65568 | tf_op jit(solution)/shard_map/while/body/eval_jaxpr/ppermute | solution.py:17
  651.1 9.8 %collective-permute-done.4 = f32[1,256,64]{2,1,0:T(8,128)S(1)} collective-permute-done((f32[1,256,64]{2,1,0:T(8,128)S(1)}, f32[1,256,64]{2,1,0:T(8,128)S(1)}, u32[]{:S(2)}, u32[]{:S(2)}) %collective-permute-start.4) | collective-permute-done | bytes 65568 | tf_op jit(solution)/shard_map/while/body/eval_jaxpr/ppermute | solution.py:17
  663.6 7.1 collective-permute-done
  675.1 9.8 %collective-permute-done.2 = f32[1,256,64]{2,1,0:T(8,128)S(1)} collective-permute-done((f32[1,256,64]{2,1,0:T(8,128)S(1)}, f32[1,256,64]{2,1,0:T(8,128)S(1)}, u32[]{:S(2)}, u32[]{:S(2)}) %collective-permute-start.2) | collective-permute-done | bytes 65568 | tf_op jit(solution)/shard_map/while/body/eval_jaxpr/ppermute | solution.py:17
  689.5 9.8 %collective-permute-done.4 = f32[1,256,64]{2,1,0:T(8,128)S(1)} collective-permute-done((f32[1,256,64]{2,1,0:T(8,128)S(1)}, f32[1,256,64]{2,1,0:T(8,128)S(1)}, u32[]{:S(2)}, u32[]{:S(2)}) %collective-permute-start.4) | collective-permute-done | bytes 65568 | tf_op jit(solution)/shard_map/while/body/eval_jaxpr/ppermute | solution.py:17
  702.1 7.0 collective-permute-done
  713.6 9.8 %collective-permute-done.2 = f32[1,256,64]{2,1,0:T(8,128)S(1)} collective-permute-done((f32[1,256,64]{2,1,0:T(8,128)S(1)}, f32[1,256,64]{2,1,0:T(8,128)S(1)}, u32[]{:S(2)}, u32[]{:S(2)}) %collective-permute-start.2) | collective-permute-done | bytes 65568 | tf_op jit(solution)/shard_map/while/body/eval_jaxpr/ppermute | solution.py:17
  727.9 9.8 %collective-permute-done.4 = f32[1,256,64]{2,1,0:T(8,128)S(1)} collective-permute-done((f32[1,256,64]{2,1,0:T(8,128)S(1)}, f32[1,256,64]{2,1,0:T(8,128)S(1)}, u32[]{:S(2)}, u32[]{:S(2)}) %collective-permute-start.4) | collective-permute-done | bytes 65568 | tf_op jit(solution)/shard_map/while/body/eval_jaxpr/ppermute | solution.py:17
  740.5 7.0 collective-permute-done
  752.0 9.8 %collective-permute-done.2 = f32[1,256,64]{2,1,0:T(8,128)S(1)} collective-permute-done((f32[1,256,64]{2,1,0:T(8,128)S(1)}, f32[1,256,64]{2,1,0:T(8,128)S(1)}, u32[]{:S(2)}, u32[]{:S(2)}) %collective-permute-start.2) | collective-permute-done | bytes 65568 | tf_op jit(solution)/shard_map/while/body/eval_jaxpr/ppermute | solution.py:17
  766.4 9.8 %collective-permute-done.4 = f32[1,256,64]{2,1,0:T(8,128)S(1)} collective-permute-done((f32[1,256,64]{2,1,0:T(8,128)S(1)}, f32[1,256,64]{2,1,0:T(8,128)S(1)}, u32[]{:S(2)}, u32[]{:S(2)}) %collective-permute-start.4) | collective-permute-done | bytes 65568 | tf_op jit(solution)/shard_map/while/body/eval_jaxpr/ppermute | solution.py:17
  778.9 7.0 collective-permute-done
  790.4 9.8 %collective-permute-done.2 = f32[1,256,64]{2,1,0:T(8,128)S(1)} collective-permute-done((f32[1,256,64]{2,1,0:T(8,128)S(1)}, f32[1,256,64]{2,1,0:T(8,128)S(1)}, u32[]{:S(2)}, u32[]{:S(2)}) %collective-permute-start.2) | collective-permute-done | bytes 65568 | tf_op jit(solution)/shard_map/while/body/eval_jaxpr/ppermute | solution.py:17
  804.8 9.8 %collective-permute-done.4 = f32[1,256,64]{2,1,0:T(8,128)S(1)} collective-permute-done((f32[1,256,64]{2,1,0:T(8,128)S(1)}, f32[1,256,64]{2,1,0:T(8,128)S(1)}, u32[]{:S(2)}, u32[]{:S(2)}) %collective-permute-start.4) | collective-permute-done | bytes 65568 | tf_op jit(solution)/shard_map/while/body/eval_jaxpr/ppermute | solution.py:17
  (226 shorter events, 236.0 us)
Async XLA Ops:
  1.2 19.7 %collective-permute-start.5 = (f32[1,512,128]{2,1,0:T(8,128)S(1)}, f32[1,512,128]{2,1,0:T(8,128)S(1)}, u32[]{:S(2)}, u32[]{:S(2)}) collective-permute-start(f32[1,512,128]{2,1,0:T(8,128)S(1)} %get-tuple-element.142), channel_id=1, source_target_pairs={{1,0},{2,1},{3,2},{4,3},{5,4},{6,5},{7,6},{8,7},{9,8},{10,9},{11,1... | collective-permute-start | bytes 786440 | tf_op jit(solution)/shard_map/ppermute | solution.py:18
  8.5 21.7 %collective-permute-start.6 = (f32[1,512,128]{2,1,0:T(8,128)S(1)}, f32[1,512,128]{2,1,0:T(8,128)S(1)}, u32[]{:S(2)}, u32[]{:S(2)}) collective-permute-start(f32[1,512,128]{2,1,0:T(8,128)S(1)} %get-tuple-element.143), channel_id=1, source_target_pairs={{0,1},{1,2},{2,3},{3,4},{4,5},{5,6},{6,7},{7,8},{8,9},{9,10},{10,1... | collective-permute-start | bytes 786440 | tf_op jit(solution)/shard_map/ppermute | solution.py:17
  30.7 10.2 %collective-permute-start.7 = (f32[1,512,128]{2,1,0:T(8,128)S(1)}, f32[1,512,128]{2,1,0:T(8,128)S(1)}, u32[]{:S(2)}, u32[]{:S(2)}) collective-permute-start(f32[1,512,128]{2,1,0:T(8,128)S(1)} %get-tuple-element.140), channel_id=1, source_target_pairs={{1,0},{2,1},{3,2},{4,3},{5,4},{6,5},{7,6},{8,7},{9,8},{10,9},{11,1... | collective-permute-start | bytes 786440 | tf_op jit(solution)/shard_map/ppermute | solution.py:18
  32.6 15.6 %collective-permute-start.8 = (f32[1,512,128]{2,1,0:T(8,128)S(1)}, f32[1,512,128]{2,1,0:T(8,128)S(1)}, u32[]{:S(2)}, u32[]{:S(2)}) collective-permute-start(f32[1,512,128]{2,1,0:T(8,128)S(1)} %get-tuple-element.141), channel_id=1, source_target_pairs={{0,1},{1,2},{2,3},{3,4},{4,5},{5,6},{6,7},{7,8},{8,9},{9,10},{10,1... | collective-permute-start | bytes 786440 | tf_op jit(solution)/shard_map/ppermute | solution.py:17
  48.7 42.1 %collective-permute-start.10 = (f32[1,512,128]{2,1,0:T(8,128)S(1)}, f32[1,512,128]{2,1,0:T(8,128)S(1)}, u32[]{:S(2)}, u32[]{:S(2)}) collective-permute-start(f32[1,512,128]{2,1,0:T(8,128)S(1)} %get-tuple-element.139), channel_id=1, source_target_pairs={{0,1},{1,2},{2,3},{3,4},{4,5},{5,6},{6,7},{7,8},{8,9},{9,10},{10,1... | collective-permute-start | bytes 786440 | tf_op jit(solution)/shard_map/ppermute | solution.py:17
  50.6 40.2 %collective-permute-start.9 = (f32[1,512,128]{2,1,0:T(8,128)S(1)}, f32[1,512,128]{2,1,0:T(8,128)S(1)}, u32[]{:S(2)}, u32[]{:S(2)}) collective-permute-start(f32[1,512,128]{2,1,0:T(8,128)S(1)} %get-tuple-element.138), channel_id=1, source_target_pairs={{1,0},{2,1},{3,2},{4,3},{5,4},{6,5},{7,6},{8,7},{9,8},{10,9},{11,1... | collective-permute-start | bytes 786440 | tf_op jit(solution)/shard_map/ppermute | solution.py:18
  86.4 30.9 %collective-permute-start.13 = (f32[1,256,64]{2,1,0:T(8,128)S(1)}, f32[1,256,64]{2,1,0:T(8,128)S(1)}, u32[]{:S(2)}, u32[]{:S(2)}) collective-permute-start(f32[1,256,64]{2,1,0:T(8,128)S(1)} %multiply_bitcast_fusion.2), channel_id=1, source_target_pairs={{1,0},{2,1},{3,2},{4,3},{5,4},{6,5},{7,6},{8,7},{9,8},{10,9},{11,1... | collective-permute-start | bytes 196616 | tf_op jit(solution)/shard_map/ppermute | solution.py:18
  88.4 29.0 %collective-permute-start.14 = (f32[1,256,64]{2,1,0:T(8,128)S(1)}, f32[1,256,64]{2,1,0:T(8,128)S(1)}, u32[]{:S(2)}, u32[]{:S(2)}) collective-permute-start(f32[1,256,64]{2,1,0:T(8,128)S(1)} %multiply_bitcast_fusion.2), channel_id=1, source_target_pairs={{0,1},{1,2},{2,3},{3,4},{4,5},{5,6},{6,7},{7,8},{8,9},{9,10},{10,1... | collective-permute-start | bytes 196616 | tf_op jit(solution)/shard_map/ppermute | solution.py:17
  117.5 23.7 %collective-permute-start.15 = (f32[1,256,64]{2,1,0:T(8,128)S(1)}, f32[1,256,64]{2,1,0:T(8,128)S(1)}, u32[]{:S(2)}, u32[]{:S(2)}) collective-permute-start(f32[1,256,64]{2,1,0:T(8,128)S(1)} %add_divide_fusion.2), channel_id=1, source_target_pairs={{1,0},{2,1},{3,2},{4,3},{5,4},{6,5},{7,6},{8,7},{9,8},{10,9},{11,1... | collective-permute-start | bytes 196616 | tf_op jit(solution)/shard_map/ppermute | solution.py:18
  126.7 14.5 %collective-permute-start.16 = (f32[1,256,64]{2,1,0:T(8,128)S(1)}, f32[1,256,64]{2,1,0:T(8,128)S(1)}, u32[]{:S(2)}, u32[]{:S(2)}) collective-permute-start(f32[1,256,64]{2,1,0:T(8,128)S(1)} %add_divide_fusion.2), channel_id=1, source_target_pairs={{0,1},{1,2},{2,3},{3,4},{4,5},{5,6},{6,7},{7,8},{8,9},{9,10},{10,1... | collective-permute-start | bytes 196616 | tf_op jit(solution)/shard_map/ppermute | solution.py:17
  129.4 20.2 %collective-permute-start.11 = (f32[1,512,128]{2,1,0:T(8,128)}, f32[1,512,128]{2,1,0:T(8,128)S(1)}, u32[]{:S(2)}, u32[]{:S(2)}) collective-permute-start(f32[1,512,128]{2,1,0:T(8,128)} %get-tuple-element.134), channel_id=1, source_target_pairs={{1,0},{2,1},{3,2},{4,3},{5,4},{6,5},{7,6},{8,7},{9,8},{10,9},{11,1... | collective-permute-start | bytes 786440 | tf_op jit(solution)/shard_map/ppermute | solution.py:18
  139.1 14.3 %collective-permute-start.12 = (f32[1,512,128]{2,1,0:T(8,128)}, f32[1,512,128]{2,1,0:T(8,128)}, u32[]{:S(2)}, u32[]{:S(2)}) collective-permute-start(f32[1,512,128]{2,1,0:T(8,128)} %get-tuple-element.135), channel_id=1, source_target_pairs={{0,1},{1,2},{2,3},{3,4},{4,5},{5,6},{6,7},{7,8},{8,9},{9,10},{10,1... | collective-permute-start | bytes 786440 | tf_op jit(solution)/shard_map/ppermute | solution.py:17
  181.0 9.0 %collective-permute-start = (f32[1,256,64]{2,1,0:T(8,128)S(1)}, f32[1,256,64]{2,1,0:T(8,128)S(1)}, u32[]{:S(2)}, u32[]{:S(2)}) collective-permute-start(f32[1,256,64]{2,1,0:T(8,128)S(1)} %broadcast_select_fusion.4), channel_id=1, source_target_pairs={{32,0},{64,32},{96,64},{128,96},{160,128},{192,160},{224,192},{256... | collective-permute-start | bytes 196616 | tf_op jit(solution)/shard_map/while/body/eval_jaxpr/ppermute | solution.py:26
  190.0 10.8 %collective-permute-start.1 = (f32[1,256,64]{2,1,0:T(8,128)S(1)}, f32[1,256,64]{2,1,0:T(8,128)S(1)}, u32[]{:S(2)}, u32[]{:S(2)}) collective-permute-start(f32[1,256,64]{2,1,0:T(8,128)S(1)} %broadcast_select_fusion.5), channel_id=1, source_target_pairs={{1,0},{2,1},{3,2},{4,3},{5,4},{6,5},{7,6},{8,7},{9,8},{10,9},{11,1... | collective-permute-start | bytes 196616 | tf_op jit(solution)/shard_map/while/body/eval_jaxpr/ppermute | solution.py:18
  195.6 12.5 %collective-permute-start.2 = (f32[1,256,64]{2,1,0:T(8,128)S(1)}, f32[1,256,64]{2,1,0:T(8,128)S(1)}, u32[]{:S(2)}, u32[]{:S(2)}) collective-permute-start(f32[1,256,64]{2,1,0:T(8,128)S(1)} %broadcast_select_fusion.5), channel_id=1, source_target_pairs={{0,1},{1,2},{2,3},{3,4},{4,5},{5,6},{6,7},{7,8},{8,9},{9,10},{10,1... | collective-permute-start | bytes 196616 | tf_op jit(solution)/shard_map/while/body/eval_jaxpr/ppermute | solution.py:17
  208.3 6.5 collective-permute-start.3
  210.9 13.8 %collective-permute-start.4 = (f32[1,256,64]{2,1,0:T(8,128)S(1)}, f32[1,256,64]{2,1,0:T(8,128)S(1)}, u32[]{:S(2)}, u32[]{:S(2)}) collective-permute-start(f32[1,256,64]{2,1,0:T(8,128)S(1)} %get-tuple-element.190), channel_id=1, source_target_pairs={{0,1},{1,2},{2,3},{3,4},{4,5},{5,6},{6,7},{7,8},{8,9},{9,10},{10,1... | collective-permute-start | bytes 196616 | tf_op jit(solution)/shard_map/while/body/eval_jaxpr/ppermute | solution.py:17
  225.4 9.0 %collective-permute-start = (f32[1,256,64]{2,1,0:T(8,128)S(1)}, f32[1,256,64]{2,1,0:T(8,128)S(1)}, u32[]{:S(2)}, u32[]{:S(2)}) collective-permute-start(f32[1,256,64]{2,1,0:T(8,128)S(1)} %broadcast_select_fusion.4), channel_id=1, source_target_pairs={{32,0},{64,32},{96,64},{128,96},{160,128},{192,160},{224,192},{256... | collective-permute-start | bytes 196616 | tf_op jit(solution)/shard_map/while/body/eval_jaxpr/ppermute | solution.py:26
  234.4 8.6 %collective-permute-start.1 = (f32[1,256,64]{2,1,0:T(8,128)S(1)}, f32[1,256,64]{2,1,0:T(8,128)S(1)}, u32[]{:S(2)}, u32[]{:S(2)}) collective-permute-start(f32[1,256,64]{2,1,0:T(8,128)S(1)} %broadcast_select_fusion.5), channel_id=1, source_target_pairs={{1,0},{2,1},{3,2},{4,3},{5,4},{6,5},{7,6},{8,7},{9,8},{10,9},{11,1... | collective-permute-start | bytes 196616 | tf_op jit(solution)/shard_map/while/body/eval_jaxpr/ppermute | solution.py:18
  236.4 14.9 %collective-permute-start.2 = (f32[1,256,64]{2,1,0:T(8,128)S(1)}, f32[1,256,64]{2,1,0:T(8,128)S(1)}, u32[]{:S(2)}, u32[]{:S(2)}) collective-permute-start(f32[1,256,64]{2,1,0:T(8,128)S(1)} %broadcast_select_fusion.5), channel_id=1, source_target_pairs={{0,1},{1,2},{2,3},{3,4},{4,5},{5,6},{6,7},{7,8},{8,9},{9,10},{10,1... | collective-permute-start | bytes 196616 | tf_op jit(solution)/shard_map/while/body/eval_jaxpr/ppermute | solution.py:17
  253.4 12.3 %collective-permute-start.4 = (f32[1,256,64]{2,1,0:T(8,128)S(1)}, f32[1,256,64]{2,1,0:T(8,128)S(1)}, u32[]{:S(2)}, u32[]{:S(2)}) collective-permute-start(f32[1,256,64]{2,1,0:T(8,128)S(1)} %get-tuple-element.190), channel_id=1, source_target_pairs={{0,1},{1,2},{2,3},{3,4},{4,5},{5,6},{6,7},{7,8},{8,9},{9,10},{10,1... | collective-permute-start | bytes 196616 | tf_op jit(solution)/shard_map/while/body/eval_jaxpr/ppermute | solution.py:17
  266.5 9.0 %collective-permute-start = (f32[1,256,64]{2,1,0:T(8,128)S(1)}, f32[1,256,64]{2,1,0:T(8,128)S(1)}, u32[]{:S(2)}, u32[]{:S(2)}) collective-permute-start(f32[1,256,64]{2,1,0:T(8,128)S(1)} %broadcast_select_fusion.4), channel_id=1, source_target_pairs={{32,0},{64,32},{96,64},{128,96},{160,128},{192,160},{224,192},{256... | collective-permute-start | bytes 196616 | tf_op jit(solution)/shard_map/while/body/eval_jaxpr/ppermute | solution.py:26
  277.4 12.3 %collective-permute-start.2 = (f32[1,256,64]{2,1,0:T(8,128)S(1)}, f32[1,256,64]{2,1,0:T(8,128)S(1)}, u32[]{:S(2)}, u32[]{:S(2)}) collective-permute-start(f32[1,256,64]{2,1,0:T(8,128)S(1)} %broadcast_select_fusion.5), channel_id=1, source_target_pairs={{0,1},{1,2},{2,3},{3,4},{4,5},{5,6},{6,7},{7,8},{8,9},{9,10},{10,1... | collective-permute-start | bytes 196616 | tf_op jit(solution)/shard_map/while/body/eval_jaxpr/ppermute | solution.py:17
  291.8 12.3 %collective-permute-start.4 = (f32[1,256,64]{2,1,0:T(8,128)S(1)}, f32[1,256,64]{2,1,0:T(8,128)S(1)}, u32[]{:S(2)}, u32[]{:S(2)}) collective-permute-start(f32[1,256,64]{2,1,0:T(8,128)S(1)} %get-tuple-element.190), channel_id=1, source_target_pairs={{0,1},{1,2},{2,3},{3,4},{4,5},{5,6},{6,7},{7,8},{8,9},{9,10},{10,1... | collective-permute-start | bytes 196616 | tf_op jit(solution)/shard_map/while/body/eval_jaxpr/ppermute | solution.py:17
  304.9 9.0 %collective-permute-start = (f32[1,256,64]{2,1,0:T(8,128)S(1)}, f32[1,256,64]{2,1,0:T(8,128)S(1)}, u32[]{:S(2)}, u32[]{:S(2)}) collective-permute-start(f32[1,256,64]{2,1,0:T(8,128)S(1)} %broadcast_select_fusion.4), channel_id=1, source_target_pairs={{32,0},{64,32},{96,64},{128,96},{160,128},{192,160},{224,192},{256... | collective-permute-start | bytes 196616 | tf_op jit(solution)/shard_map/while/body/eval_jaxpr/ppermute | solution.py:26
  315.8 12.3 %collective-permute-start.2 = (f32[1,256,64]{2,1,0:T(8,128)S(1)}, f32[1,256,64]{2,1,0:T(8,128)S(1)}, u32[]{:S(2)}, u32[]{:S(2)}) collective-permute-start(f32[1,256,64]{2,1,0:T(8,128)S(1)} %broadcast_select_fusion.5), channel_id=1, source_target_pairs={{0,1},{1,2},{2,3},{3,4},{4,5},{5,6},{6,7},{7,8},{8,9},{9,10},{10,1... | collective-permute-start | bytes 196616 | tf_op jit(solution)/shard_map/while/body/eval_jaxpr/ppermute | solution.py:17
  330.3 12.3 %collective-permute-start.4 = (f32[1,256,64]{2,1,0:T(8,128)S(1)}, f32[1,256,64]{2,1,0:T(8,128)S(1)}, u32[]{:S(2)}, u32[]{:S(2)}) collective-permute-start(f32[1,256,64]{2,1,0:T(8,128)S(1)} %get-tuple-element.190), channel_id=1, source_target_pairs={{0,1},{1,2},{2,3},{3,4},{4,5},{5,6},{6,7},{7,8},{8,9},{9,10},{10,1... | collective-permute-start | bytes 196616 | tf_op jit(solution)/shard_map/while/body/eval_jaxpr/ppermute | solution.py:17
  343.4 9.0 %collective-permute-start = (f32[1,256,64]{2,1,0:T(8,128)S(1)}, f32[1,256,64]{2,1,0:T(8,128)S(1)}, u32[]{:S(2)}, u32[]{:S(2)}) collective-permute-start(f32[1,256,64]{2,1,0:T(8,128)S(1)} %broadcast_select_fusion.4), channel_id=1, source_target_pairs={{32,0},{64,32},{96,64},{128,96},{160,128},{192,160},{224,192},{256... | collective-permute-start | bytes 196616 | tf_op jit(solution)/shard_map/while/body/eval_jaxpr/ppermute | solution.py:26
  354.3 12.3 %collective-permute-start.2 = (f32[1,256,64]{2,1,0:T(8,128)S(1)}, f32[1,256,64]{2,1,0:T(8,128)S(1)}, u32[]{:S(2)}, u32[]{:S(2)}) collective-permute-start(f32[1,256,64]{2,1,0:T(8,128)S(1)} %broadcast_select_fusion.5), channel_id=1, source_target_pairs={{0,1},{1,2},{2,3},{3,4},{4,5},{5,6},{6,7},{7,8},{8,9},{9,10},{10,1... | collective-permute-start | bytes 196616 | tf_op jit(solution)/shard_map/while/body/eval_jaxpr/ppermute | solution.py:17
  368.7 12.3 %collective-permute-start.4 = (f32[1,256,64]{2,1,0:T(8,128)S(1)}, f32[1,256,64]{2,1,0:T(8,128)S(1)}, u32[]{:S(2)}, u32[]{:S(2)}) collective-permute-start(f32[1,256,64]{2,1,0:T(8,128)S(1)} %get-tuple-element.190), channel_id=1, source_target_pairs={{0,1},{1,2},{2,3},{3,4},{4,5},{5,6},{6,7},{7,8},{8,9},{9,10},{10,1... | collective-permute-start | bytes 196616 | tf_op jit(solution)/shard_map/while/body/eval_jaxpr/ppermute | solution.py:17
  381.8 9.0 %collective-permute-start = (f32[1,256,64]{2,1,0:T(8,128)S(1)}, f32[1,256,64]{2,1,0:T(8,128)S(1)}, u32[]{:S(2)}, u32[]{:S(2)}) collective-permute-start(f32[1,256,64]{2,1,0:T(8,128)S(1)} %broadcast_select_fusion.4), channel_id=1, source_target_pairs={{32,0},{64,32},{96,64},{128,96},{160,128},{192,160},{224,192},{256... | collective-permute-start | bytes 196616 | tf_op jit(solution)/shard_map/while/body/eval_jaxpr/ppermute | solution.py:26
  392.7 12.3 %collective-permute-start.2 = (f32[1,256,64]{2,1,0:T(8,128)S(1)}, f32[1,256,64]{2,1,0:T(8,128)S(1)}, u32[]{:S(2)}, u32[]{:S(2)}) collective-permute-start(f32[1,256,64]{2,1,0:T(8,128)S(1)} %broadcast_select_fusion.5), channel_id=1, source_target_pairs={{0,1},{1,2},{2,3},{3,4},{4,5},{5,6},{6,7},{7,8},{8,9},{9,10},{10,1... | collective-permute-start | bytes 196616 | tf_op jit(solution)/shard_map/while/body/eval_jaxpr/ppermute | solution.py:17
  407.1 12.3 %collective-permute-start.4 = (f32[1,256,64]{2,1,0:T(8,128)S(1)}, f32[1,256,64]{2,1,0:T(8,128)S(1)}, u32[]{:S(2)}, u32[]{:S(2)}) collective-permute-start(f32[1,256,64]{2,1,0:T(8,128)S(1)} %get-tuple-element.190), channel_id=1, source_target_pairs={{0,1},{1,2},{2,3},{3,4},{4,5},{5,6},{6,7},{7,8},{8,9},{9,10},{10,1... | collective-permute-start | bytes 196616 | tf_op jit(solution)/shard_map/while/body/eval_jaxpr/ppermute | solution.py:17
  420.2 10.5 %collective-permute-start = (f32[1,256,64]{2,1,0:T(8,128)S(1)}, f32[1,256,64]{2,1,0:T(8,128)S(1)}, u32[]{:S(2)}, u32[]{:S(2)}) collective-permute-start(f32[1,256,64]{2,1,0:T(8,128)S(1)} %broadcast_select_fusion.4), channel_id=1, source_target_pairs={{32,0},{64,32},{96,64},{128,96},{160,128},{192,160},{224,192},{256... | collective-permute-start | bytes 196616 | tf_op jit(solution)/shard_map/while/body/eval_jaxpr/ppermute | solution.py:26
  432.6 13.8 %collective-permute-start.2 = (f32[1,256,64]{2,1,0:T(8,128)S(1)}, f32[1,256,64]{2,1,0:T(8,128)S(1)}, u32[]{:S(2)}, u32[]{:S(2)}) collective-permute-start(f32[1,256,64]{2,1,0:T(8,128)S(1)} %broadcast_select_fusion.5), channel_id=1, source_target_pairs={{0,1},{1,2},{2,3},{3,4},{4,5},{5,6},{6,7},{7,8},{8,9},{9,10},{10,1... | collective-permute-start | bytes 196616 | tf_op jit(solution)/shard_map/while/body/eval_jaxpr/ppermute | solution.py:17
  448.5 13.7 %collective-permute-start.4 = (f32[1,256,64]{2,1,0:T(8,128)S(1)}, f32[1,256,64]{2,1,0:T(8,128)S(1)}, u32[]{:S(2)}, u32[]{:S(2)}) collective-permute-start(f32[1,256,64]{2,1,0:T(8,128)S(1)} %get-tuple-element.190), channel_id=1, source_target_pairs={{0,1},{1,2},{2,3},{3,4},{4,5},{5,6},{6,7},{7,8},{8,9},{9,10},{10,1... | collective-permute-start | bytes 196616 | tf_op jit(solution)/shard_map/while/body/eval_jaxpr/ppermute | solution.py:17
  463.0 10.3 %collective-permute-start = (f32[1,256,64]{2,1,0:T(8,128)S(1)}, f32[1,256,64]{2,1,0:T(8,128)S(1)}, u32[]{:S(2)}, u32[]{:S(2)}) collective-permute-start(f32[1,256,64]{2,1,0:T(8,128)S(1)} %broadcast_select_fusion.4), channel_id=1, source_target_pairs={{32,0},{64,32},{96,64},{128,96},{160,128},{192,160},{224,192},{256... | collective-permute-start | bytes 196616 | tf_op jit(solution)/shard_map/while/body/eval_jaxpr/ppermute | solution.py:26
  475.2 12.3 %collective-permute-start.2 = (f32[1,256,64]{2,1,0:T(8,128)S(1)}, f32[1,256,64]{2,1,0:T(8,128)S(1)}, u32[]{:S(2)}, u32[]{:S(2)}) collective-permute-start(f32[1,256,64]{2,1,0:T(8,128)S(1)} %broadcast_select_fusion.5), channel_id=1, source_target_pairs={{0,1},{1,2},{2,3},{3,4},{4,5},{5,6},{6,7},{7,8},{8,9},{9,10},{10,1... | collective-permute-start | bytes 196616 | tf_op jit(solution)/shard_map/while/body/eval_jaxpr/ppermute | solution.py:17
  489.6 12.3 %collective-permute-start.4 = (f32[1,256,64]{2,1,0:T(8,128)S(1)}, f32[1,256,64]{2,1,0:T(8,128)S(1)}, u32[]{:S(2)}, u32[]{:S(2)}) collective-permute-start(f32[1,256,64]{2,1,0:T(8,128)S(1)} %get-tuple-element.190), channel_id=1, source_target_pairs={{0,1},{1,2},{2,3},{3,4},{4,5},{5,6},{6,7},{7,8},{8,9},{9,10},{10,1... | collective-permute-start | bytes 196616 | tf_op jit(solution)/shard_map/while/body/eval_jaxpr/ppermute | solution.py:17
  502.7 10.2 %collective-permute-start = (f32[1,256,64]{2,1,0:T(8,128)S(1)}, f32[1,256,64]{2,1,0:T(8,128)S(1)}, u32[]{:S(2)}, u32[]{:S(2)}) collective-permute-start(f32[1,256,64]{2,1,0:T(8,128)S(1)} %broadcast_select_fusion.4), channel_id=1, source_target_pairs={{32,0},{64,32},{96,64},{128,96},{160,128},{192,160},{224,192},{256... | collective-permute-start | bytes 196616 | tf_op jit(solution)/shard_map/while/body/eval_jaxpr/ppermute | solution.py:26
  514.8 13.7 %collective-permute-start.2 = (f32[1,256,64]{2,1,0:T(8,128)S(1)}, f32[1,256,64]{2,1,0:T(8,128)S(1)}, u32[]{:S(2)}, u32[]{:S(2)}) collective-permute-start(f32[1,256,64]{2,1,0:T(8,128)S(1)} %broadcast_select_fusion.5), channel_id=1, source_target_pairs={{0,1},{1,2},{2,3},{3,4},{4,5},{5,6},{6,7},{7,8},{8,9},{9,10},{10,1... | collective-permute-start | bytes 196616 | tf_op jit(solution)/shard_map/while/body/eval_jaxpr/ppermute | solution.py:17
  530.6 12.3 %collective-permute-start.4 = (f32[1,256,64]{2,1,0:T(8,128)S(1)}, f32[1,256,64]{2,1,0:T(8,128)S(1)}, u32[]{:S(2)}, u32[]{:S(2)}) collective-permute-start(f32[1,256,64]{2,1,0:T(8,128)S(1)} %get-tuple-element.190), channel_id=1, source_target_pairs={{0,1},{1,2},{2,3},{3,4},{4,5},{5,6},{6,7},{7,8},{8,9},{9,10},{10,1... | collective-permute-start | bytes 196616 | tf_op jit(solution)/shard_map/while/body/eval_jaxpr/ppermute | solution.py:17
  543.7 10.4 %collective-permute-start = (f32[1,256,64]{2,1,0:T(8,128)S(1)}, f32[1,256,64]{2,1,0:T(8,128)S(1)}, u32[]{:S(2)}, u32[]{:S(2)}) collective-permute-start(f32[1,256,64]{2,1,0:T(8,128)S(1)} %broadcast_select_fusion.4), channel_id=1, source_target_pairs={{32,0},{64,32},{96,64},{128,96},{160,128},{192,160},{224,192},{256... | collective-permute-start | bytes 196616 | tf_op jit(solution)/shard_map/while/body/eval_jaxpr/ppermute | solution.py:26
  554.1 5.8 collective-permute-start.1
  556.1 12.3 %collective-permute-start.2 = (f32[1,256,64]{2,1,0:T(8,128)S(1)}, f32[1,256,64]{2,1,0:T(8,128)S(1)}, u32[]{:S(2)}, u32[]{:S(2)}) collective-permute-start(f32[1,256,64]{2,1,0:T(8,128)S(1)} %broadcast_select_fusion.5), channel_id=1, source_target_pairs={{0,1},{1,2},{2,3},{3,4},{4,5},{5,6},{6,7},{7,8},{8,9},{9,10},{10,1... | collective-permute-start | bytes 196616 | tf_op jit(solution)/shard_map/while/body/eval_jaxpr/ppermute | solution.py:17
  570.5 12.3 %collective-permute-start.4 = (f32[1,256,64]{2,1,0:T(8,128)S(1)}, f32[1,256,64]{2,1,0:T(8,128)S(1)}, u32[]{:S(2)}, u32[]{:S(2)}) collective-permute-start(f32[1,256,64]{2,1,0:T(8,128)S(1)} %get-tuple-element.190), channel_id=1, source_target_pairs={{0,1},{1,2},{2,3},{3,4},{4,5},{5,6},{6,7},{7,8},{8,9},{9,10},{10,1... | collective-permute-start | bytes 196616 | tf_op jit(solution)/shard_map/while/body/eval_jaxpr/ppermute | solution.py:17
  583.6 10.2 %collective-permute-start = (f32[1,256,64]{2,1,0:T(8,128)S(1)}, f32[1,256,64]{2,1,0:T(8,128)S(1)}, u32[]{:S(2)}, u32[]{:S(2)}) collective-permute-start(f32[1,256,64]{2,1,0:T(8,128)S(1)} %broadcast_select_fusion.4), channel_id=1, source_target_pairs={{32,0},{64,32},{96,64},{128,96},{160,128},{192,160},{224,192},{256... | collective-permute-start | bytes 196616 | tf_op jit(solution)/shard_map/while/body/eval_jaxpr/ppermute | solution.py:26
  595.8 12.3 %collective-permute-start.2 = (f32[1,256,64]{2,1,0:T(8,128)S(1)}, f32[1,256,64]{2,1,0:T(8,128)S(1)}, u32[]{:S(2)}, u32[]{:S(2)}) collective-permute-start(f32[1,256,64]{2,1,0:T(8,128)S(1)} %broadcast_select_fusion.5), channel_id=1, source_target_pairs={{0,1},{1,2},{2,3},{3,4},{4,5},{5,6},{6,7},{7,8},{8,9},{9,10},{10,1... | collective-permute-start | bytes 196616 | tf_op jit(solution)/shard_map/while/body/eval_jaxpr/ppermute | solution.py:17
  610.1 12.3 %collective-permute-start.4 = (f32[1,256,64]{2,1,0:T(8,128)S(1)}, f32[1,256,64]{2,1,0:T(8,128)S(1)}, u32[]{:S(2)}, u32[]{:S(2)}) collective-permute-start(f32[1,256,64]{2,1,0:T(8,128)S(1)} %get-tuple-element.190), channel_id=1, source_target_pairs={{0,1},{1,2},{2,3},{3,4},{4,5},{5,6},{6,7},{7,8},{8,9},{9,10},{10,1... | collective-permute-start | bytes 196616 | tf_op jit(solution)/shard_map/while/body/eval_jaxpr/ppermute | solution.py:17
  623.3 9.0 %collective-permute-start = (f32[1,256,64]{2,1,0:T(8,128)S(1)}, f32[1,256,64]{2,1,0:T(8,128)S(1)}, u32[]{:S(2)}, u32[]{:S(2)}) collective-permute-start(f32[1,256,64]{2,1,0:T(8,128)S(1)} %broadcast_select_fusion.4), channel_id=1, source_target_pairs={{32,0},{64,32},{96,64},{128,96},{160,128},{192,160},{224,192},{256... | collective-permute-start | bytes 196616 | tf_op jit(solution)/shard_map/while/body/eval_jaxpr/ppermute | solution.py:26
  634.2 12.3 %collective-permute-start.2 = (f32[1,256,64]{2,1,0:T(8,128)S(1)}, f32[1,256,64]{2,1,0:T(8,128)S(1)}, u32[]{:S(2)}, u32[]{:S(2)}) collective-permute-start(f32[1,256,64]{2,1,0:T(8,128)S(1)} %broadcast_select_fusion.5), channel_id=1, source_target_pairs={{0,1},{1,2},{2,3},{3,4},{4,5},{5,6},{6,7},{7,8},{8,9},{9,10},{10,1... | collective-permute-start | bytes 196616 | tf_op jit(solution)/shard_map/while/body/eval_jaxpr/ppermute | solution.py:17
  648.6 12.3 %collective-permute-start.4 = (f32[1,256,64]{2,1,0:T(8,128)S(1)}, f32[1,256,64]{2,1,0:T(8,128)S(1)}, u32[]{:S(2)}, u32[]{:S(2)}) collective-permute-start(f32[1,256,64]{2,1,0:T(8,128)S(1)} %get-tuple-element.190), channel_id=1, source_target_pairs={{0,1},{1,2},{2,3},{3,4},{4,5},{5,6},{6,7},{7,8},{8,9},{9,10},{10,1... | collective-permute-start | bytes 196616 | tf_op jit(solution)/shard_map/while/body/eval_jaxpr/ppermute | solution.py:17
  661.7 9.0 %collective-permute-start = (f32[1,256,64]{2,1,0:T(8,128)S(1)}, f32[1,256,64]{2,1,0:T(8,128)S(1)}, u32[]{:S(2)}, u32[]{:S(2)}) collective-permute-start(f32[1,256,64]{2,1,0:T(8,128)S(1)} %broadcast_select_fusion.4), channel_id=1, source_target_pairs={{32,0},{64,32},{96,64},{128,96},{160,128},{192,160},{224,192},{256... | collective-permute-start | bytes 196616 | tf_op jit(solution)/shard_map/while/body/eval_jaxpr/ppermute | solution.py:26
  672.6 12.3 %collective-permute-start.2 = (f32[1,256,64]{2,1,0:T(8,128)S(1)}, f32[1,256,64]{2,1,0:T(8,128)S(1)}, u32[]{:S(2)}, u32[]{:S(2)}) collective-permute-start(f32[1,256,64]{2,1,0:T(8,128)S(1)} %broadcast_select_fusion.5), channel_id=1, source_target_pairs={{0,1},{1,2},{2,3},{3,4},{4,5},{5,6},{6,7},{7,8},{8,9},{9,10},{10,1... | collective-permute-start | bytes 196616 | tf_op jit(solution)/shard_map/while/body/eval_jaxpr/ppermute | solution.py:17
  687.0 12.3 %collective-permute-start.4 = (f32[1,256,64]{2,1,0:T(8,128)S(1)}, f32[1,256,64]{2,1,0:T(8,128)S(1)}, u32[]{:S(2)}, u32[]{:S(2)}) collective-permute-start(f32[1,256,64]{2,1,0:T(8,128)S(1)} %get-tuple-element.190), channel_id=1, source_target_pairs={{0,1},{1,2},{2,3},{3,4},{4,5},{5,6},{6,7},{7,8},{8,9},{9,10},{10,1... | collective-permute-start | bytes 196616 | tf_op jit(solution)/shard_map/while/body/eval_jaxpr/ppermute | solution.py:17
  700.1 9.0 %collective-permute-start = (f32[1,256,64]{2,1,0:T(8,128)S(1)}, f32[1,256,64]{2,1,0:T(8,128)S(1)}, u32[]{:S(2)}, u32[]{:S(2)}) collective-permute-start(f32[1,256,64]{2,1,0:T(8,128)S(1)} %broadcast_select_fusion.4), channel_id=1, source_target_pairs={{32,0},{64,32},{96,64},{128,96},{160,128},{192,160},{224,192},{256... | collective-permute-start | bytes 196616 | tf_op jit(solution)/shard_map/while/body/eval_jaxpr/ppermute | solution.py:26
  711.1 12.3 %collective-permute-start.2 = (f32[1,256,64]{2,1,0:T(8,128)S(1)}, f32[1,256,64]{2,1,0:T(8,128)S(1)}, u32[]{:S(2)}, u32[]{:S(2)}) collective-permute-start(f32[1,256,64]{2,1,0:T(8,128)S(1)} %broadcast_select_fusion.5), channel_id=1, source_target_pairs={{0,1},{1,2},{2,3},{3,4},{4,5},{5,6},{6,7},{7,8},{8,9},{9,10},{10,1... | collective-permute-start | bytes 196616 | tf_op jit(solution)/shard_map/while/body/eval_jaxpr/ppermute | solution.py:17
  725.4 12.3 %collective-permute-start.4 = (f32[1,256,64]{2,1,0:T(8,128)S(1)}, f32[1,256,64]{2,1,0:T(8,128)S(1)}, u32[]{:S(2)}, u32[]{:S(2)}) collective-permute-start(f32[1,256,64]{2,1,0:T(8,128)S(1)} %get-tuple-element.190), channel_id=1, source_target_pairs={{0,1},{1,2},{2,3},{3,4},{4,5},{5,6},{6,7},{7,8},{8,9},{9,10},{10,1... | collective-permute-start | bytes 196616 | tf_op jit(solution)/shard_map/while/body/eval_jaxpr/ppermute | solution.py:17
  738.6 9.0 %collective-permute-start = (f32[1,256,64]{2,1,0:T(8,128)S(1)}, f32[1,256,64]{2,1,0:T(8,128)S(1)}, u32[]{:S(2)}, u32[]{:S(2)}) collective-permute-start(f32[1,256,64]{2,1,0:T(8,128)S(1)} %broadcast_select_fusion.4), channel_id=1, source_target_pairs={{32,0},{64,32},{96,64},{128,96},{160,128},{192,160},{224,192},{256... | collective-permute-start | bytes 196616 | tf_op jit(solution)/shard_map/while/body/eval_jaxpr/ppermute | solution.py:26
  749.5 12.3 %collective-permute-start.2 = (f32[1,256,64]{2,1,0:T(8,128)S(1)}, f32[1,256,64]{2,1,0:T(8,128)S(1)}, u32[]{:S(2)}, u32[]{:S(2)}) collective-permute-start(f32[1,256,64]{2,1,0:T(8,128)S(1)} %broadcast_select_fusion.5), channel_id=1, source_target_pairs={{0,1},{1,2},{2,3},{3,4},{4,5},{5,6},{6,7},{7,8},{8,9},{9,10},{10,1... | collective-permute-start | bytes 196616 | tf_op jit(solution)/shard_map/while/body/eval_jaxpr/ppermute | solution.py:17
  763.9 12.3 %collective-permute-start.4 = (f32[1,256,64]{2,1,0:T(8,128)S(1)}, f32[1,256,64]{2,1,0:T(8,128)S(1)}, u32[]{:S(2)}, u32[]{:S(2)}) collective-permute-start(f32[1,256,64]{2,1,0:T(8,128)S(1)} %get-tuple-element.190), channel_id=1, source_target_pairs={{0,1},{1,2},{2,3},{3,4},{4,5},{5,6},{6,7},{7,8},{8,9},{9,10},{10,1... | collective-permute-start | bytes 196616 | tf_op jit(solution)/shard_map/while/body/eval_jaxpr/ppermute | solution.py:17
  777.0 9.0 %collective-permute-start = (f32[1,256,64]{2,1,0:T(8,128)S(1)}, f32[1,256,64]{2,1,0:T(8,128)S(1)}, u32[]{:S(2)}, u32[]{:S(2)}) collective-permute-start(f32[1,256,64]{2,1,0:T(8,128)S(1)} %broadcast_select_fusion.4), channel_id=1, source_target_pairs={{32,0},{64,32},{96,64},{128,96},{160,128},{192,160},{224,192},{256... | collective-permute-start | bytes 196616 | tf_op jit(solution)/shard_map/while/body/eval_jaxpr/ppermute | solution.py:26
  787.9 12.3 %collective-permute-start.2 = (f32[1,256,64]{2,1,0:T(8,128)S(1)}, f32[1,256,64]{2,1,0:T(8,128)S(1)}, u32[]{:S(2)}, u32[]{:S(2)}) collective-permute-start(f32[1,256,64]{2,1,0:T(8,128)S(1)} %broadcast_select_fusion.5), channel_id=1, source_target_pairs={{0,1},{1,2},{2,3},{3,4},{4,5},{5,6},{6,7},{7,8},{8,9},{9,10},{10,1... | collective-permute-start | bytes 196616 | tf_op jit(solution)/shard_map/while/body/eval_jaxpr/ppermute | solution.py:17
  802.3 12.3 %collective-permute-start.4 = (f32[1,256,64]{2,1,0:T(8,128)S(1)}, f32[1,256,64]{2,1,0:T(8,128)S(1)}, u32[]{:S(2)}, u32[]{:S(2)}) collective-permute-start(f32[1,256,64]{2,1,0:T(8,128)S(1)} %get-tuple-element.190), channel_id=1, source_target_pairs={{0,1},{1,2},{2,3},{3,4},{4,5},{5,6},{6,7},{7,8},{8,9},{9,10},{10,1... | collective-permute-start | bytes 196616 | tf_op jit(solution)/shard_map/while/body/eval_jaxpr/ppermute | solution.py:17
  (31 other events, 187.1 us)
where the time goes:
time: 824 us; the launch traced here: 818 us
  waiting for transfers between devices  485 us (59%)
  starting transfers between devices  226 us (27%)
  local copies, waits for them, and re-layouts  59.1 us (7%)
  other arithmetic  46.3 us (6%)
    ppermute x38, waiting for transfers between devices, with_halo(): before = lax.ppermute(last, axis, up)  330 us
    ppermute x16, waiting for transfers between devices, shifted(): return lax.ppermute(value, axis, pairs)  118 us
    ppermute x38, starting transfers between devices, with_halo(): after = lax.ppermute(initial, axis, down)  106 us
    ppermute x38, starting transfers between devices, with_halo(): before = lax.ppermute(last, axis, up)  88.7 us
    reduce_sum x3, local copies, waits for them, and re-layouts, restrict(): return blocks.mean(axis=(1, 3, 5))  54.3 us
    ppermute x38, waiting for transfers between devices, with_halo(): after = lax.ppermute(initial, axis, down)  36.4 us
    ppermute x16, starting transfers between devices, shifted(): return lax.ppermute(value, axis, pairs)  32.1 us
    reduce_sum x5, other arithmetic, restrict(): return blocks.mean(axis=(1, 3, 5))  25.5 us
  transfers between devices with their start and end apart: 92, of which 86 were waited for; matrix products, arithmetic and copies ran while one was open for 7% of the time, Pallas kernels for 0%

commit v1 on v0

v1 whole, which is shorter than its diff:
```python
import jax
import jax.numpy as jnp
from jax import lax
from jax.experimental import pallas as pl
from jax.experimental.pallas import tpu as pltpu
from jax.sharding import PartitionSpec as P

FINE_STEPS = 2
SWEEPS = 2
SLABS = 32
SLICES = 16
PLANE = 128
BLOCK = 4
EXACT = lax.Precision.HIGHEST


def params():
    return pltpu.CompilerParams(vmem_limit_bytes=40 * 1024 * 1024)


def halving(half):
    row = lax.broadcasted_iota(jnp.int32, (128, 128), 0)
    lane = lax.broadcasted_iota(jnp.int32, (128, 128), 1)
    return jnp.where(lane == row // 2 + 64 * half, 0.125, 0.0).astype(jnp.float32)


def restrict_kernel(field_ref, out_ref):
    total = jnp.zeros((PLANE, 128), jnp.float32)
    for half in range(2):
        rows = None
        for plane in range(2):
            for r in range(2):
                part = field_ref[plane, pl.ds(2 * half + r, PLANE, stride=4), :]
                rows = part if rows is None else rows + part
        total = total + jnp.dot(rows, halving(half), precision=EXACT, preferred_element_type=jnp.float32)
    out_ref[...] = total


def restrict(field):
    return pl.pallas_call(
        restrict_kernel,
        out_shape=jax.ShapeDtypeStruct((PLANE, 128), jnp.float32),
        compiler_params=params(),
    )(field)


def prolong_add_kernel(delta_ref, field_ref, out_ref):
    row = lax.broadcasted_iota(jnp.int32, (128, 128), 0)
    lane = lax.broadcasted_iota(jnp.int32, (128, 128), 1)
    delta = delta_ref[...]
    for half in range(2):
        spread = jnp.where(row == lane // 2 + 64 * half, 1.0, 0.0).astype(jnp.float32)
        wide = jnp.dot(delta, spread, precision=EXACT, preferred_element_type=jnp.float32)
        for plane in range(2):
            for r in range(2):
                rows = pl.ds(2 * half + r, PLANE, stride=4)
                out_ref[plane, rows, :] = field_ref[plane, rows, :] + wide


def prolong_add(delta, field):
    return pl.pallas_call(
        prolong_add_kernel,
        out_shape=jax.ShapeDtypeStruct(field.shape, jnp.float32),
        compiler_params=params(),
    )(delta, field)


def lanes_of(shape):
    lane = lax.broadcasted_iota(jnp.int32, shape, len(shape) - 1)
    return lane < 64, lane % 64


def beside_z(value, z):
    before = jnp.where(z == 0, 0.0, pltpu.roll(value, 1, 1))
    after = jnp.where(z == 63, 0.0, pltpu.roll(value, 127, 1))
    return before + after


def plane_sweep_kernel(state_ref, start_ref, before_ref, after_ref, keep_ref, spread_ref, out_ref):
    value = state_ref[...]
    low, z = lanes_of(value.shape)
    row = lax.broadcasted_iota(jnp.int32, value.shape, 0)
    swapped = pltpu.roll(value, 64, 1)
    earlier = jnp.where(row == 0, 0.0, pltpu.roll(swapped, 1, 0))
    later = jnp.where(row == PLANE - 1, 0.0, pltpu.roll(swapped, PLANE - 1, 0))
    total = before_ref[...] + after_ref[...] + swapped + jnp.where(low, earlier, later) + beside_z(value, z)
    out_ref[...] = keep_ref[...] * start_ref[...] + spread_ref[...] * total


def plane_sweep(state, start, before, after, keep, spread):
    return pl.pallas_call(
        plane_sweep_kernel,
        out_shape=jax.ShapeDtypeStruct(state.shape, jnp.float32),
        compiler_params=params(),
    )(state, start, before, after, keep, spread)


def sweep_rows(source, start, keep, spread, target, first, last, low_end, high_end):
    shape = (SLABS, 128)
    low, z = lanes_of(shape)
    x = lax.broadcasted_iota(jnp.int32, shape, 0)
    zero = jnp.zeros(shape, jnp.float32)

    def swapped(q):
        return pltpu.roll(source[q], 64, 1) if low_end <= q < high_end else zero

    earlier, here = swapped(first - 1), swapped(first)
    for q in range(first, last):
        later = swapped(q + 1)
        value = source[q]
        total = here + jnp.where(low, earlier, later) + beside_z(value, z)
        total = total + jnp.where(x == 0, 0.0, pltpu.roll(value, 1, 0))
        total = total + jnp.where(x == SLABS - 1, 0.0, pltpu.roll(value, SLABS - 1, 0))
        target[q] = keep[q] * start[q] + spread[q] * total
        earlier, here = here, later


def coarse_step(fields, keep, spread, at, low_end, high_end):
    start, middle, result = fields.at[at], fields.at[2], fields.at[1 - at]
    sweep_rows(start, start, keep, spread, middle, low_end, high_end, low_end, high_end)
    sweep_rows(middle, start, keep, spread, result, low_end + 1, high_end - 1, low_end, high_end)
    return 1 - at


def first_links_kernel(c4_ref, c3_ref, c2_ref, c1_ref, keep_ref, spread_ref, out_ref, fields):
    rows = c4_ref.shape[0]
    fields[0] = c4_ref[...]
    at, low_end, high_end = 0, 0, rows
    for added in (c3_ref, c2_ref, c1_ref, None):
        at = coarse_step(fields, keep_ref, spread_ref, at, low_end, high_end)
        low_end, high_end = low_end + 1, high_end - 1
        if added is not None:
            for q in range(low_end, high_end):
                fields[at, q] = fields[at, q] + added[q - low_end]
    out_ref[...] = fields[at, low_end:high_end]


def power_kernel(links, window_ref, base_ref, keep_ref, spread_ref, out_ref, fields):
    rows = window_ref.shape[0]
    fields[0] = window_ref[...]
    at = 0
    for link in range(links):
        at = coarse_step(fields, keep_ref, spread_ref, at, link, rows - link)
    out_ref[...] = base_ref[...] + fields[at, links : rows - links]


def chain_call(kernel, rows, *operands):
    return pl.pallas_call(
        kernel,
        out_shape=jax.ShapeDtypeStruct((BLOCK, SLABS, 128), jnp.float32),
        scratch_shapes=[pltpu.VMEM((3, rows, SLABS, 128), jnp.float32)],
        compiler_params=params(),
    )(*operands)


def facing(distance, late):
    pairs = []
    for i in range(SLABS - distance):
        if (i // distance) % 2 == late:
            pairs += [(i, i + distance), (i + distance, i)]
    return pairs


def from_later(value, links, pairs):
    both = [((n + links) * SLABS + i, n * SLABS + j) for n in range(SLICES - links) for i, j in pairs]
    return lax.ppermute(value, ("tm", "space"), both)


def beside_later(value, links, distance, slab):
    one = from_later(value, links, facing(distance, 0))
    other = from_later(value, links, facing(distance, 1))
    upper = (slab // distance) % 2 == 1
    return jnp.where(upper, one, other), jnp.where(upper, other, one)


def windows(plane, reach):
    blocks = plane.reshape(SLABS, BLOCK, 128)
    padded = jnp.pad(blocks, ((reach, reach), (0, 0), (0, 0)))
    return jnp.concatenate([padded[i : i + SLABS] for i in range(2 * reach + 1)], axis=1)


def to_rows(plane, reach):
    arrived = lax.all_to_all(windows(plane, reach), "space", 0, 0)
    return jnp.transpose(arrived, (1, 0, 2))


def inside_planes(padded):
    center = padded[1:-1]
    beside_all = padded[2:] + padded[:-2]
    planes = jnp.pad(center, ((0, 0), (1, 1), (1, 1)))
    beside_all = beside_all + planes[:, 2:, 1:-1] + planes[:, :-2, 1:-1]
    beside_all = beside_all + planes[:, 1:-1, 2:] + planes[:, 1:-1, :-2]
    return beside_all


def per_device(end_state, cond, receivers, residuals):
    start_field = end_state[0]
    row_count, width_y, width_z = start_field.shape
    plane_size = width_y * width_z
    slab = lax.axis_index("space")
    slice_index = lax.axis_index("tm")
    odd = slab % 2 == 1
    is_final = slice_index == SLICES - 1

    def trade(first, last):
        across = lax.ppermute(jnp.where(odd, last, first), "space", facing(1, 1))
        along = lax.ppermute(jnp.where(odd, first, last), "space", facing(1, 0))
        return jnp.where(odd, along, across), jnp.where(odd, across, along)

    local_row = receivers[0] // plane_size - slab * row_count
    inside = (local_row >= 0) & (local_row < row_count)
    target = jnp.where(inside, local_row * plane_size + receivers[0] % plane_size, row_count * plane_size)
    flat_source = jnp.zeros((row_count * plane_size,), jnp.float32).at[target].add(residuals[0], mode="drop")
    source = flat_source.reshape(row_count, width_y, width_z)

    coarse_cond = restrict(cond) / FINE_STEPS
    plane_spread = 1.0 / (coarse_cond + 1.5)
    plane_keep = coarse_cond * plane_spread
    plane_spread = 0.25 * plane_spread
    row_cond = to_rows(coarse_cond, 2)
    place = (slab - 2) * BLOCK + lax.broadcasted_iota(jnp.int32, row_cond.shape, 0)
    within = (place >= 0) & (place < PLANE)
    row_spread = jnp.where(within, 1.0 / (row_cond + 1.5), 0.0)
    row_keep = row_cond * row_spread
    row_spread = 0.25 * row_spread

    diagonal = cond + 6.0
    field_now = start_field
    coarse_start = restrict(start_field)
    coarse_now = coarse_start
    sweep = 0
    for step_index in range(FINE_STEPS):
        rhs_term = cond * field_now + source
        for sweep_index in range(SWEEPS):
            first, last = field_now[0], field_now[1]
            if sweep in (1, 2):
                first = jnp.concatenate([first, coarse_now])
                last = jnp.concatenate([last, coarse_now])
            before, after = trade(first, last)
            padded = jnp.concatenate([before[None, :width_y], field_now, after[None, :width_y]])
            field_now = (rhs_term + inside_planes(padded)) / diagonal
            if sweep in (1, 2):
                coarse_now = plane_sweep(
                    coarse_now, coarse_start, before[width_y:], after[width_y:], plane_keep, plane_spread
                )
            sweep += 1
    direct = coarse_now

    term = restrict(field_now) - jnp.where(is_final, 0.0, direct)
    rows = to_rows(term, 1)
    later = [(i, i) for i in range(SLABS)]
    links = [from_later(rows[4 - k : 8 + k], k, later) for k in (4, 3, 2, 1)]
    inner = slice(BLOCK, 4 * BLOCK)
    total = chain_call(first_links_kernel, 12, *links, row_keep[inner], row_spread[inner])

    centre = from_later(total, 4, later)
    before, after = beside_later(total, 4, 1, slab)
    window = jnp.concatenate([before, centre, after])
    total = chain_call(
        lambda *refs: power_kernel(4, *refs), 12, window, total, row_keep[inner], row_spread[inner]
    )

    centre = from_later(total, 8, later)
    before, after = beside_later(total, 8, 1, slab)
    before_two, after_two = beside_later(total, 8, 2, slab)
    window = jnp.concatenate([before_two, before, centre, after, after_two])
    total = chain_call(lambda *refs: power_kernel(8, *refs), 20, window, total, row_keep, row_spread)

    back = lax.all_to_all(jnp.transpose(total, (1, 0, 2)), "space", 0, 0)
    propagated = jnp.where(is_final, direct, back.reshape(PLANE, 128))
    return prolong_add(propagated - direct, field_now)[None]


def solution(mesh):
    in_specs = (P("tm", "space", None, None), P("space", None, None), P("tm", None), P("tm", None))
    out_specs = P("tm", "space", None, None)
    return jax.shard_map(
        per_device, mesh=mesh, in_specs=in_specs, out_specs=out_specs, check_vma=False
    )
```

time: 824 us -> 224 us (0.27)
  the two profiles are of different devices: /device:TPU:390 before, /device:TPU:7 now
where the time goes in v1:
time: 224 us; the launch traced here: 223 us
  starting transfers between devices  107 us (48%)
  waiting for transfers between devices  63.2 us (28%)
  blocking collectives  34.5 us (15%)
  other arithmetic  8.16 us (4%)
  Pallas kernels  6.7 us (3%)
  local copies, waits for them, and re-layouts  3.48 us (2%)
    all_to_all x2, starting transfers between devices, to_rows(): arrived = lax.all_to_all(windows(plane, reach), 'space', 0, 0)  65.4 us
    all_to_all x1, blocking collectives, per_device(): back = lax.all_to_all(jnp.transpose(total, (1, 0, 2)), 'space', 0, 0)  34.5 us
    all_to_all x2, waiting for transfers between devices, to_rows(): arrived = lax.all_to_all(windows(plane, reach), 'space', 0, 0)  32.1 us
    ppermute x12, waiting for transfers between devices, from_later(): return lax.ppermute(value, ('tm', 'space'), both)  23.4 us
    ppermute x12, starting transfers between devices, from_later(): return lax.ppermute(value, ('tm', 'space'), both)  17.4 us
    ppermute x4, starting transfers between devices, trade(): across = lax.ppermute(jnp.where(odd, last, first), 'space', facing(1, 1))  16.2 us
    ppermute x4, waiting for transfers between devices, trade(): across = lax.ppermute(jnp.where(odd, last, first), 'space', facing(1, 1))  7.69 us
    ppermute x4, starting transfers between devices, trade(): along = lax.ppermute(jnp.where(odd, first, last), 'space', facing(1, 0))  7.68 us
  transfers between devices with their start and end apart: 22, of which 12 were waited for; matrix products, arithmetic and copies ran while one was open for 2% of the time, Pallas kernels for 0%

profile of v1, /device:TPU:7, one launch (start us, length us, event | category | flops | bytes accessed | tf_op | source)
XLA Modules:
  0.0 223.3 jit_solution(10728492746883225478)
XLA Ops:
  0.0 1.1 select_bitcast_fusion.7
  1.1 0.0 copy-start.2
  1.1 3.8 %collective-permute-start = (f32[512,128]{1,0:T(8,128)S(1)}, f32[512,128]{1,0:T(8,128)S(1)}, u32[]{:S(2)}, u32[]{:S(2)}) collective-permute-start(f32[512,128]{1,0:T(8,128)S(1)} %get-tuple-element.23), channel_id=1, source_target_pairs={{1,2},{2,1},{3,4},{4,3},{5,6},{6,5},{7,8},{8,7},{9,10},{10,9},{11,... | collective-permute-start | bytes 786440 | tf_op jit(solution)/shard_map/ppermute | solution.py:206
  4.9 1.9 collective-permute-start.1
  6.9 0.3 shard_map.46.state_ref.start_ref
  7.2 2.2 scatter_custom_fusion
  9.4 0.0 copy-start
  9.4 0.0 collective-permute-done
  9.4 0.0 collective-permute-done.1
  9.5 1.0 copy-done
  10.5 0.4 fusion.5
  11.0 3.6 %collective-permute-start.3 = (f32[640,128]{1,0:T(8,128)S(1)}, f32[640,128]{1,0:T(8,128)S(1)}, u32[]{:S(2)}, u32[]{:S(2)}) collective-permute-start(f32[640,128]{1,0:T(8,128)S(1)} %get-tuple-element.11), channel_id=1, source_target_pairs={{1,2},{2,1},{3,4},{4,3},{5,6},{6,5},{7,8},{8,7},{9,10},{10,9},{11,... | collective-permute-start | bytes 983048 | tf_op jit(solution)/shard_map/ppermute | solution.py:206
  14.6 1.9 collective-permute-start.2
  16.5 0.3 shard_map.47
  16.8 2.6 %collective-permute-done.3 = f32[640,128]{1,0:T(8,128)S(1)} collective-permute-done((f32[640,128]{1,0:T(8,128)S(1)}, f32[640,128]{1,0:T(8,128)S(1)}, u32[]{:S(2)}, u32[]{:S(2)}) %collective-permute-start.3) | collective-permute-done | bytes 327712 | tf_op jit(solution)/shard_map/ppermute | solution.py:206
  19.4 0.0 collective-permute-done.2
  19.5 0.4 fusion.11
  19.9 0.1 shard_map.48.state_ref
  20.1 3.6 %collective-permute-start.5 = (f32[640,128]{1,0:T(8,128)S(1)}, f32[640,128]{1,0:T(8,128)S(1)}, u32[]{:S(2)}, u32[]{:S(2)}) collective-permute-start(f32[640,128]{1,0:T(8,128)S(1)} %get-tuple-element.9), channel_id=1, source_target_pairs={{1,2},{2,1},{3,4},{4,3},{5,6},{6,5},{7,8},{8,7},{9,10},{10,9},{11,... | collective-permute-start | bytes 983048 | tf_op jit(solution)/shard_map/ppermute | solution.py:206
  23.7 1.9 collective-permute-start.4
  25.6 2.9 %collective-permute-done.5 = f32[640,128]{1,0:T(8,128)S(1)} collective-permute-done((f32[640,128]{1,0:T(8,128)S(1)}, f32[640,128]{1,0:T(8,128)S(1)}, u32[]{:S(2)}, u32[]{:S(2)}) %collective-permute-start.5) | collective-permute-done | bytes 327712 | tf_op jit(solution)/shard_map/ppermute | solution.py:206
  28.5 0.0 collective-permute-done.4
  28.5 0.1 broadcast_select_fusion
  28.7 0.4 fusion.17
  29.1 0.8 select_bitcast_fusion.3
  29.9 5.3 %collective-permute-start.6 = (f32[512,128]{1,0:T(8,128)}, f32[512,128]{1,0:T(8,128)}, u32[]{:S(2)}, u32[]{:S(2)}) collective-permute-start(f32[512,128]{1,0:T(8,128)} %get-tuple-element.15), channel_id=1, source_target_pairs={{1,2},{2,1},{3,4},{4,3},{5,6},{6,5},{7,8},{8,7},{9,10},{10,9},{11,... | collective-permute-start | bytes 786440 | tf_op jit(solution)/shard_map/ppermute | solution.py:206
  35.2 1.9 collective-permute-start.7
  37.2 0.1 shard_map.49
  37.3 2.3 %collective-permute-done.6 = f32[512,128]{1,0:T(8,128)} collective-permute-done((f32[512,128]{1,0:T(8,128)}, f32[512,128]{1,0:T(8,128)}, u32[]{:S(2)}, u32[]{:S(2)}) %collective-permute-start.6) | collective-permute-done | bytes 262176 | tf_op jit(solution)/shard_map/ppermute | solution.py:206
  39.6 1.1 select_bitcast_fusion.1
  40.6 0.4 fusion.23.field_ref
  41.0 0.3 shard_map.50
  41.4 0.8 pad_maximum_fusion.12
  42.1 58.4 %all-to-all-start = ((f32[32,12,128]{2,1,0:T(8,128)}), f32[32,12,128]{2,1,0:T(8,128)S(1)}, u32[]{:S(2)}, u32[]{:S(2)}) async-start(f32[32,12,128]{2,1,0:T(8,128)} %pad_maximum_fusion.12), calls=%async_computation | async-start | bytes 524288 | tf_op jit(solution)/shard_map/all_to_all | solution.py:183
  100.5 2.1 concatenate.65
  102.6 15.5 %all-to-all-done = f32[32,12,128]{2,1,0:T(8,128)S(1)} async-done(((f32[32,12,128]{2,1,0:T(8,128)}), f32[32,12,128]{2,1,0:T(8,128)S(1)}, u32[]{:S(2)}, u32[]{:S(2)}) %all-to-all-start) | async-done | bytes 196640 | tf_op jit(solution)/shard_map/all_to_all | solution.py:183
  118.1 7.0 %all-to-all-start.1 = ((f32[32,20,128]{2,1,0:T(8,128)}), f32[32,20,128]{2,1,0:T(8,128)S(1)}, u32[]{:S(2)}, u32[]{:S(2)}) async-start(f32[32,20,128]{2,1,0:T(8,128)} %concatenate.65), calls=%async_computation.1 | async-start | bytes 786432 | tf_op jit(solution)/shard_map/all_to_all | solution.py:183
  125.1 0.1 copy.23
  125.2 1.3 collective-permute-start.8
  126.6 2.1 collective-permute-start.9
  128.7 2.2 collective-permute-start.10
  130.9 1.9 collective-permute-start.11
  132.8 16.6 %all-to-all-done.1 = f32[32,20,128]{2,1,0:T(8,128)S(1)} async-done(((f32[32,20,128]{2,1,0:T(8,128)}), f32[32,20,128]{2,1,0:T(8,128)S(1)}, u32[]{:S(2)}, u32[]{:S(2)}) %all-to-all-start.1) | async-done | bytes 327712 | tf_op jit(solution)/shard_map/all_to_all | solution.py:183
  149.4 0.1 fusion.36
  149.6 3.6 %collective-permute-done.11.c1_ref = f32[6,32,128]{2,1,0:T(8,128)S(1)} collective-permute-done((f32[6,32,128]{2,1,0:T(8,128)S(1)}, f32[6,32,128]{2,1,0:T(8,128)S(1)}, u32[]{:S(2)}, u32[]{:S(2)}) %collective-permute-start.11) | collective-permute-done | bytes 98336 | tf_op jit(solution)/shard_map/ppermute | solution.py:166
  153.2 1.0 shard_map.51.refs_1_
  154.2 1.3 collective-permute-start.12
  155.5 1.3 collective-permute-start.13
  156.8 1.3 collective-permute-start.14
  158.1 2.3 %collective-permute-done.12 = f32[4,32,128]{2,1,0:T(8,128)S(1)} collective-permute-done((f32[4,32,128]{2,1,0:T(8,128)S(1)}, f32[4,32,128]{2,1,0:T(8,128)S(1)}, u32[]{:S(2)}, u32[]{:S(2)}) %collective-permute-start.12) | collective-permute-done | bytes 65568 | tf_op jit(solution)/shard_map/ppermute | solution.py:166
  160.3 3.1 %collective-permute-done.13 = f32[4,32,128]{2,1,0:T(8,128)S(1)} collective-permute-done((f32[4,32,128]{2,1,0:T(8,128)S(1)}, f32[4,32,128]{2,1,0:T(8,128)S(1)}, u32[]{:S(2)}, u32[]{:S(2)}) %collective-permute-start.13) | collective-permute-done | bytes 65568 | tf_op jit(solution)/shard_map/ppermute | solution.py:166
  163.4 0.5 collective-permute-done.14
  163.9 1.0 shard_map.52.refs_1_
  164.9 1.3 collective-permute-start.15
  166.2 0.7 collective-permute-start.16
  166.9 1.3 collective-permute-start.17
  168.2 1.3 collective-permute-start.18
  169.5 1.5 collective-permute-start.19
  171.0 3.5 %collective-permute-done.15 = f32[4,32,128]{2,1,0:T(8,128)S(1)} collective-permute-done((f32[4,32,128]{2,1,0:T(8,128)S(1)}, f32[4,32,128]{2,1,0:T(8,128)S(1)}, u32[]{:S(2)}, u32[]{:S(2)}) %collective-permute-start.15) | collective-permute-done | bytes 65568 | tf_op jit(solution)/shard_map/ppermute | solution.py:166
  174.5 5.4 %collective-permute-done.17 = f32[4,32,128]{2,1,0:T(8,128)S(1)} collective-permute-done((f32[4,32,128]{2,1,0:T(8,128)S(1)}, f32[4,32,128]{2,1,0:T(8,128)S(1)}, u32[]{:S(2)}, u32[]{:S(2)}) %collective-permute-start.17) | collective-permute-done | bytes 65568 | tf_op jit(solution)/shard_map/ppermute | solution.py:166
  179.9 5.1 %collective-permute-done.18 = f32[4,32,128]{2,1,0:T(8,128)S(1)} collective-permute-done((f32[4,32,128]{2,1,0:T(8,128)S(1)}, f32[4,32,128]{2,1,0:T(8,128)S(1)}, u32[]{:S(2)}, u32[]{:S(2)}) %collective-permute-start.18) | collective-permute-done | bytes 65568 | tf_op jit(solution)/shard_map/ppermute | solution.py:166
  185.1 2.6 %shard_map.53 = f32[4,32,128]{2,1,0:T(8,128)S(1)} custom-call(f32[20,32,128]{2,1,0:T(8,128)S(1)} %select_dynamic-update-slice_fusion.refs_0_, f32[4,32,128]{2,1,0:T(8,128)S(1)} %shard_map.52.refs_1_, f32[20,32,128]{2,1,0:T(8,128)S(1)} %get-tuple-element.26.refs_2_, f32[20,32,128]{2,1,0:T(8,128)S(1)} %get-tuple-element.25.refs_3_), custom_call_target="tpu_custom_call" | custom-call | tf_op jit(solution)/shard_map/pallas_call | solution.py:148
  187.8 34.5 %all_to_all.15 = f32[32,4,128]{2,1,0:T(4,128)S(1)} all-to-all(f32[32,4,128]{2,1,0:T(4,128)S(1)} %copy.15), channel_id=1, replica_groups=mesh['tm'=16,'space'=32] {'space'}, dimensions={0} | all-to-all | bytes 131072 | tf_op jit(solution)/shard_map/all_to_all | solution.py:269
  222.3 1.1 shard_map.54
  (42 shorter events, 0.7 us)
Async XLA Ops:
  0.0 6.8 %copy-start.1 = (f32[1,2,512,128]{3,2,1,0:T(8,128)S(1)}, f32[1,2,512,128]{3,2,1,0:T(8,128)}, u32[]{:S(2)}) copy-start(f32[1,2,512,128]{3,2,1,0:T(8,128)} %param.4) | copy-start | bytes 1572868
  1.1 6.0 %copy-start.2 = (s32[1,256]{1,0:T(1,128)S(1)}, s32[1,256]{1,0:T(1,128)}, u32[]{:S(2)}) copy-start(s32[1,256]{1,0:T(1,128)} %param.6) | copy-start | bytes 3076
  1.1 8.3 %collective-permute-start = (f32[512,128]{1,0:T(8,128)S(1)}, f32[512,128]{1,0:T(8,128)S(1)}, u32[]{:S(2)}, u32[]{:S(2)}) collective-permute-start(f32[512,128]{1,0:T(8,128)S(1)} %get-tuple-element.23), channel_id=1, source_target_pairs={{1,2},{2,1},{3,4},{4,3},{5,6},{6,5},{7,8},{8,7},{9,10},{10,9},{11,... | collective-permute-start | bytes 786440 | tf_op jit(solution)/shard_map/ppermute | solution.py:206
  4.9 4.5 %collective-permute-start.1 = (f32[512,128]{1,0:T(8,128)S(1)}, f32[512,128]{1,0:T(8,128)S(1)}, u32[]{:S(2)}, u32[]{:S(2)}) collective-permute-start(f32[512,128]{1,0:T(8,128)S(1)} %get-tuple-element.24), channel_id=1, source_target_pairs={{0,1},{1,0},{2,3},{3,2},{4,5},{5,4},{6,7},{7,6},{8,9},{9,8},{10,11... | collective-permute-start | bytes 786440 | tf_op jit(solution)/shard_map/ppermute | solution.py:207
  9.4 1.0 copy-start
  11.0 8.4 %collective-permute-start.3 = (f32[640,128]{1,0:T(8,128)S(1)}, f32[640,128]{1,0:T(8,128)S(1)}, u32[]{:S(2)}, u32[]{:S(2)}) collective-permute-start(f32[640,128]{1,0:T(8,128)S(1)} %get-tuple-element.11), channel_id=1, source_target_pairs={{1,2},{2,1},{3,4},{4,3},{5,6},{6,5},{7,8},{8,7},{9,10},{10,9},{11,... | collective-permute-start | bytes 983048 | tf_op jit(solution)/shard_map/ppermute | solution.py:206
  14.6 4.8 %collective-permute-start.2 = (f32[640,128]{1,0:T(8,128)S(1)}, f32[640,128]{1,0:T(8,128)S(1)}, u32[]{:S(2)}, u32[]{:S(2)}) collective-permute-start(f32[640,128]{1,0:T(8,128)S(1)} %get-tuple-element.12), channel_id=1, source_target_pairs={{0,1},{1,0},{2,3},{3,2},{4,5},{5,4},{6,7},{7,6},{8,9},{9,8},{10,11... | collective-permute-start | bytes 983048 | tf_op jit(solution)/shard_map/ppermute | solution.py:207
  20.1 8.4 %collective-permute-start.5 = (f32[640,128]{1,0:T(8,128)S(1)}, f32[640,128]{1,0:T(8,128)S(1)}, u32[]{:S(2)}, u32[]{:S(2)}) collective-permute-start(f32[640,128]{1,0:T(8,128)S(1)} %get-tuple-element.9), channel_id=1, source_target_pairs={{1,2},{2,1},{3,4},{4,3},{5,6},{6,5},{7,8},{8,7},{9,10},{10,9},{11,... | collective-permute-start | bytes 983048 | tf_op jit(solution)/shard_map/ppermute | solution.py:206
  23.7 4.8 %collective-permute-start.4 = (f32[640,128]{1,0:T(8,128)S(1)}, f32[640,128]{1,0:T(8,128)S(1)}, u32[]{:S(2)}, u32[]{:S(2)}) collective-permute-start(f32[640,128]{1,0:T(8,128)S(1)} %get-tuple-element.10), channel_id=1, source_target_pairs={{0,1},{1,0},{2,3},{3,2},{4,5},{5,4},{6,7},{7,6},{8,9},{9,8},{10,11... | collective-permute-start | bytes 983048 | tf_op jit(solution)/shard_map/ppermute | solution.py:207
  29.9 9.6 %collective-permute-start.6 = (f32[512,128]{1,0:T(8,128)}, f32[512,128]{1,0:T(8,128)}, u32[]{:S(2)}, u32[]{:S(2)}) collective-permute-start(f32[512,128]{1,0:T(8,128)} %get-tuple-element.15), channel_id=1, source_target_pairs={{1,2},{2,1},{3,4},{4,3},{5,6},{6,5},{7,8},{8,7},{9,10},{10,9},{11,... | collective-permute-start | bytes 786440 | tf_op jit(solution)/shard_map/ppermute | solution.py:206
  35.2 4.4 %collective-permute-start.7 = (f32[512,128]{1,0:T(8,128)}, f32[512,128]{1,0:T(8,128)}, u32[]{:S(2)}, u32[]{:S(2)}) collective-permute-start(f32[512,128]{1,0:T(8,128)} %get-tuple-element.16), channel_id=1, source_target_pairs={{0,1},{1,0},{2,3},{3,2},{4,5},{5,4},{6,7},{7,6},{8,9},{9,8},{10,11... | collective-permute-start | bytes 786440 | tf_op jit(solution)/shard_map/ppermute | solution.py:207
  42.1 76.0 %all-to-all-start = ((f32[32,12,128]{2,1,0:T(8,128)}), f32[32,12,128]{2,1,0:T(8,128)S(1)}, u32[]{:S(2)}, u32[]{:S(2)}) async-start(f32[32,12,128]{2,1,0:T(8,128)} %pad_maximum_fusion.12), calls=%async_computation | async-start | bytes 524288 | tf_op jit(solution)/shard_map/all_to_all | solution.py:183
  118.1 31.4 %all-to-all-start.1 = ((f32[32,20,128]{2,1,0:T(8,128)}), f32[32,20,128]{2,1,0:T(8,128)S(1)}, u32[]{:S(2)}, u32[]{:S(2)}) async-start(f32[32,20,128]{2,1,0:T(8,128)} %concatenate.65), calls=%async_computation.1 | async-start | bytes 786432 | tf_op jit(solution)/shard_map/all_to_all | solution.py:183
  125.2 28.0 %collective-permute-start.8 = (f32[12,32,128]{2,1,0:T(8,128)S(1)}, f32[12,32,128]{2,1,0:T(8,128)S(1)}, u32[]{:S(2)}, u32[]{:S(2)}) collective-permute-start(f32[12,32,128]{2,1,0:T(8,128)S(1)} %bitcast.78), channel_id=1, source_target_pairs={{128,0},{129,1},{130,2},{131,3},{132,4},{133,5},{134,6},{135,7},{1... | collective-permute-start | bytes 589832 | tf_op jit(solution)/shard_map/ppermute | solution.py:166
  126.6 26.6 %collective-permute-start.9 = (f32[10,32,128]{2,1,0:T(8,128)S(1)}, f32[10,32,128]{2,1,0:T(8,128)S(1)}, u32[]{:S(2)}, u32[]{:S(2)}) collective-permute-start(f32[10,32,128]{2,1,0:T(8,128)S(1)} %slice.232), channel_id=1, source_target_pairs={{96,0},{97,1},{98,2},{99,3},{100,4},{101,5},{102,6},{103,7},{104,8... | collective-permute-start | bytes 491528 | tf_op jit(solution)/shard_map/ppermute | solution.py:166
  128.7 24.5 %collective-permute-start.10 = (f32[8,32,128]{2,1,0:T(8,128)S(1)}, f32[8,32,128]{2,1,0:T(8,128)S(1)}, u32[]{:S(2)}, u32[]{:S(2)}) collective-permute-start(f32[8,32,128]{2,1,0:T(8,128)S(1)} %slice.233), channel_id=1, source_target_pairs={{64,0},{65,1},{66,2},{67,3},{68,4},{69,5},{70,6},{71,7},{72,8},{73... | collective-permute-start | bytes 393224 | tf_op jit(solution)/shard_map/ppermute | solution.py:166
  130.9 22.3 %collective-permute-start.11 = (f32[6,32,128]{2,1,0:T(8,128)S(1)}, f32[6,32,128]{2,1,0:T(8,128)S(1)}, u32[]{:S(2)}, u32[]{:S(2)}) collective-permute-start(f32[6,32,128]{2,1,0:T(8,128)S(1)} %slice.234), channel_id=1, source_target_pairs={{32,0},{33,1},{34,2},{35,3},{36,4},{37,5},{38,6},{39,7},{40,8},{41... | collective-permute-start | bytes 294920 | tf_op jit(solution)/shard_map/ppermute | solution.py:166
  154.2 6.2 %collective-permute-start.12 = (f32[4,32,128]{2,1,0:T(8,128)S(1)}, f32[4,32,128]{2,1,0:T(8,128)S(1)}, u32[]{:S(2)}, u32[]{:S(2)}) collective-permute-start(f32[4,32,128]{2,1,0:T(8,128)S(1)} %shard_map.51.refs_1_), channel_id=1, source_target_pairs={{128,1},{129,0},{130,3},{131,2},{132,5},{133,4},{134,7},{135,6},{1... | collective-permute-start | bytes 196616 | tf_op jit(solution)/shard_map/ppermute | solution.py:166
  155.5 7.9 %collective-permute-start.13 = (f32[4,32,128]{2,1,0:T(8,128)S(1)}, f32[4,32,128]{2,1,0:T(8,128)S(1)}, u32[]{:S(2)}, u32[]{:S(2)}) collective-permute-start(f32[4,32,128]{2,1,0:T(8,128)S(1)} %shard_map.51.refs_1_), channel_id=1, source_target_pairs={{129,2},{130,1},{131,4},{132,3},{133,6},{134,5},{135,8},{136,7},{1... | collective-permute-start | bytes 196616 | tf_op jit(solution)/shard_map/ppermute | solution.py:166
  156.8 7.1 %collective-permute-start.14 = (f32[4,32,128]{2,1,0:T(8,128)S(1)}, f32[4,32,128]{2,1,0:T(8,128)S(1)}, u32[]{:S(2)}, u32[]{:S(2)}) collective-permute-start(f32[4,32,128]{2,1,0:T(8,128)S(1)} %shard_map.51.refs_1_), channel_id=1, source_target_pairs={{128,0},{129,1},{130,2},{131,3},{132,4},{133,5},{134,6},{135,7},{1... | collective-permute-start | bytes 196616 | tf_op jit(solution)/shard_map/ppermute | solution.py:166
  164.9 9.6 %collective-permute-start.15 = (f32[4,32,128]{2,1,0:T(8,128)S(1)}, f32[4,32,128]{2,1,0:T(8,128)S(1)}, u32[]{:S(2)}, u32[]{:S(2)}) collective-permute-start(f32[4,32,128]{2,1,0:T(8,128)S(1)} %shard_map.52.refs_1_), channel_id=1, source_target_pairs={{256,2},{258,0},{257,3},{259,1},{260,6},{262,4},{261,7},{263,5},{2... | collective-permute-start | bytes 196616 | tf_op jit(solution)/shard_map/ppermute | solution.py:166
  166.2 8.3 %collective-permute-start.16 = (f32[4,32,128]{2,1,0:T(8,128)S(1)}, f32[4,32,128]{2,1,0:T(8,128)S(1)}, u32[]{:S(2)}, u32[]{:S(2)}) collective-permute-start(f32[4,32,128]{2,1,0:T(8,128)S(1)} %shard_map.52.refs_1_), channel_id=1, source_target_pairs={{258,4},{260,2},{259,5},{261,3},{262,8},{264,6},{263,9},{265,7},{2... | collective-permute-start | bytes 196616 | tf_op jit(solution)/shard_map/ppermute | solution.py:166
  166.9 13.0 %collective-permute-start.17 = (f32[4,32,128]{2,1,0:T(8,128)S(1)}, f32[4,32,128]{2,1,0:T(8,128)S(1)}, u32[]{:S(2)}, u32[]{:S(2)}) collective-permute-start(f32[4,32,128]{2,1,0:T(8,128)S(1)} %shard_map.52.refs_1_), channel_id=1, source_target_pairs={{256,1},{257,0},{258,3},{259,2},{260,5},{261,4},{262,7},{263,6},{2... | collective-permute-start | bytes 196616 | tf_op jit(solution)/shard_map/ppermute | solution.py:166
  168.2 16.8 %collective-permute-start.18 = (f32[4,32,128]{2,1,0:T(8,128)S(1)}, f32[4,32,128]{2,1,0:T(8,128)S(1)}, u32[]{:S(2)}, u32[]{:S(2)}) collective-permute-start(f32[4,32,128]{2,1,0:T(8,128)S(1)} %shard_map.52.refs_1_), channel_id=1, source_target_pairs={{257,2},{258,1},{259,4},{260,3},{261,6},{262,5},{263,8},{264,7},{2... | collective-permute-start | bytes 196616 | tf_op jit(solution)/shard_map/ppermute | solution.py:166
  169.5 15.5 %collective-permute-start.19 = (f32[4,32,128]{2,1,0:T(8,128)S(1)}, f32[4,32,128]{2,1,0:T(8,128)S(1)}, u32[]{:S(2)}, u32[]{:S(2)}) collective-permute-start(f32[4,32,128]{2,1,0:T(8,128)S(1)} %shard_map.52.refs_1_), channel_id=1, source_target_pairs={{256,0},{257,1},{258,2},{259,3},{260,4},{261,5},{262,6},{263,7},{2... | collective-permute-start | bytes 196616 | tf_op jit(solution)/shard_map/ppermute | solution.py:166

commit v2 on v1

--- a/solution.py
+++ b/solution.py
@@ -217,13 +217,6 @@
     plane_spread = 1.0 / (coarse_cond + 1.5)
     plane_keep = coarse_cond * plane_spread
     plane_spread = 0.25 * plane_spread
-    row_cond = to_rows(coarse_cond, 2)
-    place = (slab - 2) * BLOCK + lax.broadcasted_iota(jnp.int32, row_cond.shape, 0)
-    within = (place >= 0) & (place < PLANE)
-    row_spread = jnp.where(within, 1.0 / (row_cond + 1.5), 0.0)
-    row_keep = row_cond * row_spread
-    row_spread = 0.25 * row_spread
-
     diagonal = cond + 6.0
     field_now = start_field
     coarse_start = restrict(start_field)
@@ -244,7 +237,18 @@
                     coarse_now, coarse_start, before[width_y:], after[width_y:], plane_keep, plane_spread
                 )
             sweep += 1
+            if sweep == 1:
+                coarse_cond, field_now = lax.optimization_barrier((coarse_cond, field_now))
+                row_cond = to_rows(coarse_cond, 2)
+            if sweep == 3:
+                row_cond, field_now = lax.optimization_barrier((row_cond, field_now))
     direct = coarse_now
+
+    place = (slab - 2) * BLOCK + lax.broadcasted_iota(jnp.int32, row_cond.shape, 0)
+    within = (place >= 0) & (place < PLANE)
+    row_spread = jnp.where(within, 1.0 / (row_cond + 1.5), 0.0)
+    row_keep = row_cond * row_spread
+    row_spread = 0.25 * row_spread
 
     term = restrict(field_now) - jnp.where(is_final, 0.0, direct)
     rows = to_rows(term, 1)

time: 224 us -> 225 us (level)
  waiting for transfers between devices: 63.2 us -> 75.1 us
  starting transfers between devices: 107 us -> 99.2 us
  blocking collectives: 34.5 us -> 28 us
    all_to_all x2, waiting for transfers between devices: 32.1 us -> 41.6 us  [to_rows(): arrived = lax.all_to_all(windows(plane, reach), 'space', 0, 0)]
    all_to_all x1, blocking collectives: 34.5 us -> 28 us  [per_device(): back = lax.all_to_all(jnp.transpose(total, (1, 0, 2)), 'space', 0, 0)]
    ppermute x12, waiting for transfers between devices: 23.4 us -> 29.1 us  [from_later(): return lax.ppermute(value, ('tm', 'space'), both)]
    all_to_all x2, starting transfers between devices: 65.4 us -> 60.3 us  [to_rows(): arrived = lax.all_to_all(windows(plane, reach), 'space', 0, 0)]
    ppermute x4, waiting for transfers between devices: 7.69 us -> 4.36 us  [trade(): across = lax.ppermute(jnp.where(odd, last, first), 'space', facing(1, 1))]
    ppermute x4, starting transfers between devices: 16.2 us -> 13.7 us  [trade(): across = lax.ppermute(jnp.where(odd, last, first), 'space', facing(1, 1))]
  transfers between devices with their start and end apart: 22 -> 22, of which waited for: 12 -> 11; matrix products, arithmetic and copies ran while one was open for 2% -> 3% of each run, Pallas kernels for 0% -> 0%
where the time goes in v2:
time: 225 us; the launch traced here: 224 us
  starting transfers between devices  99.2 us (44%)
  waiting for transfers between devices  75.1 us (33%)
  blocking collectives  28 us (12%)
  other arithmetic  9.06 us (4%)
  Pallas kernels  6.7 us (3%)
  local copies, waits for them, and re-layouts  5.06 us (2%)
    all_to_all x2, starting transfers between devices, to_rows(): arrived = lax.all_to_all(windows(plane, reach), 'space', 0, 0)  60.3 us
    all_to_all x2, waiting for transfers between devices, to_rows(): arrived = lax.all_to_all(windows(plane, reach), 'space', 0, 0)  41.6 us
    ppermute x12, waiting for transfers between devices, from_later(): return lax.ppermute(value, ('tm', 'space'), both)  29.1 us
    all_to_all x1, blocking collectives, per_device(): back = lax.all_to_all(jnp.transpose(total, (1, 0, 2)), 'space', 0, 0)  28 us
    ppermute x12, starting transfers between devices, from_later(): return lax.ppermute(value, ('tm', 'space'), both)  17.4 us
    ppermute x4, starting transfers between devices, trade(): across = lax.ppermute(jnp.where(odd, last, first), 'space', facing(1, 1))  13.7 us
    ppermute x4, starting transfers between devices, trade(): along = lax.ppermute(jnp.where(odd, first, last), 'space', facing(1, 0))  7.68 us
    pallas_call x3, Pallas kernels, chain_call(): pl.pallas_call(kernel, out_shape=jax.ShapeDtypeStruct((BLOCK, SLABS, 128)...  4.54 us
  transfers between devices with their start and end apart: 22, of which 11 were waited for; matrix products, arithmetic and copies ran while one was open for 3% of the time, Pallas kernels for 0%

profile of v2, /device:TPU:7, one launch (start us, length us, event | category | flops | bytes accessed | tf_op | source)
XLA Modules:
  0.0 223.7 jit_solution(9640905280657546462)
XLA Ops:
  0.0 1.1 select_bitcast_fusion.7
  1.1 0.0 copy-start
  1.1 3.9 %collective-permute-start = (f32[512,128]{1,0:T(8,128)S(1)}, f32[512,128]{1,0:T(8,128)S(1)}, u32[]{:S(2)}, u32[]{:S(2)}) collective-permute-start(f32[512,128]{1,0:T(8,128)S(1)} %get-tuple-element.31), channel_id=1, source_target_pairs={{1,2},{2,1},{3,4},{4,3},{5,6},{6,5},{7,8},{8,7},{9,10},{10,9},{11,... | collective-permute-start | bytes 786440 | tf_op jit(solution)/shard_map/ppermute | solution.py:206
  5.0 1.9 collective-permute-start.1
  7.0 0.3 shard_map.46.state_ref.start_ref
  7.3 0.3 shard_map.47
  7.6 2.2 scatter_custom_fusion
  9.9 0.0 collective-permute-done
  9.9 0.4 fusion.5
  10.5 3.6 %collective-permute-start.3 = (f32[640,128]{1,0:T(8,128)S(1)}, f32[640,128]{1,0:T(8,128)S(1)}, u32[]{:S(2)}, u32[]{:S(2)}) collective-permute-start(f32[640,128]{1,0:T(8,128)S(1)} %get-tuple-element.19), channel_id=1, source_target_pairs={{1,2},{2,1},{3,4},{4,3},{5,6},{6,5},{7,8},{8,7},{9,10},{10,9},{11,... | collective-permute-start | bytes 983048 | tf_op jit(solution)/shard_map/ppermute | solution.py:206
  14.1 1.9 collective-permute-start.2
  16.0 2.9 %collective-permute-done.3 = f32[640,128]{1,0:T(8,128)S(1)} collective-permute-done((f32[640,128]{1,0:T(8,128)S(1)}, f32[640,128]{1,0:T(8,128)S(1)}, u32[]{:S(2)}, u32[]{:S(2)}) %collective-permute-start.3) | collective-permute-done | bytes 327712 | tf_op jit(solution)/shard_map/ppermute | solution.py:206
  18.9 0.0 collective-permute-done.2
  19.0 0.4 fusion.11
  19.5 0.1 shard_map.48.state_ref
  19.7 3.6 %collective-permute-start.5 = (f32[640,128]{1,0:T(8,128)S(1)}, f32[640,128]{1,0:T(8,128)S(1)}, u32[]{:S(2)}, u32[]{:S(2)}) collective-permute-start(f32[640,128]{1,0:T(8,128)S(1)} %get-tuple-element.17), channel_id=1, source_target_pairs={{1,2},{2,1},{3,4},{4,3},{5,6},{6,5},{7,8},{8,7},{9,10},{10,9},{11,... | collective-permute-start | bytes 983048 | tf_op jit(solution)/shard_map/ppermute | solution.py:206
  23.2 1.9 collective-permute-start.4
  25.2 2.1 concatenate.60
  27.3 44.5 %all-to-all-start = ((f32[32,20,128]{2,1,0:T(8,128)}), f32[32,20,128]{2,1,0:T(8,128)S(1)}, u32[]{:S(2)}, u32[]{:S(2)}) async-start(f32[32,20,128]{2,1,0:T(8,128)} %concatenate.60), calls=%async_computation | async-start | bytes 786432 | tf_op jit(solution)/shard_map/all_to_all | solution.py:183
  71.9 1.0 broadcast_select_fusion
  72.9 0.7 copy-done.2
  73.6 0.1 copy-done.3
  73.8 0.4 fusion.17
  74.2 20.4 %all-to-all-done = f32[32,20,128]{2,1,0:T(8,128)S(1)} async-done(((f32[32,20,128]{2,1,0:T(8,128)}), f32[32,20,128]{2,1,0:T(8,128)S(1)}, u32[]{:S(2)}, u32[]{:S(2)}) %all-to-all-start) | async-done | bytes 327712 | tf_op jit(solution)/shard_map/all_to_all | solution.py:183
  94.6 0.1 copy.18
  94.6 0.8 select_bitcast_fusion.3
  95.5 2.6 %collective-permute-start.6 = (f32[512,128]{1,0:T(8,128)}, f32[512,128]{1,0:T(8,128)S(1)}, u32[]{:S(2)}, u32[]{:S(2)}) collective-permute-start(f32[512,128]{1,0:T(8,128)} %get-tuple-element.23), channel_id=1, source_target_pairs={{1,2},{2,1},{3,4},{4,3},{5,6},{6,5},{7,8},{8,7},{9,10},{10,9},{11,... | collective-permute-start | bytes 786440 | tf_op jit(solution)/shard_map/ppermute | solution.py:206
  98.1 1.9 collective-permute-start.7
  100.1 0.8 slice.224.before_ref
  100.9 0.8 slice.225.after_ref
  101.8 0.1 shard_map.49
  101.9 1.5 collective-permute-done.6
  103.4 1.0 select_bitcast_fusion.1
  104.4 0.4 fusion.23.field_ref
  104.8 0.3 shard_map.50
  105.1 0.8 pad_maximum_fusion.12
  105.9 15.8 %all-to-all-start.1 = ((f32[32,12,128]{2,1,0:T(8,128)}), f32[32,12,128]{2,1,0:T(8,128)S(1)}, u32[]{:S(2)}, u32[]{:S(2)}) async-start(f32[32,12,128]{2,1,0:T(8,128)} %pad_maximum_fusion.12), calls=%async_computation.1 | async-start | bytes 524288 | tf_op jit(solution)/shard_map/all_to_all | solution.py:183
  121.7 21.2 %all-to-all-done.1 = f32[32,12,128]{2,1,0:T(8,128)S(1)} async-done(((f32[32,12,128]{2,1,0:T(8,128)}), f32[32,12,128]{2,1,0:T(8,128)S(1)}, u32[]{:S(2)}, u32[]{:S(2)}) %all-to-all-start.1) | async-done | bytes 196640 | tf_op jit(solution)/shard_map/all_to_all | solution.py:183
  142.9 0.1 copy.19
  143.0 1.3 collective-permute-start.8
  144.3 2.1 collective-permute-start.9
  146.5 2.2 collective-permute-start.10
  148.7 1.9 collective-permute-start.11
  150.6 0.1 fusion.34
  150.8 10.0 %collective-permute-done.11.c1_ref = f32[6,32,128]{2,1,0:T(8,128)S(1)} collective-permute-done((f32[6,32,128]{2,1,0:T(8,128)S(1)}, f32[6,32,128]{2,1,0:T(8,128)S(1)}, u32[]{:S(2)}, u32[]{:S(2)}) %collective-permute-start.11) | collective-permute-done | bytes 98336 | tf_op jit(solution)/shard_map/ppermute | solution.py:166
  160.8 1.0 shard_map.51.refs_1_
  161.8 1.3 collective-permute-start.12
  163.1 1.3 collective-permute-start.13
  164.4 1.3 collective-permute-start.14
  165.7 2.2 collective-permute-done.12
  167.9 1.8 collective-permute-done.13
  169.8 1.2 collective-permute-done.14
  171.0 1.0 shard_map.52.refs_1_
  172.0 1.3 collective-permute-start.15
  173.3 0.7 collective-permute-start.16
  174.0 1.3 collective-permute-start.17
  175.3 1.3 collective-permute-start.18
  176.6 1.5 collective-permute-start.19
  178.1 0.7 collective-permute-done.15
  178.8 5.5 %collective-permute-done.17 = f32[4,32,128]{2,1,0:T(8,128)S(1)} collective-permute-done((f32[4,32,128]{2,1,0:T(8,128)S(1)}, f32[4,32,128]{2,1,0:T(8,128)S(1)}, u32[]{:S(2)}, u32[]{:S(2)}) %collective-permute-start.17) | collective-permute-done | bytes 65568 | tf_op jit(solution)/shard_map/ppermute | solution.py:166
  184.3 7.6 %collective-permute-done.18 = f32[4,32,128]{2,1,0:T(8,128)S(1)} collective-permute-done((f32[4,32,128]{2,1,0:T(8,128)S(1)}, f32[4,32,128]{2,1,0:T(8,128)S(1)}, u32[]{:S(2)}, u32[]{:S(2)}) %collective-permute-start.18) | collective-permute-done | bytes 65568 | tf_op jit(solution)/shard_map/ppermute | solution.py:166
  191.9 2.6 %shard_map.53 = f32[4,32,128]{2,1,0:T(8,128)S(1)} custom-call(f32[20,32,128]{2,1,0:T(8,128)S(1)} %select_dynamic-update-slice_fusion.refs_0_, f32[4,32,128]{2,1,0:T(8,128)S(1)} %shard_map.52.refs_1_, f32[20,32,128]{2,1,0:T(8,128)S(1)} %get-tuple-element.34.refs_2_, f32[20,32,128]{2,1,0:T(8,128)S(1)} %get-tuple-element.33.refs_3_), custom_call_target="tpu_custom_call" | custom-call | tf_op jit(solution)/shard_map/pallas_call | solution.py:148
  194.6 28.0 %all_to_all.15 = f32[32,4,128]{2,1,0:T(4,128)S(1)} all-to-all(f32[32,4,128]{2,1,0:T(4,128)S(1)} %copy.15), channel_id=1, replica_groups=mesh['tm'=16,'space'=32] {'space'}, dimensions={0} | all-to-all | bytes 131072 | tf_op jit(solution)/shard_map/all_to_all | solution.py:273
  222.6 1.1 shard_map.54
  (47 shorter events, 0.7 us)
Async XLA Ops:
  0.0 7.0 %copy-start.4 = (s32[1,256]{1,0:T(1,128)S(1)}, s32[1,256]{1,0:T(1,128)}, u32[]{:S(2)}) copy-start(s32[1,256]{1,0:T(1,128)} %param.6) | copy-start | bytes 3076
  0.0 7.0 %copy-start.1 = (f32[1,2,512,128]{3,2,1,0:T(8,128)S(1)}, f32[1,2,512,128]{3,2,1,0:T(8,128)}, u32[]{:S(2)}) copy-start(f32[1,2,512,128]{3,2,1,0:T(8,128)} %param.4) | copy-start | bytes 1572868
  1.1 6.2 %copy-start = (f32[2,512,128]{2,1,0:T(8,128)S(1)}, f32[2,512,128]{2,1,0:T(8,128)}, u32[]{:S(2)}) copy-start(f32[2,512,128]{2,1,0:T(8,128)} %field_ref.1) | copy-start | bytes 1572868
  1.1 8.7 %collective-permute-start = (f32[512,128]{1,0:T(8,128)S(1)}, f32[512,128]{1,0:T(8,128)S(1)}, u32[]{:S(2)}, u32[]{:S(2)}) collective-permute-start(f32[512,128]{1,0:T(8,128)S(1)} %get-tuple-element.31), channel_id=1, source_target_pairs={{1,2},{2,1},{3,4},{4,3},{5,6},{6,5},{7,8},{8,7},{9,10},{10,9},{11,... | collective-permute-start | bytes 786440 | tf_op jit(solution)/shard_map/ppermute | solution.py:206
  5.0 4.8 %collective-permute-start.1 = (f32[512,128]{1,0:T(8,128)S(1)}, f32[512,128]{1,0:T(8,128)S(1)}, u32[]{:S(2)}, u32[]{:S(2)}) collective-permute-start(f32[512,128]{1,0:T(8,128)S(1)} %get-tuple-element.32), channel_id=1, source_target_pairs={{0,1},{1,0},{2,3},{3,2},{4,5},{5,4},{6,7},{7,6},{8,9},{9,8},{10,11... | collective-permute-start | bytes 786440 | tf_op jit(solution)/shard_map/ppermute | solution.py:207
  10.5 8.4 %collective-permute-start.3 = (f32[640,128]{1,0:T(8,128)S(1)}, f32[640,128]{1,0:T(8,128)S(1)}, u32[]{:S(2)}, u32[]{:S(2)}) collective-permute-start(f32[640,128]{1,0:T(8,128)S(1)} %get-tuple-element.19), channel_id=1, source_target_pairs={{1,2},{2,1},{3,4},{4,3},{5,6},{6,5},{7,8},{8,7},{9,10},{10,9},{11,... | collective-permute-start | bytes 983048 | tf_op jit(solution)/shard_map/ppermute | solution.py:206
  14.1 4.8 %collective-permute-start.2 = (f32[640,128]{1,0:T(8,128)S(1)}, f32[640,128]{1,0:T(8,128)S(1)}, u32[]{:S(2)}, u32[]{:S(2)}) collective-permute-start(f32[640,128]{1,0:T(8,128)S(1)} %get-tuple-element.20), channel_id=1, source_target_pairs={{0,1},{1,0},{2,3},{3,2},{4,5},{5,4},{6,7},{7,6},{8,9},{9,8},{10,11... | collective-permute-start | bytes 983048 | tf_op jit(solution)/shard_map/ppermute | solution.py:207
  19.7 52.2 %collective-permute-start.5 = (f32[640,128]{1,0:T(8,128)S(1)}, f32[640,128]{1,0:T(8,128)S(1)}, u32[]{:S(2)}, u32[]{:S(2)}) collective-permute-start(f32[640,128]{1,0:T(8,128)S(1)} %get-tuple-element.17), channel_id=1, source_target_pairs={{1,2},{2,1},{3,4},{4,3},{5,6},{6,5},{7,8},{8,7},{9,10},{10,9},{11,... | collective-permute-start | bytes 983048 | tf_op jit(solution)/shard_map/ppermute | solution.py:206
  23.2 48.6 %collective-permute-start.4 = (f32[640,128]{1,0:T(8,128)S(1)}, f32[640,128]{1,0:T(8,128)}, u32[]{:S(2)}, u32[]{:S(2)}) collective-permute-start(f32[640,128]{1,0:T(8,128)S(1)} %get-tuple-element.18), channel_id=1, source_target_pairs={{0,1},{1,0},{2,3},{3,2},{4,5},{5,4},{6,7},{7,6},{8,9},{9,8},{10,11... | collective-permute-start | bytes 983048 | tf_op jit(solution)/shard_map/ppermute | solution.py:207
  27.3 67.3 %all-to-all-start = ((f32[32,20,128]{2,1,0:T(8,128)}), f32[32,20,128]{2,1,0:T(8,128)S(1)}, u32[]{:S(2)}, u32[]{:S(2)}) async-start(f32[32,20,128]{2,1,0:T(8,128)} %concatenate.60), calls=%async_computation | async-start | bytes 786432 | tf_op jit(solution)/shard_map/all_to_all | solution.py:183
  72.9 0.7 copy-start.2
  72.9 0.8 copy-start.3
  95.5 7.9 %collective-permute-start.6 = (f32[512,128]{1,0:T(8,128)}, f32[512,128]{1,0:T(8,128)S(1)}, u32[]{:S(2)}, u32[]{:S(2)}) collective-permute-start(f32[512,128]{1,0:T(8,128)} %get-tuple-element.23), channel_id=1, source_target_pairs={{1,2},{2,1},{3,4},{4,3},{5,6},{6,5},{7,8},{8,7},{9,10},{10,9},{11,... | collective-permute-start | bytes 786440 | tf_op jit(solution)/shard_map/ppermute | solution.py:206
  98.1 5.2 %collective-permute-start.7 = (f32[512,128]{1,0:T(8,128)}, f32[512,128]{1,0:T(8,128)}, u32[]{:S(2)}, u32[]{:S(2)}) collective-permute-start(f32[512,128]{1,0:T(8,128)} %get-tuple-element.24), channel_id=1, source_target_pairs={{0,1},{1,0},{2,3},{3,2},{4,5},{5,4},{6,7},{7,6},{8,9},{9,8},{10,11... | collective-permute-start | bytes 786440 | tf_op jit(solution)/shard_map/ppermute | solution.py:207
  105.9 37.1 %all-to-all-start.1 = ((f32[32,12,128]{2,1,0:T(8,128)}), f32[32,12,128]{2,1,0:T(8,128)S(1)}, u32[]{:S(2)}, u32[]{:S(2)}) async-start(f32[32,12,128]{2,1,0:T(8,128)} %pad_maximum_fusion.12), calls=%async_computation.1 | async-start | bytes 524288 | tf_op jit(solution)/shard_map/all_to_all | solution.py:183
  143.0 17.8 %collective-permute-start.8 = (f32[12,32,128]{2,1,0:T(8,128)S(1)}, f32[12,32,128]{2,1,0:T(8,128)S(1)}, u32[]{:S(2)}, u32[]{:S(2)}) collective-permute-start(f32[12,32,128]{2,1,0:T(8,128)S(1)} %bitcast.70), channel_id=1, source_target_pairs={{128,0},{129,1},{130,2},{131,3},{132,4},{133,5},{134,6},{135,7},{1... | collective-permute-start | bytes 589832 | tf_op jit(solution)/shard_map/ppermute | solution.py:166
  144.3 16.5 %collective-permute-start.9 = (f32[10,32,128]{2,1,0:T(8,128)S(1)}, f32[10,32,128]{2,1,0:T(8,128)S(1)}, u32[]{:S(2)}, u32[]{:S(2)}) collective-permute-start(f32[10,32,128]{2,1,0:T(8,128)S(1)} %slice.228), channel_id=1, source_target_pairs={{96,0},{97,1},{98,2},{99,3},{100,4},{101,5},{102,6},{103,7},{104,8... | collective-permute-start | bytes 491528 | tf_op jit(solution)/shard_map/ppermute | solution.py:166
  146.5 14.4 %collective-permute-start.10 = (f32[8,32,128]{2,1,0:T(8,128)S(1)}, f32[8,32,128]{2,1,0:T(8,128)S(1)}, u32[]{:S(2)}, u32[]{:S(2)}) collective-permute-start(f32[8,32,128]{2,1,0:T(8,128)S(1)} %slice.229), channel_id=1, source_target_pairs={{64,0},{65,1},{66,2},{67,3},{68,4},{69,5},{70,6},{71,7},{72,8},{73... | collective-permute-start | bytes 393224 | tf_op jit(solution)/shard_map/ppermute | solution.py:166
  148.7 12.1 %collective-permute-start.11 = (f32[6,32,128]{2,1,0:T(8,128)S(1)}, f32[6,32,128]{2,1,0:T(8,128)S(1)}, u32[]{:S(2)}, u32[]{:S(2)}) collective-permute-start(f32[6,32,128]{2,1,0:T(8,128)S(1)} %slice.230), channel_id=1, source_target_pairs={{32,0},{33,1},{34,2},{35,3},{36,4},{37,5},{38,6},{39,7},{40,8},{41... | collective-permute-start | bytes 294920 | tf_op jit(solution)/shard_map/ppermute | solution.py:166
  161.8 6.1 %collective-permute-start.12 = (f32[4,32,128]{2,1,0:T(8,128)S(1)}, f32[4,32,128]{2,1,0:T(8,128)S(1)}, u32[]{:S(2)}, u32[]{:S(2)}) collective-permute-start(f32[4,32,128]{2,1,0:T(8,128)S(1)} %shard_map.51.refs_1_), channel_id=1, source_target_pairs={{128,1},{129,0},{130,3},{131,2},{132,5},{133,4},{134,7},{135,6},{1... | collective-permute-start | bytes 196616 | tf_op jit(solution)/shard_map/ppermute | solution.py:166
  163.1 6.6 %collective-permute-start.13 = (f32[4,32,128]{2,1,0:T(8,128)S(1)}, f32[4,32,128]{2,1,0:T(8,128)S(1)}, u32[]{:S(2)}, u32[]{:S(2)}) collective-permute-start(f32[4,32,128]{2,1,0:T(8,128)S(1)} %shard_map.51.refs_1_), channel_id=1, source_target_pairs={{129,2},{130,1},{131,4},{132,3},{133,6},{134,5},{135,8},{136,7},{1... | collective-permute-start | bytes 196616 | tf_op jit(solution)/shard_map/ppermute | solution.py:166
  164.4 6.6 %collective-permute-start.14 = (f32[4,32,128]{2,1,0:T(8,128)S(1)}, f32[4,32,128]{2,1,0:T(8,128)S(1)}, u32[]{:S(2)}, u32[]{:S(2)}) collective-permute-start(f32[4,32,128]{2,1,0:T(8,128)S(1)} %shard_map.51.refs_1_), channel_id=1, source_target_pairs={{128,0},{129,1},{130,2},{131,3},{132,4},{133,5},{134,6},{135,7},{1... | collective-permute-start | bytes 196616 | tf_op jit(solution)/shard_map/ppermute | solution.py:166
  172.0 6.8 %collective-permute-start.15 = (f32[4,32,128]{2,1,0:T(8,128)S(1)}, f32[4,32,128]{2,1,0:T(8,128)S(1)}, u32[]{:S(2)}, u32[]{:S(2)}) collective-permute-start(f32[4,32,128]{2,1,0:T(8,128)S(1)} %shard_map.52.refs_1_), channel_id=1, source_target_pairs={{256,2},{258,0},{257,3},{259,1},{260,6},{262,4},{261,7},{263,5},{2... | collective-permute-start | bytes 196616 | tf_op jit(solution)/shard_map/ppermute | solution.py:166
  173.3 5.5 %collective-permute-start.16 = (f32[4,32,128]{2,1,0:T(8,128)S(1)}, f32[4,32,128]{2,1,0:T(8,128)S(1)}, u32[]{:S(2)}, u32[]{:S(2)}) collective-permute-start(f32[4,32,128]{2,1,0:T(8,128)S(1)} %shard_map.52.refs_1_), channel_id=1, source_target_pairs={{258,4},{260,2},{259,5},{261,3},{262,8},{264,6},{263,9},{265,7},{2... | collective-permute-start | bytes 196616 | tf_op jit(solution)/shard_map/ppermute | solution.py:166
  174.0 10.3 %collective-permute-start.17 = (f32[4,32,128]{2,1,0:T(8,128)S(1)}, f32[4,32,128]{2,1,0:T(8,128)S(1)}, u32[]{:S(2)}, u32[]{:S(2)}) collective-permute-start(f32[4,32,128]{2,1,0:T(8,128)S(1)} %shard_map.52.refs_1_), channel_id=1, source_target_pairs={{256,1},{257,0},{258,3},{259,2},{260,5},{261,4},{262,7},{263,6},{2... | collective-permute-start | bytes 196616 | tf_op jit(solution)/shard_map/ppermute | solution.py:166
  175.3 16.6 %collective-permute-start.18 = (f32[4,32,128]{2,1,0:T(8,128)S(1)}, f32[4,32,128]{2,1,0:T(8,128)S(1)}, u32[]{:S(2)}, u32[]{:S(2)}) collective-permute-start(f32[4,32,128]{2,1,0:T(8,128)S(1)} %shard_map.52.refs_1_), channel_id=1, source_target_pairs={{257,2},{258,1},{259,4},{260,3},{261,6},{262,5},{263,8},{264,7},{2... | collective-permute-start | bytes 196616 | tf_op jit(solution)/shard_map/ppermute | solution.py:166
  176.6 15.3 %collective-permute-start.19 = (f32[4,32,128]{2,1,0:T(8,128)S(1)}, f32[4,32,128]{2,1,0:T(8,128)S(1)}, u32[]{:S(2)}, u32[]{:S(2)}) collective-permute-start(f32[4,32,128]{2,1,0:T(8,128)S(1)} %shard_map.52.refs_1_), channel_id=1, source_target_pairs={{256,0},{257,1},{258,2},{259,3},{260,4},{261,5},{262,6},{263,7},{2... | collective-permute-start | bytes 196616 | tf_op jit(solution)/shard_map/ppermute | solution.py:166

commit v3 on v1

--- a/solution.py
+++ b/solution.py
@@ -179,8 +179,8 @@
     return jnp.concatenate([padded[i : i + SLABS] for i in range(2 * reach + 1)], axis=1)
 
 
-def to_rows(plane, reach):
-    arrived = lax.all_to_all(windows(plane, reach), "space", 0, 0)
+def to_rows(parts):
+    arrived = lax.all_to_all(parts, "space", 0, 0)
     return jnp.transpose(arrived, (1, 0, 2))
 
 
@@ -202,52 +202,74 @@
     odd = slab % 2 == 1
     is_final = slice_index == SLICES - 1
 
-    def trade(first, last):
-        across = lax.ppermute(jnp.where(odd, last, first), "space", facing(1, 1))
-        along = lax.ppermute(jnp.where(odd, first, last), "space", facing(1, 0))
+    def trade(to_before, to_after):
+        across = lax.ppermute(jnp.where(odd, to_after, to_before), "space", facing(1, 1))
+        along = lax.ppermute(jnp.where(odd, to_before, to_after), "space", facing(1, 0))
         return jnp.where(odd, along, across), jnp.where(odd, across, along)
 
-    local_row = receivers[0] // plane_size - slab * row_count
-    inside = (local_row >= 0) & (local_row < row_count)
-    target = jnp.where(inside, local_row * plane_size + receivers[0] % plane_size, row_count * plane_size)
-    flat_source = jnp.zeros((row_count * plane_size,), jnp.float32).at[target].add(residuals[0], mode="drop")
-    source = flat_source.reshape(row_count, width_y, width_z)
+    ring = slice_index % 4
+    quarter = width_y // 4
+    share = lax.dynamic_slice_in_dim(cond, ring * quarter, quarter, axis=1)
+    share = jnp.stack(trade(share[0], share[1]))
+    for bit in (1, 2):
+        upper = (ring // bit) % 2 == 1
+        other = lax.ppermute(share, "tm", [(n, n ^ bit) for n in range(SLICES)])
+        share = jnp.concatenate([jnp.where(upper, other, share), jnp.where(upper, share, other)], axis=1)
+    wide_cond = jnp.concatenate([share[:1], cond, share[1:]])
+
+    local_row = receivers[0] // plane_size - slab * row_count + 1
+    inside = (local_row >= 0) & (local_row < row_count + 2)
+    wide_size = (row_count + 2) * plane_size
+    target = jnp.where(inside, local_row * plane_size + receivers[0] % plane_size, wide_size)
+    flat_source = jnp.zeros((wide_size,), jnp.float32).at[target].add(residuals[0], mode="drop")
+    wide_source = flat_source.reshape(row_count + 2, width_y, width_z)
+    plane_place = slab * row_count - 1 + jnp.arange(row_count + 2)
+    in_grid = ((plane_place >= 0) & (plane_place < SLABS * row_count))[:, None, None]
 
     coarse_cond = restrict(cond) / FINE_STEPS
     plane_spread = 1.0 / (coarse_cond + 1.5)
     plane_keep = coarse_cond * plane_spread
     plane_spread = 0.25 * plane_spread
-    row_cond = to_rows(coarse_cond, 2)
+    coarse_start = restrict(start_field)
+
+    def two_sweeps(padded):
+        wide = padded[1:-1]
+        rhs_term = wide_cond * wide + wide_source
+        diagonal = wide_cond + 6.0
+        wide = jnp.where(in_grid, (rhs_term + inside_planes(padded)) / diagonal, 0.0)
+        return (rhs_term[1:-1] + inside_planes(wide)) / diagonal[1:-1]
+
+    before, after = trade(start_field, start_field)
+    coarse_now = plane_sweep(
+        coarse_start, coarse_start, restrict(before), restrict(after), plane_keep, plane_spread
+    )
+    field_now = two_sweeps(jnp.concatenate([before, start_field, after]))
+    slab_rows = row_count * width_y
+    sent = jnp.concatenate([field_now.reshape(slab_rows, width_z), coarse_now])
+    before, after = trade(sent, sent)
+    direct = plane_sweep(
+        coarse_now, coarse_start, before[slab_rows:], after[slab_rows:], plane_keep, plane_spread
+    )
+    before = before[:slab_rows].reshape(start_field.shape)
+    after = after[:slab_rows].reshape(start_field.shape)
+    field_now = two_sweeps(jnp.concatenate([before, field_now, after]))
+
+    term = restrict(field_now) - jnp.where(is_final, 0.0, direct)
+    second_half = slice_index % 2 == 1
+    cond_windows = windows(coarse_cond, 2)
+    cond_windows = jnp.where(second_half, cond_windows[:, 10:], cond_windows[:, :10])
+    arrived = to_rows(jnp.concatenate([windows(term, 1), cond_windows], axis=1))
+    rows, own_cond = arrived[:12], arrived[12:]
+    other_cond = lax.ppermute(own_cond, "tm", [(n, n ^ 1) for n in range(SLICES)])
+    row_cond = jnp.concatenate(
+        [jnp.where(second_half, other_cond, own_cond), jnp.where(second_half, own_cond, other_cond)]
+    )
     place = (slab - 2) * BLOCK + lax.broadcasted_iota(jnp.int32, row_cond.shape, 0)
     within = (place >= 0) & (place < PLANE)
     row_spread = jnp.where(within, 1.0 / (row_cond + 1.5), 0.0)
     row_keep = row_cond * row_spread
     row_spread = 0.25 * row_spread
 
-    diagonal = cond + 6.0
-    field_now = start_field
-    coarse_start = restrict(start_field)
-    coarse_now = coarse_start
-    sweep = 0
-    for step_index in range(FINE_STEPS):
-        rhs_term = cond * field_now + source
-        for sweep_index in range(SWEEPS):
-            first, last = field_now[0], field_now[1]
-            if sweep in (1, 2):
-                first = jnp.concatenate([first, coarse_now])
-                last = jnp.concatenate([last, coarse_now])
-            before, after = trade(first, last)
-            padded = jnp.concatenate([before[None, :width_y], field_now, after[None, :width_y]])
-            field_now = (rhs_term + inside_planes(padded)) / diagonal
-            if sweep in (1, 2):
-                coarse_now = plane_sweep(
-                    coarse_now, coarse_start, before[width_y:], after[width_y:], plane_keep, plane_spread
-                )
-            sweep += 1
-    direct = coarse_now
-
-    term = restrict(field_now) - jnp.where(is_final, 0.0, direct)
-    rows = to_rows(term, 1)
     later = [(i, i) for i in range(SLABS)]
     links = [from_later(rows[4 - k : 8 + k], k, later) for k in (4, 3, 2, 1)]
     inner = slice(BLOCK, 4 * BLOCK)

time: 224 us -> 216 us (0.964)
  blocking collectives: 34.5 us -> 99.1 us
  starting transfers between devices: 107 us -> 47.5 us
  waiting for transfers between devices: 63.2 us -> 44.1 us
    all_to_all x0 -> x1, blocking collectives: none -> 70.1 us  [to_rows(): arrived = lax.all_to_all(parts, 'space', 0, 0)]
    all_to_all x2 -> x0, starting transfers between devices: 65.4 us -> none  [to_rows(): arrived = lax.all_to_all(windows(plane, reach), 'space', 0, 0)]
    all_to_all x2 -> x0, waiting for transfers between devices: 32.1 us -> none  [to_rows(): arrived = lax.all_to_all(windows(plane, reach), 'space', 0, 0)]
    ppermute x12, waiting for transfers between devices: 23.4 us -> 31.6 us  [from_later(): return lax.ppermute(value, ('tm', 'space'), both)]
    all_to_all x1, blocking collectives: 34.5 us -> 29 us  [per_device(): back = lax.all_to_all(jnp.transpose(total, (1, 0, 2)), 'space', 0, 0)]
    ppermute x8 -> x9, waiting for transfers between devices: 7.7 us -> 12.6 us  [the longest x2 6.81 us: per_device(): other = lax.ppermute(share, 'tm', [(n, n ^ bit) for n in range(SLICES)])]
    ppermute x8 -> x9, starting transfers between devices: 23.9 us -> 28.5 us  [the longest x2 10.1 us: per_device(): other = lax.ppermute(share, 'tm', [(n, n ^ bit) for n in range(SLICES)])]
    unnamed x7 -> x17, local copies, waits for them, and re-layouts: 0.99 us -> 4.62 us
  transfers between devices with their start and end apart: 22 -> 21, of which waited for: 12 -> 11; matrix products, arithmetic and copies ran while one was open for 2% -> 1% of each run, Pallas kernels for 0% -> 0%
where the time goes in v3:
time: 216 us; the launch traced here: 214 us
  blocking collectives  99.1 us (46%)
  starting transfers between devices  47.5 us (22%)
  waiting for transfers between devices  44.1 us (20%)
  other arithmetic  9.7 us (4%)
  Pallas kernels  7.25 us (3%)
  local copies, waits for them, and re-layouts  5.02 us (2%)
    all_to_all x1, blocking collectives, to_rows(): arrived = lax.all_to_all(parts, 'space', 0, 0)  70.1 us
    ppermute x12, waiting for transfers between devices, from_later(): return lax.ppermute(value, ('tm', 'space'), both)  31.6 us
    all_to_all x1, blocking collectives, per_device(): back = lax.all_to_all(jnp.transpose(total, (1, 0, 2)), 'space', 0, 0)  29 us
    ppermute x12, starting transfers between devices, from_later(): return lax.ppermute(value, ('tm', 'space'), both)  19 us
    ppermute x2, starting transfers between devices, per_device(): other = lax.ppermute(share, 'tm', [(n, n ^ bit) for n in range(SLICES)])  10.1 us
    ppermute x3, starting transfers between devices, trade(): lax.ppermute(jnp.where(odd, to_after, to_before), 'space', facing(1, 1))  9.53 us
    ppermute x2, waiting for transfers between devices, per_device(): other = lax.ppermute(share, 'tm', [(n, n ^ bit) for n in range(SLICES)])  6.81 us
    ppermute x3, starting transfers between devices, trade(): lax.ppermute(jnp.where(odd, to_before, to_after), 'space', facing(1, 0))  6.43 us
  transfers between devices with their start and end apart: 21, of which 11 were waited for; matrix products, arithmetic and copies ran while one was open for 1% of the time, Pallas kernels for 0%

profile of v3, /device:TPU:7, one launch (start us, length us, event | category | flops | bytes accessed | tf_op | source)
XLA Modules:
  0.0 213.5 jit_solution(2203589426343263732)
XLA Ops:
  0.0 0.9 select_bitcast_fusion.3
  0.9 2.6 %collective-permute-start.2 = (f32[128,128]{1,0:T(8,128)S(1)}, f32[128,128]{1,0:T(8,128)S(1)}, u32[]{:S(2)}, u32[]{:S(2)}) collective-permute-start(f32[128,128]{1,0:T(8,128)S(1)} %get-tuple-element.18), channel_id=1, source_target_pairs={{0,1},{1,0},{2,3},{3,2},{4,5},{5,4},{6,7},{7,6},{8,9},{9,8},{10,11... | collective-permute-start | bytes 196616 | tf_op jit(solution)/shard_map/ppermute | solution.py:207
  3.5 3.1 %collective-permute-start.3 = (f32[128,128]{1,0:T(8,128)S(1)}, f32[128,128]{1,0:T(8,128)S(1)}, u32[]{:S(2)}, u32[]{:S(2)}) collective-permute-start(f32[128,128]{1,0:T(8,128)S(1)} %get-tuple-element.19), channel_id=1, source_target_pairs={{1,2},{2,1},{3,4},{4,3},{5,6},{6,5},{7,8},{8,7},{9,10},{10,9},{11,... | collective-permute-start | bytes 196616 | tf_op jit(solution)/shard_map/ppermute | solution.py:206
  6.6 2.5 %collective-permute-start.1 = (f32[2,512,128]{2,1,0:T(8,128)}, f32[2,512,128]{2,1,0:T(8,128)}, u32[]{:S(2)}, u32[]{:S(2)}) collective-permute-start(f32[2,512,128]{2,1,0:T(8,128)} %bitcast.38), channel_id=1, source_target_pairs={{1,2},{2,1},{3,4},{4,3},{5,6},{6,5},{7,8},{8,7},{9,10},{10,9},{11,... | collective-permute-start | bytes 1572872 | tf_op jit(solution)/shard_map/ppermute | solution.py:206
  9.1 1.9 collective-permute-start
  11.0 1.0 copy-done
  12.1 0.3 shard_map.49
  12.4 2.6 %collective-permute-start.4 = (f32[2,128,128]{2,1,0:T(8,128)S(1)}, f32[2,128,128]{2,1,0:T(8,128)S(1)}, u32[]{:S(2)}, u32[]{:S(2)}) collective-permute-start(f32[2,128,128]{2,1,0:T(8,128)S(1)} %pad_maximum_fusion.13), channel_id=1, source_target_pairs={{0,32},{32,0},{64,96},{96,64},{128,160},{160,128},{192,224},{224,1... | collective-permute-start | bytes 393224 | tf_op jit(solution)/shard_map/ppermute | solution.py:216
  15.1 4.0 %collective-permute-done.4 = f32[2,128,128]{2,1,0:T(8,128)S(1)} collective-permute-done((f32[2,128,128]{2,1,0:T(8,128)S(1)}, f32[2,128,128]{2,1,0:T(8,128)S(1)}, u32[]{:S(2)}, u32[]{:S(2)}) %collective-permute-start.4) | collective-permute-done | bytes 131104 | tf_op jit(solution)/shard_map/ppermute | solution.py:216
  19.1 7.5 %collective-permute-start.5 = (f32[2,256,128]{2,1,0:T(8,128)S(1)}, f32[2,256,128]{2,1,0:T(8,128)S(1)}, u32[]{:S(2)}, u32[]{:S(2)}) collective-permute-start(f32[2,256,128]{2,1,0:T(8,128)S(1)} %pad_maximum_fusion.11), channel_id=1, source_target_pairs={{0,64},{32,96},{64,0},{96,32},{128,192},{160,224},{192,128},{224,1... | collective-permute-start | bytes 786440 | tf_op jit(solution)/shard_map/ppermute | solution.py:216
  26.7 0.3 shard_map.46.state_ref.start_ref
  27.0 2.4 %scatter_custom_fusion = f32[262144]{0:T(1024)S(1)} fusion(s32[256]{0:T(256)S(1)} %bitcast.61, f32[256]{0:T(256)} %bitcast.62, f32[]{:T(128)} %constant.147.clone.1), kind=kCustom, calls=%fused_computation.60 | custom fusion | flops 256 | bytes 1049088 | tf_op jit(solution)/shard_map/scatter-add | solution.py:224
  29.4 2.8 %collective-permute-done.5 = f32[2,256,128]{2,1,0:T(8,128)S(1)} collective-permute-done((f32[2,256,128]{2,1,0:T(8,128)S(1)}, f32[2,256,128]{2,1,0:T(8,128)S(1)}, u32[]{:S(2)}, u32[]{:S(2)}) %collective-permute-start.5) | collective-permute-done | bytes 262176 | tf_op jit(solution)/shard_map/ppermute | solution.py:216
  32.3 1.4 broadcast_select_fusion.2
  33.7 0.3 shard_map.48.after_ref
  34.0 0.3 shard_map.47.before_ref
  34.4 0.9 copy-done.1
  35.3 0.7 fusion.14
  36.1 0.3 fusion.20
  36.4 0.6 copy-done.3
  37.0 0.1 shard_map.50.state_ref
  37.1 0.9 pad_maximum_fusion.4
  38.0 4.0 %collective-permute-start.7 = (f32[1152,128]{1,0:T(8,128)}, f32[1152,128]{1,0:T(8,128)}, u32[]{:S(2)}, u32[]{:S(2)}) collective-permute-start(f32[1152,128]{1,0:T(8,128)} %pad_maximum_fusion.4), channel_id=1, source_target_pairs={{1,2},{2,1},{3,4},{4,3},{5,6},{6,5},{7,8},{8,7},{9,10},{10,9},{11,... | collective-permute-start | bytes 1769480 | tf_op jit(solution)/shard_map/ppermute | solution.py:206
  42.0 1.9 collective-permute-start.6
  43.9 0.1 fusion.31
  44.1 5.7 %collective-permute-done.7 = f32[1152,128]{1,0:T(8,128)} collective-permute-done((f32[1152,128]{1,0:T(8,128)}, f32[1152,128]{1,0:T(8,128)}, u32[]{:S(2)}, u32[]{:S(2)}) %collective-permute-start.7) | collective-permute-done | bytes 589856 | tf_op jit(solution)/shard_map/ppermute | solution.py:206
  49.8 1.3 broadcast_select_fusion
  51.3 0.1 pad_maximum_fusion
  51.4 0.9 copy-done.6
  52.2 0.7 fusion.13
  53.0 1.2 copy-done.4
  54.2 0.3 fusion.26.field_ref
  54.5 0.3 shard_map.52
  54.8 0.1 shard_map.51
  55.0 0.1 pad_maximum_fusion.5
  55.1 70.1 %all_to_all.10 = f32[32,22,128]{2,1,0:T(8,128)S(1)} all-to-all(f32[32,22,128]{2,1,0:T(8,128)S(1)} %pad_maximum_fusion.5), channel_id=1, replica_groups=mesh['tm'=16,'space'=32] {'space'}, dimensions={0} | all-to-all | bytes 720896 | tf_op jit(solution)/shard_map/all_to_all | solution.py:183
  125.2 0.1 copy.17
  125.3 2.5 %collective-permute-start.12 = (f32[10,32,128]{2,1,0:T(8,128)S(1)}, f32[10,32,128]{2,1,0:T(8,128)S(1)}, u32[]{:S(2)}, u32[]{:S(2)}) collective-permute-start(f32[10,32,128]{2,1,0:T(8,128)S(1)} %slice.239), channel_id=1, source_target_pairs={{0,32},{32,0},{64,96},{96,64},{128,160},{160,128},{192,224},{224,1... | collective-permute-start | bytes 491528 | tf_op jit(solution)/shard_map/ppermute | solution.py:263
  127.8 2.8 %collective-permute-start.11 = (f32[6,32,128]{2,1,0:T(8,128)S(1)}, f32[6,32,128]{2,1,0:T(8,128)S(1)}, u32[]{:S(2)}, u32[]{:S(2)}) collective-permute-start(f32[6,32,128]{2,1,0:T(8,128)S(1)} %slice.238), channel_id=1, source_target_pairs={{32,0},{33,1},{34,2},{35,3},{36,4},{37,5},{38,6},{39,7},{40,8},{41... | collective-permute-start | bytes 294920 | tf_op jit(solution)/shard_map/ppermute | solution.py:166
  130.7 3.0 %collective-permute-start.10 = (f32[8,32,128]{2,1,0:T(8,128)S(1)}, f32[8,32,128]{2,1,0:T(8,128)S(1)}, u32[]{:S(2)}, u32[]{:S(2)}) collective-permute-start(f32[8,32,128]{2,1,0:T(8,128)S(1)} %slice.237), channel_id=1, source_target_pairs={{64,0},{65,1},{66,2},{67,3},{68,4},{69,5},{70,6},{71,7},{72,8},{73... | collective-permute-start | bytes 393224 | tf_op jit(solution)/shard_map/ppermute | solution.py:166
  133.7 1.3 collective-permute-start.8
  135.1 1.9 collective-permute-start.9
  137.0 0.1 fusion.32
  137.2 2.3 %collective-permute-done.10.c2_ref = f32[8,32,128]{2,1,0:T(8,128)S(1)} collective-permute-done((f32[8,32,128]{2,1,0:T(8,128)S(1)}, f32[8,32,128]{2,1,0:T(8,128)S(1)}, u32[]{:S(2)}, u32[]{:S(2)}) %collective-permute-start.10) | collective-permute-done | bytes 131104 | tf_op jit(solution)/shard_map/ppermute | solution.py:166
  139.5 2.5 %collective-permute-done.8.c4_ref = f32[12,32,128]{2,1,0:T(8,128)S(1)} collective-permute-done((f32[12,32,128]{2,1,0:T(8,128)S(1)}, f32[12,32,128]{2,1,0:T(8,128)S(1)}, u32[]{:S(2)}, u32[]{:S(2)}) %collective-permute-start.8) | collective-permute-done | bytes 196640 | tf_op jit(solution)/shard_map/ppermute | solution.py:166
  142.0 1.2 collective-permute-done.9.c3_ref
  143.1 1.0 shard_map.53.refs_1_
  144.1 1.3 collective-permute-start.14
  145.4 1.3 collective-permute-start.13
  146.7 1.3 collective-permute-start.15
  148.0 8.0 %collective-permute-done.14 = f32[4,32,128]{2,1,0:T(8,128)S(1)} collective-permute-done((f32[4,32,128]{2,1,0:T(8,128)S(1)}, f32[4,32,128]{2,1,0:T(8,128)S(1)}, u32[]{:S(2)}, u32[]{:S(2)}) %collective-permute-start.14) | collective-permute-done | bytes 65568 | tf_op jit(solution)/shard_map/ppermute | solution.py:166
  156.0 0.8 collective-permute-done.13
  156.8 2.0 collective-permute-done.15
  158.8 1.0 shard_map.54.refs_1_
  159.8 0.7 collective-permute-start.17
  160.5 1.3 collective-permute-start.16
  161.8 1.3 collective-permute-start.20
  163.1 1.3 collective-permute-start.19
  164.4 1.5 collective-permute-start.18
  165.9 11.3 %collective-permute-done.16 = f32[4,32,128]{2,1,0:T(8,128)S(1)} collective-permute-done((f32[4,32,128]{2,1,0:T(8,128)S(1)}, f32[4,32,128]{2,1,0:T(8,128)S(1)}, u32[]{:S(2)}, u32[]{:S(2)}) %collective-permute-start.16) | collective-permute-done | bytes 65568 | tf_op jit(solution)/shard_map/ppermute | solution.py:166
  177.3 3.5 %collective-permute-done.19 = f32[4,32,128]{2,1,0:T(8,128)S(1)} collective-permute-done((f32[4,32,128]{2,1,0:T(8,128)S(1)}, f32[4,32,128]{2,1,0:T(8,128)S(1)}, u32[]{:S(2)}, u32[]{:S(2)}) %collective-permute-start.19) | collective-permute-done | bytes 65568 | tf_op jit(solution)/shard_map/ppermute | solution.py:166
  180.8 2.6 %shard_map.55 = f32[4,32,128]{2,1,0:T(8,128)S(1)} custom-call(f32[20,32,128]{2,1,0:T(8,128)S(1)} %select_dynamic-update-slice_fusion.refs_0_, f32[4,32,128]{2,1,0:T(8,128)S(1)} %shard_map.54.refs_1_, f32[20,32,128]{2,1,0:T(8,128)S(1)} %get-tuple-element.22.refs_2_, f32[20,32,128]{2,1,0:T(8,128)S(1)} %get-tuple-element.21.refs_3_), custom_call_target="tpu_custom_call" | custom-call | tf_op jit(solution)/shard_map/pallas_call | solution.py:148
  183.5 29.0 %all_to_all.11 = f32[32,4,128]{2,1,0:T(4,128)S(1)} all-to-all(f32[32,4,128]{2,1,0:T(4,128)S(1)} %copy.15), channel_id=1, replica_groups=mesh['tm'=16,'space'=32] {'space'}, dimensions={0} | all-to-all | bytes 131072 | tf_op jit(solution)/shard_map/all_to_all | solution.py:291
  212.4 1.1 shard_map.56
  (57 shorter events, 0.8 us)
Async XLA Ops:
  0.9 11.5 %collective-permute-start.2 = (f32[128,128]{1,0:T(8,128)S(1)}, f32[128,128]{1,0:T(8,128)S(1)}, u32[]{:S(2)}, u32[]{:S(2)}) collective-permute-start(f32[128,128]{1,0:T(8,128)S(1)} %get-tuple-element.18), channel_id=1, source_target_pairs={{0,1},{1,0},{2,3},{3,2},{4,5},{5,4},{6,7},{7,6},{8,9},{9,8},{10,11... | collective-permute-start | bytes 196616 | tf_op jit(solution)/shard_map/ppermute | solution.py:207
  3.5 8.9 %collective-permute-start.3 = (f32[128,128]{1,0:T(8,128)S(1)}, f32[128,128]{1,0:T(8,128)S(1)}, u32[]{:S(2)}, u32[]{:S(2)}) collective-permute-start(f32[128,128]{1,0:T(8,128)S(1)} %get-tuple-element.19), channel_id=1, source_target_pairs={{1,2},{2,1},{3,4},{4,3},{5,6},{6,5},{7,8},{8,7},{9,10},{10,9},{11,... | collective-permute-start | bytes 196616 | tf_op jit(solution)/shard_map/ppermute | solution.py:206
  6.6 25.7 %collective-permute-start.1 = (f32[2,512,128]{2,1,0:T(8,128)}, f32[2,512,128]{2,1,0:T(8,128)}, u32[]{:S(2)}, u32[]{:S(2)}) collective-permute-start(f32[2,512,128]{2,1,0:T(8,128)} %bitcast.38), channel_id=1, source_target_pairs={{1,2},{2,1},{3,4},{4,3},{5,6},{6,5},{7,8},{8,7},{9,10},{10,9},{11,... | collective-permute-start | bytes 1572872 | tf_op jit(solution)/shard_map/ppermute | solution.py:206
  9.1 23.3 %collective-permute-start = (f32[2,512,128]{2,1,0:T(8,128)}, f32[2,512,128]{2,1,0:T(8,128)}, u32[]{:S(2)}, u32[]{:S(2)}) collective-permute-start(f32[2,512,128]{2,1,0:T(8,128)} %bitcast.39), channel_id=1, source_target_pairs={{0,1},{1,0},{2,3},{3,2},{4,5},{5,4},{6,7},{7,6},{8,9},{9,8},{10,11... | collective-permute-start | bytes 1572872 | tf_op jit(solution)/shard_map/ppermute | solution.py:207
  11.0 1.0 copy-start
  12.3 14.3 %copy-start.7 = (s32[1,256]{1,0:T(1,128)S(1)}, s32[1,256]{1,0:T(1,128)}, u32[]{:S(2)}) copy-start(s32[1,256]{1,0:T(1,128)} %param.6) | copy-start | bytes 3076
  12.3 14.3 %copy-start.2 = (f32[1,2,512,128]{3,2,1,0:T(8,128)S(1)}, f32[1,2,512,128]{3,2,1,0:T(8,128)}, u32[]{:S(2)}) copy-start(f32[1,2,512,128]{3,2,1,0:T(8,128)} %param.4) | copy-start | bytes 1572868
  12.4 6.6 %collective-permute-start.4 = (f32[2,128,128]{2,1,0:T(8,128)S(1)}, f32[2,128,128]{2,1,0:T(8,128)S(1)}, u32[]{:S(2)}, u32[]{:S(2)}) collective-permute-start(f32[2,128,128]{2,1,0:T(8,128)S(1)} %pad_maximum_fusion.13), channel_id=1, source_target_pairs={{0,32},{32,0},{64,96},{96,64},{128,160},{160,128},{192,224},{224,1... | collective-permute-start | bytes 393224 | tf_op jit(solution)/shard_map/ppermute | solution.py:216
  19.1 13.2 %collective-permute-start.5 = (f32[2,256,128]{2,1,0:T(8,128)S(1)}, f32[2,256,128]{2,1,0:T(8,128)S(1)}, u32[]{:S(2)}, u32[]{:S(2)}) collective-permute-start(f32[2,256,128]{2,1,0:T(8,128)S(1)} %pad_maximum_fusion.11), channel_id=1, source_target_pairs={{0,64},{32,96},{64,0},{96,32},{128,192},{160,224},{192,128},{224,1... | collective-permute-start | bytes 786440 | tf_op jit(solution)/shard_map/ppermute | solution.py:216
  32.3 2.0 copy-start.5
  34.3 1.0 copy-start.1
  36.0 1.0 copy-start.3
  38.0 11.8 %collective-permute-start.7 = (f32[1152,128]{1,0:T(8,128)}, f32[1152,128]{1,0:T(8,128)}, u32[]{:S(2)}, u32[]{:S(2)}) collective-permute-start(f32[1152,128]{1,0:T(8,128)} %pad_maximum_fusion.4), channel_id=1, source_target_pairs={{1,2},{2,1},{3,4},{4,3},{5,6},{6,5},{7,8},{8,7},{9,10},{10,9},{11,... | collective-permute-start | bytes 1769480 | tf_op jit(solution)/shard_map/ppermute | solution.py:206
  42.0 7.9 %collective-permute-start.6 = (f32[1152,128]{1,0:T(8,128)}, f32[1152,128]{1,0:T(8,128)}, u32[]{:S(2)}, u32[]{:S(2)}) collective-permute-start(f32[1152,128]{1,0:T(8,128)} %pad_maximum_fusion.4), channel_id=1, source_target_pairs={{0,1},{1,0},{2,3},{3,2},{4,5},{5,4},{6,7},{7,6},{8,9},{9,8},{10,11... | collective-permute-start | bytes 1769480 | tf_op jit(solution)/shard_map/ppermute | solution.py:207
  51.3 1.0 copy-start.6
  53.0 1.2 copy-start.4
  125.3 9.7 %collective-permute-start.12 = (f32[10,32,128]{2,1,0:T(8,128)S(1)}, f32[10,32,128]{2,1,0:T(8,128)S(1)}, u32[]{:S(2)}, u32[]{:S(2)}) collective-permute-start(f32[10,32,128]{2,1,0:T(8,128)S(1)} %slice.239), channel_id=1, source_target_pairs={{0,32},{32,0},{64,96},{96,64},{128,160},{160,128},{192,224},{224,1... | collective-permute-start | bytes 491528 | tf_op jit(solution)/shard_map/ppermute | solution.py:263
  127.8 9.3 %collective-permute-start.11 = (f32[6,32,128]{2,1,0:T(8,128)S(1)}, f32[6,32,128]{2,1,0:T(8,128)S(1)}, u32[]{:S(2)}, u32[]{:S(2)}) collective-permute-start(f32[6,32,128]{2,1,0:T(8,128)S(1)} %slice.238), channel_id=1, source_target_pairs={{32,0},{33,1},{34,2},{35,3},{36,4},{37,5},{38,6},{39,7},{40,8},{41... | collective-permute-start | bytes 294920 | tf_op jit(solution)/shard_map/ppermute | solution.py:166
  130.7 8.8 %collective-permute-start.10 = (f32[8,32,128]{2,1,0:T(8,128)S(1)}, f32[8,32,128]{2,1,0:T(8,128)S(1)}, u32[]{:S(2)}, u32[]{:S(2)}) collective-permute-start(f32[8,32,128]{2,1,0:T(8,128)S(1)} %slice.237), channel_id=1, source_target_pairs={{64,0},{65,1},{66,2},{67,3},{68,4},{69,5},{70,6},{71,7},{72,8},{73... | collective-permute-start | bytes 393224 | tf_op jit(solution)/shard_map/ppermute | solution.py:166
  133.7 8.2 %collective-permute-start.8 = (f32[12,32,128]{2,1,0:T(8,128)S(1)}, f32[12,32,128]{2,1,0:T(8,128)S(1)}, u32[]{:S(2)}, u32[]{:S(2)}) collective-permute-start(f32[12,32,128]{2,1,0:T(8,128)S(1)} %slice.235), channel_id=1, source_target_pairs={{128,0},{129,1},{130,2},{131,3},{132,4},{133,5},{134,6},{135,7},{1... | collective-permute-start | bytes 589832 | tf_op jit(solution)/shard_map/ppermute | solution.py:166
  135.1 8.0 %collective-permute-start.9 = (f32[10,32,128]{2,1,0:T(8,128)S(1)}, f32[10,32,128]{2,1,0:T(8,128)S(1)}, u32[]{:S(2)}, u32[]{:S(2)}) collective-permute-start(f32[10,32,128]{2,1,0:T(8,128)S(1)} %get-tuple-element.20), channel_id=1, source_target_pairs={{96,0},{97,1},{98,2},{99,3},{100,4},{101,5},{102,6},{103,7},{104,8... | collective-permute-start | bytes 491528 | tf_op jit(solution)/shard_map/ppermute | solution.py:166
  144.1 11.9 %collective-permute-start.14 = (f32[4,32,128]{2,1,0:T(8,128)S(1)}, f32[4,32,128]{2,1,0:T(8,128)S(1)}, u32[]{:S(2)}, u32[]{:S(2)}) collective-permute-start(f32[4,32,128]{2,1,0:T(8,128)S(1)} %shard_map.53.refs_1_), channel_id=1, source_target_pairs={{129,2},{130,1},{131,4},{132,3},{133,6},{134,5},{135,8},{136,7},{1... | collective-permute-start | bytes 196616 | tf_op jit(solution)/shard_map/ppermute | solution.py:166
  145.4 11.3 %collective-permute-start.13 = (f32[4,32,128]{2,1,0:T(8,128)S(1)}, f32[4,32,128]{2,1,0:T(8,128)S(1)}, u32[]{:S(2)}, u32[]{:S(2)}) collective-permute-start(f32[4,32,128]{2,1,0:T(8,128)S(1)} %shard_map.53.refs_1_), channel_id=1, source_target_pairs={{128,1},{129,0},{130,3},{131,2},{132,5},{133,4},{134,7},{135,6},{1... | collective-permute-start | bytes 196616 | tf_op jit(solution)/shard_map/ppermute | solution.py:166
  146.7 12.1 %collective-permute-start.15 = (f32[4,32,128]{2,1,0:T(8,128)S(1)}, f32[4,32,128]{2,1,0:T(8,128)S(1)}, u32[]{:S(2)}, u32[]{:S(2)}) collective-permute-start(f32[4,32,128]{2,1,0:T(8,128)S(1)} %shard_map.53.refs_1_), channel_id=1, source_target_pairs={{128,0},{129,1},{130,2},{131,3},{132,4},{133,5},{134,6},{135,7},{1... | collective-permute-start | bytes 196616 | tf_op jit(solution)/shard_map/ppermute | solution.py:166
  159.8 6.1 %collective-permute-start.17 = (f32[4,32,128]{2,1,0:T(8,128)S(1)}, f32[4,32,128]{2,1,0:T(8,128)S(1)}, u32[]{:S(2)}, u32[]{:S(2)}) collective-permute-start(f32[4,32,128]{2,1,0:T(8,128)S(1)} %shard_map.54.refs_1_), channel_id=1, source_target_pairs={{258,4},{260,2},{259,5},{261,3},{262,8},{264,6},{263,9},{265,7},{2... | collective-permute-start | bytes 196616 | tf_op jit(solution)/shard_map/ppermute | solution.py:166
  160.5 16.8 %collective-permute-start.16 = (f32[4,32,128]{2,1,0:T(8,128)S(1)}, f32[4,32,128]{2,1,0:T(8,128)S(1)}, u32[]{:S(2)}, u32[]{:S(2)}) collective-permute-start(f32[4,32,128]{2,1,0:T(8,128)S(1)} %shard_map.54.refs_1_), channel_id=1, source_target_pairs={{256,2},{258,0},{257,3},{259,1},{260,6},{262,4},{261,7},{263,5},{2... | collective-permute-start | bytes 196616 | tf_op jit(solution)/shard_map/ppermute | solution.py:166
  161.8 18.9 %collective-permute-start.20 = (f32[4,32,128]{2,1,0:T(8,128)S(1)}, f32[4,32,128]{2,1,0:T(8,128)S(1)}, u32[]{:S(2)}, u32[]{:S(2)}) collective-permute-start(f32[4,32,128]{2,1,0:T(8,128)S(1)} %shard_map.54.refs_1_), channel_id=1, source_target_pairs={{256,0},{257,1},{258,2},{259,3},{260,4},{261,5},{262,6},{263,7},{2... | collective-permute-start | bytes 196616 | tf_op jit(solution)/shard_map/ppermute | solution.py:166
  163.1 17.6 %collective-permute-start.19 = (f32[4,32,128]{2,1,0:T(8,128)S(1)}, f32[4,32,128]{2,1,0:T(8,128)S(1)}, u32[]{:S(2)}, u32[]{:S(2)}) collective-permute-start(f32[4,32,128]{2,1,0:T(8,128)S(1)} %shard_map.54.refs_1_), channel_id=1, source_target_pairs={{257,2},{258,1},{259,4},{260,3},{261,6},{262,5},{263,8},{264,7},{2... | collective-permute-start | bytes 196616 | tf_op jit(solution)/shard_map/ppermute | solution.py:166
  164.4 16.3 %collective-permute-start.18 = (f32[4,32,128]{2,1,0:T(8,128)S(1)}, f32[4,32,128]{2,1,0:T(8,128)S(1)}, u32[]{:S(2)}, u32[]{:S(2)}) collective-permute-start(f32[4,32,128]{2,1,0:T(8,128)S(1)} %shard_map.54.refs_1_), channel_id=1, source_target_pairs={{256,1},{257,0},{258,3},{259,2},{260,5},{261,4},{262,7},{263,6},{2... | collective-permute-start | bytes 196616 | tf_op jit(solution)/shard_map/ppermute | solution.py:166

commit v4 on v3

--- a/solution.py
+++ b/solution.py
@@ -240,6 +240,26 @@
         return (rhs_term[1:-1] + inside_planes(wide)) / diagonal[1:-1]
 
     before, after = trade(start_field, start_field)
+
+    tall = jnp.pad(coarse_cond, ((2 * BLOCK, 2 * BLOCK), (0, 0)))
+    shares = []
+    for i in range(2):
+        at = (slab - 2 * slice_index - i) % SLABS
+        window = lax.dynamic_slice_in_dim(tall, at * BLOCK, 5 * BLOCK, axis=0)
+        pairs = [
+            (n * SLABS + j, n * SLABS + (j - 2 * n - i) % SLABS) for n in range(SLICES) for j in range(SLABS)
+        ]
+        shares.append(lax.ppermute(window, ("tm", "space"), pairs))
+    gathered = jnp.stack(shares)
+    for bit in (1, 2, 4, 8):
+        upper = (slice_index // bit) % 2 == 1
+        other = lax.ppermute(gathered, "tm", [(n, n ^ bit) for n in range(SLICES)])
+        gathered = jnp.concatenate([jnp.where(upper, other, gathered), jnp.where(upper, gathered, other)])
+    turned = lax.dynamic_slice_in_dim(
+        jnp.concatenate([gathered, gathered]), (SLABS - slab) % SLABS, SLABS, axis=0
+    )
+    row_cond = jnp.transpose(turned, (1, 0, 2))
+
     coarse_now = plane_sweep(
         coarse_start, coarse_start, restrict(before), restrict(after), plane_keep, plane_spread
     )
@@ -255,15 +275,7 @@
     field_now = two_sweeps(jnp.concatenate([before, field_now, after]))
 
     term = restrict(field_now) - jnp.where(is_final, 0.0, direct)
-    second_half = slice_index % 2 == 1
-    cond_windows = windows(coarse_cond, 2)
-    cond_windows = jnp.where(second_half, cond_windows[:, 10:], cond_windows[:, :10])
-    arrived = to_rows(jnp.concatenate([windows(term, 1), cond_windows], axis=1))
-    rows, own_cond = arrived[:12], arrived[12:]
-    other_cond = lax.ppermute(own_cond, "tm", [(n, n ^ 1) for n in range(SLICES)])
-    row_cond = jnp.concatenate(
-        [jnp.where(second_half, other_cond, own_cond), jnp.where(second_half, own_cond, other_cond)]
-    )
+    rows = to_rows(windows(term, 1))
     place = (slab - 2) * BLOCK + lax.broadcasted_iota(jnp.int32, row_cond.shape, 0)
     within = (place >= 0) & (place < PLANE)
     row_spread = jnp.where(within, 1.0 / (row_cond + 1.5), 0.0)
@@ -283,9 +295,15 @@
     )
 
     centre = from_later(total, 8, later)
-    before, after = beside_later(total, 8, 1, slab)
-    before_two, after_two = beside_later(total, 8, 2, slab)
-    window = jnp.concatenate([before_two, before, centre, after, after_two])
+    near = from_later(total, 8, facing(1, 1))
+    outward = [(j - 2, j) for j in range(2, SLABS, 2)] + [(j + 2, j) for j in range(1, SLABS - 2, 2)]
+    far = from_later(total, 8, outward)
+    swapped = lax.ppermute(jnp.stack([centre, near]), "space", facing(1, 0))
+    window = jnp.where(
+        odd,
+        jnp.concatenate([swapped[1], swapped[0], centre, near, far]),
+        jnp.concatenate([far, near, centre, swapped[0], swapped[1]]),
+    )
     total = chain_call(lambda *refs: power_kernel(8, *refs), 20, window, total, row_keep, row_spread)
 
     back = lax.all_to_all(jnp.transpose(total, (1, 0, 2)), "space", 0, 0)

time: 216 us -> 209 us (0.968)
  blocking collectives: 99.1 us -> 28.8 us
  starting transfers between devices: 47.5 us -> 106 us
  waiting for transfers between devices: 44.1 us -> 46.3 us
    all_to_all x1 -> x0, blocking collectives: 70.1 us -> none  [to_rows(): arrived = lax.all_to_all(parts, 'space', 0, 0)]
    ppermute x1 -> x7, starting transfers between devices: 2.45 us -> 37.7 us  [the longest x2 20.3 us: per_device(): shares.append(lax.ppermute(window, ('tm', 'space'), pairs))]
    all_to_all x0 -> x1, starting transfers between devices: none -> 29.7 us  [to_rows(): arrived = lax.all_to_all(parts, 'space', 0, 0)]
    ppermute x1 -> x7, waiting for transfers between devices: 0.01 us -> 22.2 us  [the longest x4 14.6 us: per_device(): other = lax.ppermute(gathered, 'tm', [(n, n ^ bit) for n in range(SLICES)])]
    ppermute x12 -> x10, waiting for transfers between devices: 31.6 us -> 24.1 us  [from_later(): return lax.ppermute(value, ('tm', 'space'), both)]
    ppermute x2, waiting for transfers between devices: 6.81 us -> 0.01 us  [per_device(): other = lax.ppermute(share, 'tm', [(n, n ^ bit) for n in range(SLICES)])]
    ppermute x3, waiting for transfers between devices: 5.75 us -> 0.01 us  [trade(): lax.ppermute(jnp.where(odd, to_after, to_before), 'space', facing(1, 1))]
    ppermute x2, starting transfers between devices: 10.1 us -> 4.51 us  [per_device(): other = lax.ppermute(share, 'tm', [(n, n ^ bit) for n in range(SLICES)])]
  transfers between devices with their start and end apart: 21 -> 26, of which waited for: 11 -> 10; matrix products, arithmetic and copies ran while one was open for 1% -> 5% of each run, Pallas kernels for 0% -> 1%
where the time goes in v4:
time: 209 us; the launch traced here: 206 us
  starting transfers between devices  106 us (51%)
  waiting for transfers between devices  46.3 us (22%)
  blocking collectives  28.8 us (14%)
  other arithmetic  11.3 us (5%)
  Pallas kernels  7.25 us (3%)
  local copies, waits for them, and re-layouts  5.08 us (2%)
    all_to_all x1, starting transfers between devices, to_rows(): arrived = lax.all_to_all(parts, 'space', 0, 0)  29.7 us
    all_to_all x1, blocking collectives, per_device(): back = lax.all_to_all(jnp.transpose(total, (1, 0, 2)), 'space', 0, 0)  28.8 us
    ppermute x10, waiting for transfers between devices, from_later(): return lax.ppermute(value, ('tm', 'space'), both)  24.1 us
    ppermute x2, starting transfers between devices, per_device(): shares.append(lax.ppermute(window, ('tm', 'space'), pairs))  20.3 us
    ppermute x10, starting transfers between devices, from_later(): return lax.ppermute(value, ('tm', 'space'), both)  18.1 us
    ppermute x4, starting transfers between devices, per_device(): other = lax.ppermute(gathered, 'tm', [(n, n ^ bit) for n in range(SLICES)])  15.2 us
    ppermute x4, waiting for transfers between devices, per_device(): other = lax.ppermute(gathered, 'tm', [(n, n ^ bit) for n in range(SLICES)])  14.6 us
    ppermute x3, starting transfers between devices, trade(): lax.ppermute(jnp.where(odd, to_after, to_before), 'space', facing(1, 1))  9.41 us
  transfers between devices with their start and end apart: 26, of which 10 were waited for; matrix products, arithmetic and copies ran while one was open for 5% of the time, Pallas kernels for 1%

profile of v4, /device:TPU:7, one launch (start us, length us, event | category | flops | bytes accessed | tf_op | source)
XLA Modules:
  0.0 205.5 jit_solution(2286024915803737308)
XLA Ops:
  0.0 0.9 select_bitcast_fusion.3
  0.9 2.6 %collective-permute-start.2 = (f32[128,128]{1,0:T(8,128)S(1)}, f32[128,128]{1,0:T(8,128)S(1)}, u32[]{:S(2)}, u32[]{:S(2)}) collective-permute-start(f32[128,128]{1,0:T(8,128)S(1)} %get-tuple-element.18), channel_id=1, source_target_pairs={{0,1},{1,0},{2,3},{3,2},{4,5},{5,4},{6,7},{7,6},{8,9},{9,8},{10,11... | collective-permute-start | bytes 196616 | tf_op jit(solution)/shard_map/ppermute | solution.py:207
  3.5 3.1 %collective-permute-start.3 = (f32[128,128]{1,0:T(8,128)S(1)}, f32[128,128]{1,0:T(8,128)S(1)}, u32[]{:S(2)}, u32[]{:S(2)}) collective-permute-start(f32[128,128]{1,0:T(8,128)S(1)} %get-tuple-element.19), channel_id=1, source_target_pairs={{1,2},{2,1},{3,4},{4,3},{5,6},{6,5},{7,8},{8,7},{9,10},{10,9},{11,... | collective-permute-start | bytes 196616 | tf_op jit(solution)/shard_map/ppermute | solution.py:206
  6.6 2.5 %collective-permute-start.1 = (f32[2,512,128]{2,1,0:T(8,128)}, f32[2,512,128]{2,1,0:T(8,128)}, u32[]{:S(2)}, u32[]{:S(2)}) collective-permute-start(f32[2,512,128]{2,1,0:T(8,128)} %bitcast.55), channel_id=1, source_target_pairs={{1,2},{2,1},{3,4},{4,3},{5,6},{6,5},{7,8},{8,7},{9,10},{10,9},{11,... | collective-permute-start | bytes 1572872 | tf_op jit(solution)/shard_map/ppermute | solution.py:206
  9.1 1.9 collective-permute-start
  11.0 1.0 copy-done
  12.0 0.3 shard_map.49
  12.4 2.6 %collective-permute-start.4 = (f32[2,128,128]{2,1,0:T(8,128)S(1)}, f32[2,128,128]{2,1,0:T(8,128)S(1)}, u32[]{:S(2)}, u32[]{:S(2)}) collective-permute-start(f32[2,128,128]{2,1,0:T(8,128)S(1)} %pad_maximum_fusion.9), channel_id=1, source_target_pairs={{0,32},{32,0},{64,96},{96,64},{128,160},{160,128},{192,224},{224,1... | collective-permute-start | bytes 393224 | tf_op jit(solution)/shard_map/ppermute | solution.py:216
  15.1 14.1 %collective-permute-start.13 = (f32[20,128]{1,0:T(8,128)S(1)}, f32[20,128]{1,0:T(8,128)S(1)}, u32[]{:S(2)}, u32[]{:S(2)}) collective-permute-start(f32[20,128]{1,0:T(8,128)S(1)} %get-tuple-element.37), channel_id=1, source_target_pairs={{0,31},{1,0},{2,1},{3,2},{4,3},{5,4},{6,5},{7,6},{8,7},{9,8},{10,9... | collective-permute-start | bytes 30728 | tf_op jit(solution)/shard_map/ppermute | solution.py:252
  29.2 6.2 %collective-permute-start.12 = (f32[20,128]{1,0:T(8,128)S(1)}, f32[20,128]{1,0:T(8,128)S(1)}, u32[]{:S(2)}, u32[]{:S(2)}) collective-permute-start(f32[20,128]{1,0:T(8,128)S(1)} %get-tuple-element.36), channel_id=1, source_target_pairs={{0,0},{1,1},{2,2},{3,3},{4,4},{5,5},{6,6},{7,7},{8,8},{9,9},{10,10... | collective-permute-start | bytes 30728 | tf_op jit(solution)/shard_map/ppermute | solution.py:252
  35.5 1.9 collective-permute-start.5
  37.5 0.3 shard_map.46.state_ref.start_ref
  37.9 2.4 %scatter_custom_fusion = f32[262144]{0:T(1024)S(1)} fusion(s32[256]{0:T(256)S(1)} %bitcast.78, f32[256]{0:T(256)} %bitcast.79, f32[]{:T(128)} %constant.194.clone.1), kind=kCustom, calls=%fused_computation.64 | custom fusion | flops 256 | bytes 1049088 | tf_op jit(solution)/shard_map/scatter-add | solution.py:224
  40.3 6.6 %collective-permute-done.13 = f32[20,128]{1,0:T(8,128)S(1)} collective-permute-done((f32[20,128]{1,0:T(8,128)S(1)}, f32[20,128]{1,0:T(8,128)S(1)}, u32[]{:S(2)}, u32[]{:S(2)}) %collective-permute-start.13) | collective-permute-done | bytes 10272 | tf_op jit(solution)/shard_map/ppermute | solution.py:252
  46.9 1.9 collective-permute-start.14
  49.0 1.4 broadcast_select_fusion.2
  50.3 0.3 shard_map.47.before_ref
  50.6 0.3 shard_map.48.after_ref
  51.0 0.9 copy-done.1
  51.9 0.7 fusion.14
  52.7 0.3 fusion.20
  53.1 0.6 copy-done.3
  53.8 0.9 pad_maximum_fusion.4
  54.6 3.8 %collective-permute-start.7 = (f32[1152,128]{1,0:T(8,128)}, f32[1152,128]{1,0:T(8,128)}, u32[]{:S(2)}, u32[]{:S(2)}) collective-permute-start(f32[1152,128]{1,0:T(8,128)} %pad_maximum_fusion.4), channel_id=1, source_target_pairs={{1,2},{2,1},{3,4},{4,3},{5,6},{6,5},{7,8},{8,7},{9,10},{10,9},{11,... | collective-permute-start | bytes 1769480 | tf_op jit(solution)/shard_map/ppermute | solution.py:206
  58.5 1.9 collective-permute-start.6
  60.5 5.3 %collective-permute-start.15 = (f32[4,20,128]{2,0,1:T(4,128)S(1)}, f32[4,20,128]{2,0,1:T(4,128)S(1)}, u32[]{:S(2)}, u32[]{:S(2)}) collective-permute-start(f32[4,20,128]{2,0,1:T(4,128)S(1)} %pad_maximum_fusion.12), channel_id=1, source_target_pairs={{0,64},{32,96},{64,0},{96,32},{128,192},{160,224},{192,128},{224,1... | collective-permute-start | bytes 122888 | tf_op jit(solution)/shard_map/ppermute | solution.py:256
  65.9 1.3 collective-permute-done.15
  67.2 0.7 pad_maximum_fusion.11
  67.9 3.9 %collective-permute-start.16 = (f32[8,20,128]{2,0,1:T(8,128)}, f32[8,20,128]{2,0,1:T(8,128)S(1)}, u32[]{:S(2)}, u32[]{:S(2)}) collective-permute-start(f32[8,20,128]{2,0,1:T(8,128)} %pad_maximum_fusion.11), channel_id=1, source_target_pairs={{0,128},{32,160},{64,192},{96,224},{128,0},{160,32},{192,64},{224,... | collective-permute-start | bytes 245768 | tf_op jit(solution)/shard_map/ppermute | solution.py:256
  71.8 1.3 broadcast_select_fusion
  73.4 0.9 copy-done.6
  74.2 0.7 fusion.13
  75.0 1.2 copy-done.4
  76.2 0.3 fusion.26.field_ref
  76.5 0.3 shard_map.52
  76.8 0.1 shard_map.51
  77.0 0.8 pad_maximum_fusion.6
  77.7 29.7 %all-to-all-start = ((f32[32,12,128]{2,1,0:T(8,128)}), f32[32,12,128]{2,1,0:T(8,128)S(1)}, u32[]{:S(2)}, u32[]{:S(2)}) async-start(f32[32,12,128]{2,1,0:T(8,128)} %pad_maximum_fusion.6), calls=%async_computation | async-start | bytes 524288 | tf_op jit(solution)/shard_map/all_to_all | solution.py:183
  107.5 4.1 %collective-permute-start.17 = (f32[16,20,128]{2,0,1:T(8,128)S(1)}, f32[16,20,128]{2,0,1:T(8,128)S(1)}, u32[]{:S(2)}, u32[]{:S(2)}) collective-permute-start(f32[16,20,128]{2,0,1:T(8,128)S(1)} %pad_maximum_fusion.8), channel_id=1, source_target_pairs={{0,256},{32,288},{64,320},{96,352},{128,384},{160,416},{192,448},{... | collective-permute-start | bytes 491528 | tf_op jit(solution)/shard_map/ppermute | solution.py:256
  111.6 13.3 %collective-permute-done.17 = f32[16,20,128]{2,0,1:T(8,128)S(1)} collective-permute-done((f32[16,20,128]{2,0,1:T(8,128)S(1)}, f32[16,20,128]{2,0,1:T(8,128)S(1)}, u32[]{:S(2)}, u32[]{:S(2)}) %collective-permute-start.17) | collective-permute-done | bytes 163872 | tf_op jit(solution)/shard_map/ppermute | solution.py:256
  125.0 0.2 fusion.34
  125.3 1.3 collective-permute-start.8
  126.6 5.2 %collective-permute-start.9 = (f32[10,32,128]{2,1,0:T(8,128)S(1)}, f32[10,32,128]{2,1,0:T(8,128)S(1)}, u32[]{:S(2)}, u32[]{:S(2)}) collective-permute-start(f32[10,32,128]{2,1,0:T(8,128)S(1)} %slice.207), channel_id=1, source_target_pairs={{96,0},{97,1},{98,2},{99,3},{100,4},{101,5},{102,6},{103,7},{104,8... | collective-permute-start | bytes 491528 | tf_op jit(solution)/shard_map/ppermute | solution.py:166
  131.8 1.9 collective-permute-start.10
  133.7 1.9 collective-permute-start.11
  135.8 8.1 %collective-permute-done.11.c1_ref = f32[6,32,128]{2,1,0:T(8,128)S(1)} collective-permute-done((f32[6,32,128]{2,1,0:T(8,128)S(1)}, f32[6,32,128]{2,1,0:T(8,128)S(1)}, u32[]{:S(2)}, u32[]{:S(2)}) %collective-permute-start.11) | collective-permute-done | bytes 98336 | tf_op jit(solution)/shard_map/ppermute | solution.py:166
  143.9 1.0 shard_map.53.refs_1_
  144.9 1.3 collective-permute-start.18
  146.2 1.3 collective-permute-start.19
  147.5 1.3 collective-permute-start.20
  148.8 3.8 %collective-permute-done.18 = f32[4,32,128]{2,1,0:T(8,128)S(1)} collective-permute-done((f32[4,32,128]{2,1,0:T(8,128)S(1)}, f32[4,32,128]{2,1,0:T(8,128)S(1)}, u32[]{:S(2)}, u32[]{:S(2)}) %collective-permute-start.18) | collective-permute-done | bytes 65568 | tf_op jit(solution)/shard_map/ppermute | solution.py:166
  152.6 1.6 collective-permute-done.19
  154.3 1.4 collective-permute-done.20
  155.6 1.0 shard_map.54.refs_1_
  156.6 1.3 collective-permute-start.22
  157.9 1.3 collective-permute-start.21
  159.2 1.3 collective-permute-start.24
  160.5 9.0 %collective-permute-done.22 = f32[4,32,128]{2,1,0:T(8,128)S(1)} collective-permute-done((f32[4,32,128]{2,1,0:T(8,128)S(1)}, f32[4,32,128]{2,1,0:T(8,128)S(1)}, u32[]{:S(2)}, u32[]{:S(2)}) %collective-permute-start.22) | collective-permute-done | bytes 65568 | tf_op jit(solution)/shard_map/ppermute | solution.py:166
  169.6 2.1 %collective-permute-start.23 = (f32[2,4,32,128]{3,2,1,0:T(8,128)S(1)}, f32[2,4,32,128]{3,2,1,0:T(8,128)S(1)}, u32[]{:S(2)}, u32[]{:S(2)}) collective-permute-start(f32[2,4,32,128]{3,2,1,0:T(8,128)S(1)} %pad_maximum_fusion.10), channel_id=1, source_target_pairs={{0,1},{1,0},{2,3},{3,2},{4,5},{5,4},{6,7},{7,6},{8,9},{9,8},{10,11... | collective-permute-start | bytes 393224 | tf_op jit(solution)/shard_map/ppermute | solution.py:301
  171.7 0.1 collective-permute-done.24
  171.9 1.0 collective-permute-done.23
  172.9 2.6 %shard_map.55 = f32[4,32,128]{2,1,0:T(8,128)S(1)} custom-call(f32[20,32,128]{2,1,0:T(8,128)S(1)} %broadcast_select_fusion.4.refs_0_, f32[4,32,128]{2,1,0:T(8,128)S(1)} %shard_map.54.refs_1_, f32[20,32,128]{2,1,0:T(8,128)S(1)} %fusion.35.refs_2_, f32[20,32,128]{2,1,0:T(8,128)S(1)} %get-tuple-element.5.refs_3_), custom_call_target="tpu_custom_call" | custom-call | tf_op jit(solution)/shard_map/pallas_call | solution.py:148
  175.6 28.8 %all_to_all.10 = f32[32,4,128]{2,1,0:T(4,128)S(1)} all-to-all(f32[32,4,128]{2,1,0:T(4,128)S(1)} %copy.15), channel_id=1, replica_groups=mesh['tm'=16,'space'=32] {'space'}, dimensions={0} | all-to-all | bytes 131072 | tf_op jit(solution)/shard_map/all_to_all | solution.py:309
  204.4 1.1 shard_map.56
  (79 shorter events, 1.4 us)
Async XLA Ops:
  0.9 11.5 %collective-permute-start.2 = (f32[128,128]{1,0:T(8,128)S(1)}, f32[128,128]{1,0:T(8,128)S(1)}, u32[]{:S(2)}, u32[]{:S(2)}) collective-permute-start(f32[128,128]{1,0:T(8,128)S(1)} %get-tuple-element.18), channel_id=1, source_target_pairs={{0,1},{1,0},{2,3},{3,2},{4,5},{5,4},{6,7},{7,6},{8,9},{9,8},{10,11... | collective-permute-start | bytes 196616 | tf_op jit(solution)/shard_map/ppermute | solution.py:207
  3.5 8.9 %collective-permute-start.3 = (f32[128,128]{1,0:T(8,128)S(1)}, f32[128,128]{1,0:T(8,128)S(1)}, u32[]{:S(2)}, u32[]{:S(2)}) collective-permute-start(f32[128,128]{1,0:T(8,128)S(1)} %get-tuple-element.19), channel_id=1, source_target_pairs={{1,2},{2,1},{3,4},{4,3},{5,6},{6,5},{7,8},{8,7},{9,10},{10,9},{11,... | collective-permute-start | bytes 196616 | tf_op jit(solution)/shard_map/ppermute | solution.py:206
  6.6 42.4 %collective-permute-start.1 = (f32[2,512,128]{2,1,0:T(8,128)}, f32[2,512,128]{2,1,0:T(8,128)}, u32[]{:S(2)}, u32[]{:S(2)}) collective-permute-start(f32[2,512,128]{2,1,0:T(8,128)} %bitcast.55), channel_id=1, source_target_pairs={{1,2},{2,1},{3,4},{4,3},{5,6},{6,5},{7,8},{8,7},{9,10},{10,9},{11,... | collective-permute-start | bytes 1572872 | tf_op jit(solution)/shard_map/ppermute | solution.py:206
  9.1 39.9 %collective-permute-start = (f32[2,512,128]{2,1,0:T(8,128)}, f32[2,512,128]{2,1,0:T(8,128)}, u32[]{:S(2)}, u32[]{:S(2)}) collective-permute-start(f32[2,512,128]{2,1,0:T(8,128)} %bitcast.56), channel_id=1, source_target_pairs={{0,1},{1,0},{2,3},{3,2},{4,5},{5,4},{6,7},{7,6},{8,9},{9,8},{10,11... | collective-permute-start | bytes 1572872 | tf_op jit(solution)/shard_map/ppermute | solution.py:207
  11.0 1.0 copy-start
  12.3 25.1 %copy-start.7 = (s32[1,256]{1,0:T(1,128)S(1)}, s32[1,256]{1,0:T(1,128)}, u32[]{:S(2)}) copy-start(s32[1,256]{1,0:T(1,128)} %param.6) | copy-start | bytes 3076
  12.3 25.2 %copy-start.2 = (f32[1,2,512,128]{3,2,1,0:T(8,128)S(1)}, f32[1,2,512,128]{3,2,1,0:T(8,128)}, u32[]{:S(2)}) copy-start(f32[1,2,512,128]{3,2,1,0:T(8,128)} %param.4) | copy-start | bytes 1572868
  12.4 23.1 %collective-permute-start.4 = (f32[2,128,128]{2,1,0:T(8,128)S(1)}, f32[2,128,128]{2,1,0:T(8,128)S(1)}, u32[]{:S(2)}, u32[]{:S(2)}) collective-permute-start(f32[2,128,128]{2,1,0:T(8,128)S(1)} %pad_maximum_fusion.9), channel_id=1, source_target_pairs={{0,32},{32,0},{64,96},{96,64},{128,160},{160,128},{192,224},{224,1... | collective-permute-start | bytes 393224 | tf_op jit(solution)/shard_map/ppermute | solution.py:216
  15.1 31.8 %collective-permute-start.13 = (f32[20,128]{1,0:T(8,128)S(1)}, f32[20,128]{1,0:T(8,128)S(1)}, u32[]{:S(2)}, u32[]{:S(2)}) collective-permute-start(f32[20,128]{1,0:T(8,128)S(1)} %get-tuple-element.37), channel_id=1, source_target_pairs={{0,31},{1,0},{2,1},{3,2},{4,3},{5,4},{6,5},{7,6},{8,7},{9,8},{10,9... | collective-permute-start | bytes 30728 | tf_op jit(solution)/shard_map/ppermute | solution.py:252
  29.2 11.0 %collective-permute-start.12 = (f32[20,128]{1,0:T(8,128)S(1)}, f32[20,128]{1,0:T(8,128)S(1)}, u32[]{:S(2)}, u32[]{:S(2)}) collective-permute-start(f32[20,128]{1,0:T(8,128)S(1)} %get-tuple-element.36), channel_id=1, source_target_pairs={{0,0},{1,1},{2,2},{3,3},{4,4},{5,5},{6,6},{7,7},{8,8},{9,9},{10,10... | collective-permute-start | bytes 30728 | tf_op jit(solution)/shard_map/ppermute | solution.py:252
  35.5 13.3 %collective-permute-start.5 = (f32[2,256,128]{2,1,0:T(8,128)S(1)}, f32[2,256,128]{2,1,0:T(8,128)S(1)}, u32[]{:S(2)}, u32[]{:S(2)}) collective-permute-start(f32[2,256,128]{2,1,0:T(8,128)S(1)} %pad_maximum_fusion.5), channel_id=1, source_target_pairs={{0,64},{32,96},{64,0},{96,32},{128,192},{160,224},{192,128},{224,1... | collective-permute-start | bytes 786440 | tf_op jit(solution)/shard_map/ppermute | solution.py:216
  46.9 13.5 %collective-permute-start.14 = (f32[2,20,128]{2,0,1:T(2,128)S(1)}, f32[2,20,128]{2,0,1:T(2,128)S(1)}, u32[]{:S(2)}, u32[]{:S(2)}) collective-permute-start(f32[2,20,128]{2,0,1:T(2,128)S(1)} %pad_maximum_fusion.13), channel_id=1, source_target_pairs={{0,32},{32,0},{64,96},{96,64},{128,160},{160,128},{192,224},{224,1... | collective-permute-start | bytes 61448 | tf_op jit(solution)/shard_map/ppermute | solution.py:256
  48.9 2.0 copy-start.5
  50.9 1.0 copy-start.1
  52.6 1.0 copy-start.3
  54.6 17.2 %collective-permute-start.7 = (f32[1152,128]{1,0:T(8,128)}, f32[1152,128]{1,0:T(8,128)}, u32[]{:S(2)}, u32[]{:S(2)}) collective-permute-start(f32[1152,128]{1,0:T(8,128)} %pad_maximum_fusion.4), channel_id=1, source_target_pairs={{1,2},{2,1},{3,4},{4,3},{5,6},{6,5},{7,8},{8,7},{9,10},{10,9},{11,... | collective-permute-start | bytes 1769480 | tf_op jit(solution)/shard_map/ppermute | solution.py:206
  58.5 13.3 %collective-permute-start.6 = (f32[1152,128]{1,0:T(8,128)}, f32[1152,128]{1,0:T(8,128)}, u32[]{:S(2)}, u32[]{:S(2)}) collective-permute-start(f32[1152,128]{1,0:T(8,128)} %pad_maximum_fusion.4), channel_id=1, source_target_pairs={{0,1},{1,0},{2,3},{3,2},{4,5},{5,4},{6,7},{7,6},{8,9},{9,8},{10,11... | collective-permute-start | bytes 1769480 | tf_op jit(solution)/shard_map/ppermute | solution.py:207
  60.5 6.7 %collective-permute-start.15 = (f32[4,20,128]{2,0,1:T(4,128)S(1)}, f32[4,20,128]{2,0,1:T(4,128)S(1)}, u32[]{:S(2)}, u32[]{:S(2)}) collective-permute-start(f32[4,20,128]{2,0,1:T(4,128)S(1)} %pad_maximum_fusion.12), channel_id=1, source_target_pairs={{0,64},{32,96},{64,0},{96,32},{128,192},{160,224},{192,128},{224,1... | collective-permute-start | bytes 122888 | tf_op jit(solution)/shard_map/ppermute | solution.py:256
  67.9 39.6 %collective-permute-start.16 = (f32[8,20,128]{2,0,1:T(8,128)}, f32[8,20,128]{2,0,1:T(8,128)S(1)}, u32[]{:S(2)}, u32[]{:S(2)}) collective-permute-start(f32[8,20,128]{2,0,1:T(8,128)} %pad_maximum_fusion.11), channel_id=1, source_target_pairs={{0,128},{32,160},{64,192},{96,224},{128,0},{160,32},{192,64},{224,... | collective-permute-start | bytes 245768 | tf_op jit(solution)/shard_map/ppermute | solution.py:256
  73.3 1.0 copy-start.6
  75.0 1.2 copy-start.4
  77.7 47.4 %all-to-all-start = ((f32[32,12,128]{2,1,0:T(8,128)}), f32[32,12,128]{2,1,0:T(8,128)S(1)}, u32[]{:S(2)}, u32[]{:S(2)}) async-start(f32[32,12,128]{2,1,0:T(8,128)} %pad_maximum_fusion.6), calls=%async_computation | async-start | bytes 524288 | tf_op jit(solution)/shard_map/all_to_all | solution.py:183
  107.5 17.4 %collective-permute-start.17 = (f32[16,20,128]{2,0,1:T(8,128)S(1)}, f32[16,20,128]{2,0,1:T(8,128)S(1)}, u32[]{:S(2)}, u32[]{:S(2)}) collective-permute-start(f32[16,20,128]{2,0,1:T(8,128)S(1)} %pad_maximum_fusion.8), channel_id=1, source_target_pairs={{0,256},{32,288},{64,320},{96,352},{128,384},{160,416},{192,448},{... | collective-permute-start | bytes 491528 | tf_op jit(solution)/shard_map/ppermute | solution.py:256
  125.3 18.7 %collective-permute-start.8 = (f32[12,32,128]{2,1,0:T(8,128)S(1)}, f32[12,32,128]{2,1,0:T(8,128)S(1)}, u32[]{:S(2)}, u32[]{:S(2)}) collective-permute-start(f32[12,32,128]{2,1,0:T(8,128)S(1)} %bitcast.68), channel_id=1, source_target_pairs={{128,0},{129,1},{130,2},{131,3},{132,4},{133,5},{134,6},{135,7},{1... | collective-permute-start | bytes 589832 | tf_op jit(solution)/shard_map/ppermute | solution.py:166
  126.6 17.3 %collective-permute-start.9 = (f32[10,32,128]{2,1,0:T(8,128)S(1)}, f32[10,32,128]{2,1,0:T(8,128)S(1)}, u32[]{:S(2)}, u32[]{:S(2)}) collective-permute-start(f32[10,32,128]{2,1,0:T(8,128)S(1)} %slice.207), channel_id=1, source_target_pairs={{96,0},{97,1},{98,2},{99,3},{100,4},{101,5},{102,6},{103,7},{104,8... | collective-permute-start | bytes 491528 | tf_op jit(solution)/shard_map/ppermute | solution.py:166
  131.8 12.1 %collective-permute-start.10 = (f32[8,32,128]{2,1,0:T(8,128)S(1)}, f32[8,32,128]{2,1,0:T(8,128)S(1)}, u32[]{:S(2)}, u32[]{:S(2)}) collective-permute-start(f32[8,32,128]{2,1,0:T(8,128)S(1)} %slice.208), channel_id=1, source_target_pairs={{64,0},{65,1},{66,2},{67,3},{68,4},{69,5},{70,6},{71,7},{72,8},{73... | collective-permute-start | bytes 393224 | tf_op jit(solution)/shard_map/ppermute | solution.py:166
  133.7 10.2 %collective-permute-start.11 = (f32[6,32,128]{2,1,0:T(8,128)S(1)}, f32[6,32,128]{2,1,0:T(8,128)S(1)}, u32[]{:S(2)}, u32[]{:S(2)}) collective-permute-start(f32[6,32,128]{2,1,0:T(8,128)S(1)} %slice.209), channel_id=1, source_target_pairs={{32,0},{33,1},{34,2},{35,3},{36,4},{37,5},{38,6},{39,7},{40,8},{41... | collective-permute-start | bytes 294920 | tf_op jit(solution)/shard_map/ppermute | solution.py:166
  144.9 7.7 %collective-permute-start.18 = (f32[4,32,128]{2,1,0:T(8,128)S(1)}, f32[4,32,128]{2,1,0:T(8,128)S(1)}, u32[]{:S(2)}, u32[]{:S(2)}) collective-permute-start(f32[4,32,128]{2,1,0:T(8,128)S(1)} %shard_map.53.refs_1_), channel_id=1, source_target_pairs={{128,1},{129,0},{130,3},{131,2},{132,5},{133,4},{134,7},{135,6},{1... | collective-permute-start | bytes 196616 | tf_op jit(solution)/shard_map/ppermute | solution.py:166
  146.2 8.0 %collective-permute-start.19 = (f32[4,32,128]{2,1,0:T(8,128)S(1)}, f32[4,32,128]{2,1,0:T(8,128)S(1)}, u32[]{:S(2)}, u32[]{:S(2)}) collective-permute-start(f32[4,32,128]{2,1,0:T(8,128)S(1)} %shard_map.53.refs_1_), channel_id=1, source_target_pairs={{129,2},{130,1},{131,4},{132,3},{133,6},{134,5},{135,8},{136,7},{1... | collective-permute-start | bytes 196616 | tf_op jit(solution)/shard_map/ppermute | solution.py:166
  147.5 8.1 %collective-permute-start.20 = (f32[4,32,128]{2,1,0:T(8,128)S(1)}, f32[4,32,128]{2,1,0:T(8,128)S(1)}, u32[]{:S(2)}, u32[]{:S(2)}) collective-permute-start(f32[4,32,128]{2,1,0:T(8,128)S(1)} %shard_map.53.refs_1_), channel_id=1, source_target_pairs={{128,0},{129,1},{130,2},{131,3},{132,4},{133,5},{134,6},{135,7},{1... | collective-permute-start | bytes 196616 | tf_op jit(solution)/shard_map/ppermute | solution.py:166
  156.6 12.9 %collective-permute-start.22 = (f32[4,32,128]{2,1,0:T(8,128)S(1)}, f32[4,32,128]{2,1,0:T(8,128)S(1)}, u32[]{:S(2)}, u32[]{:S(2)}) collective-permute-start(f32[4,32,128]{2,1,0:T(8,128)S(1)} %shard_map.54.refs_1_), channel_id=1, source_target_pairs={{257,2},{258,1},{259,4},{260,3},{261,6},{262,5},{263,8},{264,7},{2... | collective-permute-start | bytes 196616 | tf_op jit(solution)/shard_map/ppermute | solution.py:166
  157.9 11.6 %collective-permute-start.21 = (f32[4,32,128]{2,1,0:T(8,128)S(1)}, f32[4,32,128]{2,1,0:T(8,128)S(1)}, u32[]{:S(2)}, u32[]{:S(2)}) collective-permute-start(f32[4,32,128]{2,1,0:T(8,128)S(1)} %shard_map.54.refs_1_), channel_id=1, source_target_pairs={{256,0},{257,1},{258,2},{259,3},{260,4},{261,5},{262,6},{263,7},{2... | collective-permute-start | bytes 196616 | tf_op jit(solution)/shard_map/ppermute | solution.py:166
  159.2 12.6 %collective-permute-start.24 = (f32[4,32,128]{2,1,0:T(8,128)S(1)}, f32[4,32,128]{2,1,0:T(8,128)S(1)}, u32[]{:S(2)}, u32[]{:S(2)}) collective-permute-start(f32[4,32,128]{2,1,0:T(8,128)S(1)} %shard_map.54.refs_1_), channel_id=1, source_target_pairs={{256,2},{258,4},{260,6},{262,8},{264,10},{266,12},{268,14},{270,16... | collective-permute-start | bytes 196616 | tf_op jit(solution)/shard_map/ppermute | solution.py:166
  169.6 3.2 %collective-permute-start.23 = (f32[2,4,32,128]{3,2,1,0:T(8,128)S(1)}, f32[2,4,32,128]{3,2,1,0:T(8,128)S(1)}, u32[]{:S(2)}, u32[]{:S(2)}) collective-permute-start(f32[2,4,32,128]{3,2,1,0:T(8,128)S(1)} %pad_maximum_fusion.10), channel_id=1, source_target_pairs={{0,1},{1,0},{2,3},{3,2},{4,5},{5,4},{6,7},{7,6},{8,9},{9,8},{10,11... | collective-permute-start | bytes 393224 | tf_op jit(solution)/shard_map/ppermute | solution.py:301

commit v5 on v3

--- a/solution.py
+++ b/solution.py
@@ -15,7 +15,7 @@
 
 
 def params():
-    return pltpu.CompilerParams(vmem_limit_bytes=40 * 1024 * 1024)
+    return pltpu.CompilerParams(vmem_limit_bytes=12 * 1024 * 1024)
 
 
 def halving(half):
@@ -76,6 +76,48 @@
     return before + after
 
 
+def beside_in_plane(value):
+    rows = value.shape[0]
+    row = lax.broadcasted_iota(jnp.int32, value.shape, 0)
+    lane = lax.broadcasted_iota(jnp.int32, value.shape, 1)
+    above = jnp.where(row == 0, 0.0, pltpu.roll(value, 1, 0))
+    below = jnp.where(row == rows - 1, 0.0, pltpu.roll(value, rows - 1, 0))
+    before = jnp.where(lane == 0, 0.0, pltpu.roll(value, 1, 1))
+    after = jnp.where(lane == 127, 0.0, pltpu.roll(value, 127, 1))
+    return above + below + before + after
+
+
+def step_kernel(place_ref, across_ref, along_ref, field_ref, share_ref, cond_ref, source_ref, out_ref):
+    odd = place_ref[0] == 1
+    planes = [jnp.where(odd, along_ref[p], across_ref[p]) for p in range(2)]
+    planes += [field_ref[p] for p in range(2)]
+    planes += [jnp.where(odd, across_ref[p], along_ref[p]) for p in range(2)]
+    conds = [share_ref[0], cond_ref[0], cond_ref[1], share_ref[1]]
+    terms, diagonals, wide = [], [], []
+    for i in range(4):
+        value = planes[i + 1]
+        terms.append(conds[i] * value + source_ref[i])
+        diagonals.append(conds[i] + 6.0)
+        total = planes[i] + planes[i + 2] + beside_in_plane(value)
+        wide.append((terms[i] + total) / diagonals[i])
+    wide[0] = jnp.where(place_ref[1] == 1, wide[0], 0.0)
+    wide[3] = jnp.where(place_ref[2] == 1, wide[3], 0.0)
+    for p in range(2):
+        total = wide[p] + wide[p + 2] + beside_in_plane(wide[p + 1])
+        out_ref[p] = (terms[p + 1] + total) / diagonals[p + 1]
+
+
+def fine_step(place, *operands):
+    in_vmem = pl.BlockSpec(memory_space=pltpu.VMEM)
+    return pl.pallas_call(
+        step_kernel,
+        out_shape=jax.ShapeDtypeStruct(operands[2].shape, jnp.float32),
+        in_specs=[pl.BlockSpec(memory_space=pltpu.SMEM)] + [in_vmem] * len(operands),
+        out_specs=in_vmem,
+        compiler_params=params(),
+    )(place, *operands)
+
+
 def plane_sweep_kernel(state_ref, start_ref, before_ref, after_ref, keep_ref, spread_ref, out_ref):
     value = state_ref[...]
     low, z = lanes_of(value.shape)
@@ -184,15 +226,6 @@
     return jnp.transpose(arrived, (1, 0, 2))
 
 
-def inside_planes(padded):
-    center = padded[1:-1]
-    beside_all = padded[2:] + padded[:-2]
-    planes = jnp.pad(center, ((0, 0), (1, 1), (1, 1)))
-    beside_all = beside_all + planes[:, 2:, 1:-1] + planes[:, :-2, 1:-1]
-    beside_all = beside_all + planes[:, 1:-1, 2:] + planes[:, 1:-1, :-2]
-    return beside_all
-
-
 def per_device(end_state, cond, receivers, residuals):
     start_field = end_state[0]
     row_count, width_y, width_z = start_field.shape
@@ -202,20 +235,25 @@
     odd = slab % 2 == 1
     is_final = slice_index == SLICES - 1
 
-    def trade(to_before, to_after):
-        across = lax.ppermute(jnp.where(odd, to_after, to_before), "space", facing(1, 1))
-        along = lax.ppermute(jnp.where(odd, to_before, to_after), "space", facing(1, 0))
+    def across_chips(value):
+        return lax.ppermute(value, "space", facing(1, 1))
+
+    def in_chip(value):
+        return lax.ppermute(value, "space", facing(1, 0))
+
+    def by_side(along, across):
         return jnp.where(odd, along, across), jnp.where(odd, across, along)
 
     ring = slice_index % 4
     quarter = width_y // 4
     share = lax.dynamic_slice_in_dim(cond, ring * quarter, quarter, axis=1)
-    share = jnp.stack(trade(share[0], share[1]))
+    across = across_chips(jnp.where(odd, share[1], share[0]))
+    along = in_chip(jnp.where(odd, share[0], share[1]))
+    share = jnp.stack(by_side(along, across))
     for bit in (1, 2):
         upper = (ring // bit) % 2 == 1
         other = lax.ppermute(share, "tm", [(n, n ^ bit) for n in range(SLICES)])
         share = jnp.concatenate([jnp.where(upper, other, share), jnp.where(upper, share, other)], axis=1)
-    wide_cond = jnp.concatenate([share[:1], cond, share[1:]])
 
     local_row = receivers[0] // plane_size - slab * row_count + 1
     inside = (local_row >= 0) & (local_row < row_count + 2)
@@ -223,8 +261,7 @@
     target = jnp.where(inside, local_row * plane_size + receivers[0] % plane_size, wide_size)
     flat_source = jnp.zeros((wide_size,), jnp.float32).at[target].add(residuals[0], mode="drop")
     wide_source = flat_source.reshape(row_count + 2, width_y, width_z)
-    plane_place = slab * row_count - 1 + jnp.arange(row_count + 2)
-    in_grid = ((plane_place >= 0) & (plane_place < SLABS * row_count))[:, None, None]
+    place = jnp.stack([odd, slab > 0, slab < SLABS - 1]).astype(jnp.int32)
 
     coarse_cond = restrict(cond) / FINE_STEPS
     plane_spread = 1.0 / (coarse_cond + 1.5)
@@ -232,27 +269,19 @@
     plane_spread = 0.25 * plane_spread
     coarse_start = restrict(start_field)
 
-    def two_sweeps(padded):
-        wide = padded[1:-1]
-        rhs_term = wide_cond * wide + wide_source
-        diagonal = wide_cond + 6.0
-        wide = jnp.where(in_grid, (rhs_term + inside_planes(padded)) / diagonal, 0.0)
-        return (rhs_term[1:-1] + inside_planes(wide)) / diagonal[1:-1]
-
-    before, after = trade(start_field, start_field)
+    across, along = across_chips(start_field), in_chip(start_field)
     coarse_now = plane_sweep(
-        coarse_start, coarse_start, restrict(before), restrict(after), plane_keep, plane_spread
-    )
-    field_now = two_sweeps(jnp.concatenate([before, start_field, after]))
-    slab_rows = row_count * width_y
-    sent = jnp.concatenate([field_now.reshape(slab_rows, width_z), coarse_now])
-    before, after = trade(sent, sent)
+        coarse_start, coarse_start, *by_side(restrict(along), restrict(across)), plane_keep, plane_spread
+    )
+    field_now = fine_step(place, across, along, start_field, share, cond, wide_source)
+
+    sent = jnp.concatenate([field_now.reshape(row_count * width_y, width_z), coarse_now])
+    across, along = across_chips(sent), in_chip(sent)
     direct = plane_sweep(
-        coarse_now, coarse_start, before[slab_rows:], after[slab_rows:], plane_keep, plane_spread
-    )
-    before = before[:slab_rows].reshape(start_field.shape)
-    after = after[:slab_rows].reshape(start_field.shape)
-    field_now = two_sweeps(jnp.concatenate([before, field_now, after]))
+        coarse_now, coarse_start, *by_side(along[-PLANE:], across[-PLANE:]), plane_keep, plane_spread
+    )
+    across, along = (value[:-PLANE].reshape(start_field.shape) for value in (across, along))
+    field_now = fine_step(place, across, along, field_now, share, cond, wide_source)
 
     term = restrict(field_now) - jnp.where(is_final, 0.0, direct)
     second_half = slice_index % 2 == 1
@@ -264,8 +293,8 @@
     row_cond = jnp.concatenate(
         [jnp.where(second_half, other_cond, own_cond), jnp.where(second_half, own_cond, other_cond)]
     )
-    place = (slab - 2) * BLOCK + lax.broadcasted_iota(jnp.int32, row_cond.shape, 0)
-    within = (place >= 0) & (place < PLANE)
+    row_place = (slab - 2) * BLOCK + lax.broadcasted_iota(jnp.int32, row_cond.shape, 0)
+    within = (row_place >= 0) & (row_place < PLANE)
     row_spread = jnp.where(within, 1.0 / (row_cond + 1.5), 0.0)
     row_keep = row_cond * row_spread
     row_spread = 0.25 * row_spread
@@ -283,9 +312,15 @@
     )
 
     centre = from_later(total, 8, later)
-    before, after = beside_later(total, 8, 1, slab)
-    before_two, after_two = beside_later(total, 8, 2, slab)
-    window = jnp.concatenate([before_two, before, centre, after, after_two])
+    near = from_later(total, 8, facing(1, 1))
+    outward = [(j - 2, j) for j in range(2, SLABS, 2)] + [(j + 2, j) for j in range(1, SLABS - 2, 2)]
+    far = from_later(total, 8, outward)
+    swapped = lax.ppermute(jnp.stack([centre, near]), "space", facing(1, 0))
+    window = jnp.where(
+        odd,
+        jnp.concatenate([swapped[1], swapped[0], centre, near, far]),
+        jnp.concatenate([far, near, centre, swapped[0], swapped[1]]),
+    )
     total = chain_call(lambda *refs: power_kernel(8, *refs), 20, window, total, row_keep, row_spread)
 
     back = lax.all_to_all(jnp.transpose(total, (1, 0, 2)), "space", 0, 0)

time: 216 us -> 206 us (0.954)
  blocking collectives: 99.1 us -> 92.6 us
  waiting for transfers between devices: 44.1 us -> 38.6 us
  Pallas kernels: 7.25 us -> 10.5 us
  other arithmetic: 9.7 us -> 6.66 us
    ppermute x12 -> x10, waiting for transfers between devices: 31.6 us -> 26 us  [from_later(): return lax.ppermute(value, ('tm', 'space'), both)]
    all_to_all x1, blocking collectives: 70.1 us -> 66.7 us  [to_rows(): arrived = lax.all_to_all(parts, 'space', 0, 0)]
    pallas_call x0 -> x2, Pallas kernels: none -> 3.19 us  [fine_step(): pl.pallas_call(step_kernel, out_shape=jax.ShapeDtypeStruct(operands[2].sh...]
    select_n x5 -> x4, other arithmetic: 5.01 us -> 1.83 us  [the longest x2 0.9 us: by_side(): return (jnp.where(odd, along, across), jnp.where(odd, across, along))]
    all_to_all x1, blocking collectives: 29 us -> 25.9 us  [per_device(): back = lax.all_to_all(jnp.transpose(total, (1, 0, 2)), 'space', 0, 0)]
    ppermute x12 -> x10, starting transfers between devices: 19 us -> 16.2 us  [from_later(): return lax.ppermute(value, ('tm', 'space'), both)]
    ppermute x6 -> x7, starting transfers between devices: 16 us -> 18.6 us  [the longest x3 9.54 us: across_chips(): return lax.ppermute(value, 'space', facing(1, 1))]
    unnamed x17 -> x22, local copies, waits for them, and re-layouts: 4.62 us -> 3.87 us
  transfers between devices with their start and end apart: 21 -> 20, of which waited for: 11 -> 11; matrix products, arithmetic and copies ran while one was open for 1% -> 2% of each run, Pallas kernels for 0% -> 0%
where the time goes in v5:
time: 206 us; the launch traced here: 203 us
  blocking collectives  92.6 us (45%)
  starting transfers between devices  47.3 us (23%)
  waiting for transfers between devices  38.6 us (19%)
  Pallas kernels  10.5 us (5%)
  other arithmetic  6.66 us (3%)
  local copies, waits for them, and re-layouts  6.29 us (3%)
    all_to_all x1, blocking collectives, to_rows(): arrived = lax.all_to_all(parts, 'space', 0, 0)  66.7 us
    ppermute x10, waiting for transfers between devices, from_later(): return lax.ppermute(value, ('tm', 'space'), both)  26 us
    all_to_all x1, blocking collectives, per_device(): back = lax.all_to_all(jnp.transpose(total, (1, 0, 2)), 'space', 0, 0)  25.9 us
    ppermute x10, starting transfers between devices, from_later(): return lax.ppermute(value, ('tm', 'space'), both)  16.2 us
    ppermute x2, starting transfers between devices, per_device(): other = lax.ppermute(share, 'tm', [(n, n ^ bit) for n in range(SLICES)])  9.98 us
    ppermute x3, starting transfers between devices, across_chips(): return lax.ppermute(value, 'space', facing(1, 1))  9.54 us
    ppermute x2, waiting for transfers between devices, per_device(): other = lax.ppermute(share, 'tm', [(n, n ^ bit) for n in range(SLICES)])  6.84 us
    ppermute x3, starting transfers between devices, in_chip(): return lax.ppermute(value, 'space', facing(1, 0))  6.43 us
  transfers between devices with their start and end apart: 20, of which 11 were waited for; matrix products, arithmetic and copies ran while one was open for 2% of the time, Pallas kernels for 0%

profile of v5, /device:TPU:7, one launch (start us, length us, event | category | flops | bytes accessed | tf_op | source)
XLA Modules:
  0.0 202.6 jit_solution(3834007357240398142)
XLA Ops:
  0.0 0.9 select_bitcast_fusion.3
  0.9 2.6 %collective-permute-start.2 = (f32[128,128]{1,0:T(8,128)S(1)}, f32[128,128]{1,0:T(8,128)S(1)}, u32[]{:S(2)}, u32[]{:S(2)}) collective-permute-start(f32[128,128]{1,0:T(8,128)S(1)} %get-tuple-element.11), channel_id=1, source_target_pairs={{0,1},{1,0},{2,3},{3,2},{4,5},{5,4},{6,7},{7,6},{8,9},{9,8},{10,11... | collective-permute-start | bytes 196616 | tf_op jit(solution)/shard_map/ppermute | solution.py:242
  3.5 3.1 %collective-permute-start.3 = (f32[128,128]{1,0:T(8,128)S(1)}, f32[128,128]{1,0:T(8,128)S(1)}, u32[]{:S(2)}, u32[]{:S(2)}) collective-permute-start(f32[128,128]{1,0:T(8,128)S(1)} %get-tuple-element.12), channel_id=1, source_target_pairs={{1,2},{2,1},{3,4},{4,3},{5,6},{6,5},{7,8},{8,7},{9,10},{10,9},{11,... | collective-permute-start | bytes 196616 | tf_op jit(solution)/shard_map/ppermute | solution.py:239
  6.6 2.5 %collective-permute-start.1 = (f32[2,512,128]{2,1,0:T(8,128)}, f32[2,512,128]{2,1,0:T(8,128)S(1)}, u32[]{:S(2)}, u32[]{:S(2)}) collective-permute-start(f32[2,512,128]{2,1,0:T(8,128)} %bitcast.58), channel_id=1, source_target_pairs={{1,2},{2,1},{3,4},{4,3},{5,6},{6,5},{7,8},{8,7},{9,10},{10,9},{11,... | collective-permute-start | bytes 1572872 | tf_op jit(solution)/shard_map/ppermute | solution.py:239
  9.1 1.9 collective-permute-start
  11.0 1.0 copy-done
  12.0 0.3 shard_map.49
  12.4 2.5 %collective-permute-start.4 = (f32[2,128,128]{2,1,0:T(8,128)S(1)}, f32[2,128,128]{2,1,0:T(8,128)S(1)}, u32[]{:S(2)}, u32[]{:S(2)}) collective-permute-start(f32[2,128,128]{2,1,0:T(8,128)S(1)} %pad_maximum_fusion.10), channel_id=1, source_target_pairs={{0,32},{32,0},{64,96},{96,64},{128,160},{160,128},{192,224},{224,1... | collective-permute-start | bytes 393224 | tf_op jit(solution)/shard_map/ppermute | solution.py:255
  14.9 4.0 %collective-permute-done.4 = f32[2,128,128]{2,1,0:T(8,128)S(1)} collective-permute-done((f32[2,128,128]{2,1,0:T(8,128)S(1)}, f32[2,128,128]{2,1,0:T(8,128)S(1)}, u32[]{:S(2)}, u32[]{:S(2)}) %collective-permute-start.4) | collective-permute-done | bytes 131104 | tf_op jit(solution)/shard_map/ppermute | solution.py:255
  18.9 7.5 %collective-permute-start.5 = (f32[2,256,128]{2,1,0:T(8,128)S(1)}, f32[2,256,128]{2,1,0:T(8,128)}, u32[]{:S(2)}, u32[]{:S(2)}) collective-permute-start(f32[2,256,128]{2,1,0:T(8,128)S(1)} %pad_maximum_fusion.8), channel_id=1, source_target_pairs={{0,64},{32,96},{64,0},{96,32},{128,192},{160,224},{192,128},{224,1... | collective-permute-start | bytes 786440 | tf_op jit(solution)/shard_map/ppermute | solution.py:255
  26.5 0.3 shard_map.46.state_ref.start_ref
  26.8 2.4 %scatter_custom_fusion = f32[262144]{0:T(1024)S(1)} fusion(s32[256]{0:T(256)S(1)} %bitcast.77, f32[256]{0:T(256)} %bitcast.78, f32[]{:T(128)} %constant.130.clone.1), kind=kCustom, calls=%fused_computation.3 | custom fusion | flops 256 | bytes 1049088 | tf_op jit(solution)/shard_map/scatter-add | solution.py:262
  29.2 0.1 add_convert_fusion.place_ref
  29.3 2.9 %collective-permute-done.5 = f32[2,256,128]{2,1,0:T(8,128)} collective-permute-done((f32[2,256,128]{2,1,0:T(8,128)S(1)}, f32[2,256,128]{2,1,0:T(8,128)}, u32[]{:S(2)}, u32[]{:S(2)}) %collective-permute-start.5) | collective-permute-done | bytes 262176 | tf_op jit(solution)/shard_map/ppermute | solution.py:255
  32.2 1.0 broadcast_select_fusion.2
  33.2 0.3 shard_map.48
  33.5 0.8 copy-done.3
  34.3 0.3 shard_map.47
  34.6 0.1 shard_map.50.state_ref
  34.7 0.3 copy-done.5
  35.1 0.4 copy-done.1
  35.5 0.2 copy-done.4
  35.7 1.0 copy-done.6
  36.7 1.5 shard_map.51.field_ref
  38.3 0.9 pad_maximum_fusion
  39.1 4.0 %collective-permute-start.7 = (f32[1152,128]{1,0:T(8,128)}, f32[1152,128]{1,0:T(8,128)}, u32[]{:S(2)}, u32[]{:S(2)}) collective-permute-start(f32[1152,128]{1,0:T(8,128)} %pad_maximum_fusion), channel_id=1, source_target_pairs={{1,2},{2,1},{3,4},{4,3},{5,6},{6,5},{7,8},{8,7},{9,10},{10,9},{11,... | collective-permute-start | bytes 1769480 | tf_op jit(solution)/shard_map/ppermute | solution.py:239
  43.1 1.9 collective-permute-start.6
  45.1 0.1 fusion.3
  45.2 5.7 %collective-permute-done.7 = f32[1152,128]{1,0:T(8,128)} collective-permute-done((f32[1152,128]{1,0:T(8,128)}, f32[1152,128]{1,0:T(8,128)}, u32[]{:S(2)}, u32[]{:S(2)}) %collective-permute-start.7) | collective-permute-done | bytes 589856 | tf_op jit(solution)/shard_map/ppermute | solution.py:239
  51.0 1.1 slice.107
  52.1 1.1 slice.108
  53.2 1.7 shard_map.53.field_ref
  54.8 0.3 shard_map.54
  55.1 0.9 slice_select_fusion
  56.0 0.1 shard_map.52
  56.2 0.1 pad_maximum_fusion.2
  56.2 66.7 %all_to_all.10 = f32[32,22,128]{2,1,0:T(8,128)S(1)} all-to-all(f32[32,22,128]{2,1,0:T(8,128)S(1)} %pad_maximum_fusion.2), channel_id=1, replica_groups=mesh['tm'=16,'space'=32] {'space'}, dimensions={0} | all-to-all | bytes 720896 | tf_op jit(solution)/shard_map/all_to_all | solution.py:225
  122.9 0.1 copy.17
  123.0 2.5 %collective-permute-start.12 = (f32[10,32,128]{2,1,0:T(8,128)S(1)}, f32[10,32,128]{2,1,0:T(8,128)S(1)}, u32[]{:S(2)}, u32[]{:S(2)}) collective-permute-start(f32[10,32,128]{2,1,0:T(8,128)S(1)} %slice.113), channel_id=1, source_target_pairs={{0,32},{32,0},{64,96},{96,64},{128,160},{160,128},{192,224},{224,1... | collective-permute-start | bytes 491528 | tf_op jit(solution)/shard_map/ppermute | solution.py:292
  125.5 1.3 collective-permute-start.8
  126.8 2.7 %collective-permute-start.10 = (f32[8,32,128]{2,1,0:T(8,128)S(1)}, f32[8,32,128]{2,1,0:T(8,128)S(1)}, u32[]{:S(2)}, u32[]{:S(2)}) collective-permute-start(f32[8,32,128]{2,1,0:T(8,128)S(1)} %slice.111), channel_id=1, source_target_pairs={{64,0},{65,1},{66,2},{67,3},{68,4},{69,5},{70,6},{71,7},{72,8},{73... | collective-permute-start | bytes 393224 | tf_op jit(solution)/shard_map/ppermute | solution.py:208
  129.6 2.5 %collective-permute-start.11 = (f32[6,32,128]{2,1,0:T(8,128)S(1)}, f32[6,32,128]{2,1,0:T(8,128)S(1)}, u32[]{:S(2)}, u32[]{:S(2)}) collective-permute-start(f32[6,32,128]{2,1,0:T(8,128)S(1)} %slice.112), channel_id=1, source_target_pairs={{32,0},{33,1},{34,2},{35,3},{36,4},{37,5},{38,6},{39,7},{40,8},{41... | collective-permute-start | bytes 294920 | tf_op jit(solution)/shard_map/ppermute | solution.py:208
  132.2 1.9 collective-permute-start.9
  134.1 0.1 fusion.4
  134.3 3.8 %collective-permute-done.11.c1_ref = f32[6,32,128]{2,1,0:T(8,128)S(1)} collective-permute-done((f32[6,32,128]{2,1,0:T(8,128)S(1)}, f32[6,32,128]{2,1,0:T(8,128)S(1)}, u32[]{:S(2)}, u32[]{:S(2)}) %collective-permute-start.11) | collective-permute-done | bytes 98336 | tf_op jit(solution)/shard_map/ppermute | solution.py:208
  138.1 1.5 collective-permute-done.9.c3_ref
  139.6 1.0 shard_map.55.refs_1_
  140.5 1.3 collective-permute-start.13
  141.8 1.3 collective-permute-start.14
  143.1 1.3 collective-permute-start.15
  144.4 7.9 %collective-permute-done.13 = f32[4,32,128]{2,1,0:T(8,128)S(1)} collective-permute-done((f32[4,32,128]{2,1,0:T(8,128)S(1)}, f32[4,32,128]{2,1,0:T(8,128)S(1)}, u32[]{:S(2)}, u32[]{:S(2)}) %collective-permute-start.13) | collective-permute-done | bytes 65568 | tf_op jit(solution)/shard_map/ppermute | solution.py:208
  152.4 1.8 collective-permute-done.14
  154.2 2.5 %collective-permute-done.15 = f32[4,32,128]{2,1,0:T(8,128)S(1)} collective-permute-done((f32[4,32,128]{2,1,0:T(8,128)S(1)}, f32[4,32,128]{2,1,0:T(8,128)S(1)}, u32[]{:S(2)}, u32[]{:S(2)}) %collective-permute-start.15) | collective-permute-done | bytes 65568 | tf_op jit(solution)/shard_map/ppermute | solution.py:208
  156.6 1.0 shard_map.56.refs_1_
  157.6 1.3 collective-permute-start.17
  158.9 1.3 collective-permute-start.16
  160.2 1.3 collective-permute-start.19
  161.5 3.5 %collective-permute-done.17 = f32[4,32,128]{2,1,0:T(8,128)S(1)} collective-permute-done((f32[4,32,128]{2,1,0:T(8,128)S(1)}, f32[4,32,128]{2,1,0:T(8,128)S(1)}, u32[]{:S(2)}, u32[]{:S(2)}) %collective-permute-start.17) | collective-permute-done | bytes 65568 | tf_op jit(solution)/shard_map/ppermute | solution.py:208
  165.0 2.8 %collective-permute-done.16 = f32[4,32,128]{2,1,0:T(8,128)S(1)} collective-permute-done((f32[4,32,128]{2,1,0:T(8,128)S(1)}, f32[4,32,128]{2,1,0:T(8,128)S(1)}, u32[]{:S(2)}, u32[]{:S(2)}) %collective-permute-start.16) | collective-permute-done | bytes 65568 | tf_op jit(solution)/shard_map/ppermute | solution.py:208
  167.8 2.7 %collective-permute-start.18 = (f32[2,4,32,128]{3,2,1,0:T(8,128)S(1)}, f32[2,4,32,128]{3,2,1,0:T(8,128)S(1)}, u32[]{:S(2)}, u32[]{:S(2)}) collective-permute-start(f32[2,4,32,128]{3,2,1,0:T(8,128)S(1)} %pad_maximum_fusion.11), channel_id=1, source_target_pairs={{0,1},{1,0},{2,3},{3,2},{4,5},{5,4},{6,7},{7,6},{8,9},{9,8},{10,11... | collective-permute-start | bytes 393224 | tf_op jit(solution)/shard_map/ppermute | solution.py:318
  170.5 2.3 %collective-permute-done.19 = f32[4,32,128]{2,1,0:T(8,128)S(1)} collective-permute-done((f32[4,32,128]{2,1,0:T(8,128)S(1)}, f32[4,32,128]{2,1,0:T(8,128)S(1)}, u32[]{:S(2)}, u32[]{:S(2)}) %collective-permute-start.19) | collective-permute-done | bytes 65568 | tf_op jit(solution)/shard_map/ppermute | solution.py:208
  172.9 2.6 %shard_map.57 = f32[4,32,128]{2,1,0:T(8,128)S(1)} custom-call(f32[20,32,128]{2,1,0:T(8,128)S(1)} %broadcast_select_fusion.refs_0_, f32[4,32,128]{2,1,0:T(8,128)S(1)} %shard_map.56.refs_1_, f32[20,32,128]{2,1,0:T(8,128)S(1)} %get-tuple-element.15.refs_2_, f32[20,32,128]{2,1,0:T(8,128)S(1)} %get-tuple-element.14.refs_3_), custom_call_target="tpu_custom_call" | custom-call | tf_op jit(solution)/shard_map/pallas_call | solution.py:190
  175.6 25.9 %all_to_all.11 = f32[32,4,128]{2,1,0:T(4,128)S(1)} all-to-all(f32[32,4,128]{2,1,0:T(4,128)S(1)} %copy.15), channel_id=1, replica_groups=mesh['tm'=16,'space'=32] {'space'}, dimensions={0} | all-to-all | bytes 131072 | tf_op jit(solution)/shard_map/all_to_all | solution.py:326
  201.5 1.1 shard_map.58
  (52 shorter events, 0.6 us)
Async XLA Ops:
  0.9 11.5 %collective-permute-start.2 = (f32[128,128]{1,0:T(8,128)S(1)}, f32[128,128]{1,0:T(8,128)S(1)}, u32[]{:S(2)}, u32[]{:S(2)}) collective-permute-start(f32[128,128]{1,0:T(8,128)S(1)} %get-tuple-element.11), channel_id=1, source_target_pairs={{0,1},{1,0},{2,3},{3,2},{4,5},{5,4},{6,7},{7,6},{8,9},{9,8},{10,11... | collective-permute-start | bytes 196616 | tf_op jit(solution)/shard_map/ppermute | solution.py:242
  3.5 8.9 %collective-permute-start.3 = (f32[128,128]{1,0:T(8,128)S(1)}, f32[128,128]{1,0:T(8,128)S(1)}, u32[]{:S(2)}, u32[]{:S(2)}) collective-permute-start(f32[128,128]{1,0:T(8,128)S(1)} %get-tuple-element.12), channel_id=1, source_target_pairs={{1,2},{2,1},{3,4},{4,3},{5,6},{6,5},{7,8},{8,7},{9,10},{10,9},{11,... | collective-permute-start | bytes 196616 | tf_op jit(solution)/shard_map/ppermute | solution.py:239
  6.6 26.6 %collective-permute-start.1 = (f32[2,512,128]{2,1,0:T(8,128)}, f32[2,512,128]{2,1,0:T(8,128)S(1)}, u32[]{:S(2)}, u32[]{:S(2)}) collective-permute-start(f32[2,512,128]{2,1,0:T(8,128)} %bitcast.58), channel_id=1, source_target_pairs={{1,2},{2,1},{3,4},{4,3},{5,6},{6,5},{7,8},{8,7},{9,10},{10,9},{11,... | collective-permute-start | bytes 1572872 | tf_op jit(solution)/shard_map/ppermute | solution.py:239
  9.1 25.2 %collective-permute-start = (f32[2,512,128]{2,1,0:T(8,128)}, f32[2,512,128]{2,1,0:T(8,128)S(1)}, u32[]{:S(2)}, u32[]{:S(2)}) collective-permute-start(f32[2,512,128]{2,1,0:T(8,128)} %bitcast.59), channel_id=1, source_target_pairs={{0,1},{1,0},{2,3},{3,2},{4,5},{5,4},{6,7},{7,6},{8,9},{9,8},{10,11... | collective-permute-start | bytes 1572872 | tf_op jit(solution)/shard_map/ppermute | solution.py:242
  11.0 1.0 copy-start
  12.4 6.5 %collective-permute-start.4 = (f32[2,128,128]{2,1,0:T(8,128)S(1)}, f32[2,128,128]{2,1,0:T(8,128)S(1)}, u32[]{:S(2)}, u32[]{:S(2)}) collective-permute-start(f32[2,128,128]{2,1,0:T(8,128)S(1)} %pad_maximum_fusion.10), channel_id=1, source_target_pairs={{0,32},{32,0},{64,96},{96,64},{128,160},{160,128},{192,224},{224,1... | collective-permute-start | bytes 393224 | tf_op jit(solution)/shard_map/ppermute | solution.py:255
  14.9 11.6 %copy-start.2 = (f32[1,2,512,128]{3,2,1,0:T(8,128)S(1)}, f32[1,2,512,128]{3,2,1,0:T(8,128)}, u32[]{:S(2)}) copy-start(f32[1,2,512,128]{3,2,1,0:T(8,128)} %param.4) | copy-start | bytes 1572868
  18.9 7.6 %copy-start.7 = (s32[1,256]{1,0:T(1,128)S(1)}, s32[1,256]{1,0:T(1,128)}, u32[]{:S(2)}) copy-start(s32[1,256]{1,0:T(1,128)} %param.6) | copy-start | bytes 3076
  18.9 13.3 %collective-permute-start.5 = (f32[2,256,128]{2,1,0:T(8,128)S(1)}, f32[2,256,128]{2,1,0:T(8,128)}, u32[]{:S(2)}, u32[]{:S(2)}) collective-permute-start(f32[2,256,128]{2,1,0:T(8,128)S(1)} %pad_maximum_fusion.8), channel_id=1, source_target_pairs={{0,64},{32,96},{64,0},{96,32},{128,192},{160,224},{192,128},{224,1... | collective-permute-start | bytes 786440 | tf_op jit(solution)/shard_map/ppermute | solution.py:255
  33.5 0.8 copy-start.3
  34.3 1.2 copy-start.1
  34.3 0.8 copy-start.5
  34.3 1.4 copy-start.4
  35.7 1.0 copy-start.6
  39.1 11.8 %collective-permute-start.7 = (f32[1152,128]{1,0:T(8,128)}, f32[1152,128]{1,0:T(8,128)}, u32[]{:S(2)}, u32[]{:S(2)}) collective-permute-start(f32[1152,128]{1,0:T(8,128)} %pad_maximum_fusion), channel_id=1, source_target_pairs={{1,2},{2,1},{3,4},{4,3},{5,6},{6,5},{7,8},{8,7},{9,10},{10,9},{11,... | collective-permute-start | bytes 1769480 | tf_op jit(solution)/shard_map/ppermute | solution.py:239
  43.1 8.9 %collective-permute-start.6 = (f32[1152,128]{1,0:T(8,128)}, f32[1152,128]{1,0:T(8,128)}, u32[]{:S(2)}, u32[]{:S(2)}) collective-permute-start(f32[1152,128]{1,0:T(8,128)} %pad_maximum_fusion), channel_id=1, source_target_pairs={{0,1},{1,0},{2,3},{3,2},{4,5},{5,4},{6,7},{7,6},{8,9},{9,8},{10,11... | collective-permute-start | bytes 1769480 | tf_op jit(solution)/shard_map/ppermute | solution.py:242
  123.0 9.1 %collective-permute-start.12 = (f32[10,32,128]{2,1,0:T(8,128)S(1)}, f32[10,32,128]{2,1,0:T(8,128)S(1)}, u32[]{:S(2)}, u32[]{:S(2)}) collective-permute-start(f32[10,32,128]{2,1,0:T(8,128)S(1)} %slice.113), channel_id=1, source_target_pairs={{0,32},{32,0},{64,96},{96,64},{128,160},{160,128},{192,224},{224,1... | collective-permute-start | bytes 491528 | tf_op jit(solution)/shard_map/ppermute | solution.py:292
  125.5 12.5 %collective-permute-start.8 = (f32[12,32,128]{2,1,0:T(8,128)S(1)}, f32[12,32,128]{2,1,0:T(8,128)S(1)}, u32[]{:S(2)}, u32[]{:S(2)}) collective-permute-start(f32[12,32,128]{2,1,0:T(8,128)S(1)} %slice.109), channel_id=1, source_target_pairs={{128,0},{129,1},{130,2},{131,3},{132,4},{133,5},{134,6},{135,7},{1... | collective-permute-start | bytes 589832 | tf_op jit(solution)/shard_map/ppermute | solution.py:208
  126.8 11.2 %collective-permute-start.10 = (f32[8,32,128]{2,1,0:T(8,128)S(1)}, f32[8,32,128]{2,1,0:T(8,128)S(1)}, u32[]{:S(2)}, u32[]{:S(2)}) collective-permute-start(f32[8,32,128]{2,1,0:T(8,128)S(1)} %slice.111), channel_id=1, source_target_pairs={{64,0},{65,1},{66,2},{67,3},{68,4},{69,5},{70,6},{71,7},{72,8},{73... | collective-permute-start | bytes 393224 | tf_op jit(solution)/shard_map/ppermute | solution.py:208
  129.6 8.5 %collective-permute-start.11 = (f32[6,32,128]{2,1,0:T(8,128)S(1)}, f32[6,32,128]{2,1,0:T(8,128)S(1)}, u32[]{:S(2)}, u32[]{:S(2)}) collective-permute-start(f32[6,32,128]{2,1,0:T(8,128)S(1)} %slice.112), channel_id=1, source_target_pairs={{32,0},{33,1},{34,2},{35,3},{36,4},{37,5},{38,6},{39,7},{40,8},{41... | collective-permute-start | bytes 294920 | tf_op jit(solution)/shard_map/ppermute | solution.py:208
  132.2 7.4 %collective-permute-start.9 = (f32[10,32,128]{2,1,0:T(8,128)S(1)}, f32[10,32,128]{2,1,0:T(8,128)S(1)}, u32[]{:S(2)}, u32[]{:S(2)}) collective-permute-start(f32[10,32,128]{2,1,0:T(8,128)S(1)} %get-tuple-element.13), channel_id=1, source_target_pairs={{96,0},{97,1},{98,2},{99,3},{100,4},{101,5},{102,6},{103,7},{104,8... | collective-permute-start | bytes 491528 | tf_op jit(solution)/shard_map/ppermute | solution.py:208
  140.5 11.8 %collective-permute-start.13 = (f32[4,32,128]{2,1,0:T(8,128)S(1)}, f32[4,32,128]{2,1,0:T(8,128)S(1)}, u32[]{:S(2)}, u32[]{:S(2)}) collective-permute-start(f32[4,32,128]{2,1,0:T(8,128)S(1)} %shard_map.55.refs_1_), channel_id=1, source_target_pairs={{128,1},{129,0},{130,3},{131,2},{132,5},{133,4},{134,7},{135,6},{1... | collective-permute-start | bytes 196616 | tf_op jit(solution)/shard_map/ppermute | solution.py:208
  141.8 12.3 %collective-permute-start.14 = (f32[4,32,128]{2,1,0:T(8,128)S(1)}, f32[4,32,128]{2,1,0:T(8,128)S(1)}, u32[]{:S(2)}, u32[]{:S(2)}) collective-permute-start(f32[4,32,128]{2,1,0:T(8,128)S(1)} %shard_map.55.refs_1_), channel_id=1, source_target_pairs={{129,2},{130,1},{131,4},{132,3},{133,6},{134,5},{135,8},{136,7},{1... | collective-permute-start | bytes 196616 | tf_op jit(solution)/shard_map/ppermute | solution.py:208
  143.1 13.5 %collective-permute-start.15 = (f32[4,32,128]{2,1,0:T(8,128)S(1)}, f32[4,32,128]{2,1,0:T(8,128)S(1)}, u32[]{:S(2)}, u32[]{:S(2)}) collective-permute-start(f32[4,32,128]{2,1,0:T(8,128)S(1)} %shard_map.55.refs_1_), channel_id=1, source_target_pairs={{128,0},{129,1},{130,2},{131,3},{132,4},{133,5},{134,6},{135,7},{1... | collective-permute-start | bytes 196616 | tf_op jit(solution)/shard_map/ppermute | solution.py:208
  157.6 7.4 %collective-permute-start.17 = (f32[4,32,128]{2,1,0:T(8,128)S(1)}, f32[4,32,128]{2,1,0:T(8,128)S(1)}, u32[]{:S(2)}, u32[]{:S(2)}) collective-permute-start(f32[4,32,128]{2,1,0:T(8,128)S(1)} %shard_map.56.refs_1_), channel_id=1, source_target_pairs={{257,2},{258,1},{259,4},{260,3},{261,6},{262,5},{263,8},{264,7},{2... | collective-permute-start | bytes 196616 | tf_op jit(solution)/shard_map/ppermute | solution.py:208
  158.9 8.8 %collective-permute-start.16 = (f32[4,32,128]{2,1,0:T(8,128)S(1)}, f32[4,32,128]{2,1,0:T(8,128)S(1)}, u32[]{:S(2)}, u32[]{:S(2)}) collective-permute-start(f32[4,32,128]{2,1,0:T(8,128)S(1)} %shard_map.56.refs_1_), channel_id=1, source_target_pairs={{256,0},{257,1},{258,2},{259,3},{260,4},{261,5},{262,6},{263,7},{2... | collective-permute-start | bytes 196616 | tf_op jit(solution)/shard_map/ppermute | solution.py:208
  160.2 12.5 %collective-permute-start.19 = (f32[4,32,128]{2,1,0:T(8,128)S(1)}, f32[4,32,128]{2,1,0:T(8,128)S(1)}, u32[]{:S(2)}, u32[]{:S(2)}) collective-permute-start(f32[4,32,128]{2,1,0:T(8,128)S(1)} %shard_map.56.refs_1_), channel_id=1, source_target_pairs={{256,2},{258,4},{260,6},{262,8},{264,10},{266,12},{268,14},{270,16... | collective-permute-start | bytes 196616 | tf_op jit(solution)/shard_map/ppermute | solution.py:208
  167.8 5.0 %collective-permute-start.18 = (f32[2,4,32,128]{3,2,1,0:T(8,128)S(1)}, f32[2,4,32,128]{3,2,1,0:T(8,128)S(1)}, u32[]{:S(2)}, u32[]{:S(2)}) collective-permute-start(f32[2,4,32,128]{3,2,1,0:T(8,128)S(1)} %pad_maximum_fusion.11), channel_id=1, source_target_pairs={{0,1},{1,0},{2,3},{3,2},{4,5},{5,4},{6,7},{7,6},{8,9},{9,8},{10,11... | collective-permute-start | bytes 393224 | tf_op jit(solution)/shard_map/ppermute | solution.py:318

commit v6 on v5

--- a/solution.py
+++ b/solution.py
@@ -15,7 +15,7 @@
 
 
 def params():
-    return pltpu.CompilerParams(vmem_limit_bytes=12 * 1024 * 1024)
+    return pltpu.CompilerParams(vmem_limit_bytes=16 * 1024 * 1024)
 
 
 def halving(half):
@@ -24,16 +24,17 @@
     return jnp.where(lane == row // 2 + 64 * half, 0.125, 0.0).astype(jnp.float32)
 
 
-def restrict_kernel(field_ref, out_ref):
+def restricted(ref, rows):
     total = jnp.zeros((PLANE, 128), jnp.float32)
     for half in range(2):
-        rows = None
-        for plane in range(2):
-            for r in range(2):
-                part = field_ref[plane, pl.ds(2 * half + r, PLANE, stride=4), :]
-                rows = part if rows is None else rows + part
-        total = total + jnp.dot(rows, halving(half), precision=EXACT, preferred_element_type=jnp.float32)
-    out_ref[...] = total
+        parts = [ref[pl.ds(p * rows + 2 * half + r, PLANE, stride=4), :] for p in range(2) for r in range(2)]
+        summed = (parts[0] + parts[1]) + (parts[2] + parts[3])
+        total = total + jnp.dot(summed, halving(half), precision=EXACT, preferred_element_type=jnp.float32)
+    return total
+
+
+def restrict_kernel(field_ref, out_ref):
+    out_ref[...] = restricted(field_ref, field_ref.shape[0] // 2)
 
 
 def restrict(field):
@@ -41,7 +42,7 @@
         restrict_kernel,
         out_shape=jax.ShapeDtypeStruct((PLANE, 128), jnp.float32),
         compiler_params=params(),
-    )(field)
+    )(field.reshape(-1, 128))
 
 
 def prolong_add_kernel(delta_ref, field_ref, out_ref):
@@ -87,11 +88,16 @@
     return above + below + before + after
 
 
-def step_kernel(place_ref, across_ref, along_ref, field_ref, share_ref, cond_ref, source_ref, out_ref):
+def two_sweeps(place_ref, across_ref, along_ref, field_ref, share_ref, cond_ref, source_ref):
     odd = place_ref[0] == 1
-    planes = [jnp.where(odd, along_ref[p], across_ref[p]) for p in range(2)]
-    planes += [field_ref[p] for p in range(2)]
-    planes += [jnp.where(odd, across_ref[p], along_ref[p]) for p in range(2)]
+    rows = cond_ref.shape[1]
+
+    def plane(ref, p):
+        return ref[p * rows : (p + 1) * rows, :]
+
+    planes = [jnp.where(odd, plane(along_ref, p), plane(across_ref, p)) for p in range(2)]
+    planes += [plane(field_ref, p) for p in range(2)]
+    planes += [jnp.where(odd, plane(across_ref, p), plane(along_ref, p)) for p in range(2)]
     conds = [share_ref[0], cond_ref[0], cond_ref[1], share_ref[1]]
     terms, diagonals, wide = [], [], []
     for i in range(4):
@@ -102,39 +108,56 @@
         wide.append((terms[i] + total) / diagonals[i])
     wide[0] = jnp.where(place_ref[1] == 1, wide[0], 0.0)
     wide[3] = jnp.where(place_ref[2] == 1, wide[3], 0.0)
+    swept = []
     for p in range(2):
         total = wide[p] + wide[p + 2] + beside_in_plane(wide[p + 1])
-        out_ref[p] = (terms[p + 1] + total) / diagonals[p + 1]
-
-
-def fine_step(place, *operands):
-    in_vmem = pl.BlockSpec(memory_space=pltpu.VMEM)
-    return pl.pallas_call(
-        step_kernel,
-        out_shape=jax.ShapeDtypeStruct(operands[2].shape, jnp.float32),
-        in_specs=[pl.BlockSpec(memory_space=pltpu.SMEM)] + [in_vmem] * len(operands),
-        out_specs=in_vmem,
-        compiler_params=params(),
-    )(place, *operands)
-
-
-def plane_sweep_kernel(state_ref, start_ref, before_ref, after_ref, keep_ref, spread_ref, out_ref):
-    value = state_ref[...]
+        swept.append((terms[p + 1] + total) / diagonals[p + 1])
+    return swept
+
+
+def plane_sweep(value, start, beside, keep, spread):
     low, z = lanes_of(value.shape)
     row = lax.broadcasted_iota(jnp.int32, value.shape, 0)
     swapped = pltpu.roll(value, 64, 1)
     earlier = jnp.where(row == 0, 0.0, pltpu.roll(swapped, 1, 0))
     later = jnp.where(row == PLANE - 1, 0.0, pltpu.roll(swapped, PLANE - 1, 0))
-    total = before_ref[...] + after_ref[...] + swapped + jnp.where(low, earlier, later) + beside_z(value, z)
-    out_ref[...] = keep_ref[...] * start_ref[...] + spread_ref[...] * total
-
-
-def plane_sweep(state, start, before, after, keep, spread):
+    total = beside + swapped + jnp.where(low, earlier, later) + beside_z(value, z)
+    return keep * start + spread * total
+
+
+def first_step_kernel(*refs):
+    start_ref, keep_ref, spread_ref, out_ref = refs[7:]
+    across_ref, along_ref, cond_ref = refs[1], refs[2], refs[5]
+    rows = cond_ref.shape[1]
+    for p, value in enumerate(two_sweeps(*refs[:7])):
+        out_ref[p * rows : (p + 1) * rows, :] = value
+    beside = restricted(across_ref, rows) + restricted(along_ref, rows)
+    start = start_ref[...]
+    out_ref[2 * rows :, :] = plane_sweep(start, start, beside, keep_ref[...], spread_ref[...])
+
+
+def second_step_kernel(*refs):
+    start_ref, keep_ref, spread_ref, field_ref, term_ref, direct_ref = refs[7:]
+    place_ref, across_ref, along_ref, sent_ref, cond_ref = refs[0], refs[1], refs[2], refs[3], refs[5]
+    rows = cond_ref.shape[1]
+    for p, value in enumerate(two_sweeps(*refs[:7])):
+        field_ref[p * rows : (p + 1) * rows, :] = value
+    tail = slice(2 * rows, 2 * rows + PLANE)
+    beside = across_ref[tail, :] + along_ref[tail, :]
+    direct = plane_sweep(sent_ref[tail, :], start_ref[...], beside, keep_ref[...], spread_ref[...])
+    direct_ref[...] = direct
+    term_ref[...] = restricted(field_ref, rows) - jnp.where(place_ref[3] == 1, 0.0, direct)
+
+
+def step_call(kernel, shapes, place, *operands):
+    in_vmem = pl.BlockSpec(memory_space=pltpu.VMEM)
     return pl.pallas_call(
-        plane_sweep_kernel,
-        out_shape=jax.ShapeDtypeStruct(state.shape, jnp.float32),
+        kernel,
+        out_shape=[jax.ShapeDtypeStruct(shape, jnp.float32) for shape in shapes],
+        in_specs=[pl.BlockSpec(memory_space=pltpu.SMEM)] + [in_vmem] * len(operands),
+        out_specs=[in_vmem] * len(shapes),
         compiler_params=params(),
-    )(state, start, before, after, keep, spread)
+    )(place, *operands)
 
 
 def sweep_rows(source, start, keep, spread, target, first, last, low_end, high_end):
@@ -164,16 +187,17 @@
     return 1 - at
 
 
-def first_links_kernel(c4_ref, c3_ref, c2_ref, c1_ref, keep_ref, spread_ref, out_ref, fields):
-    rows = c4_ref.shape[0]
-    fields[0] = c4_ref[...]
+def first_links_kernel(left_ref, c4_ref, c3_ref, c2_ref, c1_ref, keep_ref, spread_ref, out_ref, fields):
+    rows = keep_ref.shape[0]
+    for q in range(rows):
+        fields[0, q] = jnp.where(left_ref[0] >= 4, c4_ref[q], 0.0)
     at, low_end, high_end = 0, 0, rows
-    for added in (c3_ref, c2_ref, c1_ref, None):
+    for link, added in ((3, c3_ref), (2, c2_ref), (1, c1_ref), (0, None)):
         at = coarse_step(fields, keep_ref, spread_ref, at, low_end, high_end)
         low_end, high_end = low_end + 1, high_end - 1
         if added is not None:
             for q in range(low_end, high_end):
-                fields[at, q] = fields[at, q] + added[q - low_end]
+                fields[at, q] = fields[at, q] + jnp.where(left_ref[0] >= link, added[q - low_end], 0.0)
     out_ref[...] = fields[at, low_end:high_end]
 
 
@@ -186,9 +210,11 @@
     out_ref[...] = base_ref[...] + fields[at, links : rows - links]
 
 
-def chain_call(kernel, rows, *operands):
+def chain_call(kernel, rows, *operands, scalars=0):
+    spaces = [pltpu.SMEM] * scalars + [pltpu.VMEM] * (len(operands) - scalars)
     return pl.pallas_call(
         kernel,
+        in_specs=[pl.BlockSpec(memory_space=space) for space in spaces],
         out_shape=jax.ShapeDtypeStruct((BLOCK, SLABS, 128), jnp.float32),
         scratch_shapes=[pltpu.VMEM((3, rows, SLABS, 128), jnp.float32)],
         compiler_params=params(),
@@ -261,7 +287,7 @@
     target = jnp.where(inside, local_row * plane_size + receivers[0] % plane_size, wide_size)
     flat_source = jnp.zeros((wide_size,), jnp.float32).at[target].add(residuals[0], mode="drop")
     wide_source = flat_source.reshape(row_count + 2, width_y, width_z)
-    place = jnp.stack([odd, slab > 0, slab < SLABS - 1]).astype(jnp.int32)
+    place = jnp.stack([odd, slab > 0, slab < SLABS - 1, is_final]).astype(jnp.int32)
 
     coarse_cond = restrict(cond) / FINE_STEPS
     plane_spread = 1.0 / (coarse_cond + 1.5)
@@ -269,30 +295,29 @@
     plane_spread = 0.25 * plane_spread
     coarse_start = restrict(start_field)
 
-    across, along = across_chips(start_field), in_chip(start_field)
-    coarse_now = plane_sweep(
-        coarse_start, coarse_start, *by_side(restrict(along), restrict(across)), plane_keep, plane_spread
-    )
-    field_now = fine_step(place, across, along, start_field, share, cond, wide_source)
-
-    sent = jnp.concatenate([field_now.reshape(row_count * width_y, width_z), coarse_now])
+    slab_rows = row_count * width_y
+    start_rows = start_field.reshape(slab_rows, width_z)
+    around = (share, cond, wide_source, coarse_start, plane_keep, plane_spread)
+    across, along = across_chips(start_rows), in_chip(start_rows)
+    sent, = step_call(
+        first_step_kernel, [(slab_rows + PLANE, 128)], place, across, along, start_rows, *around
+    )
     across, along = across_chips(sent), in_chip(sent)
-    direct = plane_sweep(
-        coarse_now, coarse_start, *by_side(along[-PLANE:], across[-PLANE:]), plane_keep, plane_spread
-    )
-    across, along = (value[:-PLANE].reshape(start_field.shape) for value in (across, along))
-    field_now = fine_step(place, across, along, field_now, share, cond, wide_source)
-
-    term = restrict(field_now) - jnp.where(is_final, 0.0, direct)
-    second_half = slice_index % 2 == 1
-    cond_windows = windows(coarse_cond, 2)
-    cond_windows = jnp.where(second_half, cond_windows[:, 10:], cond_windows[:, :10])
-    arrived = to_rows(jnp.concatenate([windows(term, 1), cond_windows], axis=1))
-    rows, own_cond = arrived[:12], arrived[12:]
-    other_cond = lax.ppermute(own_cond, "tm", [(n, n ^ 1) for n in range(SLICES)])
-    row_cond = jnp.concatenate(
-        [jnp.where(second_half, other_cond, own_cond), jnp.where(second_half, own_cond, other_cond)]
-    )
+    field_now, term, direct = step_call(
+        second_step_kernel, [(slab_rows, 128), (PLANE, 128), (PLANE, 128)], place, across, along, sent, *around
+    )
+    field_now = field_now.reshape(start_field.shape)
+
+    turn = slice_index % 5
+    cond_block = lax.dynamic_slice_in_dim(windows(coarse_cond, 2), turn * BLOCK, BLOCK, axis=1)
+    arrived = to_rows(jnp.concatenate([windows(term, 1), cond_block], axis=1))
+    links, blocks = {}, [arrived[12:]]
+    for k in (1, 2, 3, 4):
+        pairs = [((n + k if n + k < SLICES else n + k - 15), n) for n in range(SLICES - 1)]
+        links[k] = lax.ppermute(jnp.concatenate([arrived[4 - k : 8 + k], arrived[12:]]), "tm", pairs)
+        blocks.append(links[k][-BLOCK:])
+    row_cond = jnp.concatenate(blocks + blocks[:-1])
+    row_cond = lax.dynamic_slice_in_dim(row_cond, (5 - turn) % 5 * BLOCK, 5 * BLOCK, axis=0)
     row_place = (slab - 2) * BLOCK + lax.broadcasted_iota(jnp.int32, row_cond.shape, 0)
     within = (row_place >= 0) & (row_place < PLANE)
     row_spread = jnp.where(within, 1.0 / (row_cond + 1.5), 0.0)
@@ -300,9 +325,11 @@
     row_spread = 0.25 * row_spread
 
     later = [(i, i) for i in range(SLABS)]
-    links = [from_later(rows[4 - k : 8 + k], k, later) for k in (4, 3, 2, 1)]
     inner = slice(BLOCK, 4 * BLOCK)
-    total = chain_call(first_links_kernel, 12, *links, row_keep[inner], row_spread[inner])
+    left = (SLICES - 1 - slice_index)[None].astype(jnp.int32)
+    total = chain_call(
+        first_links_kernel, 12, left, *(links[k] for k in (4, 3, 2, 1)), row_keep[inner], row_spread[inner], scalars=1
+    )
 
     centre = from_later(total, 4, later)
     before, after = beside_later(total, 4, 1, slab)

time: 206 us -> 209 us (1.015)
  the two profiles are of different devices: /device:TPU:7 before, /device:TPU:35 now
where the time goes in v6:
time: 209 us; the launch traced here: 208 us
  starting transfers between devices  92.1 us (44%)
  waiting for transfers between devices  62.3 us (30%)
  blocking collectives  29.9 us (14%)
  Pallas kernels  11.3 us (5%)
  local copies, waits for them, and re-layouts  6.65 us (3%)
  other arithmetic  4.53 us (2%)
    all_to_all x1, starting transfers between devices, to_rows(): arrived = lax.all_to_all(parts, 'space', 0, 0)  49.2 us
    all_to_all x1, blocking collectives, per_device(): back = lax.all_to_all(jnp.transpose(total, (1, 0, 2)), 'space', 0, 0)  29.9 us
    all_to_all x1, waiting for transfers between devices, to_rows(): arrived = lax.all_to_all(parts, 'space', 0, 0)  20.9 us
    ppermute x4, waiting for transfers between devices, per_device(): lax.ppermute(jnp.concatenate([arrived[4 - k:8 + k], arrived[12:]]), 'tm',...  19.4 us
    ppermute x3, starting transfers between devices, across_chips(): return lax.ppermute(value, 'space', facing(1, 1))  10.9 us
    ppermute x6, waiting for transfers between devices, from_later(): return lax.ppermute(value, ('tm', 'space'), both)  9.78 us
    ppermute x6, starting transfers between devices, from_later(): return lax.ppermute(value, ('tm', 'space'), both)  9.64 us
    ppermute x4, starting transfers between devices, per_device(): lax.ppermute(jnp.concatenate([arrived[4 - k:8 + k], arrived[12:]]), 'tm',...  7.91 us
  transfers between devices with their start and end apart: 20, of which 13 were waited for; matrix products, arithmetic and copies ran while one was open for 2% of the time, Pallas kernels for 0%

profile of v6, /device:TPU:35, one launch (start us, length us, event | category | flops | bytes accessed | tf_op | source)
XLA Modules:
  0.0 207.6 jit_solution(14311626170011782015)
XLA Ops:
  0.0 0.9 select_bitcast_fusion.3
  0.9 2.6 %collective-permute-start.2 = (f32[128,128]{1,0:T(8,128)S(1)}, f32[128,128]{1,0:T(8,128)S(1)}, u32[]{:S(2)}, u32[]{:S(2)}) collective-permute-start(f32[128,128]{1,0:T(8,128)S(1)} %get-tuple-element.15), channel_id=1, source_target_pairs={{0,1},{1,0},{2,3},{3,2},{4,5},{5,4},{6,7},{7,6},{8,9},{9,8},{10,11... | collective-permute-start | bytes 196616 | tf_op jit(solution)/shard_map/ppermute | solution.py:268
  3.5 3.1 %collective-permute-start.3 = (f32[128,128]{1,0:T(8,128)S(1)}, f32[128,128]{1,0:T(8,128)S(1)}, u32[]{:S(2)}, u32[]{:S(2)}) collective-permute-start(f32[128,128]{1,0:T(8,128)S(1)} %get-tuple-element.16), channel_id=1, source_target_pairs={{1,2},{2,1},{3,4},{4,3},{5,6},{6,5},{7,8},{8,7},{9,10},{10,9},{11,... | collective-permute-start | bytes 196616 | tf_op jit(solution)/shard_map/ppermute | solution.py:265
  6.6 2.5 %collective-permute-start = (f32[1024,128]{1,0:T(8,128)}, f32[1024,128]{1,0:T(8,128)S(1)}, u32[]{:S(2)}, u32[]{:S(2)}) collective-permute-start(f32[1024,128]{1,0:T(8,128)} %bitcast.59), channel_id=1, source_target_pairs={{1,2},{2,1},{3,4},{4,3},{5,6},{6,5},{7,8},{8,7},{9,10},{10,9},{11,... | collective-permute-start | bytes 1572872 | tf_op jit(solution)/shard_map/ppermute | solution.py:265
  9.1 1.9 collective-permute-start.1
  11.0 0.0 copy-start
  11.0 1.0 copy-done
  12.1 0.3 shard_map.47
  12.3 0.0 collective-permute-done.2
  12.4 0.0 collective-permute-done.3
  12.4 2.2 %collective-permute-start.4 = (f32[2,128,128]{2,1,0:T(8,128)S(1)}, f32[2,128,128]{2,1,0:T(8,128)S(1)}, u32[]{:S(2)}, u32[]{:S(2)}) collective-permute-start(f32[2,128,128]{2,1,0:T(8,128)S(1)} %pad_maximum_fusion.7), channel_id=1, source_target_pairs={{0,32},{32,0},{64,96},{96,64},{128,160},{160,128},{192,224},{224,1... | collective-permute-start | bytes 393224 | tf_op jit(solution)/shard_map/ppermute | solution.py:281
  14.6 0.0 copy-start.2
  14.6 4.2 %collective-permute-done.4 = f32[2,128,128]{2,1,0:T(8,128)S(1)} collective-permute-done((f32[2,128,128]{2,1,0:T(8,128)S(1)}, f32[2,128,128]{2,1,0:T(8,128)S(1)}, u32[]{:S(2)}, u32[]{:S(2)}) %collective-permute-start.4) | collective-permute-done | bytes 131104 | tf_op jit(solution)/shard_map/ppermute | solution.py:281
  18.9 0.0 copy-start.5
  18.9 3.8 %collective-permute-start.5 = (f32[2,256,128]{2,1,0:T(8,128)S(1)}, f32[2,256,128]{2,1,0:T(8,128)S(1)}, u32[]{:S(2)}, u32[]{:S(2)}) collective-permute-start(f32[2,256,128]{2,1,0:T(8,128)S(1)} %pad_maximum_fusion.1), channel_id=1, source_target_pairs={{0,64},{32,96},{64,0},{96,32},{128,192},{160,224},{192,128},{224,1... | collective-permute-start | bytes 786440 | tf_op jit(solution)/shard_map/ppermute | solution.py:281
  22.8 0.3 shard_map.46.refs_7_
  23.1 2.4 %scatter_custom_fusion = f32[262144]{0:T(1024)S(1)} fusion(s32[256]{0:T(256)S(1)} %bitcast.78, f32[256]{0:T(256)} %bitcast.79, f32[]{:T(128)} %constant.132.clone.1), kind=kCustom, calls=%fused_computation.2 | custom fusion | flops 256 | bytes 1049088 | tf_op jit(solution)/shard_map/scatter-add | solution.py:288
  25.5 0.1 add_convert_fusion.refs_0_
  25.5 3.2 %collective-permute-done.5 = f32[2,256,128]{2,1,0:T(8,128)S(1)} collective-permute-done((f32[2,256,128]{2,1,0:T(8,128)S(1)}, f32[2,256,128]{2,1,0:T(8,128)S(1)}, u32[]{:S(2)}, u32[]{:S(2)}) %collective-permute-start.5) | collective-permute-done | bytes 262176 | tf_op jit(solution)/shard_map/ppermute | solution.py:281
  28.8 0.0 copy-start.1
  28.9 0.0 copy-start.3
  28.9 0.8 copy-done.3
  29.7 0.4 copy-done.1
  30.1 1.0 copy-done.4
  31.1 2.4 %shard_map.48.refs_3_ = f32[1152,128]{1,0:T(8,128)S(1)} custom-call(s32[4]{0:T(128)S(1)} %add_convert_fusion.refs_0_, f32[1024,128]{1,0:T(8,128)S(1)} %copy-done.4, f32[1024,128]{1,0:T(8,128)} %collective-permute-done.1.refs_2_, f32[1024,128]{1,0:T(8,128)S(1)} %bitcast.62, f32[2,512,128]{2,1,0:T(8,128)S(1)} %pad_maximum_fusion.refs_4_, ...), custom_call_target="tpu_custom_call" | custom-call | tf_op jit(solution)/shard_map/pallas_call | solution.py:154
  33.5 5.4 %collective-permute-start.6 = (f32[1152,128]{1,0:T(8,128)S(1)}, f32[1152,128]{1,0:T(8,128)}, u32[]{:S(2)}, u32[]{:S(2)}) collective-permute-start(f32[1152,128]{1,0:T(8,128)S(1)} %shard_map.48.refs_3_), channel_id=1, source_target_pairs={{1,2},{2,1},{3,4},{4,3},{5,6},{6,5},{7,8},{8,7},{9,10},{10,9},{11,... | collective-permute-start | bytes 1769480 | tf_op jit(solution)/shard_map/ppermute | solution.py:265
  38.9 1.9 collective-permute-start.7
  40.9 2.1 %concatenate.36 = f32[32,20,128]{2,1,0:T(8,128)} concatenate(f32[32,4,128]{2,1,0:T(4,128)S(1)} %get-tuple-element.34, f32[32,4,128]{2,1,0:T(4,128)S(1)} %get-tuple-element.32, f32[32,4,128]{2,1,0:T(4,128)S(1)} %bitcast.76, f32[32,4,128]{2,1,0:T(4,128)S(1)} %get-tuple-element.33, f32[32,4,128]{2,1,0:T(4,128)S(1)} %get-tuple-element.31), dimensions={1} | concatenate | bytes 655360 | tf_op jit(solution)/shard_map/concatenate | solution.py:247
  43.0 3.6 %collective-permute-done.6.refs_1_ = f32[1152,128]{1,0:T(8,128)} collective-permute-done((f32[1152,128]{1,0:T(8,128)S(1)}, f32[1152,128]{1,0:T(8,128)}, u32[]{:S(2)}, u32[]{:S(2)}) %collective-permute-start.6) | collective-permute-done | bytes 589856 | tf_op jit(solution)/shard_map/ppermute | solution.py:265
  46.6 0.0 collective-permute-done.7.refs_2_
  46.6 2.5 %shard_map.49 = (f32[1024,128]{1,0:T(8,128)S(1)}, f32[128,128]{1,0:T(8,128)S(1)}, f32[128,128]{1,0:T(8,128)S(1)}) custom-call(s32[4]{0:T(128)S(1)} %add_convert_fusion.refs_0_, f32[1152,128]{1,0:T(8,128)} %collective-permute-done.6.refs_1_, f32[1152,128]{1,0:T(8,128)} %collective-permute-done.7.refs_2_, f32[1152,128]{1,0:T(8,128)S(1)} %shard_map.48.refs_3_, ...), custom_call_target="tpu_custom_call" | custom-call | tf_op jit(solution)/shard_map/pallas_call | solution.py:154
  49.1 0.9 pad_slice_fusion.1
  50.1 0.8 pad_maximum_fusion.2
  50.8 49.2 %all-to-all-start = ((f32[32,16,128]{2,1,0:T(8,128)}), f32[32,16,128]{2,1,0:T(8,128)S(1)}, u32[]{:S(2)}, u32[]{:S(2)}) async-start(f32[32,16,128]{2,1,0:T(8,128)} %pad_maximum_fusion.2), calls=%async_computation | async-start | bytes 524288 | tf_op jit(solution)/shard_map/all_to_all | solution.py:251
  100.1 20.9 %all-to-all-done = f32[32,16,128]{2,1,0:T(8,128)S(1)} async-done(((f32[32,16,128]{2,1,0:T(8,128)}), f32[32,16,128]{2,1,0:T(8,128)S(1)}, u32[]{:S(2)}, u32[]{:S(2)}) %all-to-all-start) | async-done | bytes 262176 | tf_op jit(solution)/shard_map/all_to_all | solution.py:251
  121.0 0.1 copy.14
  121.2 1.9 collective-permute-start.8
  123.1 2.1 %collective-permute-start.11 = (f32[10,32,128]{2,1,0:T(8,128)S(1)}, f32[10,32,128]{2,1,0:T(8,128)S(1)}, u32[]{:S(2)}, u32[]{:S(2)}) collective-permute-start(f32[10,32,128]{2,1,0:T(8,128)S(1)} %pad_maximum_fusion.6), channel_id=1, source_target_pairs={{32,0},{64,32},{96,64},{128,96},{160,128},{192,160},{224,192},{256... | collective-permute-start | bytes 491528 | tf_op jit(solution)/shard_map/ppermute | solution.py:317
  125.3 1.9 collective-permute-start.10
  127.2 1.9 collective-permute-start.9
  129.2 0.8 collective-permute-done.11.c1_ref
  129.9 5.5 %collective-permute-done.10.c2_ref = f32[12,32,128]{2,1,0:T(8,128)S(1)} collective-permute-done((f32[12,32,128]{2,1,0:T(8,128)S(1)}, f32[12,32,128]{2,1,0:T(8,128)S(1)}, u32[]{:S(2)}, u32[]{:S(2)}) %collective-permute-start.10) | collective-permute-done | bytes 196640 | tf_op jit(solution)/shard_map/ppermute | solution.py:317
  135.5 13.1 %collective-permute-done.9.c3_ref = f32[14,32,128]{2,1,0:T(8,128)S(1)} collective-permute-done((f32[14,32,128]{2,1,0:T(8,128)S(1)}, f32[14,32,128]{2,1,0:T(8,128)S(1)}, u32[]{:S(2)}, u32[]{:S(2)}) %collective-permute-start.9) | collective-permute-done | bytes 229408 | tf_op jit(solution)/shard_map/ppermute | solution.py:317
  148.6 0.0 collective-permute-done.8.c4_ref
  148.7 0.1 broadcast_multiply_fusion
  148.9 1.0 shard_map.50.refs_1_
  149.9 1.9 collective-permute-start.12
  151.8 1.9 collective-permute-start.13
  153.8 1.9 collective-permute-start.14
  155.7 0.3 collective-permute-done.12
  156.0 2.7 %collective-permute-done.13 = f32[4,32,128]{2,1,0:T(8,128)S(1)} collective-permute-done((f32[4,32,128]{2,1,0:T(8,128)S(1)}, f32[4,32,128]{2,1,0:T(8,128)S(1)}, u32[]{:S(2)}, u32[]{:S(2)}) %collective-permute-start.13) | collective-permute-done | bytes 65568 | tf_op jit(solution)/shard_map/ppermute | solution.py:234
  158.7 0.6 collective-permute-done.14
  159.3 1.0 shard_map.51.refs_1_
  160.3 1.3 collective-permute-start.15
  161.7 1.3 collective-permute-start.16
  162.9 1.3 collective-permute-start.18
  164.2 2.5 %collective-permute-done.15 = f32[4,32,128]{2,1,0:T(8,128)S(1)} collective-permute-done((f32[4,32,128]{2,1,0:T(8,128)S(1)}, f32[4,32,128]{2,1,0:T(8,128)S(1)}, u32[]{:S(2)}, u32[]{:S(2)}) %collective-permute-start.15) | collective-permute-done | bytes 65568 | tf_op jit(solution)/shard_map/ppermute | solution.py:234
  166.7 3.7 %collective-permute-done.16 = f32[4,32,128]{2,1,0:T(8,128)S(1)} collective-permute-done((f32[4,32,128]{2,1,0:T(8,128)S(1)}, f32[4,32,128]{2,1,0:T(8,128)S(1)}, u32[]{:S(2)}, u32[]{:S(2)}) %collective-permute-start.16) | collective-permute-done | bytes 65568 | tf_op jit(solution)/shard_map/ppermute | solution.py:234
  170.4 2.1 %collective-permute-start.17 = (f32[2,4,32,128]{3,2,1,0:T(8,128)S(1)}, f32[2,4,32,128]{3,2,1,0:T(8,128)S(1)}, u32[]{:S(2)}, u32[]{:S(2)}) collective-permute-start(f32[2,4,32,128]{3,2,1,0:T(8,128)S(1)} %pad_maximum_fusion.8), channel_id=1, source_target_pairs={{0,1},{1,0},{2,3},{3,2},{4,5},{5,4},{6,7},{7,6},{8,9},{9,8},{10,11... | collective-permute-start | bytes 393224 | tf_op jit(solution)/shard_map/ppermute | solution.py:345
  172.5 0.0 collective-permute-done.18
  172.6 1.1 collective-permute-done.17
  173.8 2.7 %shard_map.52 = f32[4,32,128]{2,1,0:T(8,128)S(1)} custom-call(f32[20,32,128]{2,1,0:T(8,128)S(1)} %broadcast_select_fusion.refs_0_, f32[4,32,128]{2,1,0:T(8,128)S(1)} %shard_map.51.refs_1_, f32[20,32,128]{2,1,0:T(8,128)S(1)} %get-tuple-element.12.refs_2_, f32[20,32,128]{2,1,0:T(8,128)S(1)} %get-tuple-element.11.refs_3_), custom_call_target="tpu_custom_call" | custom-call | tf_op jit(solution)/shard_map/pallas_call | solution.py:215
  176.6 29.9 %all_to_all.10 = f32[32,4,128]{2,1,0:T(4,128)S(1)} all-to-all(f32[32,4,128]{2,1,0:T(4,128)S(1)} %copy.12), channel_id=1, replica_groups=mesh['tm'=16,'space'=32] {'space'}, dimensions={0} | all-to-all | bytes 131072 | tf_op jit(solution)/shard_map/all_to_all | solution.py:353
  206.5 1.1 shard_map.53
  (46 shorter events, 0.6 us)
Async XLA Ops:
  0.9 11.5 %collective-permute-start.2 = (f32[128,128]{1,0:T(8,128)S(1)}, f32[128,128]{1,0:T(8,128)S(1)}, u32[]{:S(2)}, u32[]{:S(2)}) collective-permute-start(f32[128,128]{1,0:T(8,128)S(1)} %get-tuple-element.15), channel_id=1, source_target_pairs={{0,1},{1,0},{2,3},{3,2},{4,5},{5,4},{6,7},{7,6},{8,9},{9,8},{10,11... | collective-permute-start | bytes 196616 | tf_op jit(solution)/shard_map/ppermute | solution.py:268
  3.5 8.9 %collective-permute-start.3 = (f32[128,128]{1,0:T(8,128)S(1)}, f32[128,128]{1,0:T(8,128)S(1)}, u32[]{:S(2)}, u32[]{:S(2)}) collective-permute-start(f32[128,128]{1,0:T(8,128)S(1)} %get-tuple-element.16), channel_id=1, source_target_pairs={{1,2},{2,1},{3,4},{4,3},{5,6},{6,5},{7,8},{8,7},{9,10},{10,9},{11,... | collective-permute-start | bytes 196616 | tf_op jit(solution)/shard_map/ppermute | solution.py:265
  6.6 22.3 %collective-permute-start = (f32[1024,128]{1,0:T(8,128)}, f32[1024,128]{1,0:T(8,128)S(1)}, u32[]{:S(2)}, u32[]{:S(2)}) collective-permute-start(f32[1024,128]{1,0:T(8,128)} %bitcast.59), channel_id=1, source_target_pairs={{1,2},{2,1},{3,4},{4,3},{5,6},{6,5},{7,8},{8,7},{9,10},{10,9},{11,... | collective-permute-start | bytes 1572872 | tf_op jit(solution)/shard_map/ppermute | solution.py:265
  9.1 20.6 %collective-permute-start.1 = (f32[1024,128]{1,0:T(8,128)}, f32[1024,128]{1,0:T(8,128)}, u32[]{:S(2)}, u32[]{:S(2)}) collective-permute-start(f32[1024,128]{1,0:T(8,128)} %bitcast.60), channel_id=1, source_target_pairs={{0,1},{1,0},{2,3},{3,2},{4,5},{5,4},{6,7},{7,6},{8,9},{9,8},{10,11... | collective-permute-start | bytes 1572872 | tf_op jit(solution)/shard_map/ppermute | solution.py:268
  11.0 1.0 copy-start
  12.4 6.5 %collective-permute-start.4 = (f32[2,128,128]{2,1,0:T(8,128)S(1)}, f32[2,128,128]{2,1,0:T(8,128)S(1)}, u32[]{:S(2)}, u32[]{:S(2)}) collective-permute-start(f32[2,128,128]{2,1,0:T(8,128)S(1)} %pad_maximum_fusion.7), channel_id=1, source_target_pairs={{0,32},{32,0},{64,96},{96,64},{128,160},{160,128},{192,224},{224,1... | collective-permute-start | bytes 393224 | tf_op jit(solution)/shard_map/ppermute | solution.py:281
  14.6 8.2 %copy-start.2 = (f32[1,2,512,128]{3,2,1,0:T(8,128)S(1)}, f32[1,2,512,128]{3,2,1,0:T(8,128)}, u32[]{:S(2)}) copy-start(f32[1,2,512,128]{3,2,1,0:T(8,128)} %param.4) | copy-start | bytes 1572868
  18.9 3.8 %copy-start.5 = (s32[1,256]{1,0:T(1,128)S(1)}, s32[1,256]{1,0:T(1,128)}, u32[]{:S(2)}) copy-start(s32[1,256]{1,0:T(1,128)} %param.6) | copy-start | bytes 3076
  18.9 9.8 %collective-permute-start.5 = (f32[2,256,128]{2,1,0:T(8,128)S(1)}, f32[2,256,128]{2,1,0:T(8,128)S(1)}, u32[]{:S(2)}, u32[]{:S(2)}) collective-permute-start(f32[2,256,128]{2,1,0:T(8,128)S(1)} %pad_maximum_fusion.1), channel_id=1, source_target_pairs={{0,64},{32,96},{64,0},{96,32},{128,192},{160,224},{192,128},{224,1... | collective-permute-start | bytes 786440 | tf_op jit(solution)/shard_map/ppermute | solution.py:281
  28.8 1.2 copy-start.1
  28.9 0.8 copy-start.3
  30.0 1.0 copy-start.4
  33.5 13.0 %collective-permute-start.6 = (f32[1152,128]{1,0:T(8,128)S(1)}, f32[1152,128]{1,0:T(8,128)}, u32[]{:S(2)}, u32[]{:S(2)}) collective-permute-start(f32[1152,128]{1,0:T(8,128)S(1)} %shard_map.48.refs_3_), channel_id=1, source_target_pairs={{1,2},{2,1},{3,4},{4,3},{5,6},{6,5},{7,8},{8,7},{9,10},{10,9},{11,... | collective-permute-start | bytes 1769480 | tf_op jit(solution)/shard_map/ppermute | solution.py:265
  38.9 7.7 %collective-permute-start.7 = (f32[1152,128]{1,0:T(8,128)S(1)}, f32[1152,128]{1,0:T(8,128)}, u32[]{:S(2)}, u32[]{:S(2)}) collective-permute-start(f32[1152,128]{1,0:T(8,128)S(1)} %shard_map.48.refs_3_), channel_id=1, source_target_pairs={{0,1},{1,0},{2,3},{3,2},{4,5},{5,4},{6,7},{7,6},{8,9},{9,8},{10,11... | collective-permute-start | bytes 1769480 | tf_op jit(solution)/shard_map/ppermute | solution.py:268
  50.8 70.2 %all-to-all-start = ((f32[32,16,128]{2,1,0:T(8,128)}), f32[32,16,128]{2,1,0:T(8,128)S(1)}, u32[]{:S(2)}, u32[]{:S(2)}) async-start(f32[32,16,128]{2,1,0:T(8,128)} %pad_maximum_fusion.2), calls=%async_computation | async-start | bytes 524288 | tf_op jit(solution)/shard_map/all_to_all | solution.py:251
  121.2 27.5 %collective-permute-start.8 = (f32[16,32,128]{2,1,0:T(8,128)S(1)}, f32[16,32,128]{2,1,0:T(8,128)S(1)}, u32[]{:S(2)}, u32[]{:S(2)}) collective-permute-start(f32[16,32,128]{2,1,0:T(8,128)S(1)} %bitcast.71), channel_id=1, source_target_pairs={{128,0},{160,32},{192,64},{224,96},{256,128},{288,160},{320,192},{... | collective-permute-start | bytes 786440 | tf_op jit(solution)/shard_map/ppermute | solution.py:317
  123.1 6.8 %collective-permute-start.11 = (f32[10,32,128]{2,1,0:T(8,128)S(1)}, f32[10,32,128]{2,1,0:T(8,128)S(1)}, u32[]{:S(2)}, u32[]{:S(2)}) collective-permute-start(f32[10,32,128]{2,1,0:T(8,128)S(1)} %pad_maximum_fusion.6), channel_id=1, source_target_pairs={{32,0},{64,32},{96,64},{128,96},{160,128},{192,160},{224,192},{256... | collective-permute-start | bytes 491528 | tf_op jit(solution)/shard_map/ppermute | solution.py:317
  125.3 10.2 %collective-permute-start.10 = (f32[12,32,128]{2,1,0:T(8,128)S(1)}, f32[12,32,128]{2,1,0:T(8,128)S(1)}, u32[]{:S(2)}, u32[]{:S(2)}) collective-permute-start(f32[12,32,128]{2,1,0:T(8,128)S(1)} %pad_maximum_fusion.4), channel_id=1, source_target_pairs={{64,0},{96,32},{128,64},{160,96},{192,128},{224,160},{256,192},{28... | collective-permute-start | bytes 589832 | tf_op jit(solution)/shard_map/ppermute | solution.py:317
  127.2 21.4 %collective-permute-start.9 = (f32[14,32,128]{2,1,0:T(8,128)S(1)}, f32[14,32,128]{2,1,0:T(8,128)S(1)}, u32[]{:S(2)}, u32[]{:S(2)}) collective-permute-start(f32[14,32,128]{2,1,0:T(8,128)S(1)} %pad_maximum_fusion.3), channel_id=1, source_target_pairs={{96,0},{128,32},{160,64},{192,96},{224,128},{256,160},{288,192},{3... | collective-permute-start | bytes 688136 | tf_op jit(solution)/shard_map/ppermute | solution.py:317
  149.9 6.1 %collective-permute-start.12 = (f32[4,32,128]{2,1,0:T(8,128)S(1)}, f32[4,32,128]{2,1,0:T(8,128)S(1)}, u32[]{:S(2)}, u32[]{:S(2)}) collective-permute-start(f32[4,32,128]{2,1,0:T(8,128)S(1)} %shard_map.50.refs_1_), channel_id=1, source_target_pairs={{128,1},{129,0},{130,3},{131,2},{132,5},{133,4},{134,7},{135,6},{1... | collective-permute-start | bytes 196616 | tf_op jit(solution)/shard_map/ppermute | solution.py:234
  151.8 6.8 %collective-permute-start.13 = (f32[4,32,128]{2,1,0:T(8,128)S(1)}, f32[4,32,128]{2,1,0:T(8,128)S(1)}, u32[]{:S(2)}, u32[]{:S(2)}) collective-permute-start(f32[4,32,128]{2,1,0:T(8,128)S(1)} %shard_map.50.refs_1_), channel_id=1, source_target_pairs={{129,2},{130,1},{131,4},{132,3},{133,6},{134,5},{135,8},{136,7},{1... | collective-permute-start | bytes 196616 | tf_op jit(solution)/shard_map/ppermute | solution.py:234
  153.8 5.6 %collective-permute-start.14 = (f32[4,32,128]{2,1,0:T(8,128)S(1)}, f32[4,32,128]{2,1,0:T(8,128)S(1)}, u32[]{:S(2)}, u32[]{:S(2)}) collective-permute-start(f32[4,32,128]{2,1,0:T(8,128)S(1)} %shard_map.50.refs_1_), channel_id=1, source_target_pairs={{128,0},{129,1},{130,2},{131,3},{132,4},{133,5},{134,6},{135,7},{1... | collective-permute-start | bytes 196616 | tf_op jit(solution)/shard_map/ppermute | solution.py:234
  160.3 6.4 %collective-permute-start.15 = (f32[4,32,128]{2,1,0:T(8,128)S(1)}, f32[4,32,128]{2,1,0:T(8,128)S(1)}, u32[]{:S(2)}, u32[]{:S(2)}) collective-permute-start(f32[4,32,128]{2,1,0:T(8,128)S(1)} %shard_map.51.refs_1_), channel_id=1, source_target_pairs={{256,0},{257,1},{258,2},{259,3},{260,4},{261,5},{262,6},{263,7},{2... | collective-permute-start | bytes 196616 | tf_op jit(solution)/shard_map/ppermute | solution.py:234
  161.7 8.8 %collective-permute-start.16 = (f32[4,32,128]{2,1,0:T(8,128)S(1)}, f32[4,32,128]{2,1,0:T(8,128)S(1)}, u32[]{:S(2)}, u32[]{:S(2)}) collective-permute-start(f32[4,32,128]{2,1,0:T(8,128)S(1)} %shard_map.51.refs_1_), channel_id=1, source_target_pairs={{257,2},{258,1},{259,4},{260,3},{261,6},{262,5},{263,8},{264,7},{2... | collective-permute-start | bytes 196616 | tf_op jit(solution)/shard_map/ppermute | solution.py:234
  162.9 9.6 %collective-permute-start.18 = (f32[4,32,128]{2,1,0:T(8,128)S(1)}, f32[4,32,128]{2,1,0:T(8,128)S(1)}, u32[]{:S(2)}, u32[]{:S(2)}) collective-permute-start(f32[4,32,128]{2,1,0:T(8,128)S(1)} %shard_map.51.refs_1_), channel_id=1, source_target_pairs={{256,2},{258,4},{260,6},{262,8},{264,10},{266,12},{268,14},{270,16... | collective-permute-start | bytes 196616 | tf_op jit(solution)/shard_map/ppermute | solution.py:234
  170.4 3.2 %collective-permute-start.17 = (f32[2,4,32,128]{3,2,1,0:T(8,128)S(1)}, f32[2,4,32,128]{3,2,1,0:T(8,128)S(1)}, u32[]{:S(2)}, u32[]{:S(2)}) collective-permute-start(f32[2,4,32,128]{3,2,1,0:T(8,128)S(1)} %pad_maximum_fusion.8), channel_id=1, source_target_pairs={{0,1},{1,0},{2,3},{3,2},{4,5},{5,4},{6,7},{7,6},{8,9},{9,8},{10,11... | collective-permute-start | bytes 393224 | tf_op jit(solution)/shard_map/ppermute | solution.py:345

commit v7 on v6

--- a/solution.py
+++ b/solution.py
@@ -187,17 +187,16 @@
     return 1 - at
 
 
-def first_links_kernel(left_ref, c4_ref, c3_ref, c2_ref, c1_ref, keep_ref, spread_ref, out_ref, fields):
-    rows = keep_ref.shape[0]
-    for q in range(rows):
-        fields[0, q] = jnp.where(left_ref[0] >= 4, c4_ref[q], 0.0)
+def first_links_kernel(c4_ref, c3_ref, c2_ref, c1_ref, keep_ref, spread_ref, out_ref, fields):
+    rows = c4_ref.shape[0]
+    fields[0] = c4_ref[...]
     at, low_end, high_end = 0, 0, rows
-    for link, added in ((3, c3_ref), (2, c2_ref), (1, c1_ref), (0, None)):
+    for added in (c3_ref, c2_ref, c1_ref, None):
         at = coarse_step(fields, keep_ref, spread_ref, at, low_end, high_end)
         low_end, high_end = low_end + 1, high_end - 1
         if added is not None:
             for q in range(low_end, high_end):
-                fields[at, q] = fields[at, q] + jnp.where(left_ref[0] >= link, added[q - low_end], 0.0)
+                fields[at, q] = fields[at, q] + added[q - low_end]
     out_ref[...] = fields[at, low_end:high_end]
 
 
@@ -210,11 +209,9 @@
     out_ref[...] = base_ref[...] + fields[at, links : rows - links]
 
 
-def chain_call(kernel, rows, *operands, scalars=0):
-    spaces = [pltpu.SMEM] * scalars + [pltpu.VMEM] * (len(operands) - scalars)
+def chain_call(kernel, rows, *operands):
     return pl.pallas_call(
         kernel,
-        in_specs=[pl.BlockSpec(memory_space=space) for space in spaces],
         out_shape=jax.ShapeDtypeStruct((BLOCK, SLABS, 128), jnp.float32),
         scratch_shapes=[pltpu.VMEM((3, rows, SLABS, 128), jnp.float32)],
         compiler_params=params(),
@@ -308,27 +305,39 @@
     )
     field_now = field_now.reshape(start_field.shape)
 
-    turn = slice_index % 5
-    cond_block = lax.dynamic_slice_in_dim(windows(coarse_cond, 2), turn * BLOCK, BLOCK, axis=1)
-    arrived = to_rows(jnp.concatenate([windows(term, 1), cond_block], axis=1))
-    links, blocks = {}, [arrived[12:]]
-    for k in (1, 2, 3, 4):
-        pairs = [((n + k if n + k < SLICES else n + k - 15), n) for n in range(SLICES - 1)]
-        links[k] = lax.ppermute(jnp.concatenate([arrived[4 - k : 8 + k], arrived[12:]]), "tm", pairs)
-        blocks.append(links[k][-BLOCK:])
-    row_cond = jnp.concatenate(blocks + blocks[:-1])
-    row_cond = lax.dynamic_slice_in_dim(row_cond, (5 - turn) % 5 * BLOCK, 5 * BLOCK, axis=0)
+    tall = jnp.pad(coarse_cond, ((2 * BLOCK, 2 * BLOCK), (0, 0)))
+    backwards = sum((slice_index // bit) % 2 * (SLICES // 2 // bit) for bit in (1, 2, 4, 8))
+    shares = []
+    for i in range(2):
+        at = (slab - 2 * backwards - i) % SLABS
+        window = lax.dynamic_slice_in_dim(tall, at * BLOCK, 5 * BLOCK, axis=0)
+        pairs = []
+        for n in range(SLICES):
+            turned = sum((n // bit) % 2 * (SLICES // 2 // bit) for bit in (1, 2, 4, 8))
+            pairs += [(n * SLABS + j, n * SLABS + (j - 2 * turned - i) % SLABS) for j in range(SLABS)]
+        shares.append(lax.ppermute(window, ("tm", "space"), pairs))
+    gathered = jnp.stack(shares)
+    for bit in (8, 4, 2, 1):
+        upper = (slice_index // bit) % 2 == 1
+        other = lax.ppermute(gathered, "tm", [(n, n ^ bit) for n in range(SLICES)])
+        gathered = jnp.concatenate([jnp.where(upper, other, gathered), jnp.where(upper, gathered, other)])
+    turned = lax.dynamic_slice_in_dim(
+        jnp.concatenate([gathered, gathered]), (SLABS - slab) % SLABS, SLABS, axis=0
+    )
+    row_cond = jnp.transpose(turned, (1, 0, 2))
+
+    rows = to_rows(windows(term, 1))
+    later = [(i, i) for i in range(SLABS)]
+    links = {k: from_later(rows[4 - k : 8 + k], k, later) for k in (1, 2, 3, 4)}
     row_place = (slab - 2) * BLOCK + lax.broadcasted_iota(jnp.int32, row_cond.shape, 0)
     within = (row_place >= 0) & (row_place < PLANE)
     row_spread = jnp.where(within, 1.0 / (row_cond + 1.5), 0.0)
     row_keep = row_cond * row_spread
     row_spread = 0.25 * row_spread
 
-    later = [(i, i) for i in range(SLABS)]
     inner = slice(BLOCK, 4 * BLOCK)
-    left = (SLICES - 1 - slice_index)[None].astype(jnp.int32)
     total = chain_call(
-        first_links_kernel, 12, left, *(links[k] for k in (4, 3, 2, 1)), row_keep[inner], row_spread[inner], scalars=1
+        first_links_kernel, 12, *(links[k] for k in (4, 3, 2, 1)), row_keep[inner], row_spread[inner]
     )
 
     centre = from_later(total, 4, later)

time: 209 us -> 207 us (level)
  the two profiles are of different devices: /device:TPU:35 before, /device:TPU:7 now
where the time goes in v7:
time: 207 us; the launch traced here: 205 us
  starting transfers between devices  107 us (52%)
  waiting for transfers between devices  47.3 us (23%)
  blocking collectives  28.7 us (14%)
  Pallas kernels  11.2 us (5%)
  other arithmetic  6.38 us (3%)
  local copies, waits for them, and re-layouts  3.56 us (2%)
    all_to_all x1, starting transfers between devices, to_rows(): arrived = lax.all_to_all(parts, 'space', 0, 0)  31.8 us
    all_to_all x1, blocking collectives, per_device(): back = lax.all_to_all(jnp.transpose(total, (1, 0, 2)), 'space', 0, 0)  28.7 us
    ppermute x10, waiting for transfers between devices, from_later(): return lax.ppermute(value, ('tm', 'space'), both)  26.8 us
    ppermute x2, starting transfers between devices, per_device(): shares.append(lax.ppermute(window, ('tm', 'space'), pairs))  23.8 us
    ppermute x10, starting transfers between devices, from_later(): return lax.ppermute(value, ('tm', 'space'), both)  14.8 us
    ppermute x4, starting transfers between devices, per_device(): other = lax.ppermute(gathered, 'tm', [(n, n ^ bit) for n in range(SLICES)])  14.3 us
    all_to_all x1, waiting for transfers between devices, to_rows(): arrived = lax.all_to_all(parts, 'space', 0, 0)  11.8 us
    ppermute x3, starting transfers between devices, across_chips(): return lax.ppermute(value, 'space', facing(1, 1))  9.2 us
  transfers between devices with their start and end apart: 26, of which 11 were waited for; matrix products, arithmetic and copies ran while one was open for 3% of the time, Pallas kernels for 3%

profile of v7, /device:TPU:7, one launch (start us, length us, event | category | flops | bytes accessed | tf_op | source)
XLA Modules:
  0.0 205.5 jit_solution(3537697908922433712)
XLA Ops:
  0.0 0.9 select_bitcast_fusion.3
  0.9 2.6 %collective-permute-start.2 = (f32[128,128]{1,0:T(8,128)S(1)}, f32[128,128]{1,0:T(8,128)S(1)}, u32[]{:S(2)}, u32[]{:S(2)}) collective-permute-start(f32[128,128]{1,0:T(8,128)S(1)} %get-tuple-element.15), channel_id=1, source_target_pairs={{0,1},{1,0},{2,3},{3,2},{4,5},{5,4},{6,7},{7,6},{8,9},{9,8},{10,11... | collective-permute-start | bytes 196616 | tf_op jit(solution)/shard_map/ppermute | solution.py:265
  3.5 3.1 %collective-permute-start.3 = (f32[128,128]{1,0:T(8,128)S(1)}, f32[128,128]{1,0:T(8,128)S(1)}, u32[]{:S(2)}, u32[]{:S(2)}) collective-permute-start(f32[128,128]{1,0:T(8,128)S(1)} %get-tuple-element.16), channel_id=1, source_target_pairs={{1,2},{2,1},{3,4},{4,3},{5,6},{6,5},{7,8},{8,7},{9,10},{10,9},{11,... | collective-permute-start | bytes 196616 | tf_op jit(solution)/shard_map/ppermute | solution.py:262
  6.6 2.5 %collective-permute-start = (f32[1024,128]{1,0:T(8,128)}, f32[1024,128]{1,0:T(8,128)S(1)}, u32[]{:S(2)}, u32[]{:S(2)}) collective-permute-start(f32[1024,128]{1,0:T(8,128)} %bitcast.61), channel_id=1, source_target_pairs={{1,2},{2,1},{3,4},{4,3},{5,6},{6,5},{7,8},{8,7},{9,10},{10,9},{11,... | collective-permute-start | bytes 1572872 | tf_op jit(solution)/shard_map/ppermute | solution.py:262
  9.1 1.9 collective-permute-start.1
  11.0 0.0 copy-start
  11.0 1.0 copy-done
  12.0 0.3 shard_map.47
  12.4 2.5 %collective-permute-start.4 = (f32[2,128,128]{2,1,0:T(8,128)S(1)}, f32[2,128,128]{2,1,0:T(8,128)S(1)}, u32[]{:S(2)}, u32[]{:S(2)}) collective-permute-start(f32[2,128,128]{2,1,0:T(8,128)S(1)} %pad_maximum_fusion.5), channel_id=1, source_target_pairs={{0,32},{32,0},{64,96},{96,64},{128,160},{160,128},{192,224},{224,1... | collective-permute-start | bytes 393224 | tf_op jit(solution)/shard_map/ppermute | solution.py:278
  15.0 15.0 %collective-permute-start.13 = (f32[20,128]{1,0:T(8,128)S(1)}, f32[20,128]{1,0:T(8,128)S(1)}, u32[]{:S(2)}, u32[]{:S(2)}) collective-permute-start(f32[20,128]{1,0:T(8,128)S(1)} %get-tuple-element.34), channel_id=1, source_target_pairs={{0,31},{1,0},{2,1},{3,2},{4,3},{5,4},{6,5},{7,6},{8,7},{9,8},{10,9... | collective-permute-start | bytes 30728 | tf_op jit(solution)/shard_map/ppermute | solution.py:318
  30.1 8.8 %collective-permute-start.12 = (f32[20,128]{1,0:T(8,128)S(1)}, f32[20,128]{1,0:T(8,128)S(1)}, u32[]{:S(2)}, u32[]{:S(2)}) collective-permute-start(f32[20,128]{1,0:T(8,128)S(1)} %get-tuple-element.33), channel_id=1, source_target_pairs={{0,0},{1,1},{2,2},{3,3},{4,4},{5,5},{6,6},{7,7},{8,8},{9,9},{10,10... | collective-permute-start | bytes 30728 | tf_op jit(solution)/shard_map/ppermute | solution.py:318
  38.9 0.0 copy-start.2
  39.0 0.0 copy-start.7
  39.0 2.6 %collective-permute-start.5 = (f32[2,256,128]{2,1,0:T(8,128)S(1)}, f32[2,256,128]{2,1,0:T(8,128)S(1)}, u32[]{:S(2)}, u32[]{:S(2)}) collective-permute-start(f32[2,256,128]{2,1,0:T(8,128)S(1)} %pad_maximum_fusion.1), channel_id=1, source_target_pairs={{0,64},{32,96},{64,0},{96,32},{128,192},{160,224},{192,128},{224,1... | collective-permute-start | bytes 786440 | tf_op jit(solution)/shard_map/ppermute | solution.py:278
  41.7 0.1 add_convert_fusion.refs_0_
  41.7 0.3 shard_map.46.refs_7_
  42.0 2.4 %scatter_custom_fusion = f32[262144]{0:T(1024)S(1)} fusion(s32[256]{0:T(256)S(1)} %bitcast.77, f32[256]{0:T(256)} %bitcast.78, f32[]{:T(128)} %constant.204.clone.1), kind=kCustom, calls=%fused_computation.6 | custom fusion | flops 256 | bytes 1049088 | tf_op jit(solution)/shard_map/scatter-add | solution.py:285
  44.5 2.3 %collective-permute-start.14 = (f32[2,20,128]{2,0,1:T(2,128)S(1)}, f32[2,20,128]{2,0,1:T(2,128)S(1)}, u32[]{:S(2)}, u32[]{:S(2)}) collective-permute-start(f32[2,20,128]{2,0,1:T(2,128)S(1)} %pad_maximum_fusion.9), channel_id=1, source_target_pairs={{0,256},{32,288},{64,320},{96,352},{128,384},{160,416},{192,448},{... | collective-permute-start | bytes 61448 | tf_op jit(solution)/shard_map/ppermute | solution.py:322
  46.8 1.9 collective-permute-done.5
  48.8 0.0 copy-start.1
  48.8 0.0 copy-start.3
  48.9 0.8 copy-done.3
  49.6 0.4 copy-done.1
  50.0 1.0 copy-done.4
  51.0 2.4 %shard_map.48.refs_3_ = f32[1152,128]{1,0:T(8,128)S(1)} custom-call(s32[4]{0:T(128)S(1)} %add_convert_fusion.refs_0_, f32[1024,128]{1,0:T(8,128)S(1)} %copy-done.4, f32[1024,128]{1,0:T(8,128)} %collective-permute-done.1.refs_2_, f32[1024,128]{1,0:T(8,128)S(1)} %bitcast.64, f32[2,512,128]{2,1,0:T(8,128)S(1)} %pad_maximum_fusion.refs_4_, ...), custom_call_target="tpu_custom_call" | custom-call | tf_op jit(solution)/shard_map/pallas_call | solution.py:154
  53.5 3.6 %collective-permute-start.6 = (f32[1152,128]{1,0:T(8,128)S(1)}, f32[1152,128]{1,0:T(8,128)}, u32[]{:S(2)}, u32[]{:S(2)}) collective-permute-start(f32[1152,128]{1,0:T(8,128)S(1)} %shard_map.48.refs_3_), channel_id=1, source_target_pairs={{1,2},{2,1},{3,4},{4,3},{5,6},{6,5},{7,8},{8,7},{9,10},{10,9},{11,... | collective-permute-start | bytes 1769480 | tf_op jit(solution)/shard_map/ppermute | solution.py:262
  57.1 1.9 collective-permute-start.7
  59.1 4.8 %collective-permute-start.15 = (f32[4,20,128]{2,0,1:T(4,128)S(1)}, f32[4,20,128]{2,0,1:T(4,128)S(1)}, u32[]{:S(2)}, u32[]{:S(2)}) collective-permute-start(f32[4,20,128]{2,0,1:T(4,128)S(1)} %pad_maximum_fusion.8), channel_id=1, source_target_pairs={{0,128},{32,160},{64,192},{96,224},{128,0},{160,32},{192,64},{224,... | collective-permute-start | bytes 122888 | tf_op jit(solution)/shard_map/ppermute | solution.py:322
  63.9 1.4 collective-permute-done.15
  65.3 0.6 pad_maximum_fusion.7
  66.0 5.2 %collective-permute-start.16 = (f32[8,20,128]{2,0,1:T(8,128)}, f32[8,20,128]{2,0,1:T(8,128)}, u32[]{:S(2)}, u32[]{:S(2)}) collective-permute-start(f32[8,20,128]{2,0,1:T(8,128)} %pad_maximum_fusion.7), channel_id=1, source_target_pairs={{0,64},{32,96},{64,0},{96,32},{128,192},{160,224},{192,128},{224,1... | collective-permute-start | bytes 245768 | tf_op jit(solution)/shard_map/ppermute | solution.py:322
  71.2 2.5 %shard_map.49 = (f32[1024,128]{1,0:T(8,128)S(1)}, f32[128,128]{1,0:T(8,128)S(1)}, f32[128,128]{1,0:T(8,128)S(1)}) custom-call(s32[4]{0:T(128)S(1)} %add_convert_fusion.refs_0_, f32[1152,128]{1,0:T(8,128)} %collective-permute-done.6.refs_1_, f32[1152,128]{1,0:T(8,128)} %collective-permute-done.7.refs_2_, f32[1152,128]{1,0:T(8,128)S(1)} %shard_map.48.refs_3_, ...), custom_call_target="tpu_custom_call" | custom-call | tf_op jit(solution)/shard_map/pallas_call | solution.py:154
  73.8 0.8 pad_maximum_fusion.2
  74.5 31.8 %all-to-all-start = ((f32[32,12,128]{2,1,0:T(8,128)}), f32[32,12,128]{2,1,0:T(8,128)S(1)}, u32[]{:S(2)}, u32[]{:S(2)}) async-start(f32[32,12,128]{2,1,0:T(8,128)} %pad_maximum_fusion.2), calls=%async_computation | async-start | bytes 524288 | tf_op jit(solution)/shard_map/all_to_all | solution.py:248
  106.3 0.9 broadcast_select_fusion.8
  107.3 2.0 collective-permute-start.17
  109.4 5.4 %collective-permute-done.17 = f32[16,20,128]{2,0,1:T(8,128)S(1)} collective-permute-done((f32[16,20,128]{2,0,1:T(8,128)S(1)}, f32[16,20,128]{2,0,1:T(8,128)S(1)}, u32[]{:S(2)}, u32[]{:S(2)}) %collective-permute-start.17) | collective-permute-done | bytes 163872 | tf_op jit(solution)/shard_map/ppermute | solution.py:322
  114.8 0.2 fusion.6
  115.0 11.8 %all-to-all-done = f32[32,12,128]{2,1,0:T(8,128)S(1)} async-done(((f32[32,12,128]{2,1,0:T(8,128)}), f32[32,12,128]{2,1,0:T(8,128)S(1)}, u32[]{:S(2)}, u32[]{:S(2)}) %all-to-all-start) | async-done | bytes 196640 | tf_op jit(solution)/shard_map/all_to_all | solution.py:248
  126.8 0.1 copy.15
  126.8 1.3 collective-permute-start.8
  128.2 1.9 collective-permute-start.9
  130.1 1.9 collective-permute-start.10
  132.1 1.9 collective-permute-start.11
  134.0 0.1 fusion.7.refs_2_
  134.1 12.6 %collective-permute-done.11.c1_ref = f32[6,32,128]{2,1,0:T(8,128)S(1)} collective-permute-done((f32[6,32,128]{2,1,0:T(8,128)S(1)}, f32[6,32,128]{2,1,0:T(8,128)S(1)}, u32[]{:S(2)}, u32[]{:S(2)}) %collective-permute-start.11) | collective-permute-done | bytes 98336 | tf_op jit(solution)/shard_map/ppermute | solution.py:231
  146.7 1.0 shard_map.50.refs_1_
  147.7 1.3 collective-permute-start.18
  149.0 1.3 collective-permute-start.19
  150.3 1.3 collective-permute-start.20
  151.6 2.2 %collective-permute-done.18 = f32[4,32,128]{2,1,0:T(8,128)S(1)} collective-permute-done((f32[4,32,128]{2,1,0:T(8,128)S(1)}, f32[4,32,128]{2,1,0:T(8,128)S(1)}, u32[]{:S(2)}, u32[]{:S(2)}) %collective-permute-start.18) | collective-permute-done | bytes 65568 | tf_op jit(solution)/shard_map/ppermute | solution.py:231
  153.8 1.7 collective-permute-done.19
  155.5 1.4 collective-permute-done.20
  156.9 1.0 shard_map.51.refs_1_
  157.9 1.3 collective-permute-start.22
  159.2 1.3 collective-permute-start.21
  160.5 1.3 collective-permute-start.24
  161.8 6.2 %collective-permute-done.22 = f32[4,32,128]{2,1,0:T(8,128)S(1)} collective-permute-done((f32[4,32,128]{2,1,0:T(8,128)S(1)}, f32[4,32,128]{2,1,0:T(8,128)S(1)}, u32[]{:S(2)}, u32[]{:S(2)}) %collective-permute-start.22) | collective-permute-done | bytes 65568 | tf_op jit(solution)/shard_map/ppermute | solution.py:231
  168.0 0.4 collective-permute-done.21
  168.5 2.1 %collective-permute-start.23 = (f32[2,4,32,128]{3,2,1,0:T(8,128)S(1)}, f32[2,4,32,128]{3,2,1,0:T(8,128)S(1)}, u32[]{:S(2)}, u32[]{:S(2)}) collective-permute-start(f32[2,4,32,128]{3,2,1,0:T(8,128)S(1)} %pad_maximum_fusion.6), channel_id=1, source_target_pairs={{0,1},{1,0},{2,3},{3,2},{4,5},{5,4},{6,7},{7,6},{8,9},{9,8},{10,11... | collective-permute-start | bytes 393224 | tf_op jit(solution)/shard_map/ppermute | solution.py:354
  170.6 2.3 %collective-permute-done.24 = f32[4,32,128]{2,1,0:T(8,128)S(1)} collective-permute-done((f32[4,32,128]{2,1,0:T(8,128)S(1)}, f32[4,32,128]{2,1,0:T(8,128)S(1)}, u32[]{:S(2)}, u32[]{:S(2)}) %collective-permute-start.24) | collective-permute-done | bytes 65568 | tf_op jit(solution)/shard_map/ppermute | solution.py:231
  173.0 2.6 %shard_map.52 = f32[4,32,128]{2,1,0:T(8,128)S(1)} custom-call(f32[20,32,128]{2,1,0:T(8,128)S(1)} %broadcast_select_fusion.refs_0_, f32[4,32,128]{2,1,0:T(8,128)S(1)} %shard_map.51.refs_1_, f32[20,32,128]{2,1,0:T(8,128)S(1)} %fusion.7.refs_2_, f32[20,32,128]{2,1,0:T(8,128)S(1)} %get-tuple-element.11.refs_3_), custom_call_target="tpu_custom_call" | custom-call | tf_op jit(solution)/shard_map/pallas_call | solution.py:213
  175.7 28.7 %all_to_all.10 = f32[32,4,128]{2,1,0:T(4,128)S(1)} all-to-all(f32[32,4,128]{2,1,0:T(4,128)S(1)} %copy.13), channel_id=1, replica_groups=mesh['tm'=16,'space'=32] {'space'}, dimensions={0} | all-to-all | bytes 131072 | tf_op jit(solution)/shard_map/all_to_all | solution.py:362
  204.4 1.1 shard_map.53
  (60 shorter events, 0.7 us)
Async XLA Ops:
  0.9 11.4 %collective-permute-start.2 = (f32[128,128]{1,0:T(8,128)S(1)}, f32[128,128]{1,0:T(8,128)S(1)}, u32[]{:S(2)}, u32[]{:S(2)}) collective-permute-start(f32[128,128]{1,0:T(8,128)S(1)} %get-tuple-element.15), channel_id=1, source_target_pairs={{0,1},{1,0},{2,3},{3,2},{4,5},{5,4},{6,7},{7,6},{8,9},{9,8},{10,11... | collective-permute-start | bytes 196616 | tf_op jit(solution)/shard_map/ppermute | solution.py:265
  3.5 8.9 %collective-permute-start.3 = (f32[128,128]{1,0:T(8,128)S(1)}, f32[128,128]{1,0:T(8,128)S(1)}, u32[]{:S(2)}, u32[]{:S(2)}) collective-permute-start(f32[128,128]{1,0:T(8,128)S(1)} %get-tuple-element.16), channel_id=1, source_target_pairs={{1,2},{2,1},{3,4},{4,3},{5,6},{6,5},{7,8},{8,7},{9,10},{10,9},{11,... | collective-permute-start | bytes 196616 | tf_op jit(solution)/shard_map/ppermute | solution.py:262
  6.6 42.2 %collective-permute-start = (f32[1024,128]{1,0:T(8,128)}, f32[1024,128]{1,0:T(8,128)S(1)}, u32[]{:S(2)}, u32[]{:S(2)}) collective-permute-start(f32[1024,128]{1,0:T(8,128)} %bitcast.61), channel_id=1, source_target_pairs={{1,2},{2,1},{3,4},{4,3},{5,6},{6,5},{7,8},{8,7},{9,10},{10,9},{11,... | collective-permute-start | bytes 1572872 | tf_op jit(solution)/shard_map/ppermute | solution.py:262
  9.1 40.6 %collective-permute-start.1 = (f32[1024,128]{1,0:T(8,128)}, f32[1024,128]{1,0:T(8,128)}, u32[]{:S(2)}, u32[]{:S(2)}) collective-permute-start(f32[1024,128]{1,0:T(8,128)} %bitcast.62), channel_id=1, source_target_pairs={{0,1},{1,0},{2,3},{3,2},{4,5},{5,4},{6,7},{7,6},{8,9},{9,8},{10,11... | collective-permute-start | bytes 1572872 | tf_op jit(solution)/shard_map/ppermute | solution.py:265
  11.0 1.0 copy-start
  12.4 26.5 %collective-permute-start.4 = (f32[2,128,128]{2,1,0:T(8,128)S(1)}, f32[2,128,128]{2,1,0:T(8,128)S(1)}, u32[]{:S(2)}, u32[]{:S(2)}) collective-permute-start(f32[2,128,128]{2,1,0:T(8,128)S(1)} %pad_maximum_fusion.5), channel_id=1, source_target_pairs={{0,32},{32,0},{64,96},{96,64},{128,160},{160,128},{192,224},{224,1... | collective-permute-start | bytes 393224 | tf_op jit(solution)/shard_map/ppermute | solution.py:278
  15.0 29.4 %collective-permute-start.13 = (f32[20,128]{1,0:T(8,128)S(1)}, f32[20,128]{1,0:T(8,128)S(1)}, u32[]{:S(2)}, u32[]{:S(2)}) collective-permute-start(f32[20,128]{1,0:T(8,128)S(1)} %get-tuple-element.34), channel_id=1, source_target_pairs={{0,31},{1,0},{2,1},{3,2},{4,3},{5,4},{6,5},{7,6},{8,7},{9,8},{10,9... | collective-permute-start | bytes 30728 | tf_op jit(solution)/shard_map/ppermute | solution.py:318
  30.1 14.4 %collective-permute-start.12 = (f32[20,128]{1,0:T(8,128)S(1)}, f32[20,128]{1,0:T(8,128)S(1)}, u32[]{:S(2)}, u32[]{:S(2)}) collective-permute-start(f32[20,128]{1,0:T(8,128)S(1)} %get-tuple-element.33), channel_id=1, source_target_pairs={{0,0},{1,1},{2,2},{3,3},{4,4},{5,5},{6,6},{7,7},{8,8},{9,9},{10,10... | collective-permute-start | bytes 30728 | tf_op jit(solution)/shard_map/ppermute | solution.py:318
  38.9 2.8 %copy-start.2 = (f32[1,2,512,128]{3,2,1,0:T(8,128)S(1)}, f32[1,2,512,128]{3,2,1,0:T(8,128)}, u32[]{:S(2)}) copy-start(f32[1,2,512,128]{3,2,1,0:T(8,128)} %param.4) | copy-start | bytes 1572868
  39.0 2.6 %copy-start.7 = (s32[1,256]{1,0:T(1,128)S(1)}, s32[1,256]{1,0:T(1,128)}, u32[]{:S(2)}) copy-start(s32[1,256]{1,0:T(1,128)} %param.6) | copy-start | bytes 3076
  39.0 9.7 %collective-permute-start.5 = (f32[2,256,128]{2,1,0:T(8,128)S(1)}, f32[2,256,128]{2,1,0:T(8,128)S(1)}, u32[]{:S(2)}, u32[]{:S(2)}) collective-permute-start(f32[2,256,128]{2,1,0:T(8,128)S(1)} %pad_maximum_fusion.1), channel_id=1, source_target_pairs={{0,64},{32,96},{64,0},{96,32},{128,192},{160,224},{192,128},{224,1... | collective-permute-start | bytes 786440 | tf_op jit(solution)/shard_map/ppermute | solution.py:278
  44.5 14.6 %collective-permute-start.14 = (f32[2,20,128]{2,0,1:T(2,128)S(1)}, f32[2,20,128]{2,0,1:T(2,128)S(1)}, u32[]{:S(2)}, u32[]{:S(2)}) collective-permute-start(f32[2,20,128]{2,0,1:T(2,128)S(1)} %pad_maximum_fusion.9), channel_id=1, source_target_pairs={{0,256},{32,288},{64,320},{96,352},{128,384},{160,416},{192,448},{... | collective-permute-start | bytes 61448 | tf_op jit(solution)/shard_map/ppermute | solution.py:322
  48.8 1.2 copy-start.1
  48.8 0.8 copy-start.3
  50.0 1.0 copy-start.4
  53.5 17.7 %collective-permute-start.6 = (f32[1152,128]{1,0:T(8,128)S(1)}, f32[1152,128]{1,0:T(8,128)}, u32[]{:S(2)}, u32[]{:S(2)}) collective-permute-start(f32[1152,128]{1,0:T(8,128)S(1)} %shard_map.48.refs_3_), channel_id=1, source_target_pairs={{1,2},{2,1},{3,4},{4,3},{5,6},{6,5},{7,8},{8,7},{9,10},{10,9},{11,... | collective-permute-start | bytes 1769480 | tf_op jit(solution)/shard_map/ppermute | solution.py:262
  57.1 14.0 %collective-permute-start.7 = (f32[1152,128]{1,0:T(8,128)S(1)}, f32[1152,128]{1,0:T(8,128)}, u32[]{:S(2)}, u32[]{:S(2)}) collective-permute-start(f32[1152,128]{1,0:T(8,128)S(1)} %shard_map.48.refs_3_), channel_id=1, source_target_pairs={{0,1},{1,0},{2,3},{3,2},{4,5},{5,4},{6,7},{7,6},{8,9},{9,8},{10,11... | collective-permute-start | bytes 1769480 | tf_op jit(solution)/shard_map/ppermute | solution.py:265
  59.1 6.1 %collective-permute-start.15 = (f32[4,20,128]{2,0,1:T(4,128)S(1)}, f32[4,20,128]{2,0,1:T(4,128)S(1)}, u32[]{:S(2)}, u32[]{:S(2)}) collective-permute-start(f32[4,20,128]{2,0,1:T(4,128)S(1)} %pad_maximum_fusion.8), channel_id=1, source_target_pairs={{0,128},{32,160},{64,192},{96,224},{128,0},{160,32},{192,64},{224,... | collective-permute-start | bytes 122888 | tf_op jit(solution)/shard_map/ppermute | solution.py:322
  65.3 0.7 copy-start.5
  66.0 40.4 %collective-permute-start.16 = (f32[8,20,128]{2,0,1:T(8,128)}, f32[8,20,128]{2,0,1:T(8,128)}, u32[]{:S(2)}, u32[]{:S(2)}) collective-permute-start(f32[8,20,128]{2,0,1:T(8,128)} %pad_maximum_fusion.7), channel_id=1, source_target_pairs={{0,64},{32,96},{64,0},{96,32},{128,192},{160,224},{192,128},{224,1... | collective-permute-start | bytes 245768 | tf_op jit(solution)/shard_map/ppermute | solution.py:322
  74.5 31.8 %copy-start.6 = (f32[4,20,128]{2,0,1:T(4,128)S(1)}, f32[4,20,128]{2,0,1:T(4,128)}, u32[]{:S(2)}) copy-start(f32[4,20,128]{2,0,1:T(4,128)} %copy-done.5) | copy-start | bytes 122884
  74.5 52.3 %all-to-all-start = ((f32[32,12,128]{2,1,0:T(8,128)}), f32[32,12,128]{2,1,0:T(8,128)S(1)}, u32[]{:S(2)}, u32[]{:S(2)}) async-start(f32[32,12,128]{2,1,0:T(8,128)} %pad_maximum_fusion.2), calls=%async_computation | async-start | bytes 524288 | tf_op jit(solution)/shard_map/all_to_all | solution.py:248
  107.3 7.5 %collective-permute-start.17 = (f32[16,20,128]{2,0,1:T(8,128)S(1)}, f32[16,20,128]{2,0,1:T(8,128)S(1)}, u32[]{:S(2)}, u32[]{:S(2)}) collective-permute-start(f32[16,20,128]{2,0,1:T(8,128)S(1)} %pad_maximum_fusion.4), channel_id=1, source_target_pairs={{0,32},{32,0},{64,96},{96,64},{128,160},{160,128},{192,224},{224,1... | collective-permute-start | bytes 491528 | tf_op jit(solution)/shard_map/ppermute | solution.py:322
  126.8 19.9 %collective-permute-start.8 = (f32[12,32,128]{2,1,0:T(8,128)S(1)}, f32[12,32,128]{2,1,0:T(8,128)S(1)}, u32[]{:S(2)}, u32[]{:S(2)}) collective-permute-start(f32[12,32,128]{2,1,0:T(8,128)S(1)} %bitcast.69), channel_id=1, source_target_pairs={{128,0},{129,1},{130,2},{131,3},{132,4},{133,5},{134,6},{135,7},{1... | collective-permute-start | bytes 589832 | tf_op jit(solution)/shard_map/ppermute | solution.py:231
  128.2 18.5 %collective-permute-start.9 = (f32[10,32,128]{2,1,0:T(8,128)S(1)}, f32[10,32,128]{2,1,0:T(8,128)S(1)}, u32[]{:S(2)}, u32[]{:S(2)}) collective-permute-start(f32[10,32,128]{2,1,0:T(8,128)S(1)} %slice.51), channel_id=1, source_target_pairs={{96,0},{97,1},{98,2},{99,3},{100,4},{101,5},{102,6},{103,7},{104,8... | collective-permute-start | bytes 491528 | tf_op jit(solution)/shard_map/ppermute | solution.py:231
  130.1 16.6 %collective-permute-start.10 = (f32[8,32,128]{2,1,0:T(8,128)S(1)}, f32[8,32,128]{2,1,0:T(8,128)S(1)}, u32[]{:S(2)}, u32[]{:S(2)}) collective-permute-start(f32[8,32,128]{2,1,0:T(8,128)S(1)} %slice.52), channel_id=1, source_target_pairs={{64,0},{65,1},{66,2},{67,3},{68,4},{69,5},{70,6},{71,7},{72,8},{73... | collective-permute-start | bytes 393224 | tf_op jit(solution)/shard_map/ppermute | solution.py:231
  132.1 14.6 %collective-permute-start.11 = (f32[6,32,128]{2,1,0:T(8,128)S(1)}, f32[6,32,128]{2,1,0:T(8,128)S(1)}, u32[]{:S(2)}, u32[]{:S(2)}) collective-permute-start(f32[6,32,128]{2,1,0:T(8,128)S(1)} %slice.53), channel_id=1, source_target_pairs={{32,0},{33,1},{34,2},{35,3},{36,4},{37,5},{38,6},{39,7},{40,8},{41... | collective-permute-start | bytes 294920 | tf_op jit(solution)/shard_map/ppermute | solution.py:231
  147.7 6.1 %collective-permute-start.18 = (f32[4,32,128]{2,1,0:T(8,128)S(1)}, f32[4,32,128]{2,1,0:T(8,128)S(1)}, u32[]{:S(2)}, u32[]{:S(2)}) collective-permute-start(f32[4,32,128]{2,1,0:T(8,128)S(1)} %shard_map.50.refs_1_), channel_id=1, source_target_pairs={{128,1},{129,0},{130,3},{131,2},{132,5},{133,4},{134,7},{135,6},{1... | collective-permute-start | bytes 196616 | tf_op jit(solution)/shard_map/ppermute | solution.py:231
  149.0 6.5 %collective-permute-start.19 = (f32[4,32,128]{2,1,0:T(8,128)S(1)}, f32[4,32,128]{2,1,0:T(8,128)S(1)}, u32[]{:S(2)}, u32[]{:S(2)}) collective-permute-start(f32[4,32,128]{2,1,0:T(8,128)S(1)} %shard_map.50.refs_1_), channel_id=1, source_target_pairs={{129,2},{130,1},{131,4},{132,3},{133,6},{134,5},{135,8},{136,7},{1... | collective-permute-start | bytes 196616 | tf_op jit(solution)/shard_map/ppermute | solution.py:231
  150.3 6.6 %collective-permute-start.20 = (f32[4,32,128]{2,1,0:T(8,128)S(1)}, f32[4,32,128]{2,1,0:T(8,128)S(1)}, u32[]{:S(2)}, u32[]{:S(2)}) collective-permute-start(f32[4,32,128]{2,1,0:T(8,128)S(1)} %shard_map.50.refs_1_), channel_id=1, source_target_pairs={{128,0},{129,1},{130,2},{131,3},{132,4},{133,5},{134,6},{135,7},{1... | collective-permute-start | bytes 196616 | tf_op jit(solution)/shard_map/ppermute | solution.py:231
  157.9 10.1 %collective-permute-start.22 = (f32[4,32,128]{2,1,0:T(8,128)S(1)}, f32[4,32,128]{2,1,0:T(8,128)S(1)}, u32[]{:S(2)}, u32[]{:S(2)}) collective-permute-start(f32[4,32,128]{2,1,0:T(8,128)S(1)} %shard_map.51.refs_1_), channel_id=1, source_target_pairs={{257,2},{258,1},{259,4},{260,3},{261,6},{262,5},{263,8},{264,7},{2... | collective-permute-start | bytes 196616 | tf_op jit(solution)/shard_map/ppermute | solution.py:231
  159.2 9.2 %collective-permute-start.21 = (f32[4,32,128]{2,1,0:T(8,128)S(1)}, f32[4,32,128]{2,1,0:T(8,128)S(1)}, u32[]{:S(2)}, u32[]{:S(2)}) collective-permute-start(f32[4,32,128]{2,1,0:T(8,128)S(1)} %shard_map.51.refs_1_), channel_id=1, source_target_pairs={{256,0},{257,1},{258,2},{259,3},{260,4},{261,5},{262,6},{263,7},{2... | collective-permute-start | bytes 196616 | tf_op jit(solution)/shard_map/ppermute | solution.py:231
  160.5 12.4 %collective-permute-start.24 = (f32[4,32,128]{2,1,0:T(8,128)S(1)}, f32[4,32,128]{2,1,0:T(8,128)S(1)}, u32[]{:S(2)}, u32[]{:S(2)}) collective-permute-start(f32[4,32,128]{2,1,0:T(8,128)S(1)} %shard_map.51.refs_1_), channel_id=1, source_target_pairs={{256,2},{258,4},{260,6},{262,8},{264,10},{266,12},{268,14},{270,16... | collective-permute-start | bytes 196616 | tf_op jit(solution)/shard_map/ppermute | solution.py:231
  168.5 4.4 %collective-permute-start.23 = (f32[2,4,32,128]{3,2,1,0:T(8,128)S(1)}, f32[2,4,32,128]{3,2,1,0:T(8,128)S(1)}, u32[]{:S(2)}, u32[]{:S(2)}) collective-permute-start(f32[2,4,32,128]{3,2,1,0:T(8,128)S(1)} %pad_maximum_fusion.6), channel_id=1, source_target_pairs={{0,1},{1,0},{2,3},{3,2},{4,5},{5,4},{6,7},{7,6},{8,9},{9,8},{10,11... | collective-permute-start | bytes 393224 | tf_op jit(solution)/shard_map/ppermute | solution.py:354

commit v8 on v7

--- a/solution.py
+++ b/solution.py
@@ -294,6 +294,31 @@
 
     slab_rows = row_count * width_y
     start_rows = start_field.reshape(slab_rows, width_z)
+    tall = jnp.pad(coarse_cond, ((2 * BLOCK, 2 * BLOCK), (0, 0)))
+    tall, share = lax.optimization_barrier((tall, share))
+    shares = []
+    for i in range(2):
+        at = (slab - 2 * (ring * 4 + slice_index // 4) - i) % SLABS
+        window = lax.dynamic_slice_in_dim(tall, at * BLOCK, 5 * BLOCK, axis=0)
+        pairs = []
+        for n in range(SLICES):
+            away = 2 * (n % 4 * 4 + n // 4) + i
+            pairs += [(n * SLABS + j, n * SLABS + (j - away) % SLABS) for j in range(SLABS)]
+        shares.append(lax.ppermute(window, ("tm", "space"), pairs))
+    gathered = jnp.stack(shares)
+    for unit in (4, 1):
+        count = gathered.shape[0]
+        parts = [gathered]
+        for k in (1, 2, 3):
+            pairs = [(n - n // unit % 4 * unit + (n // unit + k) % 4 * unit, n) for n in range(SLICES)]
+            parts.append(lax.ppermute(gathered, "tm", pairs))
+        first = (4 - slice_index // unit % 4) % 4
+        gathered = lax.dynamic_slice_in_dim(jnp.concatenate(parts + parts[:3]), first * count, 4 * count)
+    turned = lax.dynamic_slice_in_dim(
+        jnp.concatenate([gathered, gathered]), (SLABS - slab) % SLABS, SLABS, axis=0
+    )
+    row_cond = jnp.transpose(turned, (1, 0, 2))
+
     around = (share, cond, wide_source, coarse_start, plane_keep, plane_spread)
     across, along = across_chips(start_rows), in_chip(start_rows)
     sent, = step_call(
@@ -304,27 +329,6 @@
         second_step_kernel, [(slab_rows, 128), (PLANE, 128), (PLANE, 128)], place, across, along, sent, *around
     )
     field_now = field_now.reshape(start_field.shape)
-
-    tall = jnp.pad(coarse_cond, ((2 * BLOCK, 2 * BLOCK), (0, 0)))
-    backwards = sum((slice_index // bit) % 2 * (SLICES // 2 // bit) for bit in (1, 2, 4, 8))
-    shares = []
-    for i in range(2):
-        at = (slab - 2 * backwards - i) % SLABS
-        window = lax.dynamic_slice_in_dim(tall, at * BLOCK, 5 * BLOCK, axis=0)
-        pairs = []
-        for n in range(SLICES):
-            turned = sum((n // bit) % 2 * (SLICES // 2 // bit) for bit in (1, 2, 4, 8))
-            pairs += [(n * SLABS + j, n * SLABS + (j - 2 * turned - i) % SLABS) for j in range(SLABS)]
-        shares.append(lax.ppermute(window, ("tm", "space"), pairs))
-    gathered = jnp.stack(shares)
-    for bit in (8, 4, 2, 1):
-        upper = (slice_index // bit) % 2 == 1
-        other = lax.ppermute(gathered, "tm", [(n, n ^ bit) for n in range(SLICES)])
-        gathered = jnp.concatenate([jnp.where(upper, other, gathered), jnp.where(upper, gathered, other)])
-    turned = lax.dynamic_slice_in_dim(
-        jnp.concatenate([gathered, gathered]), (SLABS - slab) % SLABS, SLABS, axis=0
-    )
-    row_cond = jnp.transpose(turned, (1, 0, 2))
 
     rows = to_rows(windows(term, 1))
     later = [(i, i) for i in range(SLABS)]

time: 207 us -> 230 us (1.11)
  starting transfers between devices: 107 us -> 120 us
  local copies, waits for them, and re-layouts: 3.56 us -> 9.8 us
  waiting for transfers between devices: 47.3 us -> 51.2 us
  blocking collectives: 28.7 us -> 31.7 us
    all_to_all x1, starting transfers between devices: 31.8 us -> 18 us  [to_rows(): arrived = lax.all_to_all(parts, 'space', 0, 0)]
    ppermute x4 -> x6, starting transfers between devices: 14.3 us -> 27.3 us  [per_device(): parts.append(lax.ppermute(gathered, 'tm', pairs))]
    ppermute x2, starting transfers between devices: 23.8 us -> 29.9 us  [per_device(): shares.append(lax.ppermute(window, ('tm', 'space'), pairs))]
    unnamed x22 -> x26, local copies, waits for them, and re-layouts: 3.3 us -> 8.47 us
    ppermute x2, starting transfers between devices: 5.06 us -> 9.97 us  [per_device(): other = lax.ppermute(share, 'tm', [(n, n ^ bit) for n in range(SLICES)])]
    ppermute x2, waiting for transfers between devices: 1.94 us -> 6.72 us  [per_device(): other = lax.ppermute(share, 'tm', [(n, n ^ bit) for n in range(SLICES)])]
    all_to_all x1, waiting for transfers between devices: 11.8 us -> 15.6 us  [to_rows(): arrived = lax.all_to_all(parts, 'space', 0, 0)]
    ppermute x4 -> x6, waiting for transfers between devices: 6.74 us -> 3.52 us  [per_device(): parts.append(lax.ppermute(gathered, 'tm', pairs))]
  transfers between devices with their start and end apart: 26 -> 28, of which waited for: 11 -> 12; matrix products, arithmetic and copies ran while one was open for 3% -> 4% of each run, Pallas kernels for 3% -> 1%
where the time goes in v8:
time: 230 us; the launch traced here: 229 us
  starting transfers between devices  120 us (52%)
  waiting for transfers between devices  51.2 us (22%)
  blocking collectives  31.7 us (14%)
  Pallas kernels  11.2 us (5%)
  local copies, waits for them, and re-layouts  9.8 us (4%)
  other arithmetic  4.52 us (2%)
    all_to_all x1, blocking collectives, per_device(): back = lax.all_to_all(jnp.transpose(total, (1, 0, 2)), 'space', 0, 0)  31.7 us
    ppermute x2, starting transfers between devices, per_device(): shares.append(lax.ppermute(window, ('tm', 'space'), pairs))  29.9 us
    ppermute x6, starting transfers between devices, per_device(): parts.append(lax.ppermute(gathered, 'tm', pairs))  27.3 us
    ppermute x10, waiting for transfers between devices, from_later(): return lax.ppermute(value, ('tm', 'space'), both)  24.5 us
    all_to_all x1, starting transfers between devices, to_rows(): arrived = lax.all_to_all(parts, 'space', 0, 0)  18 us
    ppermute x10, starting transfers between devices, from_later(): return lax.ppermute(value, ('tm', 'space'), both)  16.2 us
    all_to_all x1, waiting for transfers between devices, to_rows(): arrived = lax.all_to_all(parts, 'space', 0, 0)  15.6 us
    ppermute x2, starting transfers between devices, per_device(): other = lax.ppermute(share, 'tm', [(n, n ^ bit) for n in range(SLICES)])  9.97 us
  transfers between devices with their start and end apart: 28, of which 12 were waited for; matrix products, arithmetic and copies ran while one was open for 4% of the time, Pallas kernels for 1%

profile of v8, /device:TPU:7, one launch (start us, length us, event | category | flops | bytes accessed | tf_op | source)
XLA Modules:
  0.0 228.8 jit_solution(9195324336193416618)
XLA Ops:
  0.0 0.9 select_bitcast_fusion.3
  0.9 2.6 %collective-permute-start.2 = (f32[128,128]{1,0:T(8,128)S(1)}, f32[128,128]{1,0:T(8,128)S(1)}, u32[]{:S(2)}, u32[]{:S(2)}) collective-permute-start(f32[128,128]{1,0:T(8,128)S(1)} %get-tuple-element.19), channel_id=1, source_target_pairs={{0,1},{1,0},{2,3},{3,2},{4,5},{5,4},{6,7},{7,6},{8,9},{9,8},{10,11... | collective-permute-start | bytes 196616 | tf_op jit(solution)/shard_map/ppermute | solution.py:265
  3.5 3.1 %collective-permute-start.3 = (f32[128,128]{1,0:T(8,128)S(1)}, f32[128,128]{1,0:T(8,128)S(1)}, u32[]{:S(2)}, u32[]{:S(2)}) collective-permute-start(f32[128,128]{1,0:T(8,128)S(1)} %get-tuple-element.20), channel_id=1, source_target_pairs={{1,2},{2,1},{3,4},{4,3},{5,6},{6,5},{7,8},{8,7},{9,10},{10,9},{11,... | collective-permute-start | bytes 196616 | tf_op jit(solution)/shard_map/ppermute | solution.py:262
  6.6 2.5 %collective-permute-start = (f32[1024,128]{1,0:T(8,128)}, f32[1024,128]{1,0:T(8,128)S(1)}, u32[]{:S(2)}, u32[]{:S(2)}) collective-permute-start(f32[1024,128]{1,0:T(8,128)} %bitcast.64), channel_id=1, source_target_pairs={{1,2},{2,1},{3,4},{4,3},{5,6},{6,5},{7,8},{8,7},{9,10},{10,9},{11,... | collective-permute-start | bytes 1572872 | tf_op jit(solution)/shard_map/ppermute | solution.py:262
  9.1 1.9 collective-permute-start.1
  11.0 1.0 copy-done
  12.1 0.3 shard_map.46
  12.4 2.5 %collective-permute-start.4 = (f32[2,128,128]{2,1,0:T(8,128)S(1)}, f32[2,128,128]{2,1,0:T(8,128)S(1)}, u32[]{:S(2)}, u32[]{:S(2)}) collective-permute-start(f32[2,128,128]{2,1,0:T(8,128)S(1)} %pad_maximum_fusion.4), channel_id=1, source_target_pairs={{0,32},{32,0},{64,96},{96,64},{128,160},{160,128},{192,224},{224,1... | collective-permute-start | bytes 393224 | tf_op jit(solution)/shard_map/ppermute | solution.py:278
  14.9 4.0 %collective-permute-done.4 = f32[2,128,128]{2,1,0:T(8,128)S(1)} collective-permute-done((f32[2,128,128]{2,1,0:T(8,128)S(1)}, f32[2,128,128]{2,1,0:T(8,128)S(1)}, u32[]{:S(2)}, u32[]{:S(2)}) %collective-permute-start.4) | collective-permute-done | bytes 131104 | tf_op jit(solution)/shard_map/ppermute | solution.py:278
  18.9 7.5 %collective-permute-start.5 = (f32[2,256,128]{2,1,0:T(8,128)S(1)}, f32[2,256,128]{2,1,0:T(8,128)S(1)}, u32[]{:S(2)}, u32[]{:S(2)}) collective-permute-start(f32[2,256,128]{2,1,0:T(8,128)S(1)} %pad_maximum_fusion.1), channel_id=1, source_target_pairs={{0,64},{32,96},{64,0},{96,32},{128,192},{160,224},{192,128},{224,1... | collective-permute-start | bytes 786440 | tf_op jit(solution)/shard_map/ppermute | solution.py:278
  26.6 0.3 shard_map.47.refs_7_
  26.9 2.4 %scatter_custom_fusion = f32[262144]{0:T(1024)S(1)} fusion(s32[256]{0:T(256)S(1)} %bitcast.80, f32[256]{0:T(256)} %bitcast.81, f32[]{:T(128)} %constant.175.clone.1), kind=kCustom, calls=%fused_computation.4 | custom fusion | flops 256 | bytes 1049088 | tf_op jit(solution)/shard_map/scatter-add | solution.py:285
  29.3 2.8 %collective-permute-done.5 = f32[2,256,128]{2,1,0:T(8,128)S(1)} collective-permute-done((f32[2,256,128]{2,1,0:T(8,128)S(1)}, f32[2,256,128]{2,1,0:T(8,128)S(1)}, u32[]{:S(2)}, u32[]{:S(2)}) %collective-permute-start.5) | collective-permute-done | bytes 262176 | tf_op jit(solution)/shard_map/ppermute | solution.py:278
  32.2 0.8 copy-done.3
  33.0 0.4 copy-done.1
  33.4 1.0 copy-done.4
  34.4 2.4 %shard_map.48.refs_3_ = f32[1152,128]{1,0:T(8,128)S(1)} custom-call(s32[4]{0:T(128)S(1)} %add_convert_fusion.refs_0_, f32[1024,128]{1,0:T(8,128)S(1)} %copy-done.4, f32[1024,128]{1,0:T(8,128)} %collective-permute-done.1.refs_2_, f32[1024,128]{1,0:T(8,128)S(1)} %bitcast.67, f32[2,512,128]{2,1,0:T(8,128)S(1)} %pad_maximum_fusion.refs_4_, ...), custom_call_target="tpu_custom_call" | custom-call | tf_op jit(solution)/shard_map/pallas_call | solution.py:154
  36.8 4.0 %collective-permute-start.6 = (f32[1152,128]{1,0:T(8,128)S(1)}, f32[1152,128]{1,0:T(8,128)}, u32[]{:S(2)}, u32[]{:S(2)}) collective-permute-start(f32[1152,128]{1,0:T(8,128)S(1)} %shard_map.48.refs_3_), channel_id=1, source_target_pairs={{1,2},{2,1},{3,4},{4,3},{5,6},{6,5},{7,8},{8,7},{9,10},{10,9},{11,... | collective-permute-start | bytes 1769480 | tf_op jit(solution)/shard_map/ppermute | solution.py:262
  40.8 1.9 collective-permute-start.7
  42.8 20.9 %collective-permute-start.12 = (f32[20,128]{1,0:T(8,128)S(1)}, f32[20,128]{1,0:T(8,128)S(1)}, u32[]{:S(2)}, u32[]{:S(2)}) collective-permute-start(f32[20,128]{1,0:T(8,128)S(1)} %get-tuple-element.34), channel_id=1, source_target_pairs={{0,0},{1,1},{2,2},{3,3},{4,4},{5,5},{6,6},{7,7},{8,8},{9,9},{10,10... | collective-permute-start | bytes 30728 | tf_op jit(solution)/shard_map/ppermute | solution.py:307
  63.8 9.0 %collective-permute-start.13 = (f32[20,128]{1,0:T(8,128)S(1)}, f32[20,128]{1,0:T(8,128)S(1)}, u32[]{:S(2)}, u32[]{:S(2)}) collective-permute-start(f32[20,128]{1,0:T(8,128)S(1)} %get-tuple-element.33), channel_id=1, source_target_pairs={{0,31},{1,0},{2,1},{3,2},{4,3},{5,4},{6,5},{7,6},{8,7},{9,8},{10,9... | collective-permute-start | bytes 30728 | tf_op jit(solution)/shard_map/ppermute | solution.py:307
  72.8 0.8 collective-permute-done.13
  73.6 1.9 collective-permute-start.14
  75.6 1.9 collective-permute-start.15
  77.5 3.4 %collective-permute-start.16 = (f32[2,20,128]{2,0,1:T(2,128)S(1)}, f32[2,20,128]{2,0,1:T(2,128)S(1)}, u32[]{:S(2)}, u32[]{:S(2)}) collective-permute-start(f32[2,20,128]{2,0,1:T(2,128)S(1)} %pad_maximum_fusion.6), channel_id=1, source_target_pairs={{384,0},{416,32},{448,64},{480,96},{0,128},{32,160},{64,192},{96,2... | collective-permute-start | bytes 61448 | tf_op jit(solution)/shard_map/ppermute | solution.py:314
  81.0 0.7 collective-permute-done.14
  81.7 2.8 %collective-permute-done.16 = f32[2,20,128]{2,0,1:T(2,128)S(1)} collective-permute-done((f32[2,20,128]{2,0,1:T(2,128)S(1)}, f32[2,20,128]{2,0,1:T(2,128)S(1)}, u32[]{:S(2)}, u32[]{:S(2)}) %collective-permute-start.16) | collective-permute-done | bytes 20512 | tf_op jit(solution)/shard_map/ppermute | solution.py:314
  84.6 0.7 constant_dynamic-update-slice_fusion.6
  85.3 13.9 %collective-permute-start.17 = (f32[8,20,128]{2,0,1:T(8,128)}, f32[8,20,128]{2,0,1:T(8,128)}, u32[]{:S(2)}, u32[]{:S(2)}) collective-permute-start(f32[8,20,128]{2,0,1:T(8,128)} %get-tuple-element.16), channel_id=1, source_target_pairs={{32,0},{64,32},{96,64},{0,96},{160,128},{192,160},{224,192},{128,2... | collective-permute-start | bytes 245768 | tf_op jit(solution)/shard_map/ppermute | solution.py:314
  99.2 1.9 collective-permute-start.18
  101.1 4.3 %collective-permute-start.19 = (f32[8,20,128]{2,0,1:T(8,128)}, f32[8,20,128]{2,0,1:T(8,128)}, u32[]{:S(2)}, u32[]{:S(2)}) collective-permute-start(f32[8,20,128]{2,0,1:T(8,128)} %get-tuple-element.16), channel_id=1, source_target_pairs={{96,0},{0,32},{32,64},{64,96},{224,128},{128,160},{160,192},{192,2... | collective-permute-start | bytes 245768 | tf_op jit(solution)/shard_map/ppermute | solution.py:314
  105.5 2.5 %shard_map.49 = (f32[1024,128]{1,0:T(8,128)S(1)}, f32[128,128]{1,0:T(8,128)S(1)}, f32[128,128]{1,0:T(8,128)S(1)}) custom-call(s32[4]{0:T(128)S(1)} %add_convert_fusion.refs_0_, f32[1152,128]{1,0:T(8,128)} %collective-permute-done.6.refs_1_, f32[1152,128]{1,0:T(8,128)} %collective-permute-done.7.refs_2_, f32[1152,128]{1,0:T(8,128)S(1)} %shard_map.48.refs_3_, ...), custom_call_target="tpu_custom_call" | custom-call | tf_op jit(solution)/shard_map/pallas_call | solution.py:154
  108.1 0.8 pad_maximum_fusion.2
  108.8 18.0 %all-to-all-start = ((f32[32,12,128]{2,1,0:T(8,128)}), f32[32,12,128]{2,1,0:T(8,128)S(1)}, u32[]{:S(2)}, u32[]{:S(2)}) async-start(f32[32,12,128]{2,1,0:T(8,128)} %pad_maximum_fusion.2), calls=%async_computation | async-start | bytes 524288 | tf_op jit(solution)/shard_map/all_to_all | solution.py:248
  126.9 0.9 constant_dynamic-update-slice_fusion.5
  127.8 0.9 constant_dynamic-update-slice_fusion.4
  128.7 0.9 constant_dynamic-update-slice_fusion.3
  129.6 0.9 constant_dynamic-update-slice_fusion.2
  130.5 0.9 constant_dynamic-update-slice_fusion.1
  131.4 0.9 constant_dynamic-update-slice_fusion
  132.3 15.6 %all-to-all-done = f32[32,12,128]{2,1,0:T(8,128)S(1)} async-done(((f32[32,12,128]{2,1,0:T(8,128)}), f32[32,12,128]{2,1,0:T(8,128)S(1)}, u32[]{:S(2)}, u32[]{:S(2)}) %all-to-all-start) | async-done | bytes 196640 | tf_op jit(solution)/shard_map/all_to_all | solution.py:248
  147.9 1.3 collective-permute-start.8
  149.3 2.6 %collective-permute-start.9 = (f32[10,32,128]{2,1,0:T(8,128)S(1)}, f32[10,32,128]{2,1,0:T(8,128)S(1)}, u32[]{:S(2)}, u32[]{:S(2)}) collective-permute-start(f32[10,32,128]{2,1,0:T(8,128)S(1)} %slice.51), channel_id=1, source_target_pairs={{96,0},{97,1},{98,2},{99,3},{100,4},{101,5},{102,6},{103,7},{104,8... | collective-permute-start | bytes 491528 | tf_op jit(solution)/shard_map/ppermute | solution.py:231
  151.9 2.7 %collective-permute-start.10 = (f32[8,32,128]{2,1,0:T(8,128)S(1)}, f32[8,32,128]{2,1,0:T(8,128)S(1)}, u32[]{:S(2)}, u32[]{:S(2)}) collective-permute-start(f32[8,32,128]{2,1,0:T(8,128)S(1)} %slice.52), channel_id=1, source_target_pairs={{64,0},{65,1},{66,2},{67,3},{68,4},{69,5},{70,6},{71,7},{72,8},{73... | collective-permute-start | bytes 393224 | tf_op jit(solution)/shard_map/ppermute | solution.py:231
  154.6 1.9 collective-permute-start.11
  156.5 0.2 fusion.4
  156.7 10.0 %collective-permute-done.11.c1_ref = f32[6,32,128]{2,1,0:T(8,128)S(1)} collective-permute-done((f32[6,32,128]{2,1,0:T(8,128)S(1)}, f32[6,32,128]{2,1,0:T(8,128)S(1)}, u32[]{:S(2)}, u32[]{:S(2)}) %collective-permute-start.11) | collective-permute-done | bytes 98336 | tf_op jit(solution)/shard_map/ppermute | solution.py:231
  166.7 1.0 shard_map.50.refs_1_
  167.7 1.3 collective-permute-start.20
  169.0 1.3 collective-permute-start.21
  170.3 1.3 collective-permute-start.22
  171.6 2.2 collective-permute-done.20
  173.8 1.8 collective-permute-done.21
  175.6 1.3 collective-permute-done.22
  176.9 1.0 shard_map.51.refs_1_
  177.9 1.3 collective-permute-start.24
  179.2 1.3 collective-permute-start.23
  180.5 1.3 collective-permute-start.26
  181.8 6.3 %collective-permute-done.24 = f32[4,32,128]{2,1,0:T(8,128)S(1)} collective-permute-done((f32[4,32,128]{2,1,0:T(8,128)S(1)}, f32[4,32,128]{2,1,0:T(8,128)S(1)}, u32[]{:S(2)}, u32[]{:S(2)}) %collective-permute-start.24) | collective-permute-done | bytes 65568 | tf_op jit(solution)/shard_map/ppermute | solution.py:231
  188.1 2.1 collective-permute-start.25
  190.2 3.0 %collective-permute-done.26 = f32[4,32,128]{2,1,0:T(8,128)S(1)} collective-permute-done((f32[4,32,128]{2,1,0:T(8,128)S(1)}, f32[4,32,128]{2,1,0:T(8,128)S(1)}, u32[]{:S(2)}, u32[]{:S(2)}) %collective-permute-start.26) | collective-permute-done | bytes 65568 | tf_op jit(solution)/shard_map/ppermute | solution.py:231
  193.3 2.6 %shard_map.52 = f32[4,32,128]{2,1,0:T(8,128)S(1)} custom-call(f32[20,32,128]{2,1,0:T(8,128)S(1)} %broadcast_select_fusion.refs_0_, f32[4,32,128]{2,1,0:T(8,128)S(1)} %shard_map.51.refs_1_, f32[20,32,128]{2,1,0:T(8,128)S(1)} %get-tuple-element.22.refs_2_, f32[20,32,128]{2,1,0:T(8,128)S(1)} %get-tuple-element.21.refs_3_), custom_call_target="tpu_custom_call" | custom-call | tf_op jit(solution)/shard_map/pallas_call | solution.py:213
  196.0 31.7 %all_to_all.10 = f32[32,4,128]{2,1,0:T(4,128)S(1)} all-to-all(f32[32,4,128]{2,1,0:T(4,128)S(1)} %copy.19), channel_id=1, replica_groups=mesh['tm'=16,'space'=32] {'space'}, dimensions={0} | all-to-all | bytes 131072 | tf_op jit(solution)/shard_map/all_to_all | solution.py:366
  227.7 1.1 shard_map.53
  (64 shorter events, 0.9 us)
Async XLA Ops:
  0.9 11.5 %collective-permute-start.2 = (f32[128,128]{1,0:T(8,128)S(1)}, f32[128,128]{1,0:T(8,128)S(1)}, u32[]{:S(2)}, u32[]{:S(2)}) collective-permute-start(f32[128,128]{1,0:T(8,128)S(1)} %get-tuple-element.19), channel_id=1, source_target_pairs={{0,1},{1,0},{2,3},{3,2},{4,5},{5,4},{6,7},{7,6},{8,9},{9,8},{10,11... | collective-permute-start | bytes 196616 | tf_op jit(solution)/shard_map/ppermute | solution.py:265
  3.5 8.9 %collective-permute-start.3 = (f32[128,128]{1,0:T(8,128)S(1)}, f32[128,128]{1,0:T(8,128)S(1)}, u32[]{:S(2)}, u32[]{:S(2)}) collective-permute-start(f32[128,128]{1,0:T(8,128)S(1)} %get-tuple-element.20), channel_id=1, source_target_pairs={{1,2},{2,1},{3,4},{4,3},{5,6},{6,5},{7,8},{8,7},{9,10},{10,9},{11,... | collective-permute-start | bytes 196616 | tf_op jit(solution)/shard_map/ppermute | solution.py:262
  6.6 25.6 %collective-permute-start = (f32[1024,128]{1,0:T(8,128)}, f32[1024,128]{1,0:T(8,128)S(1)}, u32[]{:S(2)}, u32[]{:S(2)}) collective-permute-start(f32[1024,128]{1,0:T(8,128)} %bitcast.64), channel_id=1, source_target_pairs={{1,2},{2,1},{3,4},{4,3},{5,6},{6,5},{7,8},{8,7},{9,10},{10,9},{11,... | collective-permute-start | bytes 1572872 | tf_op jit(solution)/shard_map/ppermute | solution.py:262
  9.1 23.9 %collective-permute-start.1 = (f32[1024,128]{1,0:T(8,128)}, f32[1024,128]{1,0:T(8,128)}, u32[]{:S(2)}, u32[]{:S(2)}) collective-permute-start(f32[1024,128]{1,0:T(8,128)} %bitcast.65), channel_id=1, source_target_pairs={{0,1},{1,0},{2,3},{3,2},{4,5},{5,4},{6,7},{7,6},{8,9},{9,8},{10,11... | collective-permute-start | bytes 1572872 | tf_op jit(solution)/shard_map/ppermute | solution.py:265
  11.0 1.0 copy-start
  12.4 6.5 %collective-permute-start.4 = (f32[2,128,128]{2,1,0:T(8,128)S(1)}, f32[2,128,128]{2,1,0:T(8,128)S(1)}, u32[]{:S(2)}, u32[]{:S(2)}) collective-permute-start(f32[2,128,128]{2,1,0:T(8,128)S(1)} %pad_maximum_fusion.4), channel_id=1, source_target_pairs={{0,32},{32,0},{64,96},{96,64},{128,160},{160,128},{192,224},{224,1... | collective-permute-start | bytes 393224 | tf_op jit(solution)/shard_map/ppermute | solution.py:278
  14.9 11.7 %copy-start.2 = (f32[1,2,512,128]{3,2,1,0:T(8,128)S(1)}, f32[1,2,512,128]{3,2,1,0:T(8,128)}, u32[]{:S(2)}) copy-start(f32[1,2,512,128]{3,2,1,0:T(8,128)} %param.4) | copy-start | bytes 1572868
  18.9 7.6 %copy-start.6 = (s32[1,256]{1,0:T(1,128)S(1)}, s32[1,256]{1,0:T(1,128)}, u32[]{:S(2)}) copy-start(s32[1,256]{1,0:T(1,128)} %param.6) | copy-start | bytes 3076
  18.9 13.1 %collective-permute-start.5 = (f32[2,256,128]{2,1,0:T(8,128)S(1)}, f32[2,256,128]{2,1,0:T(8,128)S(1)}, u32[]{:S(2)}, u32[]{:S(2)}) collective-permute-start(f32[2,256,128]{2,1,0:T(8,128)S(1)} %pad_maximum_fusion.1), channel_id=1, source_target_pairs={{0,64},{32,96},{64,0},{96,32},{128,192},{160,224},{192,128},{224,1... | collective-permute-start | bytes 786440 | tf_op jit(solution)/shard_map/ppermute | solution.py:278
  32.1 1.2 copy-start.1
  32.2 0.8 copy-start.3
  33.4 1.0 copy-start.4
  36.8 68.6 %collective-permute-start.6 = (f32[1152,128]{1,0:T(8,128)S(1)}, f32[1152,128]{1,0:T(8,128)}, u32[]{:S(2)}, u32[]{:S(2)}) collective-permute-start(f32[1152,128]{1,0:T(8,128)S(1)} %shard_map.48.refs_3_), channel_id=1, source_target_pairs={{1,2},{2,1},{3,4},{4,3},{5,6},{6,5},{7,8},{8,7},{9,10},{10,9},{11,... | collective-permute-start | bytes 1769480 | tf_op jit(solution)/shard_map/ppermute | solution.py:262
  40.8 64.6 %collective-permute-start.7 = (f32[1152,128]{1,0:T(8,128)S(1)}, f32[1152,128]{1,0:T(8,128)}, u32[]{:S(2)}, u32[]{:S(2)}) collective-permute-start(f32[1152,128]{1,0:T(8,128)S(1)} %shard_map.48.refs_3_), channel_id=1, source_target_pairs={{0,1},{1,0},{2,3},{3,2},{4,5},{5,4},{6,7},{7,6},{8,9},{9,8},{10,11... | collective-permute-start | bytes 1769480 | tf_op jit(solution)/shard_map/ppermute | solution.py:265
  42.8 30.0 %collective-permute-start.12 = (f32[20,128]{1,0:T(8,128)S(1)}, f32[20,128]{1,0:T(8,128)S(1)}, u32[]{:S(2)}, u32[]{:S(2)}) collective-permute-start(f32[20,128]{1,0:T(8,128)S(1)} %get-tuple-element.34), channel_id=1, source_target_pairs={{0,0},{1,1},{2,2},{3,3},{4,4},{5,5},{6,6},{7,7},{8,8},{9,9},{10,10... | collective-permute-start | bytes 30728 | tf_op jit(solution)/shard_map/ppermute | solution.py:307
  63.8 9.8 %collective-permute-start.13 = (f32[20,128]{1,0:T(8,128)S(1)}, f32[20,128]{1,0:T(8,128)S(1)}, u32[]{:S(2)}, u32[]{:S(2)}) collective-permute-start(f32[20,128]{1,0:T(8,128)S(1)} %get-tuple-element.33), channel_id=1, source_target_pairs={{0,31},{1,0},{2,1},{3,2},{4,3},{5,4},{6,5},{7,6},{8,7},{9,8},{10,9... | collective-permute-start | bytes 30728 | tf_op jit(solution)/shard_map/ppermute | solution.py:307
  73.6 8.0 %collective-permute-start.14 = (f32[2,20,128]{2,0,1:T(2,128)S(1)}, f32[2,20,128]{2,0,1:T(2,128)S(1)}, u32[]{:S(2)}, u32[]{:S(2)}) collective-permute-start(f32[2,20,128]{2,0,1:T(2,128)S(1)} %pad_maximum_fusion.6), channel_id=1, source_target_pairs={{128,0},{160,32},{192,64},{224,96},{256,128},{288,160},{320,192},{... | collective-permute-start | bytes 61448 | tf_op jit(solution)/shard_map/ppermute | solution.py:314
  75.6 6.1 %collective-permute-start.15 = (f32[2,20,128]{2,0,1:T(2,128)S(1)}, f32[2,20,128]{2,0,1:T(2,128)S(1)}, u32[]{:S(2)}, u32[]{:S(2)}) collective-permute-start(f32[2,20,128]{2,0,1:T(2,128)S(1)} %pad_maximum_fusion.6), channel_id=1, source_target_pairs={{256,0},{288,32},{320,64},{352,96},{384,128},{416,160},{448,192},{... | collective-permute-start | bytes 61448 | tf_op jit(solution)/shard_map/ppermute | solution.py:314
  77.5 7.0 %collective-permute-start.16 = (f32[2,20,128]{2,0,1:T(2,128)S(1)}, f32[2,20,128]{2,0,1:T(2,128)S(1)}, u32[]{:S(2)}, u32[]{:S(2)}) collective-permute-start(f32[2,20,128]{2,0,1:T(2,128)S(1)} %pad_maximum_fusion.6), channel_id=1, source_target_pairs={{384,0},{416,32},{448,64},{480,96},{0,128},{32,160},{64,192},{96,2... | collective-permute-start | bytes 61448 | tf_op jit(solution)/shard_map/ppermute | solution.py:314
  85.3 41.5 %collective-permute-start.17 = (f32[8,20,128]{2,0,1:T(8,128)}, f32[8,20,128]{2,0,1:T(8,128)}, u32[]{:S(2)}, u32[]{:S(2)}) collective-permute-start(f32[8,20,128]{2,0,1:T(8,128)} %get-tuple-element.16), channel_id=1, source_target_pairs={{32,0},{64,32},{96,64},{0,96},{160,128},{192,160},{224,192},{128,2... | collective-permute-start | bytes 245768 | tf_op jit(solution)/shard_map/ppermute | solution.py:314
  99.2 28.6 %collective-permute-start.18 = (f32[8,20,128]{2,0,1:T(8,128)}, f32[8,20,128]{2,0,1:T(8,128)}, u32[]{:S(2)}, u32[]{:S(2)}) collective-permute-start(f32[8,20,128]{2,0,1:T(8,128)} %get-tuple-element.16), channel_id=1, source_target_pairs={{64,0},{96,32},{0,64},{32,96},{192,128},{224,160},{128,192},{160,2... | collective-permute-start | bytes 245768 | tf_op jit(solution)/shard_map/ppermute | solution.py:314
  101.1 27.5 %collective-permute-start.19 = (f32[8,20,128]{2,0,1:T(8,128)}, f32[8,20,128]{2,0,1:T(8,128)}, u32[]{:S(2)}, u32[]{:S(2)}) collective-permute-start(f32[8,20,128]{2,0,1:T(8,128)} %get-tuple-element.16), channel_id=1, source_target_pairs={{96,0},{0,32},{32,64},{64,96},{224,128},{128,160},{160,192},{192,2... | collective-permute-start | bytes 245768 | tf_op jit(solution)/shard_map/ppermute | solution.py:314
  108.0 18.8 %copy-start.5 = (f32[56,20,128]{2,0,1:T(8,128)S(1)}, f32[56,20,128]{2,0,1:T(8,128)}, u32[]{:S(2)}) copy-start(f32[56,20,128]{2,0,1:T(8,128)} %get-tuple-element.15) | copy-start | bytes 1720324
  108.8 39.1 %all-to-all-start = ((f32[32,12,128]{2,1,0:T(8,128)}), f32[32,12,128]{2,1,0:T(8,128)S(1)}, u32[]{:S(2)}, u32[]{:S(2)}) async-start(f32[32,12,128]{2,1,0:T(8,128)} %pad_maximum_fusion.2), calls=%async_computation | async-start | bytes 524288 | tf_op jit(solution)/shard_map/all_to_all | solution.py:248
  147.9 18.7 %collective-permute-start.8 = (f32[12,32,128]{2,1,0:T(8,128)S(1)}, f32[12,32,128]{2,1,0:T(8,128)S(1)}, u32[]{:S(2)}, u32[]{:S(2)}) collective-permute-start(f32[12,32,128]{2,1,0:T(8,128)S(1)} %bitcast.72), channel_id=1, source_target_pairs={{128,0},{129,1},{130,2},{131,3},{132,4},{133,5},{134,6},{135,7},{1... | collective-permute-start | bytes 589832 | tf_op jit(solution)/shard_map/ppermute | solution.py:231
  149.3 17.4 %collective-permute-start.9 = (f32[10,32,128]{2,1,0:T(8,128)S(1)}, f32[10,32,128]{2,1,0:T(8,128)S(1)}, u32[]{:S(2)}, u32[]{:S(2)}) collective-permute-start(f32[10,32,128]{2,1,0:T(8,128)S(1)} %slice.51), channel_id=1, source_target_pairs={{96,0},{97,1},{98,2},{99,3},{100,4},{101,5},{102,6},{103,7},{104,8... | collective-permute-start | bytes 491528 | tf_op jit(solution)/shard_map/ppermute | solution.py:231
  151.9 14.8 %collective-permute-start.10 = (f32[8,32,128]{2,1,0:T(8,128)S(1)}, f32[8,32,128]{2,1,0:T(8,128)S(1)}, u32[]{:S(2)}, u32[]{:S(2)}) collective-permute-start(f32[8,32,128]{2,1,0:T(8,128)S(1)} %slice.52), channel_id=1, source_target_pairs={{64,0},{65,1},{66,2},{67,3},{68,4},{69,5},{70,6},{71,7},{72,8},{73... | collective-permute-start | bytes 393224 | tf_op jit(solution)/shard_map/ppermute | solution.py:231
  154.6 12.1 %collective-permute-start.11 = (f32[6,32,128]{2,1,0:T(8,128)S(1)}, f32[6,32,128]{2,1,0:T(8,128)S(1)}, u32[]{:S(2)}, u32[]{:S(2)}) collective-permute-start(f32[6,32,128]{2,1,0:T(8,128)S(1)} %slice.53), channel_id=1, source_target_pairs={{32,0},{33,1},{34,2},{35,3},{36,4},{37,5},{38,6},{39,7},{40,8},{41... | collective-permute-start | bytes 294920 | tf_op jit(solution)/shard_map/ppermute | solution.py:231
  167.7 6.1 %collective-permute-start.20 = (f32[4,32,128]{2,1,0:T(8,128)S(1)}, f32[4,32,128]{2,1,0:T(8,128)S(1)}, u32[]{:S(2)}, u32[]{:S(2)}) collective-permute-start(f32[4,32,128]{2,1,0:T(8,128)S(1)} %shard_map.50.refs_1_), channel_id=1, source_target_pairs={{128,1},{129,0},{130,3},{131,2},{132,5},{133,4},{134,7},{135,6},{1... | collective-permute-start | bytes 196616 | tf_op jit(solution)/shard_map/ppermute | solution.py:231
  169.0 6.6 %collective-permute-start.21 = (f32[4,32,128]{2,1,0:T(8,128)S(1)}, f32[4,32,128]{2,1,0:T(8,128)S(1)}, u32[]{:S(2)}, u32[]{:S(2)}) collective-permute-start(f32[4,32,128]{2,1,0:T(8,128)S(1)} %shard_map.50.refs_1_), channel_id=1, source_target_pairs={{129,2},{130,1},{131,4},{132,3},{133,6},{134,5},{135,8},{136,7},{1... | collective-permute-start | bytes 196616 | tf_op jit(solution)/shard_map/ppermute | solution.py:231
  170.3 6.6 %collective-permute-start.22 = (f32[4,32,128]{2,1,0:T(8,128)S(1)}, f32[4,32,128]{2,1,0:T(8,128)S(1)}, u32[]{:S(2)}, u32[]{:S(2)}) collective-permute-start(f32[4,32,128]{2,1,0:T(8,128)S(1)} %shard_map.50.refs_1_), channel_id=1, source_target_pairs={{128,0},{129,1},{130,2},{131,3},{132,4},{133,5},{134,6},{135,7},{1... | collective-permute-start | bytes 196616 | tf_op jit(solution)/shard_map/ppermute | solution.py:231
  177.9 10.2 %collective-permute-start.24 = (f32[4,32,128]{2,1,0:T(8,128)S(1)}, f32[4,32,128]{2,1,0:T(8,128)S(1)}, u32[]{:S(2)}, u32[]{:S(2)}) collective-permute-start(f32[4,32,128]{2,1,0:T(8,128)S(1)} %shard_map.51.refs_1_), channel_id=1, source_target_pairs={{257,2},{258,1},{259,4},{260,3},{261,6},{262,5},{263,8},{264,7},{2... | collective-permute-start | bytes 196616 | tf_op jit(solution)/shard_map/ppermute | solution.py:231
  179.2 8.9 %collective-permute-start.23 = (f32[4,32,128]{2,1,0:T(8,128)S(1)}, f32[4,32,128]{2,1,0:T(8,128)S(1)}, u32[]{:S(2)}, u32[]{:S(2)}) collective-permute-start(f32[4,32,128]{2,1,0:T(8,128)S(1)} %shard_map.51.refs_1_), channel_id=1, source_target_pairs={{256,0},{257,1},{258,2},{259,3},{260,4},{261,5},{262,6},{263,7},{2... | collective-permute-start | bytes 196616 | tf_op jit(solution)/shard_map/ppermute | solution.py:231
  180.5 12.7 %collective-permute-start.26 = (f32[4,32,128]{2,1,0:T(8,128)S(1)}, f32[4,32,128]{2,1,0:T(8,128)S(1)}, u32[]{:S(2)}, u32[]{:S(2)}) collective-permute-start(f32[4,32,128]{2,1,0:T(8,128)S(1)} %shard_map.51.refs_1_), channel_id=1, source_target_pairs={{256,2},{258,4},{260,6},{262,8},{264,10},{266,12},{268,14},{270,16... | collective-permute-start | bytes 196616 | tf_op jit(solution)/shard_map/ppermute | solution.py:231
  188.1 5.1 %collective-permute-start.25 = (f32[2,4,32,128]{3,2,1,0:T(8,128)S(1)}, f32[2,4,32,128]{3,2,1,0:T(8,128)S(1)}, u32[]{:S(2)}, u32[]{:S(2)}) collective-permute-start(f32[2,4,32,128]{3,2,1,0:T(8,128)S(1)} %pad_maximum_fusion.5), channel_id=1, source_target_pairs={{0,1},{1,0},{2,3},{3,2},{4,5},{5,4},{6,7},{7,6},{8,9},{9,8},{10,11... | collective-permute-start | bytes 393224 | tf_op jit(solution)/shard_map/ppermute | solution.py:358

commit v9 on v7

--- a/solution.py
+++ b/solution.py
@@ -305,28 +305,15 @@
     )
     field_now = field_now.reshape(start_field.shape)
 
-    tall = jnp.pad(coarse_cond, ((2 * BLOCK, 2 * BLOCK), (0, 0)))
-    backwards = sum((slice_index // bit) % 2 * (SLICES // 2 // bit) for bit in (1, 2, 4, 8))
-    shares = []
-    for i in range(2):
-        at = (slab - 2 * backwards - i) % SLABS
-        window = lax.dynamic_slice_in_dim(tall, at * BLOCK, 5 * BLOCK, axis=0)
-        pairs = []
-        for n in range(SLICES):
-            turned = sum((n // bit) % 2 * (SLICES // 2 // bit) for bit in (1, 2, 4, 8))
-            pairs += [(n * SLABS + j, n * SLABS + (j - 2 * turned - i) % SLABS) for j in range(SLABS)]
-        shares.append(lax.ppermute(window, ("tm", "space"), pairs))
-    gathered = jnp.stack(shares)
-    for bit in (8, 4, 2, 1):
-        upper = (slice_index // bit) % 2 == 1
-        other = lax.ppermute(gathered, "tm", [(n, n ^ bit) for n in range(SLICES)])
-        gathered = jnp.concatenate([jnp.where(upper, other, gathered), jnp.where(upper, gathered, other)])
-    turned = lax.dynamic_slice_in_dim(
-        jnp.concatenate([gathered, gathered]), (SLABS - slab) % SLABS, SLABS, axis=0
-    )
-    row_cond = jnp.transpose(turned, (1, 0, 2))
-
-    rows = to_rows(windows(term, 1))
+    second_half = slice_index % 2 == 1
+    cond_windows = windows(coarse_cond, 2)
+    cond_windows = jnp.where(second_half, cond_windows[:, 10:], cond_windows[:, :10])
+    arrived = to_rows(jnp.concatenate([windows(term, 1), cond_windows], axis=1))
+    rows, own_cond = arrived[:12], arrived[12:]
+    other_cond = lax.ppermute(own_cond, "tm", [(n, n ^ 1) for n in range(SLICES)])
+    row_cond = jnp.concatenate(
+        [jnp.where(second_half, other_cond, own_cond), jnp.where(second_half, own_cond, other_cond)]
+    )
     later = [(i, i) for i in range(SLABS)]
     links = {k: from_later(rows[4 - k : 8 + k], k, later) for k in (1, 2, 3, 4)}
     row_place = (slab - 2) * BLOCK + lax.broadcasted_iota(jnp.int32, row_cond.shape, 0)

time: 207 us -> 205 us (level)
  the two profiles are of different devices: /device:TPU:7 before, /device:TPU:35 now
where the time goes in v9:
time: 205 us; the launch traced here: 204 us
  blocking collectives  103 us (50%)
  starting transfers between devices  46.1 us (22%)
  waiting for transfers between devices  35.1 us (17%)
  Pallas kernels  11.2 us (5%)
  other arithmetic  3.95 us (2%)
  local copies, waits for them, and re-layouts  3.56 us (2%)
    all_to_all x1, blocking collectives, to_rows(): arrived = lax.all_to_all(parts, 'space', 0, 0)  73.3 us
    all_to_all x1, blocking collectives, per_device(): back = lax.all_to_all(jnp.transpose(total, (1, 0, 2)), 'space', 0, 0)  29.7 us
    ppermute x10, waiting for transfers between devices, from_later(): return lax.ppermute(value, ('tm', 'space'), both)  21 us
    ppermute x10, starting transfers between devices, from_later(): return lax.ppermute(value, ('tm', 'space'), both)  18.3 us
    ppermute x3, starting transfers between devices, across_chips(): return lax.ppermute(value, 'space', facing(1, 1))  10.9 us
    ppermute x2, waiting for transfers between devices, per_device(): other = lax.ppermute(share, 'tm', [(n, n ^ bit) for n in range(SLICES)])  7.49 us
    ppermute x3, starting transfers between devices, in_chip(): return lax.ppermute(value, 'space', facing(1, 0))  6.43 us
    ppermute x2, starting transfers between devices, per_device(): other = lax.ppermute(share, 'tm', [(n, n ^ bit) for n in range(SLICES)])  5.92 us
  transfers between devices with their start and end apart: 20, of which 12 were waited for; matrix products, arithmetic and copies ran while one was open for 1% of the time, Pallas kernels for 0%

profile of v9, /device:TPU:35, one launch (start us, length us, event | category | flops | bytes accessed | tf_op | source)
XLA Modules:
  0.0 203.6 jit_solution(8450353585955847365)
XLA Ops:
  0.0 0.9 select_bitcast_fusion.3
  0.9 2.6 %collective-permute-start.2 = (f32[128,128]{1,0:T(8,128)S(1)}, f32[128,128]{1,0:T(8,128)S(1)}, u32[]{:S(2)}, u32[]{:S(2)}) collective-permute-start(f32[128,128]{1,0:T(8,128)S(1)} %get-tuple-element.15), channel_id=1, source_target_pairs={{0,1},{1,0},{2,3},{3,2},{4,5},{5,4},{6,7},{7,6},{8,9},{9,8},{10,11... | collective-permute-start | bytes 196616 | tf_op jit(solution)/shard_map/ppermute | solution.py:265
  3.5 3.1 %collective-permute-start.3 = (f32[128,128]{1,0:T(8,128)S(1)}, f32[128,128]{1,0:T(8,128)S(1)}, u32[]{:S(2)}, u32[]{:S(2)}) collective-permute-start(f32[128,128]{1,0:T(8,128)S(1)} %get-tuple-element.16), channel_id=1, source_target_pairs={{1,2},{2,1},{3,4},{4,3},{5,6},{6,5},{7,8},{8,7},{9,10},{10,9},{11,... | collective-permute-start | bytes 196616 | tf_op jit(solution)/shard_map/ppermute | solution.py:262
  6.6 2.5 %collective-permute-start = (f32[1024,128]{1,0:T(8,128)}, f32[1024,128]{1,0:T(8,128)S(1)}, u32[]{:S(2)}, u32[]{:S(2)}) collective-permute-start(f32[1024,128]{1,0:T(8,128)} %bitcast.58), channel_id=1, source_target_pairs={{1,2},{2,1},{3,4},{4,3},{5,6},{6,5},{7,8},{8,7},{9,10},{10,9},{11,... | collective-permute-start | bytes 1572872 | tf_op jit(solution)/shard_map/ppermute | solution.py:262
  9.1 1.9 collective-permute-start.1
  11.0 0.0 copy-start
  11.0 1.0 copy-done
  12.1 0.3 shard_map.47
  12.3 0.0 collective-permute-done.2
  12.4 0.0 collective-permute-done.3
  12.4 2.2 %collective-permute-start.4 = (f32[2,128,128]{2,1,0:T(8,128)S(1)}, f32[2,128,128]{2,1,0:T(8,128)S(1)}, u32[]{:S(2)}, u32[]{:S(2)}) collective-permute-start(f32[2,128,128]{2,1,0:T(8,128)S(1)} %pad_maximum_fusion.9), channel_id=1, source_target_pairs={{0,32},{32,0},{64,96},{96,64},{128,160},{160,128},{192,224},{224,1... | collective-permute-start | bytes 393224 | tf_op jit(solution)/shard_map/ppermute | solution.py:278
  14.6 0.0 copy-start.2
  14.6 4.2 %collective-permute-done.4 = f32[2,128,128]{2,1,0:T(8,128)S(1)} collective-permute-done((f32[2,128,128]{2,1,0:T(8,128)S(1)}, f32[2,128,128]{2,1,0:T(8,128)S(1)}, u32[]{:S(2)}, u32[]{:S(2)}) %collective-permute-start.4) | collective-permute-done | bytes 131104 | tf_op jit(solution)/shard_map/ppermute | solution.py:278
  18.9 0.0 copy-start.5
  18.9 3.8 %collective-permute-start.5 = (f32[2,256,128]{2,1,0:T(8,128)S(1)}, f32[2,256,128]{2,1,0:T(8,128)S(1)}, u32[]{:S(2)}, u32[]{:S(2)}) collective-permute-start(f32[2,256,128]{2,1,0:T(8,128)S(1)} %pad_maximum_fusion.7), channel_id=1, source_target_pairs={{0,64},{32,96},{64,0},{96,32},{128,192},{160,224},{192,128},{224,1... | collective-permute-start | bytes 786440 | tf_op jit(solution)/shard_map/ppermute | solution.py:278
  22.8 0.3 shard_map.46.refs_7_
  23.1 2.4 %scatter_custom_fusion = f32[262144]{0:T(1024)S(1)} fusion(s32[256]{0:T(256)S(1)} %bitcast.76, f32[256]{0:T(256)} %bitcast.77, f32[]{:T(128)} %constant.126.clone.1), kind=kCustom, calls=%fused_computation.2 | custom fusion | flops 256 | bytes 1049088 | tf_op jit(solution)/shard_map/scatter-add | solution.py:285
  25.5 0.1 add_convert_fusion.refs_0_
  25.5 3.2 %collective-permute-done.5 = f32[2,256,128]{2,1,0:T(8,128)S(1)} collective-permute-done((f32[2,256,128]{2,1,0:T(8,128)S(1)}, f32[2,256,128]{2,1,0:T(8,128)S(1)}, u32[]{:S(2)}, u32[]{:S(2)}) %collective-permute-start.5) | collective-permute-done | bytes 262176 | tf_op jit(solution)/shard_map/ppermute | solution.py:278
  28.8 0.0 copy-start.1
  28.9 0.0 collective-permute-done.refs_1_
  28.9 0.0 copy-start.3
  28.9 0.8 copy-done.3
  29.7 0.4 copy-done.1
  30.1 1.0 copy-done.4
  31.1 2.4 %shard_map.48.refs_3_ = f32[1152,128]{1,0:T(8,128)S(1)} custom-call(s32[4]{0:T(128)S(1)} %add_convert_fusion.refs_0_, f32[1024,128]{1,0:T(8,128)S(1)} %copy-done.4, f32[1024,128]{1,0:T(8,128)} %collective-permute-done.1.refs_2_, f32[1024,128]{1,0:T(8,128)S(1)} %bitcast.61, f32[2,512,128]{2,1,0:T(8,128)S(1)} %pad_maximum_fusion.refs_4_, ...), custom_call_target="tpu_custom_call" | custom-call | tf_op jit(solution)/shard_map/pallas_call | solution.py:154
  33.5 5.4 %collective-permute-start.6 = (f32[1152,128]{1,0:T(8,128)S(1)}, f32[1152,128]{1,0:T(8,128)}, u32[]{:S(2)}, u32[]{:S(2)}) collective-permute-start(f32[1152,128]{1,0:T(8,128)S(1)} %shard_map.48.refs_3_), channel_id=1, source_target_pairs={{1,2},{2,1},{3,4},{4,3},{5,6},{6,5},{7,8},{8,7},{9,10},{10,9},{11,... | collective-permute-start | bytes 1769480 | tf_op jit(solution)/shard_map/ppermute | solution.py:262
  38.9 1.9 collective-permute-start.7
  40.9 0.1 fusion.3
  41.0 5.5 %collective-permute-done.6.refs_1_ = f32[1152,128]{1,0:T(8,128)} collective-permute-done((f32[1152,128]{1,0:T(8,128)S(1)}, f32[1152,128]{1,0:T(8,128)}, u32[]{:S(2)}, u32[]{:S(2)}) %collective-permute-start.6) | collective-permute-done | bytes 589856 | tf_op jit(solution)/shard_map/ppermute | solution.py:262
  46.6 0.0 collective-permute-done.7.refs_2_
  46.6 2.5 %shard_map.49 = (f32[1024,128]{1,0:T(8,128)S(1)}, f32[128,128]{1,0:T(8,128)S(1)}, f32[128,128]{1,0:T(8,128)S(1)}) custom-call(s32[4]{0:T(128)S(1)} %add_convert_fusion.refs_0_, f32[1152,128]{1,0:T(8,128)} %collective-permute-done.6.refs_1_, f32[1152,128]{1,0:T(8,128)} %collective-permute-done.7.refs_2_, f32[1152,128]{1,0:T(8,128)S(1)} %shard_map.48.refs_3_, ...), custom_call_target="tpu_custom_call" | custom-call | tf_op jit(solution)/shard_map/pallas_call | solution.py:154
  49.1 0.1 pad_maximum_fusion.1
  49.2 73.3 %all_to_all.10 = f32[32,22,128]{2,1,0:T(8,128)S(1)} all-to-all(f32[32,22,128]{2,1,0:T(8,128)S(1)} %pad_maximum_fusion.1), channel_id=1, replica_groups=mesh['tm'=16,'space'=32] {'space'}, dimensions={0} | all-to-all | bytes 720896 | tf_op jit(solution)/shard_map/all_to_all | solution.py:248
  122.6 0.1 copy.15
  122.7 2.4 %collective-permute-start.12 = (f32[10,32,128]{2,1,0:T(8,128)S(1)}, f32[10,32,128]{2,1,0:T(8,128)S(1)}, u32[]{:S(2)}, u32[]{:S(2)}) collective-permute-start(f32[10,32,128]{2,1,0:T(8,128)S(1)} %slice.93), channel_id=1, source_target_pairs={{0,32},{32,0},{64,96},{96,64},{128,160},{160,128},{192,224},{224,1... | collective-permute-start | bytes 491528 | tf_op jit(solution)/shard_map/ppermute | solution.py:313
  125.1 1.9 collective-permute-start.8
  127.1 1.9 collective-permute-start.10
  129.0 2.9 %collective-permute-start.11 = (f32[6,32,128]{2,1,0:T(8,128)S(1)}, f32[6,32,128]{2,1,0:T(8,128)S(1)}, u32[]{:S(2)}, u32[]{:S(2)}) collective-permute-start(f32[6,32,128]{2,1,0:T(8,128)S(1)} %slice.92), channel_id=1, source_target_pairs={{32,0},{33,1},{34,2},{35,3},{36,4},{37,5},{38,6},{39,7},{40,8},{41... | collective-permute-start | bytes 294920 | tf_op jit(solution)/shard_map/ppermute | solution.py:231
  131.9 0.0 collective-permute-done.12
  132.0 1.9 collective-permute-start.9
  133.9 0.1 fusion.4
  134.0 1.6 collective-permute-done.11.c1_ref
  135.6 0.0 collective-permute-done.10.c2_ref
  135.6 0.5 collective-permute-done.8.c4_ref
  136.1 8.9 %collective-permute-done.9.c3_ref = f32[10,32,128]{2,1,0:T(8,128)S(1)} collective-permute-done((f32[10,32,128]{2,1,0:T(8,128)S(1)}, f32[10,32,128]{2,1,0:T(8,128)S(1)}, u32[]{:S(2)}, u32[]{:S(2)}) %collective-permute-start.9) | collective-permute-done | bytes 163872 | tf_op jit(solution)/shard_map/ppermute | solution.py:231
  145.0 1.0 shard_map.50.refs_1_
  146.0 1.9 collective-permute-start.13
  147.9 1.9 collective-permute-start.14
  149.9 1.9 collective-permute-start.15
  151.8 0.7 collective-permute-done.13
  152.5 2.3 %collective-permute-done.14 = f32[4,32,128]{2,1,0:T(8,128)S(1)} collective-permute-done((f32[4,32,128]{2,1,0:T(8,128)S(1)}, f32[4,32,128]{2,1,0:T(8,128)S(1)}, u32[]{:S(2)}, u32[]{:S(2)}) %collective-permute-start.14) | collective-permute-done | bytes 65568 | tf_op jit(solution)/shard_map/ppermute | solution.py:231
  154.8 1.5 collective-permute-done.15
  156.3 1.0 shard_map.51.refs_1_
  157.3 1.3 collective-permute-start.16
  158.6 1.3 collective-permute-start.17
  159.9 1.3 collective-permute-start.19
  161.2 2.1 %collective-permute-done.16 = f32[4,32,128]{2,1,0:T(8,128)S(1)} collective-permute-done((f32[4,32,128]{2,1,0:T(8,128)S(1)}, f32[4,32,128]{2,1,0:T(8,128)S(1)}, u32[]{:S(2)}, u32[]{:S(2)}) %collective-permute-start.16) | collective-permute-done | bytes 65568 | tf_op jit(solution)/shard_map/ppermute | solution.py:231
  163.3 3.5 %collective-permute-done.17 = f32[4,32,128]{2,1,0:T(8,128)S(1)} collective-permute-done((f32[4,32,128]{2,1,0:T(8,128)S(1)}, f32[4,32,128]{2,1,0:T(8,128)S(1)}, u32[]{:S(2)}, u32[]{:S(2)}) %collective-permute-start.17) | collective-permute-done | bytes 65568 | tf_op jit(solution)/shard_map/ppermute | solution.py:231
  166.7 2.1 %collective-permute-start.18 = (f32[2,4,32,128]{3,2,1,0:T(8,128)S(1)}, f32[2,4,32,128]{3,2,1,0:T(8,128)S(1)}, u32[]{:S(2)}, u32[]{:S(2)}) collective-permute-start(f32[2,4,32,128]{3,2,1,0:T(8,128)S(1)} %pad_maximum_fusion.10), channel_id=1, source_target_pairs={{0,1},{1,0},{2,3},{3,2},{4,5},{5,4},{6,7},{7,6},{8,9},{9,8},{10,11... | collective-permute-start | bytes 393224 | tf_op jit(solution)/shard_map/ppermute | solution.py:341
  168.9 1.1 collective-permute-done.18
  170.1 2.6 %shard_map.52 = f32[4,32,128]{2,1,0:T(8,128)S(1)} custom-call(f32[20,32,128]{2,1,0:T(8,128)S(1)} %broadcast_select_fusion.refs_0_, f32[4,32,128]{2,1,0:T(8,128)S(1)} %shard_map.51.refs_1_, f32[20,32,128]{2,1,0:T(8,128)S(1)} %get-tuple-element.19.refs_2_, f32[20,32,128]{2,1,0:T(8,128)S(1)} %get-tuple-element.18.refs_3_), custom_call_target="tpu_custom_call" | custom-call | tf_op jit(solution)/shard_map/pallas_call | solution.py:213
  172.8 29.7 %all_to_all.11 = f32[32,4,128]{2,1,0:T(4,128)S(1)} all-to-all(f32[32,4,128]{2,1,0:T(4,128)S(1)} %copy.13), channel_id=1, replica_groups=mesh['tm'=16,'space'=32] {'space'}, dimensions={0} | all-to-all | bytes 131072 | tf_op jit(solution)/shard_map/all_to_all | solution.py:349
  202.5 1.1 shard_map.53
  (37 shorter events, 0.6 us)
Async XLA Ops:
  0.9 11.5 %collective-permute-start.2 = (f32[128,128]{1,0:T(8,128)S(1)}, f32[128,128]{1,0:T(8,128)S(1)}, u32[]{:S(2)}, u32[]{:S(2)}) collective-permute-start(f32[128,128]{1,0:T(8,128)S(1)} %get-tuple-element.15), channel_id=1, source_target_pairs={{0,1},{1,0},{2,3},{3,2},{4,5},{5,4},{6,7},{7,6},{8,9},{9,8},{10,11... | collective-permute-start | bytes 196616 | tf_op jit(solution)/shard_map/ppermute | solution.py:265
  3.5 8.9 %collective-permute-start.3 = (f32[128,128]{1,0:T(8,128)S(1)}, f32[128,128]{1,0:T(8,128)S(1)}, u32[]{:S(2)}, u32[]{:S(2)}) collective-permute-start(f32[128,128]{1,0:T(8,128)S(1)} %get-tuple-element.16), channel_id=1, source_target_pairs={{1,2},{2,1},{3,4},{4,3},{5,6},{6,5},{7,8},{8,7},{9,10},{10,9},{11,... | collective-permute-start | bytes 196616 | tf_op jit(solution)/shard_map/ppermute | solution.py:262
  6.6 22.3 %collective-permute-start = (f32[1024,128]{1,0:T(8,128)}, f32[1024,128]{1,0:T(8,128)S(1)}, u32[]{:S(2)}, u32[]{:S(2)}) collective-permute-start(f32[1024,128]{1,0:T(8,128)} %bitcast.58), channel_id=1, source_target_pairs={{1,2},{2,1},{3,4},{4,3},{5,6},{6,5},{7,8},{8,7},{9,10},{10,9},{11,... | collective-permute-start | bytes 1572872 | tf_op jit(solution)/shard_map/ppermute | solution.py:262
  9.1 20.6 %collective-permute-start.1 = (f32[1024,128]{1,0:T(8,128)}, f32[1024,128]{1,0:T(8,128)}, u32[]{:S(2)}, u32[]{:S(2)}) collective-permute-start(f32[1024,128]{1,0:T(8,128)} %bitcast.59), channel_id=1, source_target_pairs={{0,1},{1,0},{2,3},{3,2},{4,5},{5,4},{6,7},{7,6},{8,9},{9,8},{10,11... | collective-permute-start | bytes 1572872 | tf_op jit(solution)/shard_map/ppermute | solution.py:265
  11.0 1.0 copy-start
  12.4 6.5 %collective-permute-start.4 = (f32[2,128,128]{2,1,0:T(8,128)S(1)}, f32[2,128,128]{2,1,0:T(8,128)S(1)}, u32[]{:S(2)}, u32[]{:S(2)}) collective-permute-start(f32[2,128,128]{2,1,0:T(8,128)S(1)} %pad_maximum_fusion.9), channel_id=1, source_target_pairs={{0,32},{32,0},{64,96},{96,64},{128,160},{160,128},{192,224},{224,1... | collective-permute-start | bytes 393224 | tf_op jit(solution)/shard_map/ppermute | solution.py:278
  14.6 8.2 %copy-start.2 = (f32[1,2,512,128]{3,2,1,0:T(8,128)S(1)}, f32[1,2,512,128]{3,2,1,0:T(8,128)}, u32[]{:S(2)}) copy-start(f32[1,2,512,128]{3,2,1,0:T(8,128)} %param.4) | copy-start | bytes 1572868
  18.9 3.8 %copy-start.5 = (s32[1,256]{1,0:T(1,128)S(1)}, s32[1,256]{1,0:T(1,128)}, u32[]{:S(2)}) copy-start(s32[1,256]{1,0:T(1,128)} %param.6) | copy-start | bytes 3076
  18.9 9.8 %collective-permute-start.5 = (f32[2,256,128]{2,1,0:T(8,128)S(1)}, f32[2,256,128]{2,1,0:T(8,128)S(1)}, u32[]{:S(2)}, u32[]{:S(2)}) collective-permute-start(f32[2,256,128]{2,1,0:T(8,128)S(1)} %pad_maximum_fusion.7), channel_id=1, source_target_pairs={{0,64},{32,96},{64,0},{96,32},{128,192},{160,224},{192,128},{224,1... | collective-permute-start | bytes 786440 | tf_op jit(solution)/shard_map/ppermute | solution.py:278
  28.8 1.2 copy-start.1
  28.9 0.8 copy-start.3
  30.0 1.0 copy-start.4
  33.5 13.0 %collective-permute-start.6 = (f32[1152,128]{1,0:T(8,128)S(1)}, f32[1152,128]{1,0:T(8,128)}, u32[]{:S(2)}, u32[]{:S(2)}) collective-permute-start(f32[1152,128]{1,0:T(8,128)S(1)} %shard_map.48.refs_3_), channel_id=1, source_target_pairs={{1,2},{2,1},{3,4},{4,3},{5,6},{6,5},{7,8},{8,7},{9,10},{10,9},{11,... | collective-permute-start | bytes 1769480 | tf_op jit(solution)/shard_map/ppermute | solution.py:262
  38.9 7.7 %collective-permute-start.7 = (f32[1152,128]{1,0:T(8,128)S(1)}, f32[1152,128]{1,0:T(8,128)}, u32[]{:S(2)}, u32[]{:S(2)}) collective-permute-start(f32[1152,128]{1,0:T(8,128)S(1)} %shard_map.48.refs_3_), channel_id=1, source_target_pairs={{0,1},{1,0},{2,3},{3,2},{4,5},{5,4},{6,7},{7,6},{8,9},{9,8},{10,11... | collective-permute-start | bytes 1769480 | tf_op jit(solution)/shard_map/ppermute | solution.py:265
  122.7 9.2 %collective-permute-start.12 = (f32[10,32,128]{2,1,0:T(8,128)S(1)}, f32[10,32,128]{2,1,0:T(8,128)S(1)}, u32[]{:S(2)}, u32[]{:S(2)}) collective-permute-start(f32[10,32,128]{2,1,0:T(8,128)S(1)} %slice.93), channel_id=1, source_target_pairs={{0,32},{32,0},{64,96},{96,64},{128,160},{160,128},{192,224},{224,1... | collective-permute-start | bytes 491528 | tf_op jit(solution)/shard_map/ppermute | solution.py:313
  125.1 11.0 %collective-permute-start.8 = (f32[12,32,128]{2,1,0:T(8,128)S(1)}, f32[12,32,128]{2,1,0:T(8,128)S(1)}, u32[]{:S(2)}, u32[]{:S(2)}) collective-permute-start(f32[12,32,128]{2,1,0:T(8,128)S(1)} %slice.89), channel_id=1, source_target_pairs={{128,0},{129,1},{130,2},{131,3},{132,4},{133,5},{134,6},{135,7},{1... | collective-permute-start | bytes 589832 | tf_op jit(solution)/shard_map/ppermute | solution.py:231
  127.1 8.6 %collective-permute-start.10 = (f32[8,32,128]{2,1,0:T(8,128)S(1)}, f32[8,32,128]{2,1,0:T(8,128)S(1)}, u32[]{:S(2)}, u32[]{:S(2)}) collective-permute-start(f32[8,32,128]{2,1,0:T(8,128)S(1)} %slice.91), channel_id=1, source_target_pairs={{64,0},{65,1},{66,2},{67,3},{68,4},{69,5},{70,6},{71,7},{72,8},{73... | collective-permute-start | bytes 393224 | tf_op jit(solution)/shard_map/ppermute | solution.py:231
  129.0 6.6 %collective-permute-start.11 = (f32[6,32,128]{2,1,0:T(8,128)S(1)}, f32[6,32,128]{2,1,0:T(8,128)S(1)}, u32[]{:S(2)}, u32[]{:S(2)}) collective-permute-start(f32[6,32,128]{2,1,0:T(8,128)S(1)} %slice.92), channel_id=1, source_target_pairs={{32,0},{33,1},{34,2},{35,3},{36,4},{37,5},{38,6},{39,7},{40,8},{41... | collective-permute-start | bytes 294920 | tf_op jit(solution)/shard_map/ppermute | solution.py:231
  132.0 13.1 %collective-permute-start.9 = (f32[10,32,128]{2,1,0:T(8,128)S(1)}, f32[10,32,128]{2,1,0:T(8,128)S(1)}, u32[]{:S(2)}, u32[]{:S(2)}) collective-permute-start(f32[10,32,128]{2,1,0:T(8,128)S(1)} %get-tuple-element.17), channel_id=1, source_target_pairs={{96,0},{97,1},{98,2},{99,3},{100,4},{101,5},{102,6},{103,7},{104,8... | collective-permute-start | bytes 491528 | tf_op jit(solution)/shard_map/ppermute | solution.py:231
  146.0 6.5 %collective-permute-start.13 = (f32[4,32,128]{2,1,0:T(8,128)S(1)}, f32[4,32,128]{2,1,0:T(8,128)S(1)}, u32[]{:S(2)}, u32[]{:S(2)}) collective-permute-start(f32[4,32,128]{2,1,0:T(8,128)S(1)} %shard_map.50.refs_1_), channel_id=1, source_target_pairs={{128,1},{129,0},{130,3},{131,2},{132,5},{133,4},{134,7},{135,6},{1... | collective-permute-start | bytes 196616 | tf_op jit(solution)/shard_map/ppermute | solution.py:231
  147.9 6.9 %collective-permute-start.14 = (f32[4,32,128]{2,1,0:T(8,128)S(1)}, f32[4,32,128]{2,1,0:T(8,128)S(1)}, u32[]{:S(2)}, u32[]{:S(2)}) collective-permute-start(f32[4,32,128]{2,1,0:T(8,128)S(1)} %shard_map.50.refs_1_), channel_id=1, source_target_pairs={{129,2},{130,1},{131,4},{132,3},{133,6},{134,5},{135,8},{136,7},{1... | collective-permute-start | bytes 196616 | tf_op jit(solution)/shard_map/ppermute | solution.py:231
  149.9 6.5 %collective-permute-start.15 = (f32[4,32,128]{2,1,0:T(8,128)S(1)}, f32[4,32,128]{2,1,0:T(8,128)S(1)}, u32[]{:S(2)}, u32[]{:S(2)}) collective-permute-start(f32[4,32,128]{2,1,0:T(8,128)S(1)} %shard_map.50.refs_1_), channel_id=1, source_target_pairs={{128,0},{129,1},{130,2},{131,3},{132,4},{133,5},{134,6},{135,7},{1... | collective-permute-start | bytes 196616 | tf_op jit(solution)/shard_map/ppermute | solution.py:231
  157.3 6.0 %collective-permute-start.16 = (f32[4,32,128]{2,1,0:T(8,128)S(1)}, f32[4,32,128]{2,1,0:T(8,128)S(1)}, u32[]{:S(2)}, u32[]{:S(2)}) collective-permute-start(f32[4,32,128]{2,1,0:T(8,128)S(1)} %shard_map.51.refs_1_), channel_id=1, source_target_pairs={{256,0},{257,1},{258,2},{259,3},{260,4},{261,5},{262,6},{263,7},{2... | collective-permute-start | bytes 196616 | tf_op jit(solution)/shard_map/ppermute | solution.py:231
  158.6 8.1 %collective-permute-start.17 = (f32[4,32,128]{2,1,0:T(8,128)S(1)}, f32[4,32,128]{2,1,0:T(8,128)S(1)}, u32[]{:S(2)}, u32[]{:S(2)}) collective-permute-start(f32[4,32,128]{2,1,0:T(8,128)S(1)} %shard_map.51.refs_1_), channel_id=1, source_target_pairs={{257,2},{258,1},{259,4},{260,3},{261,6},{262,5},{263,8},{264,7},{2... | collective-permute-start | bytes 196616 | tf_op jit(solution)/shard_map/ppermute | solution.py:231
  159.9 9.0 %collective-permute-start.19 = (f32[4,32,128]{2,1,0:T(8,128)S(1)}, f32[4,32,128]{2,1,0:T(8,128)S(1)}, u32[]{:S(2)}, u32[]{:S(2)}) collective-permute-start(f32[4,32,128]{2,1,0:T(8,128)S(1)} %shard_map.51.refs_1_), channel_id=1, source_target_pairs={{256,2},{258,4},{260,6},{262,8},{264,10},{266,12},{268,14},{270,16... | collective-permute-start | bytes 196616 | tf_op jit(solution)/shard_map/ppermute | solution.py:231
  166.7 3.2 %collective-permute-start.18 = (f32[2,4,32,128]{3,2,1,0:T(8,128)S(1)}, f32[2,4,32,128]{3,2,1,0:T(8,128)S(1)}, u32[]{:S(2)}, u32[]{:S(2)}) collective-permute-start(f32[2,4,32,128]{3,2,1,0:T(8,128)S(1)} %pad_maximum_fusion.10), channel_id=1, source_target_pairs={{0,1},{1,0},{2,3},{3,2},{4,5},{5,4},{6,7},{7,6},{8,9},{9,8},{10,11... | collective-permute-start | bytes 393224 | tf_op jit(solution)/shard_map/ppermute | solution.py:341

commit v10 on v9

--- a/solution.py
+++ b/solution.py
@@ -88,7 +88,7 @@
     return above + below + before + after
 
 
-def two_sweeps(place_ref, across_ref, along_ref, field_ref, share_ref, cond_ref, source_ref):
+def two_sweeps(place_ref, across_ref, along_ref, field_ref, share_ref, cond_ref, source_ref, inverses):
     odd = place_ref[0] == 1
     rows = cond_ref.shape[1]
 
@@ -99,19 +99,18 @@
     planes += [plane(field_ref, p) for p in range(2)]
     planes += [jnp.where(odd, plane(across_ref, p), plane(along_ref, p)) for p in range(2)]
     conds = [share_ref[0], cond_ref[0], cond_ref[1], share_ref[1]]
-    terms, diagonals, wide = [], [], []
+    terms, wide = [], []
     for i in range(4):
         value = planes[i + 1]
         terms.append(conds[i] * value + source_ref[i])
-        diagonals.append(conds[i] + 6.0)
         total = planes[i] + planes[i + 2] + beside_in_plane(value)
-        wide.append((terms[i] + total) / diagonals[i])
+        wide.append((terms[i] + total) * inverses[i])
     wide[0] = jnp.where(place_ref[1] == 1, wide[0], 0.0)
     wide[3] = jnp.where(place_ref[2] == 1, wide[3], 0.0)
     swept = []
     for p in range(2):
         total = wide[p] + wide[p + 2] + beside_in_plane(wide[p + 1])
-        swept.append((terms[p + 1] + total) / diagonals[p + 1])
+        swept.append((terms[p + 1] + total) * inverses[p + 1])
     return swept
 
 
@@ -125,22 +124,40 @@
     return keep * start + spread * total
 
 
-def first_step_kernel(*refs):
-    start_ref, keep_ref, spread_ref, out_ref = refs[7:]
-    across_ref, along_ref, cond_ref = refs[1], refs[2], refs[5]
+def fetched_sweeps(across_from, along_from, across_ref, along_ref, arrived, place_ref, *refs):
+    fetches = [
+        pltpu.make_async_copy(across_from, across_ref, arrived.at[0]),
+        pltpu.make_async_copy(along_from, along_ref, arrived.at[1]),
+    ]
+    for fetch in fetches:
+        fetch.start()
+    share_ref, cond_ref = refs[1], refs[2]
+    inverses = [1.0 / (cond + 6.0) for cond in (share_ref[0], cond_ref[0], cond_ref[1], share_ref[1])]
+    for fetch in fetches:
+        fetch.wait()
+    return two_sweeps(place_ref, across_ref, along_ref, *refs, inverses)
+
+
+def first_step_kernel(
+    place_ref, across_from, along_from, field_ref, share_ref, cond_ref, source_ref, start_ref, keep_ref, spread_ref,
+    sent_ref, across_ref, along_ref, arrived
+):
     rows = cond_ref.shape[1]
-    for p, value in enumerate(two_sweeps(*refs[:7])):
-        out_ref[p * rows : (p + 1) * rows, :] = value
+    traded = (across_from, along_from, across_ref, along_ref, arrived)
+    for p, value in enumerate(fetched_sweeps(*traded, place_ref, field_ref, share_ref, cond_ref, source_ref)):
+        sent_ref[p * rows : (p + 1) * rows, :] = value
     beside = restricted(across_ref, rows) + restricted(along_ref, rows)
     start = start_ref[...]
-    out_ref[2 * rows :, :] = plane_sweep(start, start, beside, keep_ref[...], spread_ref[...])
-
-
-def second_step_kernel(*refs):
-    start_ref, keep_ref, spread_ref, field_ref, term_ref, direct_ref = refs[7:]
-    place_ref, across_ref, along_ref, sent_ref, cond_ref = refs[0], refs[1], refs[2], refs[3], refs[5]
+    sent_ref[2 * rows :, :] = plane_sweep(start, start, beside, keep_ref[...], spread_ref[...])
+
+
+def second_step_kernel(
+    place_ref, across_from, along_from, sent_ref, share_ref, cond_ref, source_ref, start_ref, keep_ref, spread_ref,
+    field_ref, term_ref, direct_ref, across_ref, along_ref, arrived
+):
     rows = cond_ref.shape[1]
-    for p, value in enumerate(two_sweeps(*refs[:7])):
+    traded = (across_from, along_from, across_ref, along_ref, arrived)
+    for p, value in enumerate(fetched_sweeps(*traded, place_ref, sent_ref, share_ref, cond_ref, source_ref)):
         field_ref[p * rows : (p + 1) * rows, :] = value
     tail = slice(2 * rows, 2 * rows + PLANE)
     beside = across_ref[tail, :] + along_ref[tail, :]
@@ -149,15 +166,18 @@
     term_ref[...] = restricted(field_ref, rows) - jnp.where(place_ref[3] == 1, 0.0, direct)
 
 
-def step_call(kernel, shapes, place, *operands):
+def step_call(kernel, shapes, place, traded, *operands):
     in_vmem = pl.BlockSpec(memory_space=pltpu.VMEM)
+    in_hbm = pl.BlockSpec(memory_space=pltpu.HBM)
+    scratch = [pltpu.VMEM(value.shape, jnp.float32) for value in traded]
     return pl.pallas_call(
         kernel,
         out_shape=[jax.ShapeDtypeStruct(shape, jnp.float32) for shape in shapes],
-        in_specs=[pl.BlockSpec(memory_space=pltpu.SMEM)] + [in_vmem] * len(operands),
+        in_specs=[pl.BlockSpec(memory_space=pltpu.SMEM)] + [in_hbm] * len(traded) + [in_vmem] * len(operands),
         out_specs=[in_vmem] * len(shapes),
+        scratch_shapes=scratch + [pltpu.SemaphoreType.DMA((len(traded),))],
         compiler_params=params(),
-    )(place, *operands)
+    )(place, *traded, *operands)
 
 
 def sweep_rows(source, start, keep, spread, target, first, last, low_end, high_end):
@@ -296,13 +316,10 @@
     start_rows = start_field.reshape(slab_rows, width_z)
     around = (share, cond, wide_source, coarse_start, plane_keep, plane_spread)
     across, along = across_chips(start_rows), in_chip(start_rows)
-    sent, = step_call(
-        first_step_kernel, [(slab_rows + PLANE, 128)], place, across, along, start_rows, *around
-    )
+    sent, = step_call(first_step_kernel, [(slab_rows + PLANE, 128)], place, (across, along), start_rows, *around)
     across, along = across_chips(sent), in_chip(sent)
-    field_now, term, direct = step_call(
-        second_step_kernel, [(slab_rows, 128), (PLANE, 128), (PLANE, 128)], place, across, along, sent, *around
-    )
+    shapes = [(slab_rows, 128), (PLANE, 128), (PLANE, 128)]
+    field_now, term, direct = step_call(second_step_kernel, shapes, place, (across, along), sent, *around)
     field_now = field_now.reshape(start_field.shape)
 
     second_half = slice_index % 2 == 1

time: 205 us -> 206 us (level)
  no operation moved by 1% of the time
where the time goes in v10:
time: 206 us; the launch traced here: 205 us
  blocking collectives  103 us (50%)
  starting transfers between devices  46.1 us (22%)
  waiting for transfers between devices  35 us (17%)
  Pallas kernels  12.3 us (6%)
  other arithmetic  3.95 us (2%)
  local copies, waits for them, and re-layouts  3.56 us (2%)
    all_to_all x1, blocking collectives, to_rows(): arrived = lax.all_to_all(parts, 'space', 0, 0)  73.6 us
    all_to_all x1, blocking collectives, per_device(): back = lax.all_to_all(jnp.transpose(total, (1, 0, 2)), 'space', 0, 0)  29.7 us
    ppermute x10, waiting for transfers between devices, from_later(): return lax.ppermute(value, ('tm', 'space'), both)  20.8 us
    ppermute x10, starting transfers between devices, from_later(): return lax.ppermute(value, ('tm', 'space'), both)  18.5 us
    ppermute x3, starting transfers between devices, across_chips(): return lax.ppermute(value, 'space', facing(1, 1))  10.9 us
    ppermute x2, waiting for transfers between devices, per_device(): other = lax.ppermute(share, 'tm', [(n, n ^ bit) for n in range(SLICES)])  7.49 us
    ppermute x3, starting transfers between devices, in_chip(): return lax.ppermute(value, 'space', facing(1, 0))  6.43 us
    pallas_call x2, Pallas kernels, step_call(): pl.pallas_call(kernel, out_shape=[jax.ShapeDtypeStruct(shape, jnp.float32...  6.14 us
  transfers between devices with their start and end apart: 20, of which 12 were waited for; matrix products, arithmetic and copies ran while one was open for 1% of the time, Pallas kernels for 0%

profile of v10, /device:TPU:35, one launch (start us, length us, event | category | flops | bytes accessed | tf_op | source)
XLA Modules:
  0.0 204.8 jit_solution(3382434573657527441)
XLA Ops:
  0.0 0.9 select_bitcast_fusion.3
  0.9 2.6 %collective-permute-start.2 = (f32[128,128]{1,0:T(8,128)S(1)}, f32[128,128]{1,0:T(8,128)S(1)}, u32[]{:S(2)}, u32[]{:S(2)}) collective-permute-start(f32[128,128]{1,0:T(8,128)S(1)} %get-tuple-element.15), channel_id=1, source_target_pairs={{0,1},{1,0},{2,3},{3,2},{4,5},{5,4},{6,7},{7,6},{8,9},{9,8},{10,11... | collective-permute-start | bytes 196616 | tf_op jit(solution)/shard_map/ppermute | solution.py:285
  3.5 3.1 %collective-permute-start.3 = (f32[128,128]{1,0:T(8,128)S(1)}, f32[128,128]{1,0:T(8,128)S(1)}, u32[]{:S(2)}, u32[]{:S(2)}) collective-permute-start(f32[128,128]{1,0:T(8,128)S(1)} %get-tuple-element.16), channel_id=1, source_target_pairs={{1,2},{2,1},{3,4},{4,3},{5,6},{6,5},{7,8},{8,7},{9,10},{10,9},{11,... | collective-permute-start | bytes 196616 | tf_op jit(solution)/shard_map/ppermute | solution.py:282
  6.6 2.5 %collective-permute-start = (f32[1024,128]{1,0:T(8,128)}, f32[1024,128]{1,0:T(8,128)S(1)}, u32[]{:S(2)}, u32[]{:S(2)}) collective-permute-start(f32[1024,128]{1,0:T(8,128)} %bitcast.58), channel_id=1, source_target_pairs={{1,2},{2,1},{3,4},{4,3},{5,6},{6,5},{7,8},{8,7},{9,10},{10,9},{11,... | collective-permute-start | bytes 1572872 | tf_op jit(solution)/shard_map/ppermute | solution.py:282
  9.1 1.9 collective-permute-start.1
  11.0 0.0 copy-start
  11.0 1.0 copy-done
  12.1 0.3 shard_map.47
  12.3 0.0 collective-permute-done.2
  12.4 0.0 collective-permute-done.3
  12.4 2.2 %collective-permute-start.4 = (f32[2,128,128]{2,1,0:T(8,128)S(1)}, f32[2,128,128]{2,1,0:T(8,128)S(1)}, u32[]{:S(2)}, u32[]{:S(2)}) collective-permute-start(f32[2,128,128]{2,1,0:T(8,128)S(1)} %pad_maximum_fusion.9), channel_id=1, source_target_pairs={{0,32},{32,0},{64,96},{96,64},{128,160},{160,128},{192,224},{224,1... | collective-permute-start | bytes 393224 | tf_op jit(solution)/shard_map/ppermute | solution.py:298
  14.6 0.0 copy-start.2
  14.6 4.2 %collective-permute-done.4 = f32[2,128,128]{2,1,0:T(8,128)S(1)} collective-permute-done((f32[2,128,128]{2,1,0:T(8,128)S(1)}, f32[2,128,128]{2,1,0:T(8,128)S(1)}, u32[]{:S(2)}, u32[]{:S(2)}) %collective-permute-start.4) | collective-permute-done | bytes 131104 | tf_op jit(solution)/shard_map/ppermute | solution.py:298
  18.9 0.0 copy-start.5
  18.9 3.8 %collective-permute-start.5 = (f32[2,256,128]{2,1,0:T(8,128)S(1)}, f32[2,256,128]{2,1,0:T(8,128)S(1)}, u32[]{:S(2)}, u32[]{:S(2)}) collective-permute-start(f32[2,256,128]{2,1,0:T(8,128)S(1)} %pad_maximum_fusion.7), channel_id=1, source_target_pairs={{0,64},{32,96},{64,0},{96,32},{128,192},{160,224},{192,128},{224,1... | collective-permute-start | bytes 786440 | tf_op jit(solution)/shard_map/ppermute | solution.py:298
  22.8 0.3 shard_map.46.start_ref
  23.1 2.4 %scatter_custom_fusion = f32[262144]{0:T(1024)S(1)} fusion(s32[256]{0:T(256)S(1)} %bitcast.76, f32[256]{0:T(256)} %bitcast.77, f32[]{:T(128)} %constant.126.clone.1), kind=kCustom, calls=%fused_computation.2 | custom fusion | flops 256 | bytes 1049088 | tf_op jit(solution)/shard_map/scatter-add | solution.py:305
  25.5 0.1 add_convert_fusion.place_ref
  25.5 3.2 %collective-permute-done.5 = f32[2,256,128]{2,1,0:T(8,128)S(1)} collective-permute-done((f32[2,256,128]{2,1,0:T(8,128)S(1)}, f32[2,256,128]{2,1,0:T(8,128)S(1)}, u32[]{:S(2)}, u32[]{:S(2)}) %collective-permute-start.5) | collective-permute-done | bytes 262176 | tf_op jit(solution)/shard_map/ppermute | solution.py:298
  28.8 0.0 copy-start.1
  28.9 0.0 collective-permute-done.across_from
  28.9 0.0 copy-start.3
  28.9 0.8 copy-done.3
  29.7 0.0 collective-permute-done.1.along_from
  29.7 0.4 copy-done.1
  30.1 1.0 copy-done.4
  31.1 3.0 %shard_map.48.sent_ref = f32[1152,128]{1,0:T(8,128)S(1)} custom-call(s32[4]{0:T(128)S(1)} %add_convert_fusion.place_ref, f32[1024,128]{1,0:T(8,128)S(1)} %copy-done.4, f32[1024,128]{1,0:T(8,128)} %collective-permute-done.1.along_from, f32[1024,128]{1,0:T(8,128)S(1)} %bitcast.61, f32[2,512,128]{2,1,0:T(8,128)S(1)} %pad_maximum_fusion.share_ref, ...), custom_call_target="tpu_custom_call" | custom-call | tf_op jit(solution)/shard_map/pallas_call | solution.py:173
  34.1 5.4 %collective-permute-start.6 = (f32[1152,128]{1,0:T(8,128)S(1)}, f32[1152,128]{1,0:T(8,128)}, u32[]{:S(2)}, u32[]{:S(2)}) collective-permute-start(f32[1152,128]{1,0:T(8,128)S(1)} %shard_map.48.sent_ref), channel_id=1, source_target_pairs={{1,2},{2,1},{3,4},{4,3},{5,6},{6,5},{7,8},{8,7},{9,10},{10,9},{11,... | collective-permute-start | bytes 1769480 | tf_op jit(solution)/shard_map/ppermute | solution.py:282
  39.5 1.9 collective-permute-start.7
  41.5 0.1 fusion.3
  41.6 5.5 %collective-permute-done.6.across_from = f32[1152,128]{1,0:T(8,128)} collective-permute-done((f32[1152,128]{1,0:T(8,128)S(1)}, f32[1152,128]{1,0:T(8,128)}, u32[]{:S(2)}, u32[]{:S(2)}) %collective-permute-start.6) | collective-permute-done | bytes 589856 | tf_op jit(solution)/shard_map/ppermute | solution.py:282
  47.2 3.1 %shard_map.49 = (f32[1024,128]{1,0:T(8,128)S(1)}, f32[128,128]{1,0:T(8,128)S(1)}, f32[128,128]{1,0:T(8,128)S(1)}) custom-call(s32[4]{0:T(128)S(1)} %add_convert_fusion.place_ref, f32[1152,128]{1,0:T(8,128)} %collective-permute-done.6.across_from, f32[1152,128]{1,0:T(8,128)} %collective-permute-done.7.along_from, f32[1152,128]{1,0:T(8,128)S(1)} %shard_map.48.sent_ref, ...), custom_call_target="tpu_custom_call" | custom-call | tf_op jit(solution)/shard_map/pallas_call | solution.py:173
  50.3 0.1 pad_maximum_fusion.1
  50.4 73.6 %all_to_all.10 = f32[32,22,128]{2,1,0:T(8,128)S(1)} all-to-all(f32[32,22,128]{2,1,0:T(8,128)S(1)} %pad_maximum_fusion.1), channel_id=1, replica_groups=mesh['tm'=16,'space'=32] {'space'}, dimensions={0} | all-to-all | bytes 720896 | tf_op jit(solution)/shard_map/all_to_all | solution.py:268
  124.0 0.1 copy.15
  124.1 2.2 %collective-permute-start.12 = (f32[10,32,128]{2,1,0:T(8,128)S(1)}, f32[10,32,128]{2,1,0:T(8,128)S(1)}, u32[]{:S(2)}, u32[]{:S(2)}) collective-permute-start(f32[10,32,128]{2,1,0:T(8,128)S(1)} %slice.93), channel_id=1, source_target_pairs={{0,32},{32,0},{64,96},{96,64},{128,160},{160,128},{192,224},{224,1... | collective-permute-start | bytes 491528 | tf_op jit(solution)/shard_map/ppermute | solution.py:330
  126.3 1.9 collective-permute-start.8
  128.2 1.9 collective-permute-start.10
  130.2 3.1 %collective-permute-start.11 = (f32[6,32,128]{2,1,0:T(8,128)S(1)}, f32[6,32,128]{2,1,0:T(8,128)S(1)}, u32[]{:S(2)}, u32[]{:S(2)}) collective-permute-start(f32[6,32,128]{2,1,0:T(8,128)S(1)} %slice.92), channel_id=1, source_target_pairs={{32,0},{33,1},{34,2},{35,3},{36,4},{37,5},{38,6},{39,7},{40,8},{41... | collective-permute-start | bytes 294920 | tf_op jit(solution)/shard_map/ppermute | solution.py:251
  133.3 0.0 collective-permute-done.12
  133.3 1.9 collective-permute-start.9
  135.3 0.1 fusion.4
  135.4 1.4 collective-permute-done.11.c1_ref
  136.8 0.0 collective-permute-done.10.c2_ref
  136.8 0.5 collective-permute-done.8.c4_ref
  137.3 8.9 %collective-permute-done.9.c3_ref = f32[10,32,128]{2,1,0:T(8,128)S(1)} collective-permute-done((f32[10,32,128]{2,1,0:T(8,128)S(1)}, f32[10,32,128]{2,1,0:T(8,128)S(1)}, u32[]{:S(2)}, u32[]{:S(2)}) %collective-permute-start.9) | collective-permute-done | bytes 163872 | tf_op jit(solution)/shard_map/ppermute | solution.py:251
  146.2 1.0 shard_map.50.refs_1_
  147.2 1.9 collective-permute-start.13
  149.1 1.9 collective-permute-start.14
  151.0 1.9 collective-permute-start.15
  152.9 0.7 collective-permute-done.13
  153.7 2.3 %collective-permute-done.14 = f32[4,32,128]{2,1,0:T(8,128)S(1)} collective-permute-done((f32[4,32,128]{2,1,0:T(8,128)S(1)}, f32[4,32,128]{2,1,0:T(8,128)S(1)}, u32[]{:S(2)}, u32[]{:S(2)}) %collective-permute-start.14) | collective-permute-done | bytes 65568 | tf_op jit(solution)/shard_map/ppermute | solution.py:251
  156.0 1.4 collective-permute-done.15
  157.5 1.0 shard_map.51.refs_1_
  158.4 1.3 collective-permute-start.16
  159.7 1.3 collective-permute-start.17
  161.0 1.3 collective-permute-start.19
  162.3 2.1 %collective-permute-done.16 = f32[4,32,128]{2,1,0:T(8,128)S(1)} collective-permute-done((f32[4,32,128]{2,1,0:T(8,128)S(1)}, f32[4,32,128]{2,1,0:T(8,128)S(1)}, u32[]{:S(2)}, u32[]{:S(2)}) %collective-permute-start.16) | collective-permute-done | bytes 65568 | tf_op jit(solution)/shard_map/ppermute | solution.py:251
  164.4 3.5 %collective-permute-done.17 = f32[4,32,128]{2,1,0:T(8,128)S(1)} collective-permute-done((f32[4,32,128]{2,1,0:T(8,128)S(1)}, f32[4,32,128]{2,1,0:T(8,128)S(1)}, u32[]{:S(2)}, u32[]{:S(2)}) %collective-permute-start.17) | collective-permute-done | bytes 65568 | tf_op jit(solution)/shard_map/ppermute | solution.py:251
  168.0 2.1 %collective-permute-start.18 = (f32[2,4,32,128]{3,2,1,0:T(8,128)S(1)}, f32[2,4,32,128]{3,2,1,0:T(8,128)S(1)}, u32[]{:S(2)}, u32[]{:S(2)}) collective-permute-start(f32[2,4,32,128]{3,2,1,0:T(8,128)S(1)} %pad_maximum_fusion.10), channel_id=1, source_target_pairs={{0,1},{1,0},{2,3},{3,2},{4,5},{5,4},{6,7},{7,6},{8,9},{9,8},{10,11... | collective-permute-start | bytes 393224 | tf_op jit(solution)/shard_map/ppermute | solution.py:358
  170.1 1.1 collective-permute-done.18
  171.3 2.6 %shard_map.52 = f32[4,32,128]{2,1,0:T(8,128)S(1)} custom-call(f32[20,32,128]{2,1,0:T(8,128)S(1)} %broadcast_select_fusion.refs_0_, f32[4,32,128]{2,1,0:T(8,128)S(1)} %shard_map.51.refs_1_, f32[20,32,128]{2,1,0:T(8,128)S(1)} %get-tuple-element.19.refs_2_, f32[20,32,128]{2,1,0:T(8,128)S(1)} %get-tuple-element.18.refs_3_), custom_call_target="tpu_custom_call" | custom-call | tf_op jit(solution)/shard_map/pallas_call | solution.py:233
  174.0 29.7 %all_to_all.11 = f32[32,4,128]{2,1,0:T(4,128)S(1)} all-to-all(f32[32,4,128]{2,1,0:T(4,128)S(1)} %copy.13), channel_id=1, replica_groups=mesh['tm'=16,'space'=32] {'space'}, dimensions={0} | all-to-all | bytes 131072 | tf_op jit(solution)/shard_map/all_to_all | solution.py:366
  203.7 1.1 shard_map.53
  (37 shorter events, 0.6 us)
Async XLA Ops:
  0.9 11.5 %collective-permute-start.2 = (f32[128,128]{1,0:T(8,128)S(1)}, f32[128,128]{1,0:T(8,128)S(1)}, u32[]{:S(2)}, u32[]{:S(2)}) collective-permute-start(f32[128,128]{1,0:T(8,128)S(1)} %get-tuple-element.15), channel_id=1, source_target_pairs={{0,1},{1,0},{2,3},{3,2},{4,5},{5,4},{6,7},{7,6},{8,9},{9,8},{10,11... | collective-permute-start | bytes 196616 | tf_op jit(solution)/shard_map/ppermute | solution.py:285
  3.5 8.9 %collective-permute-start.3 = (f32[128,128]{1,0:T(8,128)S(1)}, f32[128,128]{1,0:T(8,128)S(1)}, u32[]{:S(2)}, u32[]{:S(2)}) collective-permute-start(f32[128,128]{1,0:T(8,128)S(1)} %get-tuple-element.16), channel_id=1, source_target_pairs={{1,2},{2,1},{3,4},{4,3},{5,6},{6,5},{7,8},{8,7},{9,10},{10,9},{11,... | collective-permute-start | bytes 196616 | tf_op jit(solution)/shard_map/ppermute | solution.py:282
  6.6 22.3 %collective-permute-start = (f32[1024,128]{1,0:T(8,128)}, f32[1024,128]{1,0:T(8,128)S(1)}, u32[]{:S(2)}, u32[]{:S(2)}) collective-permute-start(f32[1024,128]{1,0:T(8,128)} %bitcast.58), channel_id=1, source_target_pairs={{1,2},{2,1},{3,4},{4,3},{5,6},{6,5},{7,8},{8,7},{9,10},{10,9},{11,... | collective-permute-start | bytes 1572872 | tf_op jit(solution)/shard_map/ppermute | solution.py:282
  9.1 20.6 %collective-permute-start.1 = (f32[1024,128]{1,0:T(8,128)}, f32[1024,128]{1,0:T(8,128)}, u32[]{:S(2)}, u32[]{:S(2)}) collective-permute-start(f32[1024,128]{1,0:T(8,128)} %bitcast.59), channel_id=1, source_target_pairs={{0,1},{1,0},{2,3},{3,2},{4,5},{5,4},{6,7},{7,6},{8,9},{9,8},{10,11... | collective-permute-start | bytes 1572872 | tf_op jit(solution)/shard_map/ppermute | solution.py:285
  11.0 1.0 copy-start
  12.4 6.5 %collective-permute-start.4 = (f32[2,128,128]{2,1,0:T(8,128)S(1)}, f32[2,128,128]{2,1,0:T(8,128)S(1)}, u32[]{:S(2)}, u32[]{:S(2)}) collective-permute-start(f32[2,128,128]{2,1,0:T(8,128)S(1)} %pad_maximum_fusion.9), channel_id=1, source_target_pairs={{0,32},{32,0},{64,96},{96,64},{128,160},{160,128},{192,224},{224,1... | collective-permute-start | bytes 393224 | tf_op jit(solution)/shard_map/ppermute | solution.py:298
  14.6 8.2 %copy-start.2 = (f32[1,2,512,128]{3,2,1,0:T(8,128)S(1)}, f32[1,2,512,128]{3,2,1,0:T(8,128)}, u32[]{:S(2)}) copy-start(f32[1,2,512,128]{3,2,1,0:T(8,128)} %param.4) | copy-start | bytes 1572868
  18.9 3.8 %copy-start.5 = (s32[1,256]{1,0:T(1,128)S(1)}, s32[1,256]{1,0:T(1,128)}, u32[]{:S(2)}) copy-start(s32[1,256]{1,0:T(1,128)} %param.6) | copy-start | bytes 3076
  18.9 9.8 %collective-permute-start.5 = (f32[2,256,128]{2,1,0:T(8,128)S(1)}, f32[2,256,128]{2,1,0:T(8,128)S(1)}, u32[]{:S(2)}, u32[]{:S(2)}) collective-permute-start(f32[2,256,128]{2,1,0:T(8,128)S(1)} %pad_maximum_fusion.7), channel_id=1, source_target_pairs={{0,64},{32,96},{64,0},{96,32},{128,192},{160,224},{192,128},{224,1... | collective-permute-start | bytes 786440 | tf_op jit(solution)/shard_map/ppermute | solution.py:298
  28.8 1.2 copy-start.1
  28.9 0.8 copy-start.3
  30.0 1.0 copy-start.4
  34.1 13.0 %collective-permute-start.6 = (f32[1152,128]{1,0:T(8,128)S(1)}, f32[1152,128]{1,0:T(8,128)}, u32[]{:S(2)}, u32[]{:S(2)}) collective-permute-start(f32[1152,128]{1,0:T(8,128)S(1)} %shard_map.48.sent_ref), channel_id=1, source_target_pairs={{1,2},{2,1},{3,4},{4,3},{5,6},{6,5},{7,8},{8,7},{9,10},{10,9},{11,... | collective-permute-start | bytes 1769480 | tf_op jit(solution)/shard_map/ppermute | solution.py:282
  39.5 7.7 %collective-permute-start.7 = (f32[1152,128]{1,0:T(8,128)S(1)}, f32[1152,128]{1,0:T(8,128)}, u32[]{:S(2)}, u32[]{:S(2)}) collective-permute-start(f32[1152,128]{1,0:T(8,128)S(1)} %shard_map.48.sent_ref), channel_id=1, source_target_pairs={{0,1},{1,0},{2,3},{3,2},{4,5},{5,4},{6,7},{7,6},{8,9},{9,8},{10,11... | collective-permute-start | bytes 1769480 | tf_op jit(solution)/shard_map/ppermute | solution.py:285
  124.1 9.2 %collective-permute-start.12 = (f32[10,32,128]{2,1,0:T(8,128)S(1)}, f32[10,32,128]{2,1,0:T(8,128)S(1)}, u32[]{:S(2)}, u32[]{:S(2)}) collective-permute-start(f32[10,32,128]{2,1,0:T(8,128)S(1)} %slice.93), channel_id=1, source_target_pairs={{0,32},{32,0},{64,96},{96,64},{128,160},{160,128},{192,224},{224,1... | collective-permute-start | bytes 491528 | tf_op jit(solution)/shard_map/ppermute | solution.py:330
  126.3 11.0 %collective-permute-start.8 = (f32[12,32,128]{2,1,0:T(8,128)S(1)}, f32[12,32,128]{2,1,0:T(8,128)S(1)}, u32[]{:S(2)}, u32[]{:S(2)}) collective-permute-start(f32[12,32,128]{2,1,0:T(8,128)S(1)} %slice.89), channel_id=1, source_target_pairs={{128,0},{129,1},{130,2},{131,3},{132,4},{133,5},{134,6},{135,7},{1... | collective-permute-start | bytes 589832 | tf_op jit(solution)/shard_map/ppermute | solution.py:251
  128.2 8.6 %collective-permute-start.10 = (f32[8,32,128]{2,1,0:T(8,128)S(1)}, f32[8,32,128]{2,1,0:T(8,128)S(1)}, u32[]{:S(2)}, u32[]{:S(2)}) collective-permute-start(f32[8,32,128]{2,1,0:T(8,128)S(1)} %slice.91), channel_id=1, source_target_pairs={{64,0},{65,1},{66,2},{67,3},{68,4},{69,5},{70,6},{71,7},{72,8},{73... | collective-permute-start | bytes 393224 | tf_op jit(solution)/shard_map/ppermute | solution.py:251
  130.2 6.6 %collective-permute-start.11 = (f32[6,32,128]{2,1,0:T(8,128)S(1)}, f32[6,32,128]{2,1,0:T(8,128)S(1)}, u32[]{:S(2)}, u32[]{:S(2)}) collective-permute-start(f32[6,32,128]{2,1,0:T(8,128)S(1)} %slice.92), channel_id=1, source_target_pairs={{32,0},{33,1},{34,2},{35,3},{36,4},{37,5},{38,6},{39,7},{40,8},{41... | collective-permute-start | bytes 294920 | tf_op jit(solution)/shard_map/ppermute | solution.py:251
  133.3 12.9 %collective-permute-start.9 = (f32[10,32,128]{2,1,0:T(8,128)S(1)}, f32[10,32,128]{2,1,0:T(8,128)S(1)}, u32[]{:S(2)}, u32[]{:S(2)}) collective-permute-start(f32[10,32,128]{2,1,0:T(8,128)S(1)} %get-tuple-element.17), channel_id=1, source_target_pairs={{96,0},{97,1},{98,2},{99,3},{100,4},{101,5},{102,6},{103,7},{104,8... | collective-permute-start | bytes 491528 | tf_op jit(solution)/shard_map/ppermute | solution.py:251
  147.2 6.5 %collective-permute-start.13 = (f32[4,32,128]{2,1,0:T(8,128)S(1)}, f32[4,32,128]{2,1,0:T(8,128)S(1)}, u32[]{:S(2)}, u32[]{:S(2)}) collective-permute-start(f32[4,32,128]{2,1,0:T(8,128)S(1)} %shard_map.50.refs_1_), channel_id=1, source_target_pairs={{128,1},{129,0},{130,3},{131,2},{132,5},{133,4},{134,7},{135,6},{1... | collective-permute-start | bytes 196616 | tf_op jit(solution)/shard_map/ppermute | solution.py:251
  149.1 6.9 %collective-permute-start.14 = (f32[4,32,128]{2,1,0:T(8,128)S(1)}, f32[4,32,128]{2,1,0:T(8,128)S(1)}, u32[]{:S(2)}, u32[]{:S(2)}) collective-permute-start(f32[4,32,128]{2,1,0:T(8,128)S(1)} %shard_map.50.refs_1_), channel_id=1, source_target_pairs={{129,2},{130,1},{131,4},{132,3},{133,6},{134,5},{135,8},{136,7},{1... | collective-permute-start | bytes 196616 | tf_op jit(solution)/shard_map/ppermute | solution.py:251
  151.0 6.4 %collective-permute-start.15 = (f32[4,32,128]{2,1,0:T(8,128)S(1)}, f32[4,32,128]{2,1,0:T(8,128)S(1)}, u32[]{:S(2)}, u32[]{:S(2)}) collective-permute-start(f32[4,32,128]{2,1,0:T(8,128)S(1)} %shard_map.50.refs_1_), channel_id=1, source_target_pairs={{128,0},{129,1},{130,2},{131,3},{132,4},{133,5},{134,6},{135,7},{1... | collective-permute-start | bytes 196616 | tf_op jit(solution)/shard_map/ppermute | solution.py:251
  158.4 6.0 %collective-permute-start.16 = (f32[4,32,128]{2,1,0:T(8,128)S(1)}, f32[4,32,128]{2,1,0:T(8,128)S(1)}, u32[]{:S(2)}, u32[]{:S(2)}) collective-permute-start(f32[4,32,128]{2,1,0:T(8,128)S(1)} %shard_map.51.refs_1_), channel_id=1, source_target_pairs={{256,0},{257,1},{258,2},{259,3},{260,4},{261,5},{262,6},{263,7},{2... | collective-permute-start | bytes 196616 | tf_op jit(solution)/shard_map/ppermute | solution.py:251
  159.7 8.2 %collective-permute-start.17 = (f32[4,32,128]{2,1,0:T(8,128)S(1)}, f32[4,32,128]{2,1,0:T(8,128)S(1)}, u32[]{:S(2)}, u32[]{:S(2)}) collective-permute-start(f32[4,32,128]{2,1,0:T(8,128)S(1)} %shard_map.51.refs_1_), channel_id=1, source_target_pairs={{257,2},{258,1},{259,4},{260,3},{261,6},{262,5},{263,8},{264,7},{2... | collective-permute-start | bytes 196616 | tf_op jit(solution)/shard_map/ppermute | solution.py:251
  161.0 9.0 %collective-permute-start.19 = (f32[4,32,128]{2,1,0:T(8,128)S(1)}, f32[4,32,128]{2,1,0:T(8,128)S(1)}, u32[]{:S(2)}, u32[]{:S(2)}) collective-permute-start(f32[4,32,128]{2,1,0:T(8,128)S(1)} %shard_map.51.refs_1_), channel_id=1, source_target_pairs={{256,2},{258,4},{260,6},{262,8},{264,10},{266,12},{268,14},{270,16... | collective-permute-start | bytes 196616 | tf_op jit(solution)/shard_map/ppermute | solution.py:251
  168.0 3.2 %collective-permute-start.18 = (f32[2,4,32,128]{3,2,1,0:T(8,128)S(1)}, f32[2,4,32,128]{3,2,1,0:T(8,128)S(1)}, u32[]{:S(2)}, u32[]{:S(2)}) collective-permute-start(f32[2,4,32,128]{3,2,1,0:T(8,128)S(1)} %pad_maximum_fusion.10), channel_id=1, source_target_pairs={{0,1},{1,0},{2,3},{3,2},{4,5},{5,4},{6,7},{7,6},{8,9},{9,8},{10,11... | collective-permute-start | bytes 393224 | tf_op jit(solution)/shard_map/ppermute | solution.py:358

commit v11 on v9

--- a/solution.py
+++ b/solution.py
@@ -218,6 +218,14 @@
     )(*operands)
 
 
+def snake(j):
+    return j if j // 8 % 2 == 0 else j // 8 * 8 + 7 - j % 8
+
+
+def snaked(value):
+    return jnp.concatenate([jnp.flip(value[g : g + 8], 0) if g // 8 % 2 else value[g : g + 8] for g in range(0, SLABS, 8)])
+
+
 def facing(distance, late):
     pairs = []
     for i in range(SLABS - distance):
@@ -227,14 +235,15 @@
 
 
 def from_later(value, links, pairs):
+    pairs = [(snake(i), snake(j)) for i, j in pairs]
     both = [((n + links) * SLABS + i, n * SLABS + j) for n in range(SLICES - links) for i, j in pairs]
     return lax.ppermute(value, ("tm", "space"), both)
 
 
-def beside_later(value, links, distance, slab):
+def beside_later(value, links, distance, block):
     one = from_later(value, links, facing(distance, 0))
     other = from_later(value, links, facing(distance, 1))
-    upper = (slab // distance) % 2 == 1
+    upper = (block // distance) % 2 == 1
     return jnp.where(upper, one, other), jnp.where(upper, other, one)
 
 
@@ -308,7 +317,7 @@
     second_half = slice_index % 2 == 1
     cond_windows = windows(coarse_cond, 2)
     cond_windows = jnp.where(second_half, cond_windows[:, 10:], cond_windows[:, :10])
-    arrived = to_rows(jnp.concatenate([windows(term, 1), cond_windows], axis=1))
+    arrived = to_rows(snaked(jnp.concatenate([windows(term, 1), cond_windows], axis=1)))
     rows, own_cond = arrived[:12], arrived[12:]
     other_cond = lax.ppermute(own_cond, "tm", [(n, n ^ 1) for n in range(SLICES)])
     row_cond = jnp.concatenate(
@@ -316,7 +325,9 @@
     )
     later = [(i, i) for i in range(SLABS)]
     links = {k: from_later(rows[4 - k : 8 + k], k, later) for k in (1, 2, 3, 4)}
-    row_place = (slab - 2) * BLOCK + lax.broadcasted_iota(jnp.int32, row_cond.shape, 0)
+    group = slab // 8
+    block = jnp.where(group % 2 == 1, 16 * group + 7 - slab, slab)
+    row_place = (block - 2) * BLOCK + lax.broadcasted_iota(jnp.int32, row_cond.shape, 0)
     within = (row_place >= 0) & (row_place < PLANE)
     row_spread = jnp.where(within, 1.0 / (row_cond + 1.5), 0.0)
     row_keep = row_cond * row_spread
@@ -328,7 +339,7 @@
     )
 
     centre = from_later(total, 4, later)
-    before, after = beside_later(total, 4, 1, slab)
+    before, after = beside_later(total, 4, 1, block)
     window = jnp.concatenate([before, centre, after])
     total = chain_call(
         lambda *refs: power_kernel(4, *refs), 12, window, total, row_keep[inner], row_spread[inner]
@@ -338,16 +349,16 @@
     near = from_later(total, 8, facing(1, 1))
     outward = [(j - 2, j) for j in range(2, SLABS, 2)] + [(j + 2, j) for j in range(1, SLABS - 2, 2)]
     far = from_later(total, 8, outward)
-    swapped = lax.ppermute(jnp.stack([centre, near]), "space", facing(1, 0))
+    swapped = from_later(jnp.stack([centre, near]), 0, facing(1, 0))
     window = jnp.where(
-        odd,
+        block % 2 == 1,
         jnp.concatenate([swapped[1], swapped[0], centre, near, far]),
         jnp.concatenate([far, near, centre, swapped[0], swapped[1]]),
     )
     total = chain_call(lambda *refs: power_kernel(8, *refs), 20, window, total, row_keep, row_spread)
 
     back = lax.all_to_all(jnp.transpose(total, (1, 0, 2)), "space", 0, 0)
-    propagated = jnp.where(is_final, direct, back.reshape(PLANE, 128))
+    propagated = jnp.where(is_final, direct, snaked(back).reshape(PLANE, 128))
     return prolong_add(propagated - direct, field_now)[None]
 
 

time: 205 us -> 201 us (0.980)
  the two profiles are of different devices: /device:TPU:35 before, /device:TPU:3 now
where the time goes in v11:
time: 201 us; the launch traced here: 200 us
  blocking collectives  91.1 us (45%)
  waiting for transfers between devices  44.9 us (22%)
  starting transfers between devices  44.8 us (22%)
  Pallas kernels  11.2 us (6%)
  other arithmetic  4 us (2%)
  local copies, waits for them, and re-layouts  3.63 us (2%)
    all_to_all x1, blocking collectives, to_rows(): arrived = lax.all_to_all(parts, 'space', 0, 0)  68.2 us
    ppermute x11, waiting for transfers between devices, from_later(): return lax.ppermute(value, ('tm', 'space'), both)  30.6 us
    all_to_all x1, blocking collectives, per_device(): back = lax.all_to_all(jnp.transpose(total, (1, 0, 2)), 'space', 0, 0)  22.9 us
    ppermute x11, starting transfers between devices, from_later(): return lax.ppermute(value, ('tm', 'space'), both)  16.9 us
    ppermute x3, starting transfers between devices, across_chips(): return lax.ppermute(value, 'space', facing(1, 1))  9.85 us
    ppermute x2, starting transfers between devices, per_device(): other = lax.ppermute(share, 'tm', [(n, n ^ bit) for n in range(SLICES)])  9.46 us
    ppermute x2, waiting for transfers between devices, per_device(): other = lax.ppermute(share, 'tm', [(n, n ^ bit) for n in range(SLICES)])  8.77 us
    ppermute x3, starting transfers between devices, in_chip(): return lax.ppermute(value, 'space', facing(1, 0))  6.43 us
  transfers between devices with their start and end apart: 20, of which 11 were waited for; matrix products, arithmetic and copies ran while one was open for 2% of the time, Pallas kernels for 0%

profile of v11, /device:TPU:3, one launch (start us, length us, event | category | flops | bytes accessed | tf_op | source)
XLA Modules:
  0.0 200.3 jit_solution(11783933611658020529)
XLA Ops:
  0.0 0.9 select_bitcast_fusion.3
  0.9 2.6 %collective-permute-start.2 = (f32[128,128]{1,0:T(8,128)S(1)}, f32[128,128]{1,0:T(8,128)S(1)}, u32[]{:S(2)}, u32[]{:S(2)}) collective-permute-start(f32[128,128]{1,0:T(8,128)S(1)} %get-tuple-element.15), channel_id=1, source_target_pairs={{0,1},{1,0},{2,3},{3,2},{4,5},{5,4},{6,7},{7,6},{8,9},{9,8},{10,11... | collective-permute-start | bytes 196616 | tf_op jit(solution)/shard_map/ppermute | solution.py:274
  3.5 3.1 %collective-permute-start.3 = (f32[128,128]{1,0:T(8,128)S(1)}, f32[128,128]{1,0:T(8,128)S(1)}, u32[]{:S(2)}, u32[]{:S(2)}) collective-permute-start(f32[128,128]{1,0:T(8,128)S(1)} %get-tuple-element.16), channel_id=1, source_target_pairs={{1,2},{2,1},{3,4},{4,3},{5,6},{6,5},{7,8},{8,7},{9,10},{10,9},{11,... | collective-permute-start | bytes 196616 | tf_op jit(solution)/shard_map/ppermute | solution.py:271
  6.6 2.5 %collective-permute-start = (f32[1024,128]{1,0:T(8,128)}, f32[1024,128]{1,0:T(8,128)S(1)}, u32[]{:S(2)}, u32[]{:S(2)}) collective-permute-start(f32[1024,128]{1,0:T(8,128)} %bitcast.58), channel_id=1, source_target_pairs={{1,2},{2,1},{3,4},{4,3},{5,6},{6,5},{7,8},{8,7},{9,10},{10,9},{11,... | collective-permute-start | bytes 1572872 | tf_op jit(solution)/shard_map/ppermute | solution.py:271
  9.1 1.9 collective-permute-start.1
  11.0 0.0 copy-start
  11.0 1.0 copy-done
  12.1 0.3 shard_map.47
  12.3 0.0 collective-permute-done.2
  12.4 0.0 collective-permute-done.3
  12.4 7.5 %collective-permute-start.4 = (f32[2,128,128]{2,1,0:T(8,128)S(1)}, f32[2,128,128]{2,1,0:T(8,128)S(1)}, u32[]{:S(2)}, u32[]{:S(2)}) collective-permute-start(f32[2,128,128]{2,1,0:T(8,128)S(1)} %pad_maximum_fusion.10), channel_id=1, source_target_pairs={{0,32},{32,0},{64,96},{96,64},{128,160},{160,128},{192,224},{224,1... | collective-permute-start | bytes 393224 | tf_op jit(solution)/shard_map/ppermute | solution.py:287
  20.0 0.0 copy-start.2
  20.0 3.4 %collective-permute-done.4 = f32[2,128,128]{2,1,0:T(8,128)S(1)} collective-permute-done((f32[2,128,128]{2,1,0:T(8,128)S(1)}, f32[2,128,128]{2,1,0:T(8,128)S(1)}, u32[]{:S(2)}, u32[]{:S(2)}) %collective-permute-start.4) | collective-permute-done | bytes 131104 | tf_op jit(solution)/shard_map/ppermute | solution.py:287
  23.4 0.0 copy-start.5
  23.4 1.9 collective-permute-start.5
  25.4 0.3 shard_map.46.refs_7_
  25.8 2.4 %scatter_custom_fusion = f32[262144]{0:T(1024)S(1)} fusion(s32[256]{0:T(256)S(1)} %bitcast.76, f32[256]{0:T(256)} %bitcast.77, f32[]{:T(128)} %constant.145.clone.1), kind=kCustom, calls=%fused_computation.2 | custom fusion | flops 256 | bytes 1049088 | tf_op jit(solution)/shard_map/scatter-add | solution.py:294
  28.1 0.1 add_convert_fusion.refs_0_
  28.2 5.4 %collective-permute-done.5 = f32[2,256,128]{2,1,0:T(8,128)S(1)} collective-permute-done((f32[2,256,128]{2,1,0:T(8,128)S(1)}, f32[2,256,128]{2,1,0:T(8,128)S(1)}, u32[]{:S(2)}, u32[]{:S(2)}) %collective-permute-start.5) | collective-permute-done | bytes 262176 | tf_op jit(solution)/shard_map/ppermute | solution.py:287
  33.6 0.0 copy-start.1
  33.7 0.0 collective-permute-done.refs_1_
  33.7 0.0 copy-start.3
  33.7 0.8 copy-done.3
  34.5 0.0 collective-permute-done.1.refs_2_
  34.5 0.4 copy-done.1
  34.9 1.0 copy-done.4
  35.9 2.4 %shard_map.48.refs_3_ = f32[1152,128]{1,0:T(8,128)S(1)} custom-call(s32[4]{0:T(128)S(1)} %add_convert_fusion.refs_0_, f32[1024,128]{1,0:T(8,128)S(1)} %copy-done.4, f32[1024,128]{1,0:T(8,128)} %collective-permute-done.1.refs_2_, f32[1024,128]{1,0:T(8,128)S(1)} %bitcast.61, f32[2,512,128]{2,1,0:T(8,128)S(1)} %pad_maximum_fusion.refs_4_, ...), custom_call_target="tpu_custom_call" | custom-call | tf_op jit(solution)/shard_map/pallas_call | solution.py:154
  38.4 4.3 %collective-permute-start.6 = (f32[1152,128]{1,0:T(8,128)S(1)}, f32[1152,128]{1,0:T(8,128)}, u32[]{:S(2)}, u32[]{:S(2)}) collective-permute-start(f32[1152,128]{1,0:T(8,128)S(1)} %shard_map.48.refs_3_), channel_id=1, source_target_pairs={{1,2},{2,1},{3,4},{4,3},{5,6},{6,5},{7,8},{8,7},{9,10},{10,9},{11,... | collective-permute-start | bytes 1769480 | tf_op jit(solution)/shard_map/ppermute | solution.py:271
  42.6 1.9 collective-permute-start.7
  44.6 0.1 fusion.3
  44.8 5.5 %collective-permute-done.6.refs_1_ = f32[1152,128]{1,0:T(8,128)} collective-permute-done((f32[1152,128]{1,0:T(8,128)S(1)}, f32[1152,128]{1,0:T(8,128)}, u32[]{:S(2)}, u32[]{:S(2)}) %collective-permute-start.6) | collective-permute-done | bytes 589856 | tf_op jit(solution)/shard_map/ppermute | solution.py:271
  50.3 2.5 %shard_map.49 = (f32[1024,128]{1,0:T(8,128)S(1)}, f32[128,128]{1,0:T(8,128)S(1)}, f32[128,128]{1,0:T(8,128)S(1)}) custom-call(s32[4]{0:T(128)S(1)} %add_convert_fusion.refs_0_, f32[1152,128]{1,0:T(8,128)} %collective-permute-done.6.refs_1_, f32[1152,128]{1,0:T(8,128)} %collective-permute-done.7.refs_2_, f32[1152,128]{1,0:T(8,128)S(1)} %shard_map.48.refs_3_, ...), custom_call_target="tpu_custom_call" | custom-call | tf_op jit(solution)/shard_map/pallas_call | solution.py:154
  52.9 0.1 pad_maximum_fusion.1
  53.1 68.2 %all_to_all.10 = f32[32,22,128]{2,1,0:T(8,128)S(1)} all-to-all(f32[32,22,128]{2,1,0:T(8,128)S(1)} %pad_maximum_fusion.2), channel_id=1, replica_groups=mesh['tm'=16,'space'=32] {'space'}, dimensions={0} | all-to-all | bytes 720896 | tf_op jit(solution)/shard_map/all_to_all | solution.py:257
  121.3 0.1 copy.15
  121.4 2.1 %collective-permute-start.12 = (f32[10,32,128]{2,1,0:T(8,128)S(1)}, f32[10,32,128]{2,1,0:T(8,128)S(1)}, u32[]{:S(2)}, u32[]{:S(2)}) collective-permute-start(f32[10,32,128]{2,1,0:T(8,128)S(1)} %slice.129), channel_id=1, source_target_pairs={{0,32},{32,0},{64,96},{96,64},{128,160},{160,128},{192,224},{224,1... | collective-permute-start | bytes 491528 | tf_op jit(solution)/shard_map/ppermute | solution.py:322
  123.6 1.3 collective-permute-start.8
  124.9 1.3 collective-permute-start.10
  126.2 3.1 %collective-permute-start.11 = (f32[6,32,128]{2,1,0:T(8,128)S(1)}, f32[6,32,128]{2,1,0:T(8,128)S(1)}, u32[]{:S(2)}, u32[]{:S(2)}) collective-permute-start(f32[6,32,128]{2,1,0:T(8,128)S(1)} %slice.128), channel_id=1, source_target_pairs={{32,0},{33,1},{34,2},{35,3},{36,4},{37,5},{38,6},{39,7},{47,15},{4... | collective-permute-start | bytes 294920 | tf_op jit(solution)/shard_map/ppermute | solution.py:240
  129.4 0.0 collective-permute-done.12
  129.4 1.3 collective-permute-start.9
  130.7 0.1 fusion.4
  130.9 3.3 %collective-permute-done.11.c1_ref = f32[6,32,128]{2,1,0:T(8,128)S(1)} collective-permute-done((f32[6,32,128]{2,1,0:T(8,128)S(1)}, f32[6,32,128]{2,1,0:T(8,128)S(1)}, u32[]{:S(2)}, u32[]{:S(2)}) %collective-permute-start.11) | collective-permute-done | bytes 98336 | tf_op jit(solution)/shard_map/ppermute | solution.py:240
  134.2 0.0 collective-permute-done.10.c2_ref
  134.2 0.0 collective-permute-done.8.c4_ref
  134.2 6.1 %collective-permute-done.9.c3_ref = f32[10,32,128]{2,1,0:T(8,128)S(1)} collective-permute-done((f32[10,32,128]{2,1,0:T(8,128)S(1)}, f32[10,32,128]{2,1,0:T(8,128)S(1)}, u32[]{:S(2)}, u32[]{:S(2)}) %collective-permute-start.9) | collective-permute-done | bytes 163872 | tf_op jit(solution)/shard_map/ppermute | solution.py:240
  140.3 1.0 shard_map.50.refs_1_
  141.2 1.3 collective-permute-start.13
  142.5 1.3 collective-permute-start.14
  143.9 1.3 collective-permute-start.15
  145.2 7.3 %collective-permute-done.13 = f32[4,32,128]{2,1,0:T(8,128)S(1)} collective-permute-done((f32[4,32,128]{2,1,0:T(8,128)S(1)}, f32[4,32,128]{2,1,0:T(8,128)S(1)}, u32[]{:S(2)}, u32[]{:S(2)}) %collective-permute-start.13) | collective-permute-done | bytes 65568 | tf_op jit(solution)/shard_map/ppermute | solution.py:240
  152.4 1.7 collective-permute-done.14
  154.1 1.8 collective-permute-done.15
  155.9 1.0 shard_map.51.refs_1_
  156.9 1.3 collective-permute-start.16
  158.2 1.3 collective-permute-start.17
  159.5 1.3 collective-permute-start.19
  160.8 2.0 %collective-permute-done.16 = f32[4,32,128]{2,1,0:T(8,128)S(1)} collective-permute-done((f32[4,32,128]{2,1,0:T(8,128)S(1)}, f32[4,32,128]{2,1,0:T(8,128)S(1)}, u32[]{:S(2)}, u32[]{:S(2)}) %collective-permute-start.16) | collective-permute-done | bytes 65568 | tf_op jit(solution)/shard_map/ppermute | solution.py:240
  162.8 7.4 %collective-permute-done.17 = f32[4,32,128]{2,1,0:T(8,128)S(1)} collective-permute-done((f32[4,32,128]{2,1,0:T(8,128)S(1)}, f32[4,32,128]{2,1,0:T(8,128)S(1)}, u32[]{:S(2)}, u32[]{:S(2)}) %collective-permute-start.17) | collective-permute-done | bytes 65568 | tf_op jit(solution)/shard_map/ppermute | solution.py:240
  170.2 2.1 %collective-permute-start.18 = (f32[2,4,32,128]{3,2,1,0:T(8,128)S(1)}, f32[2,4,32,128]{3,2,1,0:T(8,128)S(1)}, u32[]{:S(2)}, u32[]{:S(2)}) collective-permute-start(f32[2,4,32,128]{3,2,1,0:T(8,128)S(1)} %pad_maximum_fusion.11), channel_id=1, source_target_pairs={{0,1},{1,0},{2,3},{3,2},{4,5},{5,4},{6,7},{7,6},{15,14},{14,15},{1... | collective-permute-start | bytes 393224 | tf_op jit(solution)/shard_map/ppermute | solution.py:240
  172.3 1.1 collective-permute-done.18
  173.6 2.6 %shard_map.52 = f32[4,32,128]{2,1,0:T(8,128)S(1)} custom-call(f32[20,32,128]{2,1,0:T(8,128)S(1)} %broadcast_select_fusion.refs_0_, f32[4,32,128]{2,1,0:T(8,128)S(1)} %shard_map.51.refs_1_, f32[20,32,128]{2,1,0:T(8,128)S(1)} %get-tuple-element.23.refs_2_, f32[20,32,128]{2,1,0:T(8,128)S(1)} %get-tuple-element.22.refs_3_), custom_call_target="tpu_custom_call" | custom-call | tf_op jit(solution)/shard_map/pallas_call | solution.py:213
  176.2 22.9 %all_to_all.11 = f32[32,4,128]{2,1,0:T(4,128)S(1)} all-to-all(f32[32,4,128]{2,1,0:T(4,128)S(1)} %copy.13), channel_id=1, replica_groups=mesh['tm'=16,'space'=32] {'space'}, dimensions={0} | all-to-all | bytes 131072 | tf_op jit(solution)/shard_map/all_to_all | solution.py:360
  199.3 1.1 shard_map.53
  (45 shorter events, 0.7 us)
Async XLA Ops:
  0.9 11.5 %collective-permute-start.2 = (f32[128,128]{1,0:T(8,128)S(1)}, f32[128,128]{1,0:T(8,128)S(1)}, u32[]{:S(2)}, u32[]{:S(2)}) collective-permute-start(f32[128,128]{1,0:T(8,128)S(1)} %get-tuple-element.15), channel_id=1, source_target_pairs={{0,1},{1,0},{2,3},{3,2},{4,5},{5,4},{6,7},{7,6},{8,9},{9,8},{10,11... | collective-permute-start | bytes 196616 | tf_op jit(solution)/shard_map/ppermute | solution.py:274
  3.5 8.9 %collective-permute-start.3 = (f32[128,128]{1,0:T(8,128)S(1)}, f32[128,128]{1,0:T(8,128)S(1)}, u32[]{:S(2)}, u32[]{:S(2)}) collective-permute-start(f32[128,128]{1,0:T(8,128)S(1)} %get-tuple-element.16), channel_id=1, source_target_pairs={{1,2},{2,1},{3,4},{4,3},{5,6},{6,5},{7,8},{8,7},{9,10},{10,9},{11,... | collective-permute-start | bytes 196616 | tf_op jit(solution)/shard_map/ppermute | solution.py:271
  6.6 27.1 %collective-permute-start = (f32[1024,128]{1,0:T(8,128)}, f32[1024,128]{1,0:T(8,128)S(1)}, u32[]{:S(2)}, u32[]{:S(2)}) collective-permute-start(f32[1024,128]{1,0:T(8,128)} %bitcast.58), channel_id=1, source_target_pairs={{1,2},{2,1},{3,4},{4,3},{5,6},{6,5},{7,8},{8,7},{9,10},{10,9},{11,... | collective-permute-start | bytes 1572872 | tf_op jit(solution)/shard_map/ppermute | solution.py:271
  9.1 25.4 %collective-permute-start.1 = (f32[1024,128]{1,0:T(8,128)}, f32[1024,128]{1,0:T(8,128)}, u32[]{:S(2)}, u32[]{:S(2)}) collective-permute-start(f32[1024,128]{1,0:T(8,128)} %bitcast.59), channel_id=1, source_target_pairs={{0,1},{1,0},{2,3},{3,2},{4,5},{5,4},{6,7},{7,6},{8,9},{9,8},{10,11... | collective-permute-start | bytes 1572872 | tf_op jit(solution)/shard_map/ppermute | solution.py:274
  11.0 1.0 copy-start
  12.4 11.0 %collective-permute-start.4 = (f32[2,128,128]{2,1,0:T(8,128)S(1)}, f32[2,128,128]{2,1,0:T(8,128)S(1)}, u32[]{:S(2)}, u32[]{:S(2)}) collective-permute-start(f32[2,128,128]{2,1,0:T(8,128)S(1)} %pad_maximum_fusion.10), channel_id=1, source_target_pairs={{0,32},{32,0},{64,96},{96,64},{128,160},{160,128},{192,224},{224,1... | collective-permute-start | bytes 393224 | tf_op jit(solution)/shard_map/ppermute | solution.py:287
  20.0 5.5 %copy-start.2 = (f32[1,2,512,128]{3,2,1,0:T(8,128)S(1)}, f32[1,2,512,128]{3,2,1,0:T(8,128)}, u32[]{:S(2)}) copy-start(f32[1,2,512,128]{3,2,1,0:T(8,128)} %param.4) | copy-start | bytes 1572868
  23.4 2.0 copy-start.5
  23.4 10.2 %collective-permute-start.5 = (f32[2,256,128]{2,1,0:T(8,128)S(1)}, f32[2,256,128]{2,1,0:T(8,128)S(1)}, u32[]{:S(2)}, u32[]{:S(2)}) collective-permute-start(f32[2,256,128]{2,1,0:T(8,128)S(1)} %pad_maximum_fusion.8), channel_id=1, source_target_pairs={{0,64},{32,96},{64,0},{96,32},{128,192},{160,224},{192,128},{224,1... | collective-permute-start | bytes 786440 | tf_op jit(solution)/shard_map/ppermute | solution.py:287
  33.6 1.2 copy-start.1
  33.7 0.8 copy-start.3
  34.9 1.0 copy-start.4
  38.4 12.0 %collective-permute-start.6 = (f32[1152,128]{1,0:T(8,128)S(1)}, f32[1152,128]{1,0:T(8,128)}, u32[]{:S(2)}, u32[]{:S(2)}) collective-permute-start(f32[1152,128]{1,0:T(8,128)S(1)} %shard_map.48.refs_3_), channel_id=1, source_target_pairs={{1,2},{2,1},{3,4},{4,3},{5,6},{6,5},{7,8},{8,7},{9,10},{10,9},{11,... | collective-permute-start | bytes 1769480 | tf_op jit(solution)/shard_map/ppermute | solution.py:271
  42.6 7.7 %collective-permute-start.7 = (f32[1152,128]{1,0:T(8,128)S(1)}, f32[1152,128]{1,0:T(8,128)}, u32[]{:S(2)}, u32[]{:S(2)}) collective-permute-start(f32[1152,128]{1,0:T(8,128)S(1)} %shard_map.48.refs_3_), channel_id=1, source_target_pairs={{0,1},{1,0},{2,3},{3,2},{4,5},{5,4},{6,7},{7,6},{8,9},{9,8},{10,11... | collective-permute-start | bytes 1769480 | tf_op jit(solution)/shard_map/ppermute | solution.py:274
  121.4 8.0 %collective-permute-start.12 = (f32[10,32,128]{2,1,0:T(8,128)S(1)}, f32[10,32,128]{2,1,0:T(8,128)S(1)}, u32[]{:S(2)}, u32[]{:S(2)}) collective-permute-start(f32[10,32,128]{2,1,0:T(8,128)S(1)} %slice.129), channel_id=1, source_target_pairs={{0,32},{32,0},{64,96},{96,64},{128,160},{160,128},{192,224},{224,1... | collective-permute-start | bytes 491528 | tf_op jit(solution)/shard_map/ppermute | solution.py:322
  123.6 10.6 %collective-permute-start.8 = (f32[12,32,128]{2,1,0:T(8,128)S(1)}, f32[12,32,128]{2,1,0:T(8,128)S(1)}, u32[]{:S(2)}, u32[]{:S(2)}) collective-permute-start(f32[12,32,128]{2,1,0:T(8,128)S(1)} %slice.125), channel_id=1, source_target_pairs={{128,0},{129,1},{130,2},{131,3},{132,4},{133,5},{134,6},{135,7},{1... | collective-permute-start | bytes 589832 | tf_op jit(solution)/shard_map/ppermute | solution.py:240
  124.9 9.3 %collective-permute-start.10 = (f32[8,32,128]{2,1,0:T(8,128)S(1)}, f32[8,32,128]{2,1,0:T(8,128)S(1)}, u32[]{:S(2)}, u32[]{:S(2)}) collective-permute-start(f32[8,32,128]{2,1,0:T(8,128)S(1)} %slice.127), channel_id=1, source_target_pairs={{64,0},{65,1},{66,2},{67,3},{68,4},{69,5},{70,6},{71,7},{79,15},{7... | collective-permute-start | bytes 393224 | tf_op jit(solution)/shard_map/ppermute | solution.py:240
  126.2 7.9 %collective-permute-start.11 = (f32[6,32,128]{2,1,0:T(8,128)S(1)}, f32[6,32,128]{2,1,0:T(8,128)S(1)}, u32[]{:S(2)}, u32[]{:S(2)}) collective-permute-start(f32[6,32,128]{2,1,0:T(8,128)S(1)} %slice.128), channel_id=1, source_target_pairs={{32,0},{33,1},{34,2},{35,3},{36,4},{37,5},{38,6},{39,7},{47,15},{4... | collective-permute-start | bytes 294920 | tf_op jit(solution)/shard_map/ppermute | solution.py:240
  129.4 10.8 %collective-permute-start.9 = (f32[10,32,128]{2,1,0:T(8,128)S(1)}, f32[10,32,128]{2,1,0:T(8,128)S(1)}, u32[]{:S(2)}, u32[]{:S(2)}) collective-permute-start(f32[10,32,128]{2,1,0:T(8,128)S(1)} %get-tuple-element.21), channel_id=1, source_target_pairs={{96,0},{97,1},{98,2},{99,3},{100,4},{101,5},{102,6},{103,7},{111,1... | collective-permute-start | bytes 491528 | tf_op jit(solution)/shard_map/ppermute | solution.py:240
  141.2 11.2 %collective-permute-start.13 = (f32[4,32,128]{2,1,0:T(8,128)S(1)}, f32[4,32,128]{2,1,0:T(8,128)S(1)}, u32[]{:S(2)}, u32[]{:S(2)}) collective-permute-start(f32[4,32,128]{2,1,0:T(8,128)S(1)} %shard_map.50.refs_1_), channel_id=1, source_target_pairs={{128,1},{129,0},{130,3},{131,2},{132,5},{133,4},{134,7},{135,6},{1... | collective-permute-start | bytes 196616 | tf_op jit(solution)/shard_map/ppermute | solution.py:240
  142.5 11.6 %collective-permute-start.14 = (f32[4,32,128]{2,1,0:T(8,128)S(1)}, f32[4,32,128]{2,1,0:T(8,128)S(1)}, u32[]{:S(2)}, u32[]{:S(2)}) collective-permute-start(f32[4,32,128]{2,1,0:T(8,128)S(1)} %shard_map.50.refs_1_), channel_id=1, source_target_pairs={{129,2},{130,1},{131,4},{132,3},{133,6},{134,5},{135,15},{143,7},{... | collective-permute-start | bytes 196616 | tf_op jit(solution)/shard_map/ppermute | solution.py:240
  143.9 12.0 %collective-permute-start.15 = (f32[4,32,128]{2,1,0:T(8,128)S(1)}, f32[4,32,128]{2,1,0:T(8,128)S(1)}, u32[]{:S(2)}, u32[]{:S(2)}) collective-permute-start(f32[4,32,128]{2,1,0:T(8,128)S(1)} %shard_map.50.refs_1_), channel_id=1, source_target_pairs={{128,0},{129,1},{130,2},{131,3},{132,4},{133,5},{134,6},{135,7},{1... | collective-permute-start | bytes 196616 | tf_op jit(solution)/shard_map/ppermute | solution.py:240
  156.9 5.9 %collective-permute-start.16 = (f32[4,32,128]{2,1,0:T(8,128)S(1)}, f32[4,32,128]{2,1,0:T(8,128)S(1)}, u32[]{:S(2)}, u32[]{:S(2)}) collective-permute-start(f32[4,32,128]{2,1,0:T(8,128)S(1)} %shard_map.51.refs_1_), channel_id=1, source_target_pairs={{256,0},{257,1},{258,2},{259,3},{260,4},{261,5},{262,6},{263,7},{2... | collective-permute-start | bytes 196616 | tf_op jit(solution)/shard_map/ppermute | solution.py:240
  158.2 12.0 %collective-permute-start.17 = (f32[4,32,128]{2,1,0:T(8,128)S(1)}, f32[4,32,128]{2,1,0:T(8,128)S(1)}, u32[]{:S(2)}, u32[]{:S(2)}) collective-permute-start(f32[4,32,128]{2,1,0:T(8,128)S(1)} %shard_map.51.refs_1_), channel_id=1, source_target_pairs={{257,2},{258,1},{259,4},{260,3},{261,6},{262,5},{263,15},{271,7},{... | collective-permute-start | bytes 196616 | tf_op jit(solution)/shard_map/ppermute | solution.py:240
  159.5 12.8 %collective-permute-start.19 = (f32[4,32,128]{2,1,0:T(8,128)S(1)}, f32[4,32,128]{2,1,0:T(8,128)S(1)}, u32[]{:S(2)}, u32[]{:S(2)}) collective-permute-start(f32[4,32,128]{2,1,0:T(8,128)S(1)} %shard_map.51.refs_1_), channel_id=1, source_target_pairs={{256,2},{258,4},{260,6},{262,15},{271,13},{269,11},{267,9},{265,16... | collective-permute-start | bytes 196616 | tf_op jit(solution)/shard_map/ppermute | solution.py:240
  170.2 3.2 %collective-permute-start.18 = (f32[2,4,32,128]{3,2,1,0:T(8,128)S(1)}, f32[2,4,32,128]{3,2,1,0:T(8,128)S(1)}, u32[]{:S(2)}, u32[]{:S(2)}) collective-permute-start(f32[2,4,32,128]{3,2,1,0:T(8,128)S(1)} %pad_maximum_fusion.11), channel_id=1, source_target_pairs={{0,1},{1,0},{2,3},{3,2},{4,5},{5,4},{6,7},{7,6},{15,14},{14,15},{1... | collective-permute-start | bytes 393224 | tf_op jit(solution)/shard_map/ppermute | solution.py:240

commit v12 on v11

--- a/solution.py
+++ b/solution.py
@@ -314,15 +314,18 @@
     )
     field_now = field_now.reshape(start_field.shape)
 
-    second_half = slice_index % 2 == 1
-    cond_windows = windows(coarse_cond, 2)
-    cond_windows = jnp.where(second_half, cond_windows[:, 10:], cond_windows[:, :10])
+    bits = (ring % 2 == 1, ring // 2 == 1)
+    quarters = [windows(coarse_cond, 2)[:, 5 * i : 5 * i + 5] for i in range(4)]
+    pairs_of = [jnp.where(bits[0], quarters[i + 1], quarters[i]) for i in (0, 2)]
+    cond_windows = jnp.where(bits[1], pairs_of[1], pairs_of[0])
     arrived = to_rows(snaked(jnp.concatenate([windows(term, 1), cond_windows], axis=1)))
     rows, own_cond = arrived[:12], arrived[12:]
-    other_cond = lax.ppermute(own_cond, "tm", [(n, n ^ 1) for n in range(SLICES)])
-    row_cond = jnp.concatenate(
-        [jnp.where(second_half, other_cond, own_cond), jnp.where(second_half, own_cond, other_cond)]
-    )
+    parts = [own_cond]
+    for k in (1, 2, 3):
+        parts.append(lax.ppermute(own_cond, "tm", [(n // 4 * 4 + (n + k) % 4, n) for n in range(SLICES)]))
+    for away, bit in ((1, bits[0]), (2, bits[1])):
+        parts = [jnp.where(bit, parts[(i - away) % 4], parts[i]) for i in range(4)]
+    row_cond = jnp.concatenate(parts)
     later = [(i, i) for i in range(SLABS)]
     links = {k: from_later(rows[4 - k : 8 + k], k, later) for k in (1, 2, 3, 4)}
     group = slab // 8

time: 201 us -> 209 us (1.040)
  the two profiles are of different devices: /device:TPU:3 before, /device:TPU:7 now
where the time goes in v12:
time: 209 us; the launch traced here: 208 us
  starting transfers between devices  100 us (48%)
  waiting for transfers between devices  65.5 us (31%)
  blocking collectives  22.2 us (11%)
  Pallas kernels  11.2 us (5%)
  other arithmetic  4.74 us (2%)
  local copies, waits for them, and re-layouts  3.62 us (2%)
    all_to_all x1, starting transfers between devices, to_rows(): arrived = lax.all_to_all(parts, 'space', 0, 0)  47.3 us
    ppermute x11, waiting for transfers between devices, from_later(): return lax.ppermute(value, ('tm', 'space'), both)  30.3 us
    all_to_all x1, waiting for transfers between devices, to_rows(): arrived = lax.all_to_all(parts, 'space', 0, 0)  22.9 us
    all_to_all x1, blocking collectives, per_device(): back = lax.all_to_all(jnp.transpose(total, (1, 0, 2)), 'space', 0, 0)  22.2 us
    ppermute x11, starting transfers between devices, from_later(): return lax.ppermute(value, ('tm', 'space'), both)  18.1 us
    ppermute x2, starting transfers between devices, per_device(): other = lax.ppermute(share, 'tm', [(n, n ^ bit) for n in range(SLICES)])  9.99 us
    ppermute x3, starting transfers between devices, across_chips(): return lax.ppermute(value, 'space', facing(1, 1))  9.54 us
    ppermute x3, starting transfers between devices, per_device(): lax.ppermute(own_cond, 'tm', [(n // 4 * 4 + (n + k) % 4, n) for n in rang...  8.95 us
  transfers between devices with their start and end apart: 23, of which 11 were waited for; matrix products, arithmetic and copies ran while one was open for 1% of the time, Pallas kernels for 0%

profile of v12, /device:TPU:7, one launch (start us, length us, event | category | flops | bytes accessed | tf_op | source)
XLA Modules:
  0.0 208.3 jit_solution(17034851784520797478)
XLA Ops:
  0.0 0.9 select_bitcast_fusion.3
  0.9 2.6 %collective-permute-start.2 = (f32[128,128]{1,0:T(8,128)S(1)}, f32[128,128]{1,0:T(8,128)S(1)}, u32[]{:S(2)}, u32[]{:S(2)}) collective-permute-start(f32[128,128]{1,0:T(8,128)S(1)} %get-tuple-element.17), channel_id=1, source_target_pairs={{0,1},{1,0},{2,3},{3,2},{4,5},{5,4},{6,7},{7,6},{8,9},{9,8},{10,11... | collective-permute-start | bytes 196616 | tf_op jit(solution)/shard_map/ppermute | solution.py:274
  3.5 3.1 %collective-permute-start.3 = (f32[128,128]{1,0:T(8,128)S(1)}, f32[128,128]{1,0:T(8,128)S(1)}, u32[]{:S(2)}, u32[]{:S(2)}) collective-permute-start(f32[128,128]{1,0:T(8,128)S(1)} %get-tuple-element.18), channel_id=1, source_target_pairs={{1,2},{2,1},{3,4},{4,3},{5,6},{6,5},{7,8},{8,7},{9,10},{10,9},{11,... | collective-permute-start | bytes 196616 | tf_op jit(solution)/shard_map/ppermute | solution.py:271
  6.6 2.5 %collective-permute-start = (f32[1024,128]{1,0:T(8,128)}, f32[1024,128]{1,0:T(8,128)S(1)}, u32[]{:S(2)}, u32[]{:S(2)}) collective-permute-start(f32[1024,128]{1,0:T(8,128)} %bitcast.58), channel_id=1, source_target_pairs={{1,2},{2,1},{3,4},{4,3},{5,6},{6,5},{7,8},{8,7},{9,10},{10,9},{11,... | collective-permute-start | bytes 1572872 | tf_op jit(solution)/shard_map/ppermute | solution.py:271
  9.1 1.9 collective-permute-start.1
  11.0 0.0 copy-start
  11.0 1.0 copy-done
  12.1 0.3 shard_map.47
  12.4 0.0 collective-permute-done.3
  12.4 2.5 %collective-permute-start.4 = (f32[2,128,128]{2,1,0:T(8,128)S(1)}, f32[2,128,128]{2,1,0:T(8,128)S(1)}, u32[]{:S(2)}, u32[]{:S(2)}) collective-permute-start(f32[2,128,128]{2,1,0:T(8,128)S(1)} %pad_maximum_fusion.10), channel_id=1, source_target_pairs={{0,32},{32,0},{64,96},{96,64},{128,160},{160,128},{192,224},{224,1... | collective-permute-start | bytes 393224 | tf_op jit(solution)/shard_map/ppermute | solution.py:287
  14.9 0.0 copy-start.2
  14.9 3.9 %collective-permute-done.4 = f32[2,128,128]{2,1,0:T(8,128)S(1)} collective-permute-done((f32[2,128,128]{2,1,0:T(8,128)S(1)}, f32[2,128,128]{2,1,0:T(8,128)S(1)}, u32[]{:S(2)}, u32[]{:S(2)}) %collective-permute-start.4) | collective-permute-done | bytes 131104 | tf_op jit(solution)/shard_map/ppermute | solution.py:287
  18.9 0.0 copy-start.5
  18.9 7.5 %collective-permute-start.5 = (f32[2,256,128]{2,1,0:T(8,128)S(1)}, f32[2,256,128]{2,1,0:T(8,128)S(1)}, u32[]{:S(2)}, u32[]{:S(2)}) collective-permute-start(f32[2,256,128]{2,1,0:T(8,128)S(1)} %pad_maximum_fusion.4), channel_id=1, source_target_pairs={{0,64},{32,96},{64,0},{96,32},{128,192},{160,224},{192,128},{224,1... | collective-permute-start | bytes 786440 | tf_op jit(solution)/shard_map/ppermute | solution.py:287
  26.6 0.3 shard_map.46.refs_7_
  26.9 2.4 %scatter_custom_fusion = f32[262144]{0:T(1024)S(1)} fusion(s32[256]{0:T(256)S(1)} %bitcast.77, f32[256]{0:T(256)} %bitcast.78, f32[]{:T(128)} %constant.147.clone.1), kind=kCustom, calls=%fused_computation.2 | custom fusion | flops 256 | bytes 1049088 | tf_op jit(solution)/shard_map/scatter-add | solution.py:294
  29.2 0.1 add_convert_fusion.refs_0_
  29.3 2.8 %collective-permute-done.5 = f32[2,256,128]{2,1,0:T(8,128)S(1)} collective-permute-done((f32[2,256,128]{2,1,0:T(8,128)S(1)}, f32[2,256,128]{2,1,0:T(8,128)S(1)}, u32[]{:S(2)}, u32[]{:S(2)}) %collective-permute-start.5) | collective-permute-done | bytes 262176 | tf_op jit(solution)/shard_map/ppermute | solution.py:287
  32.1 0.0 copy-start.1
  32.2 0.0 collective-permute-done.refs_1_
  32.2 0.0 copy-start.3
  32.2 0.8 copy-done.3
  33.0 0.0 collective-permute-done.1.refs_2_
  33.0 0.4 copy-done.1
  33.4 1.0 copy-done.4
  34.4 2.4 %shard_map.48.refs_3_ = f32[1152,128]{1,0:T(8,128)S(1)} custom-call(s32[4]{0:T(128)S(1)} %add_convert_fusion.refs_0_, f32[1024,128]{1,0:T(8,128)S(1)} %copy-done.4, f32[1024,128]{1,0:T(8,128)} %collective-permute-done.1.refs_2_, f32[1024,128]{1,0:T(8,128)S(1)} %bitcast.61, f32[2,512,128]{2,1,0:T(8,128)S(1)} %pad_maximum_fusion.refs_4_, ...), custom_call_target="tpu_custom_call" | custom-call | tf_op jit(solution)/shard_map/pallas_call | solution.py:154
  36.8 4.0 %collective-permute-start.6 = (f32[1152,128]{1,0:T(8,128)S(1)}, f32[1152,128]{1,0:T(8,128)}, u32[]{:S(2)}, u32[]{:S(2)}) collective-permute-start(f32[1152,128]{1,0:T(8,128)S(1)} %shard_map.48.refs_3_), channel_id=1, source_target_pairs={{1,2},{2,1},{3,4},{4,3},{5,6},{6,5},{7,8},{8,7},{9,10},{10,9},{11,... | collective-permute-start | bytes 1769480 | tf_op jit(solution)/shard_map/ppermute | solution.py:271
  40.8 1.9 collective-permute-start.7
  42.8 0.1 fusion.5
  42.9 5.5 %collective-permute-done.6.refs_1_ = f32[1152,128]{1,0:T(8,128)} collective-permute-done((f32[1152,128]{1,0:T(8,128)S(1)}, f32[1152,128]{1,0:T(8,128)}, u32[]{:S(2)}, u32[]{:S(2)}) %collective-permute-start.6) | collective-permute-done | bytes 589856 | tf_op jit(solution)/shard_map/ppermute | solution.py:271
  48.5 0.0 collective-permute-done.7.refs_2_
  48.5 2.5 %shard_map.49 = (f32[1024,128]{1,0:T(8,128)S(1)}, f32[128,128]{1,0:T(8,128)S(1)}, f32[128,128]{1,0:T(8,128)S(1)}) custom-call(s32[4]{0:T(128)S(1)} %add_convert_fusion.refs_0_, f32[1152,128]{1,0:T(8,128)} %collective-permute-done.6.refs_1_, f32[1152,128]{1,0:T(8,128)} %collective-permute-done.7.refs_2_, f32[1152,128]{1,0:T(8,128)S(1)} %shard_map.48.refs_3_, ...), custom_call_target="tpu_custom_call" | custom-call | tf_op jit(solution)/shard_map/pallas_call | solution.py:154
  51.0 0.1 pad_maximum_fusion.1
  51.2 0.8 pad_maximum_fusion.2
  52.0 47.3 %all-to-all-start = ((f32[32,17,128]{2,1,0:T(8,128)}), f32[32,17,128]{2,1,0:T(8,128)S(1)}, u32[]{:S(2)}, u32[]{:S(2)}) async-start(f32[32,17,128]{2,1,0:T(8,128)} %pad_maximum_fusion.2), calls=%async_computation | async-start | bytes 786432 | tf_op jit(solution)/shard_map/all_to_all | solution.py:257
  99.3 22.9 %all-to-all-done = f32[32,17,128]{2,1,0:T(8,128)S(1)} async-done(((f32[32,17,128]{2,1,0:T(8,128)}), f32[32,17,128]{2,1,0:T(8,128)S(1)}, u32[]{:S(2)}, u32[]{:S(2)}) %all-to-all-start) | async-done | bytes 278560 | tf_op jit(solution)/shard_map/all_to_all | solution.py:257
  122.2 0.1 copy.15
  122.3 2.5 %collective-permute-start.12 = (f32[5,32,128]{2,1,0:T(8,128)S(1)}, f32[5,32,128]{2,1,0:T(8,128)S(1)}, u32[]{:S(2)}, u32[]{:S(2)}) collective-permute-start(f32[5,32,128]{2,1,0:T(8,128)S(1)} %slice.138), channel_id=1, source_target_pairs={{32,0},{64,32},{96,64},{0,96},{160,128},{192,160},{224,192},{128,2... | collective-permute-start | bytes 245768 | tf_op jit(solution)/shard_map/ppermute | solution.py:325
  124.7 2.7 %collective-permute-start.13 = (f32[5,32,128]{2,1,0:T(8,128)S(1)}, f32[5,32,128]{2,1,0:T(8,128)S(1)}, u32[]{:S(2)}, u32[]{:S(2)}) collective-permute-start(f32[5,32,128]{2,1,0:T(8,128)S(1)} %slice.138), channel_id=1, source_target_pairs={{64,0},{96,32},{0,64},{32,96},{192,128},{224,160},{128,192},{160,2... | collective-permute-start | bytes 245768 | tf_op jit(solution)/shard_map/ppermute | solution.py:325
  127.5 3.7 %collective-permute-start.14 = (f32[5,32,128]{2,1,0:T(8,128)S(1)}, f32[5,32,128]{2,1,0:T(8,128)S(1)}, u32[]{:S(2)}, u32[]{:S(2)}) collective-permute-start(f32[5,32,128]{2,1,0:T(8,128)S(1)} %slice.138), channel_id=1, source_target_pairs={{96,0},{0,32},{32,64},{64,96},{224,128},{128,160},{160,192},{192,2... | collective-permute-start | bytes 245768 | tf_op jit(solution)/shard_map/ppermute | solution.py:325
  131.3 1.3 collective-permute-start.8
  132.6 2.5 %collective-permute-start.9 = (f32[10,32,128]{2,1,0:T(8,128)S(1)}, f32[10,32,128]{2,1,0:T(8,128)S(1)}, u32[]{:S(2)}, u32[]{:S(2)}) collective-permute-start(f32[10,32,128]{2,1,0:T(8,128)S(1)} %slice.135), channel_id=1, source_target_pairs={{96,0},{97,1},{98,2},{99,3},{100,4},{101,5},{102,6},{103,7},{111,1... | collective-permute-start | bytes 491528 | tf_op jit(solution)/shard_map/ppermute | solution.py:240
  135.1 2.5 %collective-permute-start.10 = (f32[8,32,128]{2,1,0:T(8,128)S(1)}, f32[8,32,128]{2,1,0:T(8,128)S(1)}, u32[]{:S(2)}, u32[]{:S(2)}) collective-permute-start(f32[8,32,128]{2,1,0:T(8,128)S(1)} %slice.136), channel_id=1, source_target_pairs={{64,0},{65,1},{66,2},{67,3},{68,4},{69,5},{70,6},{71,7},{79,15},{7... | collective-permute-start | bytes 393224 | tf_op jit(solution)/shard_map/ppermute | solution.py:240
  137.7 1.9 collective-permute-start.11
  139.7 0.1 fusion.2
  139.8 7.4 %collective-permute-done.11.c1_ref = f32[6,32,128]{2,1,0:T(8,128)S(1)} collective-permute-done((f32[6,32,128]{2,1,0:T(8,128)S(1)}, f32[6,32,128]{2,1,0:T(8,128)S(1)}, u32[]{:S(2)}, u32[]{:S(2)}) %collective-permute-start.11) | collective-permute-done | bytes 98336 | tf_op jit(solution)/shard_map/ppermute | solution.py:240
  147.2 1.0 shard_map.50.refs_1_
  148.2 1.3 collective-permute-start.15
  149.5 1.3 collective-permute-start.16
  150.8 1.3 collective-permute-start.17
  152.1 8.9 %collective-permute-done.15 = f32[4,32,128]{2,1,0:T(8,128)S(1)} collective-permute-done((f32[4,32,128]{2,1,0:T(8,128)S(1)}, f32[4,32,128]{2,1,0:T(8,128)S(1)}, u32[]{:S(2)}, u32[]{:S(2)}) %collective-permute-start.15) | collective-permute-done | bytes 65568 | tf_op jit(solution)/shard_map/ppermute | solution.py:240
  161.0 1.3 collective-permute-done.16
  162.3 1.7 collective-permute-done.17
  164.0 1.0 shard_map.51.refs_1_
  165.0 1.3 collective-permute-start.18
  166.3 1.3 collective-permute-start.19
  167.6 1.3 collective-permute-start.21
  168.9 2.0 collective-permute-done.18
  170.9 8.0 %collective-permute-done.19 = f32[4,32,128]{2,1,0:T(8,128)S(1)} collective-permute-done((f32[4,32,128]{2,1,0:T(8,128)S(1)}, f32[4,32,128]{2,1,0:T(8,128)S(1)}, u32[]{:S(2)}, u32[]{:S(2)}) %collective-permute-start.19) | collective-permute-done | bytes 65568 | tf_op jit(solution)/shard_map/ppermute | solution.py:240
  178.9 2.1 %collective-permute-start.20 = (f32[2,4,32,128]{3,2,1,0:T(8,128)S(1)}, f32[2,4,32,128]{3,2,1,0:T(8,128)S(1)}, u32[]{:S(2)}, u32[]{:S(2)}) collective-permute-start(f32[2,4,32,128]{3,2,1,0:T(8,128)S(1)} %pad_maximum_fusion.11), channel_id=1, source_target_pairs={{0,1},{1,0},{2,3},{3,2},{4,5},{5,4},{6,7},{7,6},{15,14},{14,15},{1... | collective-permute-start | bytes 393224 | tf_op jit(solution)/shard_map/ppermute | solution.py:240
  181.1 1.1 collective-permute-done.20
  182.3 2.6 %shard_map.52 = f32[4,32,128]{2,1,0:T(8,128)S(1)} custom-call(f32[20,32,128]{2,1,0:T(8,128)S(1)} %broadcast_select_fusion.refs_0_, f32[4,32,128]{2,1,0:T(8,128)S(1)} %shard_map.51.refs_1_, f32[20,32,128]{2,1,0:T(8,128)S(1)} %get-tuple-element.24.refs_2_, f32[20,32,128]{2,1,0:T(8,128)S(1)} %get-tuple-element.23.refs_3_), custom_call_target="tpu_custom_call" | custom-call | tf_op jit(solution)/shard_map/pallas_call | solution.py:213
  184.9 22.2 %all_to_all.10 = f32[32,4,128]{2,1,0:T(4,128)S(1)} all-to-all(f32[32,4,128]{2,1,0:T(4,128)S(1)} %copy.13), channel_id=1, replica_groups=mesh['tm'=16,'space'=32] {'space'}, dimensions={0} | all-to-all | bytes 131072 | tf_op jit(solution)/shard_map/all_to_all | solution.py:363
  207.2 1.1 shard_map.53
  (51 shorter events, 0.7 us)
Async XLA Ops:
  0.9 11.5 %collective-permute-start.2 = (f32[128,128]{1,0:T(8,128)S(1)}, f32[128,128]{1,0:T(8,128)S(1)}, u32[]{:S(2)}, u32[]{:S(2)}) collective-permute-start(f32[128,128]{1,0:T(8,128)S(1)} %get-tuple-element.17), channel_id=1, source_target_pairs={{0,1},{1,0},{2,3},{3,2},{4,5},{5,4},{6,7},{7,6},{8,9},{9,8},{10,11... | collective-permute-start | bytes 196616 | tf_op jit(solution)/shard_map/ppermute | solution.py:274
  3.5 8.9 %collective-permute-start.3 = (f32[128,128]{1,0:T(8,128)S(1)}, f32[128,128]{1,0:T(8,128)S(1)}, u32[]{:S(2)}, u32[]{:S(2)}) collective-permute-start(f32[128,128]{1,0:T(8,128)S(1)} %get-tuple-element.18), channel_id=1, source_target_pairs={{1,2},{2,1},{3,4},{4,3},{5,6},{6,5},{7,8},{8,7},{9,10},{10,9},{11,... | collective-permute-start | bytes 196616 | tf_op jit(solution)/shard_map/ppermute | solution.py:271
  6.6 25.6 %collective-permute-start = (f32[1024,128]{1,0:T(8,128)}, f32[1024,128]{1,0:T(8,128)S(1)}, u32[]{:S(2)}, u32[]{:S(2)}) collective-permute-start(f32[1024,128]{1,0:T(8,128)} %bitcast.58), channel_id=1, source_target_pairs={{1,2},{2,1},{3,4},{4,3},{5,6},{6,5},{7,8},{8,7},{9,10},{10,9},{11,... | collective-permute-start | bytes 1572872 | tf_op jit(solution)/shard_map/ppermute | solution.py:271
  9.1 23.9 %collective-permute-start.1 = (f32[1024,128]{1,0:T(8,128)}, f32[1024,128]{1,0:T(8,128)}, u32[]{:S(2)}, u32[]{:S(2)}) collective-permute-start(f32[1024,128]{1,0:T(8,128)} %bitcast.59), channel_id=1, source_target_pairs={{0,1},{1,0},{2,3},{3,2},{4,5},{5,4},{6,7},{7,6},{8,9},{9,8},{10,11... | collective-permute-start | bytes 1572872 | tf_op jit(solution)/shard_map/ppermute | solution.py:274
  11.0 1.0 copy-start
  12.4 6.5 %collective-permute-start.4 = (f32[2,128,128]{2,1,0:T(8,128)S(1)}, f32[2,128,128]{2,1,0:T(8,128)S(1)}, u32[]{:S(2)}, u32[]{:S(2)}) collective-permute-start(f32[2,128,128]{2,1,0:T(8,128)S(1)} %pad_maximum_fusion.10), channel_id=1, source_target_pairs={{0,32},{32,0},{64,96},{96,64},{128,160},{160,128},{192,224},{224,1... | collective-permute-start | bytes 393224 | tf_op jit(solution)/shard_map/ppermute | solution.py:287
  14.9 11.6 %copy-start.2 = (f32[1,2,512,128]{3,2,1,0:T(8,128)S(1)}, f32[1,2,512,128]{3,2,1,0:T(8,128)}, u32[]{:S(2)}) copy-start(f32[1,2,512,128]{3,2,1,0:T(8,128)} %param.4) | copy-start | bytes 1572868
  18.9 7.6 %copy-start.5 = (s32[1,256]{1,0:T(1,128)S(1)}, s32[1,256]{1,0:T(1,128)}, u32[]{:S(2)}) copy-start(s32[1,256]{1,0:T(1,128)} %param.6) | copy-start | bytes 3076
  18.9 13.2 %collective-permute-start.5 = (f32[2,256,128]{2,1,0:T(8,128)S(1)}, f32[2,256,128]{2,1,0:T(8,128)S(1)}, u32[]{:S(2)}, u32[]{:S(2)}) collective-permute-start(f32[2,256,128]{2,1,0:T(8,128)S(1)} %pad_maximum_fusion.4), channel_id=1, source_target_pairs={{0,64},{32,96},{64,0},{96,32},{128,192},{160,224},{192,128},{224,1... | collective-permute-start | bytes 786440 | tf_op jit(solution)/shard_map/ppermute | solution.py:287
  32.1 1.2 copy-start.1
  32.2 0.8 copy-start.3
  33.4 1.0 copy-start.4
  36.8 11.6 %collective-permute-start.6 = (f32[1152,128]{1,0:T(8,128)S(1)}, f32[1152,128]{1,0:T(8,128)}, u32[]{:S(2)}, u32[]{:S(2)}) collective-permute-start(f32[1152,128]{1,0:T(8,128)S(1)} %shard_map.48.refs_3_), channel_id=1, source_target_pairs={{1,2},{2,1},{3,4},{4,3},{5,6},{6,5},{7,8},{8,7},{9,10},{10,9},{11,... | collective-permute-start | bytes 1769480 | tf_op jit(solution)/shard_map/ppermute | solution.py:271
  40.8 7.7 %collective-permute-start.7 = (f32[1152,128]{1,0:T(8,128)S(1)}, f32[1152,128]{1,0:T(8,128)}, u32[]{:S(2)}, u32[]{:S(2)}) collective-permute-start(f32[1152,128]{1,0:T(8,128)S(1)} %shard_map.48.refs_3_), channel_id=1, source_target_pairs={{0,1},{1,0},{2,3},{3,2},{4,5},{5,4},{6,7},{7,6},{8,9},{9,8},{10,11... | collective-permute-start | bytes 1769480 | tf_op jit(solution)/shard_map/ppermute | solution.py:274
  52.0 70.2 %all-to-all-start = ((f32[32,17,128]{2,1,0:T(8,128)}), f32[32,17,128]{2,1,0:T(8,128)S(1)}, u32[]{:S(2)}, u32[]{:S(2)}) async-start(f32[32,17,128]{2,1,0:T(8,128)} %pad_maximum_fusion.2), calls=%async_computation | async-start | bytes 786432 | tf_op jit(solution)/shard_map/all_to_all | solution.py:257
  122.3 12.9 %collective-permute-start.12 = (f32[5,32,128]{2,1,0:T(8,128)S(1)}, f32[5,32,128]{2,1,0:T(8,128)S(1)}, u32[]{:S(2)}, u32[]{:S(2)}) collective-permute-start(f32[5,32,128]{2,1,0:T(8,128)S(1)} %slice.138), channel_id=1, source_target_pairs={{32,0},{64,32},{96,64},{0,96},{160,128},{192,160},{224,192},{128,2... | collective-permute-start | bytes 245768 | tf_op jit(solution)/shard_map/ppermute | solution.py:325
  124.7 12.9 %collective-permute-start.13 = (f32[5,32,128]{2,1,0:T(8,128)S(1)}, f32[5,32,128]{2,1,0:T(8,128)S(1)}, u32[]{:S(2)}, u32[]{:S(2)}) collective-permute-start(f32[5,32,128]{2,1,0:T(8,128)S(1)} %slice.138), channel_id=1, source_target_pairs={{64,0},{96,32},{0,64},{32,96},{192,128},{224,160},{128,192},{160,2... | collective-permute-start | bytes 245768 | tf_op jit(solution)/shard_map/ppermute | solution.py:325
  127.5 12.1 %collective-permute-start.14 = (f32[5,32,128]{2,1,0:T(8,128)S(1)}, f32[5,32,128]{2,1,0:T(8,128)S(1)}, u32[]{:S(2)}, u32[]{:S(2)}) collective-permute-start(f32[5,32,128]{2,1,0:T(8,128)S(1)} %slice.138), channel_id=1, source_target_pairs={{96,0},{0,32},{32,64},{64,96},{224,128},{128,160},{160,192},{192,2... | collective-permute-start | bytes 245768 | tf_op jit(solution)/shard_map/ppermute | solution.py:325
  131.3 15.9 %collective-permute-start.8 = (f32[12,32,128]{2,1,0:T(8,128)S(1)}, f32[12,32,128]{2,1,0:T(8,128)S(1)}, u32[]{:S(2)}, u32[]{:S(2)}) collective-permute-start(f32[12,32,128]{2,1,0:T(8,128)S(1)} %slice.134), channel_id=1, source_target_pairs={{128,0},{129,1},{130,2},{131,3},{132,4},{133,5},{134,6},{135,7},{1... | collective-permute-start | bytes 589832 | tf_op jit(solution)/shard_map/ppermute | solution.py:240
  132.6 14.6 %collective-permute-start.9 = (f32[10,32,128]{2,1,0:T(8,128)S(1)}, f32[10,32,128]{2,1,0:T(8,128)S(1)}, u32[]{:S(2)}, u32[]{:S(2)}) collective-permute-start(f32[10,32,128]{2,1,0:T(8,128)S(1)} %slice.135), channel_id=1, source_target_pairs={{96,0},{97,1},{98,2},{99,3},{100,4},{101,5},{102,6},{103,7},{111,1... | collective-permute-start | bytes 491528 | tf_op jit(solution)/shard_map/ppermute | solution.py:240
  135.1 12.1 %collective-permute-start.10 = (f32[8,32,128]{2,1,0:T(8,128)S(1)}, f32[8,32,128]{2,1,0:T(8,128)S(1)}, u32[]{:S(2)}, u32[]{:S(2)}) collective-permute-start(f32[8,32,128]{2,1,0:T(8,128)S(1)} %slice.136), channel_id=1, source_target_pairs={{64,0},{65,1},{66,2},{67,3},{68,4},{69,5},{70,6},{71,7},{79,15},{7... | collective-permute-start | bytes 393224 | tf_op jit(solution)/shard_map/ppermute | solution.py:240
  137.7 9.6 %collective-permute-start.11 = (f32[6,32,128]{2,1,0:T(8,128)S(1)}, f32[6,32,128]{2,1,0:T(8,128)S(1)}, u32[]{:S(2)}, u32[]{:S(2)}) collective-permute-start(f32[6,32,128]{2,1,0:T(8,128)S(1)} %slice.137), channel_id=1, source_target_pairs={{32,0},{33,1},{34,2},{35,3},{36,4},{37,5},{38,6},{39,7},{47,15},{4... | collective-permute-start | bytes 294920 | tf_op jit(solution)/shard_map/ppermute | solution.py:240
  148.2 12.8 %collective-permute-start.15 = (f32[4,32,128]{2,1,0:T(8,128)S(1)}, f32[4,32,128]{2,1,0:T(8,128)S(1)}, u32[]{:S(2)}, u32[]{:S(2)}) collective-permute-start(f32[4,32,128]{2,1,0:T(8,128)S(1)} %shard_map.50.refs_1_), channel_id=1, source_target_pairs={{128,1},{129,0},{130,3},{131,2},{132,5},{133,4},{134,7},{135,6},{1... | collective-permute-start | bytes 196616 | tf_op jit(solution)/shard_map/ppermute | solution.py:240
  149.5 12.8 %collective-permute-start.16 = (f32[4,32,128]{2,1,0:T(8,128)S(1)}, f32[4,32,128]{2,1,0:T(8,128)S(1)}, u32[]{:S(2)}, u32[]{:S(2)}) collective-permute-start(f32[4,32,128]{2,1,0:T(8,128)S(1)} %shard_map.50.refs_1_), channel_id=1, source_target_pairs={{129,2},{130,1},{131,4},{132,3},{133,6},{134,5},{135,15},{143,7},{... | collective-permute-start | bytes 196616 | tf_op jit(solution)/shard_map/ppermute | solution.py:240
  150.8 13.2 %collective-permute-start.17 = (f32[4,32,128]{2,1,0:T(8,128)S(1)}, f32[4,32,128]{2,1,0:T(8,128)S(1)}, u32[]{:S(2)}, u32[]{:S(2)}) collective-permute-start(f32[4,32,128]{2,1,0:T(8,128)S(1)} %shard_map.50.refs_1_), channel_id=1, source_target_pairs={{128,0},{129,1},{130,2},{131,3},{132,4},{133,5},{134,6},{135,7},{1... | collective-permute-start | bytes 196616 | tf_op jit(solution)/shard_map/ppermute | solution.py:240
  165.0 5.9 %collective-permute-start.18 = (f32[4,32,128]{2,1,0:T(8,128)S(1)}, f32[4,32,128]{2,1,0:T(8,128)S(1)}, u32[]{:S(2)}, u32[]{:S(2)}) collective-permute-start(f32[4,32,128]{2,1,0:T(8,128)S(1)} %shard_map.51.refs_1_), channel_id=1, source_target_pairs={{256,0},{257,1},{258,2},{259,3},{260,4},{261,5},{262,6},{263,7},{2... | collective-permute-start | bytes 196616 | tf_op jit(solution)/shard_map/ppermute | solution.py:240
  166.3 12.6 %collective-permute-start.19 = (f32[4,32,128]{2,1,0:T(8,128)S(1)}, f32[4,32,128]{2,1,0:T(8,128)S(1)}, u32[]{:S(2)}, u32[]{:S(2)}) collective-permute-start(f32[4,32,128]{2,1,0:T(8,128)S(1)} %shard_map.51.refs_1_), channel_id=1, source_target_pairs={{257,2},{258,1},{259,4},{260,3},{261,6},{262,5},{263,15},{271,7},{... | collective-permute-start | bytes 196616 | tf_op jit(solution)/shard_map/ppermute | solution.py:240
  167.6 13.4 %collective-permute-start.21 = (f32[4,32,128]{2,1,0:T(8,128)S(1)}, f32[4,32,128]{2,1,0:T(8,128)S(1)}, u32[]{:S(2)}, u32[]{:S(2)}) collective-permute-start(f32[4,32,128]{2,1,0:T(8,128)S(1)} %shard_map.51.refs_1_), channel_id=1, source_target_pairs={{256,2},{258,4},{260,6},{262,15},{271,13},{269,11},{267,9},{265,16... | collective-permute-start | bytes 196616 | tf_op jit(solution)/shard_map/ppermute | solution.py:240
  178.9 3.2 %collective-permute-start.20 = (f32[2,4,32,128]{3,2,1,0:T(8,128)S(1)}, f32[2,4,32,128]{3,2,1,0:T(8,128)S(1)}, u32[]{:S(2)}, u32[]{:S(2)}) collective-permute-start(f32[2,4,32,128]{3,2,1,0:T(8,128)S(1)} %pad_maximum_fusion.11), channel_id=1, source_target_pairs={{0,1},{1,0},{2,3},{3,2},{4,5},{5,4},{6,7},{7,6},{15,14},{14,15},{1... | collective-permute-start | bytes 393224 | tf_op jit(solution)/shard_map/ppermute | solution.py:240

commit v13 on v11

--- a/solution.py
+++ b/solution.py
@@ -99,19 +99,19 @@
     planes += [plane(field_ref, p) for p in range(2)]
     planes += [jnp.where(odd, plane(across_ref, p), plane(along_ref, p)) for p in range(2)]
     conds = [share_ref[0], cond_ref[0], cond_ref[1], share_ref[1]]
-    terms, diagonals, wide = [], [], []
+    terms, inverses, wide = [], [], []
     for i in range(4):
         value = planes[i + 1]
         terms.append(conds[i] * value + source_ref[i])
-        diagonals.append(conds[i] + 6.0)
+        inverses.append(1.0 / (conds[i] + 6.0))
         total = planes[i] + planes[i + 2] + beside_in_plane(value)
-        wide.append((terms[i] + total) / diagonals[i])
+        wide.append((terms[i] + total) * inverses[i])
     wide[0] = jnp.where(place_ref[1] == 1, wide[0], 0.0)
     wide[3] = jnp.where(place_ref[2] == 1, wide[3], 0.0)
     swept = []
     for p in range(2):
         total = wide[p] + wide[p + 2] + beside_in_plane(wide[p + 1])
-        swept.append((terms[p + 1] + total) / diagonals[p + 1])
+        swept.append((terms[p + 1] + total) * inverses[p + 1])
     return swept
 
 

time: 201 us -> 201 us (level)
  no operation moved by 1% of the time
where the time goes in v13:
time: 201 us; the launch traced here: 200 us
  blocking collectives  90.9 us (45%)
  waiting for transfers between devices  44.9 us (22%)
  starting transfers between devices  44.8 us (22%)
  Pallas kernels  11.2 us (6%)
  other arithmetic  4 us (2%)
  local copies, waits for them, and re-layouts  3.63 us (2%)
    all_to_all x1, blocking collectives, to_rows(): arrived = lax.all_to_all(parts, 'space', 0, 0)  68.2 us
    ppermute x11, waiting for transfers between devices, from_later(): return lax.ppermute(value, ('tm', 'space'), both)  30.6 us
    all_to_all x1, blocking collectives, per_device(): back = lax.all_to_all(jnp.transpose(total, (1, 0, 2)), 'space', 0, 0)  22.7 us
    ppermute x11, starting transfers between devices, from_later(): return lax.ppermute(value, ('tm', 'space'), both)  16.9 us
    ppermute x3, starting transfers between devices, across_chips(): return lax.ppermute(value, 'space', facing(1, 1))  9.85 us
    ppermute x2, starting transfers between devices, per_device(): other = lax.ppermute(share, 'tm', [(n, n ^ bit) for n in range(SLICES)])  9.46 us
    ppermute x2, waiting for transfers between devices, per_device(): other = lax.ppermute(share, 'tm', [(n, n ^ bit) for n in range(SLICES)])  8.77 us
    ppermute x3, starting transfers between devices, in_chip(): return lax.ppermute(value, 'space', facing(1, 0))  6.43 us
  transfers between devices with their start and end apart: 20, of which 11 were waited for; matrix products, arithmetic and copies ran while one was open for 2% of the time, Pallas kernels for 0%

profile of v13, /device:TPU:3, one launch (start us, length us, event | category | flops | bytes accessed | tf_op | source)
XLA Modules:
  0.0 200.1 jit_solution(5348378601731836043)
XLA Ops:
  0.0 0.9 select_bitcast_fusion.3
  0.9 2.6 %collective-permute-start.2 = (f32[128,128]{1,0:T(8,128)S(1)}, f32[128,128]{1,0:T(8,128)S(1)}, u32[]{:S(2)}, u32[]{:S(2)}) collective-permute-start(f32[128,128]{1,0:T(8,128)S(1)} %get-tuple-element.15), channel_id=1, source_target_pairs={{0,1},{1,0},{2,3},{3,2},{4,5},{5,4},{6,7},{7,6},{8,9},{9,8},{10,11... | collective-permute-start | bytes 196616 | tf_op jit(solution)/shard_map/ppermute | solution.py:274
  3.5 3.1 %collective-permute-start.3 = (f32[128,128]{1,0:T(8,128)S(1)}, f32[128,128]{1,0:T(8,128)S(1)}, u32[]{:S(2)}, u32[]{:S(2)}) collective-permute-start(f32[128,128]{1,0:T(8,128)S(1)} %get-tuple-element.16), channel_id=1, source_target_pairs={{1,2},{2,1},{3,4},{4,3},{5,6},{6,5},{7,8},{8,7},{9,10},{10,9},{11,... | collective-permute-start | bytes 196616 | tf_op jit(solution)/shard_map/ppermute | solution.py:271
  6.6 2.5 %collective-permute-start = (f32[1024,128]{1,0:T(8,128)}, f32[1024,128]{1,0:T(8,128)S(1)}, u32[]{:S(2)}, u32[]{:S(2)}) collective-permute-start(f32[1024,128]{1,0:T(8,128)} %bitcast.58), channel_id=1, source_target_pairs={{1,2},{2,1},{3,4},{4,3},{5,6},{6,5},{7,8},{8,7},{9,10},{10,9},{11,... | collective-permute-start | bytes 1572872 | tf_op jit(solution)/shard_map/ppermute | solution.py:271
  9.1 1.9 collective-permute-start.1
  11.0 0.0 copy-start
  11.0 1.0 copy-done
  12.1 0.3 shard_map.47
  12.3 0.0 collective-permute-done.2
  12.4 0.0 collective-permute-done.3
  12.4 7.5 %collective-permute-start.4 = (f32[2,128,128]{2,1,0:T(8,128)S(1)}, f32[2,128,128]{2,1,0:T(8,128)S(1)}, u32[]{:S(2)}, u32[]{:S(2)}) collective-permute-start(f32[2,128,128]{2,1,0:T(8,128)S(1)} %pad_maximum_fusion.10), channel_id=1, source_target_pairs={{0,32},{32,0},{64,96},{96,64},{128,160},{160,128},{192,224},{224,1... | collective-permute-start | bytes 393224 | tf_op jit(solution)/shard_map/ppermute | solution.py:287
  20.0 0.0 copy-start.2
  20.0 3.4 %collective-permute-done.4 = f32[2,128,128]{2,1,0:T(8,128)S(1)} collective-permute-done((f32[2,128,128]{2,1,0:T(8,128)S(1)}, f32[2,128,128]{2,1,0:T(8,128)S(1)}, u32[]{:S(2)}, u32[]{:S(2)}) %collective-permute-start.4) | collective-permute-done | bytes 131104 | tf_op jit(solution)/shard_map/ppermute | solution.py:287
  23.4 0.0 copy-start.5
  23.4 1.9 collective-permute-start.5
  25.4 0.3 shard_map.46.refs_7_
  25.8 2.4 %scatter_custom_fusion = f32[262144]{0:T(1024)S(1)} fusion(s32[256]{0:T(256)S(1)} %bitcast.76, f32[256]{0:T(256)} %bitcast.77, f32[]{:T(128)} %constant.145.clone.1), kind=kCustom, calls=%fused_computation.2 | custom fusion | flops 256 | bytes 1049088 | tf_op jit(solution)/shard_map/scatter-add | solution.py:294
  28.1 0.1 add_convert_fusion.refs_0_
  28.2 5.4 %collective-permute-done.5 = f32[2,256,128]{2,1,0:T(8,128)S(1)} collective-permute-done((f32[2,256,128]{2,1,0:T(8,128)S(1)}, f32[2,256,128]{2,1,0:T(8,128)S(1)}, u32[]{:S(2)}, u32[]{:S(2)}) %collective-permute-start.5) | collective-permute-done | bytes 262176 | tf_op jit(solution)/shard_map/ppermute | solution.py:287
  33.6 0.0 copy-start.1
  33.7 0.0 collective-permute-done.refs_1_
  33.7 0.0 copy-start.3
  33.7 0.8 copy-done.3
  34.5 0.0 collective-permute-done.1.refs_2_
  34.5 0.4 copy-done.1
  34.9 1.0 copy-done.4
  35.9 2.4 %shard_map.48.refs_3_ = f32[1152,128]{1,0:T(8,128)S(1)} custom-call(s32[4]{0:T(128)S(1)} %add_convert_fusion.refs_0_, f32[1024,128]{1,0:T(8,128)S(1)} %copy-done.4, f32[1024,128]{1,0:T(8,128)} %collective-permute-done.1.refs_2_, f32[1024,128]{1,0:T(8,128)S(1)} %bitcast.61, f32[2,512,128]{2,1,0:T(8,128)S(1)} %pad_maximum_fusion.refs_4_, ...), custom_call_target="tpu_custom_call" | custom-call | tf_op jit(solution)/shard_map/pallas_call | solution.py:154
  38.4 4.3 %collective-permute-start.6 = (f32[1152,128]{1,0:T(8,128)S(1)}, f32[1152,128]{1,0:T(8,128)}, u32[]{:S(2)}, u32[]{:S(2)}) collective-permute-start(f32[1152,128]{1,0:T(8,128)S(1)} %shard_map.48.refs_3_), channel_id=1, source_target_pairs={{1,2},{2,1},{3,4},{4,3},{5,6},{6,5},{7,8},{8,7},{9,10},{10,9},{11,... | collective-permute-start | bytes 1769480 | tf_op jit(solution)/shard_map/ppermute | solution.py:271
  42.7 1.9 collective-permute-start.7
  44.6 0.1 fusion.3
  44.8 5.5 %collective-permute-done.6.refs_1_ = f32[1152,128]{1,0:T(8,128)} collective-permute-done((f32[1152,128]{1,0:T(8,128)S(1)}, f32[1152,128]{1,0:T(8,128)}, u32[]{:S(2)}, u32[]{:S(2)}) %collective-permute-start.6) | collective-permute-done | bytes 589856 | tf_op jit(solution)/shard_map/ppermute | solution.py:271
  50.3 0.0 collective-permute-done.7.refs_2_
  50.3 2.5 %shard_map.49 = (f32[1024,128]{1,0:T(8,128)S(1)}, f32[128,128]{1,0:T(8,128)S(1)}, f32[128,128]{1,0:T(8,128)S(1)}) custom-call(s32[4]{0:T(128)S(1)} %add_convert_fusion.refs_0_, f32[1152,128]{1,0:T(8,128)} %collective-permute-done.6.refs_1_, f32[1152,128]{1,0:T(8,128)} %collective-permute-done.7.refs_2_, f32[1152,128]{1,0:T(8,128)S(1)} %shard_map.48.refs_3_, ...), custom_call_target="tpu_custom_call" | custom-call | tf_op jit(solution)/shard_map/pallas_call | solution.py:154
  52.9 0.1 pad_maximum_fusion.1
  53.1 68.2 %all_to_all.10 = f32[32,22,128]{2,1,0:T(8,128)S(1)} all-to-all(f32[32,22,128]{2,1,0:T(8,128)S(1)} %pad_maximum_fusion.2), channel_id=1, replica_groups=mesh['tm'=16,'space'=32] {'space'}, dimensions={0} | all-to-all | bytes 720896 | tf_op jit(solution)/shard_map/all_to_all | solution.py:257
  121.3 0.1 copy.15
  121.4 2.2 %collective-permute-start.12 = (f32[10,32,128]{2,1,0:T(8,128)S(1)}, f32[10,32,128]{2,1,0:T(8,128)S(1)}, u32[]{:S(2)}, u32[]{:S(2)}) collective-permute-start(f32[10,32,128]{2,1,0:T(8,128)S(1)} %slice.129), channel_id=1, source_target_pairs={{0,32},{32,0},{64,96},{96,64},{128,160},{160,128},{192,224},{224,1... | collective-permute-start | bytes 491528 | tf_op jit(solution)/shard_map/ppermute | solution.py:322
  123.6 1.3 collective-permute-start.8
  124.9 1.3 collective-permute-start.10
  126.2 3.1 %collective-permute-start.11 = (f32[6,32,128]{2,1,0:T(8,128)S(1)}, f32[6,32,128]{2,1,0:T(8,128)S(1)}, u32[]{:S(2)}, u32[]{:S(2)}) collective-permute-start(f32[6,32,128]{2,1,0:T(8,128)S(1)} %slice.128), channel_id=1, source_target_pairs={{32,0},{33,1},{34,2},{35,3},{36,4},{37,5},{38,6},{39,7},{47,15},{4... | collective-permute-start | bytes 294920 | tf_op jit(solution)/shard_map/ppermute | solution.py:240
  129.4 1.3 collective-permute-start.9
  130.7 0.1 fusion.4
  130.9 3.3 %collective-permute-done.11.c1_ref = f32[6,32,128]{2,1,0:T(8,128)S(1)} collective-permute-done((f32[6,32,128]{2,1,0:T(8,128)S(1)}, f32[6,32,128]{2,1,0:T(8,128)S(1)}, u32[]{:S(2)}, u32[]{:S(2)}) %collective-permute-start.11) | collective-permute-done | bytes 98336 | tf_op jit(solution)/shard_map/ppermute | solution.py:240
  134.2 0.0 collective-permute-done.10.c2_ref
  134.2 0.0 collective-permute-done.8.c4_ref
  134.2 6.1 %collective-permute-done.9.c3_ref = f32[10,32,128]{2,1,0:T(8,128)S(1)} collective-permute-done((f32[10,32,128]{2,1,0:T(8,128)S(1)}, f32[10,32,128]{2,1,0:T(8,128)S(1)}, u32[]{:S(2)}, u32[]{:S(2)}) %collective-permute-start.9) | collective-permute-done | bytes 163872 | tf_op jit(solution)/shard_map/ppermute | solution.py:240
  140.3 1.0 shard_map.50.refs_1_
  141.2 1.3 collective-permute-start.13
  142.5 1.3 collective-permute-start.14
  143.9 1.3 collective-permute-start.15
  145.2 7.3 %collective-permute-done.13 = f32[4,32,128]{2,1,0:T(8,128)S(1)} collective-permute-done((f32[4,32,128]{2,1,0:T(8,128)S(1)}, f32[4,32,128]{2,1,0:T(8,128)S(1)}, u32[]{:S(2)}, u32[]{:S(2)}) %collective-permute-start.13) | collective-permute-done | bytes 65568 | tf_op jit(solution)/shard_map/ppermute | solution.py:240
  152.4 1.7 collective-permute-done.14
  154.1 1.8 collective-permute-done.15
  155.9 1.0 shard_map.51.refs_1_
  156.9 1.3 collective-permute-start.16
  158.2 1.3 collective-permute-start.17
  159.5 1.3 collective-permute-start.19
  160.8 2.0 %collective-permute-done.16 = f32[4,32,128]{2,1,0:T(8,128)S(1)} collective-permute-done((f32[4,32,128]{2,1,0:T(8,128)S(1)}, f32[4,32,128]{2,1,0:T(8,128)S(1)}, u32[]{:S(2)}, u32[]{:S(2)}) %collective-permute-start.16) | collective-permute-done | bytes 65568 | tf_op jit(solution)/shard_map/ppermute | solution.py:240
  162.8 7.4 %collective-permute-done.17 = f32[4,32,128]{2,1,0:T(8,128)S(1)} collective-permute-done((f32[4,32,128]{2,1,0:T(8,128)S(1)}, f32[4,32,128]{2,1,0:T(8,128)S(1)}, u32[]{:S(2)}, u32[]{:S(2)}) %collective-permute-start.17) | collective-permute-done | bytes 65568 | tf_op jit(solution)/shard_map/ppermute | solution.py:240
  170.2 2.1 %collective-permute-start.18 = (f32[2,4,32,128]{3,2,1,0:T(8,128)S(1)}, f32[2,4,32,128]{3,2,1,0:T(8,128)S(1)}, u32[]{:S(2)}, u32[]{:S(2)}) collective-permute-start(f32[2,4,32,128]{3,2,1,0:T(8,128)S(1)} %pad_maximum_fusion.11), channel_id=1, source_target_pairs={{0,1},{1,0},{2,3},{3,2},{4,5},{5,4},{6,7},{7,6},{15,14},{14,15},{1... | collective-permute-start | bytes 393224 | tf_op jit(solution)/shard_map/ppermute | solution.py:240
  172.3 1.1 collective-permute-done.18
  173.6 2.6 %shard_map.52 = f32[4,32,128]{2,1,0:T(8,128)S(1)} custom-call(f32[20,32,128]{2,1,0:T(8,128)S(1)} %broadcast_select_fusion.refs_0_, f32[4,32,128]{2,1,0:T(8,128)S(1)} %shard_map.51.refs_1_, f32[20,32,128]{2,1,0:T(8,128)S(1)} %get-tuple-element.23.refs_2_, f32[20,32,128]{2,1,0:T(8,128)S(1)} %get-tuple-element.22.refs_3_), custom_call_target="tpu_custom_call" | custom-call | tf_op jit(solution)/shard_map/pallas_call | solution.py:213
  176.2 22.7 %all_to_all.11 = f32[32,4,128]{2,1,0:T(4,128)S(1)} all-to-all(f32[32,4,128]{2,1,0:T(4,128)S(1)} %copy.13), channel_id=1, replica_groups=mesh['tm'=16,'space'=32] {'space'}, dimensions={0} | all-to-all | bytes 131072 | tf_op jit(solution)/shard_map/all_to_all | solution.py:360
  199.0 1.1 shard_map.53
  (45 shorter events, 0.7 us)
Async XLA Ops:
  0.9 11.5 %collective-permute-start.2 = (f32[128,128]{1,0:T(8,128)S(1)}, f32[128,128]{1,0:T(8,128)S(1)}, u32[]{:S(2)}, u32[]{:S(2)}) collective-permute-start(f32[128,128]{1,0:T(8,128)S(1)} %get-tuple-element.15), channel_id=1, source_target_pairs={{0,1},{1,0},{2,3},{3,2},{4,5},{5,4},{6,7},{7,6},{8,9},{9,8},{10,11... | collective-permute-start | bytes 196616 | tf_op jit(solution)/shard_map/ppermute | solution.py:274
  3.5 8.9 %collective-permute-start.3 = (f32[128,128]{1,0:T(8,128)S(1)}, f32[128,128]{1,0:T(8,128)S(1)}, u32[]{:S(2)}, u32[]{:S(2)}) collective-permute-start(f32[128,128]{1,0:T(8,128)S(1)} %get-tuple-element.16), channel_id=1, source_target_pairs={{1,2},{2,1},{3,4},{4,3},{5,6},{6,5},{7,8},{8,7},{9,10},{10,9},{11,... | collective-permute-start | bytes 196616 | tf_op jit(solution)/shard_map/ppermute | solution.py:271
  6.6 27.1 %collective-permute-start = (f32[1024,128]{1,0:T(8,128)}, f32[1024,128]{1,0:T(8,128)S(1)}, u32[]{:S(2)}, u32[]{:S(2)}) collective-permute-start(f32[1024,128]{1,0:T(8,128)} %bitcast.58), channel_id=1, source_target_pairs={{1,2},{2,1},{3,4},{4,3},{5,6},{6,5},{7,8},{8,7},{9,10},{10,9},{11,... | collective-permute-start | bytes 1572872 | tf_op jit(solution)/shard_map/ppermute | solution.py:271
  9.1 25.4 %collective-permute-start.1 = (f32[1024,128]{1,0:T(8,128)}, f32[1024,128]{1,0:T(8,128)}, u32[]{:S(2)}, u32[]{:S(2)}) collective-permute-start(f32[1024,128]{1,0:T(8,128)} %bitcast.59), channel_id=1, source_target_pairs={{0,1},{1,0},{2,3},{3,2},{4,5},{5,4},{6,7},{7,6},{8,9},{9,8},{10,11... | collective-permute-start | bytes 1572872 | tf_op jit(solution)/shard_map/ppermute | solution.py:274
  11.0 1.0 copy-start
  12.4 11.0 %collective-permute-start.4 = (f32[2,128,128]{2,1,0:T(8,128)S(1)}, f32[2,128,128]{2,1,0:T(8,128)S(1)}, u32[]{:S(2)}, u32[]{:S(2)}) collective-permute-start(f32[2,128,128]{2,1,0:T(8,128)S(1)} %pad_maximum_fusion.10), channel_id=1, source_target_pairs={{0,32},{32,0},{64,96},{96,64},{128,160},{160,128},{192,224},{224,1... | collective-permute-start | bytes 393224 | tf_op jit(solution)/shard_map/ppermute | solution.py:287
  20.0 5.5 %copy-start.2 = (f32[1,2,512,128]{3,2,1,0:T(8,128)S(1)}, f32[1,2,512,128]{3,2,1,0:T(8,128)}, u32[]{:S(2)}) copy-start(f32[1,2,512,128]{3,2,1,0:T(8,128)} %param.4) | copy-start | bytes 1572868
  23.4 2.0 copy-start.5
  23.4 10.2 %collective-permute-start.5 = (f32[2,256,128]{2,1,0:T(8,128)S(1)}, f32[2,256,128]{2,1,0:T(8,128)S(1)}, u32[]{:S(2)}, u32[]{:S(2)}) collective-permute-start(f32[2,256,128]{2,1,0:T(8,128)S(1)} %pad_maximum_fusion.8), channel_id=1, source_target_pairs={{0,64},{32,96},{64,0},{96,32},{128,192},{160,224},{192,128},{224,1... | collective-permute-start | bytes 786440 | tf_op jit(solution)/shard_map/ppermute | solution.py:287
  33.6 1.2 copy-start.1
  33.7 0.8 copy-start.3
  34.9 1.0 copy-start.4
  38.4 12.0 %collective-permute-start.6 = (f32[1152,128]{1,0:T(8,128)S(1)}, f32[1152,128]{1,0:T(8,128)}, u32[]{:S(2)}, u32[]{:S(2)}) collective-permute-start(f32[1152,128]{1,0:T(8,128)S(1)} %shard_map.48.refs_3_), channel_id=1, source_target_pairs={{1,2},{2,1},{3,4},{4,3},{5,6},{6,5},{7,8},{8,7},{9,10},{10,9},{11,... | collective-permute-start | bytes 1769480 | tf_op jit(solution)/shard_map/ppermute | solution.py:271
  42.7 7.7 %collective-permute-start.7 = (f32[1152,128]{1,0:T(8,128)S(1)}, f32[1152,128]{1,0:T(8,128)}, u32[]{:S(2)}, u32[]{:S(2)}) collective-permute-start(f32[1152,128]{1,0:T(8,128)S(1)} %shard_map.48.refs_3_), channel_id=1, source_target_pairs={{0,1},{1,0},{2,3},{3,2},{4,5},{5,4},{6,7},{7,6},{8,9},{9,8},{10,11... | collective-permute-start | bytes 1769480 | tf_op jit(solution)/shard_map/ppermute | solution.py:274
  121.4 8.0 %collective-permute-start.12 = (f32[10,32,128]{2,1,0:T(8,128)S(1)}, f32[10,32,128]{2,1,0:T(8,128)S(1)}, u32[]{:S(2)}, u32[]{:S(2)}) collective-permute-start(f32[10,32,128]{2,1,0:T(8,128)S(1)} %slice.129), channel_id=1, source_target_pairs={{0,32},{32,0},{64,96},{96,64},{128,160},{160,128},{192,224},{224,1... | collective-permute-start | bytes 491528 | tf_op jit(solution)/shard_map/ppermute | solution.py:322
  123.6 10.6 %collective-permute-start.8 = (f32[12,32,128]{2,1,0:T(8,128)S(1)}, f32[12,32,128]{2,1,0:T(8,128)S(1)}, u32[]{:S(2)}, u32[]{:S(2)}) collective-permute-start(f32[12,32,128]{2,1,0:T(8,128)S(1)} %slice.125), channel_id=1, source_target_pairs={{128,0},{129,1},{130,2},{131,3},{132,4},{133,5},{134,6},{135,7},{1... | collective-permute-start | bytes 589832 | tf_op jit(solution)/shard_map/ppermute | solution.py:240
  124.9 9.2 %collective-permute-start.10 = (f32[8,32,128]{2,1,0:T(8,128)S(1)}, f32[8,32,128]{2,1,0:T(8,128)S(1)}, u32[]{:S(2)}, u32[]{:S(2)}) collective-permute-start(f32[8,32,128]{2,1,0:T(8,128)S(1)} %slice.127), channel_id=1, source_target_pairs={{64,0},{65,1},{66,2},{67,3},{68,4},{69,5},{70,6},{71,7},{79,15},{7... | collective-permute-start | bytes 393224 | tf_op jit(solution)/shard_map/ppermute | solution.py:240
  126.2 7.9 %collective-permute-start.11 = (f32[6,32,128]{2,1,0:T(8,128)S(1)}, f32[6,32,128]{2,1,0:T(8,128)S(1)}, u32[]{:S(2)}, u32[]{:S(2)}) collective-permute-start(f32[6,32,128]{2,1,0:T(8,128)S(1)} %slice.128), channel_id=1, source_target_pairs={{32,0},{33,1},{34,2},{35,3},{36,4},{37,5},{38,6},{39,7},{47,15},{4... | collective-permute-start | bytes 294920 | tf_op jit(solution)/shard_map/ppermute | solution.py:240
  129.4 10.8 %collective-permute-start.9 = (f32[10,32,128]{2,1,0:T(8,128)S(1)}, f32[10,32,128]{2,1,0:T(8,128)S(1)}, u32[]{:S(2)}, u32[]{:S(2)}) collective-permute-start(f32[10,32,128]{2,1,0:T(8,128)S(1)} %get-tuple-element.21), channel_id=1, source_target_pairs={{96,0},{97,1},{98,2},{99,3},{100,4},{101,5},{102,6},{103,7},{111,1... | collective-permute-start | bytes 491528 | tf_op jit(solution)/shard_map/ppermute | solution.py:240
  141.2 11.2 %collective-permute-start.13 = (f32[4,32,128]{2,1,0:T(8,128)S(1)}, f32[4,32,128]{2,1,0:T(8,128)S(1)}, u32[]{:S(2)}, u32[]{:S(2)}) collective-permute-start(f32[4,32,128]{2,1,0:T(8,128)S(1)} %shard_map.50.refs_1_), channel_id=1, source_target_pairs={{128,1},{129,0},{130,3},{131,2},{132,5},{133,4},{134,7},{135,6},{1... | collective-permute-start | bytes 196616 | tf_op jit(solution)/shard_map/ppermute | solution.py:240
  142.5 11.6 %collective-permute-start.14 = (f32[4,32,128]{2,1,0:T(8,128)S(1)}, f32[4,32,128]{2,1,0:T(8,128)S(1)}, u32[]{:S(2)}, u32[]{:S(2)}) collective-permute-start(f32[4,32,128]{2,1,0:T(8,128)S(1)} %shard_map.50.refs_1_), channel_id=1, source_target_pairs={{129,2},{130,1},{131,4},{132,3},{133,6},{134,5},{135,15},{143,7},{... | collective-permute-start | bytes 196616 | tf_op jit(solution)/shard_map/ppermute | solution.py:240
  143.9 12.0 %collective-permute-start.15 = (f32[4,32,128]{2,1,0:T(8,128)S(1)}, f32[4,32,128]{2,1,0:T(8,128)S(1)}, u32[]{:S(2)}, u32[]{:S(2)}) collective-permute-start(f32[4,32,128]{2,1,0:T(8,128)S(1)} %shard_map.50.refs_1_), channel_id=1, source_target_pairs={{128,0},{129,1},{130,2},{131,3},{132,4},{133,5},{134,6},{135,7},{1... | collective-permute-start | bytes 196616 | tf_op jit(solution)/shard_map/ppermute | solution.py:240
  156.9 5.9 %collective-permute-start.16 = (f32[4,32,128]{2,1,0:T(8,128)S(1)}, f32[4,32,128]{2,1,0:T(8,128)S(1)}, u32[]{:S(2)}, u32[]{:S(2)}) collective-permute-start(f32[4,32,128]{2,1,0:T(8,128)S(1)} %shard_map.51.refs_1_), channel_id=1, source_target_pairs={{256,0},{257,1},{258,2},{259,3},{260,4},{261,5},{262,6},{263,7},{2... | collective-permute-start | bytes 196616 | tf_op jit(solution)/shard_map/ppermute | solution.py:240
  158.2 12.0 %collective-permute-start.17 = (f32[4,32,128]{2,1,0:T(8,128)S(1)}, f32[4,32,128]{2,1,0:T(8,128)S(1)}, u32[]{:S(2)}, u32[]{:S(2)}) collective-permute-start(f32[4,32,128]{2,1,0:T(8,128)S(1)} %shard_map.51.refs_1_), channel_id=1, source_target_pairs={{257,2},{258,1},{259,4},{260,3},{261,6},{262,5},{263,15},{271,7},{... | collective-permute-start | bytes 196616 | tf_op jit(solution)/shard_map/ppermute | solution.py:240
  159.5 12.8 %collective-permute-start.19 = (f32[4,32,128]{2,1,0:T(8,128)S(1)}, f32[4,32,128]{2,1,0:T(8,128)S(1)}, u32[]{:S(2)}, u32[]{:S(2)}) collective-permute-start(f32[4,32,128]{2,1,0:T(8,128)S(1)} %shard_map.51.refs_1_), channel_id=1, source_target_pairs={{256,2},{258,4},{260,6},{262,15},{271,13},{269,11},{267,9},{265,16... | collective-permute-start | bytes 196616 | tf_op jit(solution)/shard_map/ppermute | solution.py:240
  170.2 3.2 %collective-permute-start.18 = (f32[2,4,32,128]{3,2,1,0:T(8,128)S(1)}, f32[2,4,32,128]{3,2,1,0:T(8,128)S(1)}, u32[]{:S(2)}, u32[]{:S(2)}) collective-permute-start(f32[2,4,32,128]{3,2,1,0:T(8,128)S(1)} %pad_maximum_fusion.11), channel_id=1, source_target_pairs={{0,1},{1,0},{2,3},{3,2},{4,5},{5,4},{6,7},{7,6},{15,14},{14,15},{1... | collective-permute-start | bytes 393224 | tf_op jit(solution)/shard_map/ppermute | solution.py:240
